TPU v7x, 32 devices: a whole 2x2x4 slice. The times are simulated.
32 devices in a mesh: space: 8 (over z, x), slab: 4 (over y, core).
Axes of the slice: x: 2, y: 2, z: 4, core: 2. Of those that a mesh axis runs over, the one named last changes fastest.
Arguments:
- tokens: float32 [8192, 512], P(('space', 'slab')), may hold values from -6 to 6
- gain: float32 [512], replicated, may hold values from 0.25 to 1.75
- query_weight: float32 [512, 512], replicated, may hold values from -3.1 to 3.1
- key_weight: float32 [512, 512], replicated, may hold values from -0.25 to 0.25
- value_weight: float32 [512, 512], replicated, may hold values from -0.25 to 0.25
- output_weight: float32 [512, 512], replicated, may hold values from -0.25 to 0.25
- neighbour_list: int32 [64, 3], P(('space', 'slab')), may hold values from 0 to 5, as said below
- neighbour_count: int32 [64], P(('space', 'slab')), may hold values from 1 to 3, as said below
- cotangent: float32 [8192, 512], P(('space', 'slab')), may hold values from -6 to 6
Outputs:
- result: float32 [8192, 512], P(('space', 'slab'))
- d_tokens: float32 [8192, 512], P(('space', 'slab'))
- d_gain: float32 [512], replicated
- d_query: float32 [512, 512], replicated
- d_key: float32 [512, 512], replicated
- d_value: float32 [512, 512], replicated
- d_output: float32 [512, 512], replicated
Inputs may be any that keep to these rules, and one draw needn't show every extreme that they name: `neighbour_list`: each row holds distinct window indices, never the patch's own index 2 + p % 2. Only the first neighbour_count[p] entries of a row are live.
All inputs are finite; a program needn't handle non-finite values.
Results may differ from a plain program's by a relative error of at most 0.0003.
Values sent between devices are 32-bit elements; how exact they have to be, the bound alone decides.
No kernel may reach another device: no remote copies, remote signals or barrier semaphores. Data moves between devices by JAX's collectives and lax.ppermute only.
A program may use at most 128 MiB of HBM per device.

v0:
```python
import jax
import jax.numpy as jnp
from jax import lax
from jax.sharding import PartitionSpec as P

HEADS = 8
PT = 128


def extended(cells, sides, width):
    for axis, dim in sides:
        count = lax.axis_size(axis)
        head = lax.slice_in_dim(cells, 0, width, axis=dim)
        tail = lax.slice_in_dim(cells, cells.shape[dim] - width, cells.shape[dim], axis=dim)
        cells = jnp.concatenate(
            [
                lax.ppermute(tail, axis, [(i, (i + 1) % count) for i in range(count)]),
                cells,
                lax.ppermute(head, axis, [((i + 1) % count, i) for i in range(count)]),
            ],
            axis=dim,
        )
    return cells


def passed_along(value, axis, steps):
    count = lax.axis_size(axis)
    pairs = [(source, (source + steps) % count) for source in range(count)]
    return lax.ppermute(value, axis, pairs)


def matmul(left, right):
    return jnp.dot(left, right, precision=lax.Precision.HIGHEST, preferred_element_type=jnp.float32)


def normalize(tokens, gain):
    row_mean = jnp.mean(tokens, axis=1, keepdims=True)
    centred = tokens - row_mean
    variance = jnp.mean(centred * centred, axis=1, keepdims=True)
    return centred * lax.rsqrt(variance + 1e-05) * gain[None, :]


def attention(query, key_win, value_win, block_index, live_mask):
    patch_count = block_index.shape[0]
    model_width = query.shape[1]
    head_dim = model_width // HEADS
    picked_keys = key_win.reshape(-1, PT, model_width)[block_index].reshape(
        patch_count, -1, HEADS, head_dim
    )
    picked_values = value_win.reshape(-1, PT, model_width)[block_index].reshape(
        patch_count, -1, HEADS, head_dim
    )
    query_blocks = query.reshape(patch_count, PT, HEADS, head_dim)
    scores = jnp.einsum(
        "pqhd,pkhd->phqk", query_blocks, picked_keys, precision=lax.Precision.HIGHEST
    ) * head_dim ** (-0.5)
    key_mask = jnp.repeat(live_mask, PT, axis=1)
    scores = jnp.where(key_mask[:, None, None, :], scores, -1e30)
    row_max = jnp.max(scores, axis=3, keepdims=True)
    weights = jnp.exp(scores - row_max)
    probability = weights / jnp.sum(weights, axis=3, keepdims=True)
    mixed = jnp.einsum(
        "phqk,pkhd->pqhd", probability, picked_values, precision=lax.Precision.HIGHEST
    )
    return mixed.reshape(patch_count * PT, model_width)


def body(
    tokens,
    gain,
    query_weight,
    key_weight,
    value_weight,
    output_weight,
    neighbour_list,
    neighbour_count,
    cotangent,
):
    row_count = tokens.shape[0]
    patch_count = neighbour_list.shape[0]
    hidden, norm_pull = jax.vjp(normalize, tokens, gain)
    query = matmul(hidden, query_weight)
    own_blocks = patch_count + jnp.arange(patch_count, dtype=jnp.int32)
    block_index = jnp.concatenate([own_blocks[:, None], neighbour_list], axis=1)
    slot_ids = jnp.arange(neighbour_list.shape[1], dtype=jnp.int32)
    live_mask = jnp.concatenate(
        [jnp.ones((patch_count, 1), dtype=bool), slot_ids[None, :] < neighbour_count[:, None]],
        axis=1,
    )
    hidden_win = extended(hidden, (("space", 0),), row_count)
    key_win = matmul(hidden_win, key_weight)
    value_win = matmul(hidden_win, value_weight)

    def local_attention(query_rows, key_part, value_part):
        return attention(query_rows, key_part, value_part, block_index, live_mask)

    mixed, attention_pull = jax.vjp(local_attention, query, key_win, value_win)
    result = matmul(mixed, output_weight) + tokens
    grad_output = matmul(mixed.T, cotangent)
    d_mixed = matmul(cotangent, output_weight.T)
    d_queries, d_key_win, d_value_win = attention_pull(d_mixed)
    grad_query = matmul(hidden.T, d_queries)
    grad_key = matmul(hidden_win.T, d_key_win)
    grad_value = matmul(hidden_win.T, d_value_win)
    d_hidden_win = matmul(d_key_win, key_weight.T) + matmul(d_value_win, value_weight.T)
    d_owned = d_hidden_win[row_count : 2 * row_count]
    for offset, halo_part in ((-1, d_hidden_win[:row_count]), (1, d_hidden_win[2 * row_count :])):
        d_owned = d_owned + passed_along(halo_part, "space", offset)
    d_hidden = matmul(d_queries, query_weight.T) + d_owned
    d_norm, grad_gain = norm_pull(d_hidden)
    d_tokens = d_norm + cotangent
    grad_gain, grad_query, grad_key, grad_value, grad_output = lax.psum(
        (grad_gain, grad_query, grad_key, grad_value, grad_output), ("space", "slab")
    )
    return (result, d_tokens, grad_gain, grad_query, grad_key, grad_value, grad_output)


def solution(mesh):
    return jax.shard_map(
        body,
        mesh=mesh,
        in_specs=(
            P(("space", "slab"), None),
            P(),
            P(),
            P(),
            P(),
            P(),
            P(("space", "slab"), None),
            P(("space", "slab")),
            P(("space", "slab"), None),
        ),
        out_specs=(P(("space", "slab"), None), P(("space", "slab"), None), P(), P(), P(), P(), P()),
        check_vma=False,
    )
```

profile of v0, /device:TPU:0, one launch (start us, length us, event | category | flops | bytes accessed | tf_op | source)
XLA Modules:
  0.0 321.7 jit_solution(4198755016415703508)
XLA Ops:
  11.0 3.0 collective-permute-start
  14.0 3.1 collective-permute-start.1
  17.4 3.0 fusion.61
  25.0 11.4 %collective-permute-done = f32[256,512]{1,0:T(8,128)S(1)} collective-permute-done((f32[256,512]{1,0:T(8,128)S(1)}, f32[256,512]{1,0:T(8,128)S(1)}, u32[]{:S(2)}, u32[]{:S(2)}) %collective-permute-start) | collective-permute-done | bytes 524320 | tf_op jit(solution)/shard_map/ppermute | solution.py:17
  38.7 3.8 %fusion.42 = f32[768,512]{1,0:T(8,128)S(1)} fusion(f32[512,512]{1,0:T(8,128)S(1)} %copy-done, f32[256,512]{1,0:T(8,128)} %collective-permute-done.1, f32[256,512]{1,0:T(8,128)S(1)} %multiply_multiply_fusion, f32[256,512]{1,0:T(8,128)} %copy-done.6), kind=kOutput, calls=%fused_computation.61 | convolution fusion | flops 2416705536 | bytes 4194304 | tf_op jit(solution)/shard_map/dot_general | solution.py:33
  44.6 4.5 %reshape.227 = f32[2,512,8,64]{3,2,1,0:T(8,128)} reshape(f32[8,128,512]{2,1,0:T(8,128)} %gather_fusion.1) | data formatting | bytes 4194304 | tf_op jit(solution)/shard_map/jvp()/reshape | solution.py:47
  49.1 3.8 %copy.44 = f32[2,512,8,64]{1,3,2,0:T(8,128)} copy(f32[2,512,8,64]{3,2,1,0:T(8,128)} %reshape.227) | data formatting | bytes 4194304 | tf_op jit(solution)/shard_map/jvp()/reshape | solution.py:47
  53.0 5.6 %fusion.1 = (f32[2,8,128]{2,1,0:T(8,128)S(1)}, f32[2,8,128,512]{3,2,1,0:T(8,128)S(1)}) fusion(pred[2,512]{1,0:T(4,128)(4,1)S(1)} %bitcast.85, f32[2,512,8,64]{1,3,2,0:T(8,128)} %copy.44, f32[2,128,8,64]{1,0,3,2:T(2,128)S(1)} %copy-done.9), kind=kOutput, calls=%fused_computation.11 | convolution fusion | flops 808450048 | bytes 6824960 | tf_op jit(solution)/shard_map/jvp(pqhd,pkhd->phqk)/dot_general | solution.py:54
  61.1 3.7 %fusion.43 = f32[768,512]{1,0:T(8,128)S(1)} fusion(f32[512,512]{1,0:T(8,128)S(1)} %copy-done.20, f32[256,512]{1,0:T(8,128)} %collective-permute-done.1, f32[256,512]{1,0:T(8,128)S(1)} %multiply_multiply_fusion, f32[256,512]{1,0:T(8,128)S(1)} %copy-done.7), kind=kOutput, calls=%fused_computation.62 | convolution fusion | flops 2416705536 | bytes 4194304 | tf_op jit(solution)/shard_map/dot_general | solution.py:33
  66.8 4.4 %reshape.226 = f32[2,512,8,64]{3,2,1,0:T(8,128)} reshape(f32[8,128,512]{2,1,0:T(8,128)} %gather_fusion) | data formatting | bytes 4194304 | tf_op jit(solution)/shard_map/jvp()/reshape | solution.py:50
  71.2 4.0 %copy.45 = f32[2,512,8,64]{1,3,2,0:T(8,128)} copy(f32[2,512,8,64]{3,2,1,0:T(8,128)} %reshape.226) | data formatting | bytes 4194304 | tf_op jit(solution)/shard_map/jvp()/reshape | solution.py:50
  75.3 7.0 %fusion.14 = f32[2,512,8,64]{1,3,2,0:T(8,128)} fusion(f32[2,8,128]{2,1,0:T(8,128)S(1)} %fusion.39, f32[2,8,64,128]{3,0,2,1:T(2,128)S(1)} %bitcast.83, f32[2,8,128,512]{3,2,1,0:T(8,128)} %copy-done.1, f32[2,8,128]{2,1,0:T(8,128)S(1)} %get-tuple-element.22, pred[2,512]{1,0:T(4,128)(4,1)S(1)} %bitcast.87), kind=kOutput, calls=%fused_computation.25 | convolution fusion | flops 809500672 | bytes 6833152 | tf_op jit(solution)/shard_map/transpose(jvp(phqk,pkhd->pqhd))/dot_general | solution.py:62
  82.2 5.4 %convert_reduce_fusion = (f32[2,8,128]{2,1,0:T(8,128)S(1)}, pred[2,8,128,512]{3,2,1,0:T(32,128)(4,1)S(1)}, f32[2,8,128]{2,1,0:T(8,128)S(1)}, f32[2,8,128,512]{3,2,1,0:T(8,128)S(1)}) fusion(f32[2,8,128]{2,1,0:T(8,128)S(1)} %get-tuple-element.22, f32[2,8,128,512]{3,2,1,0:T(8,128)S(1)} %copy-done.2, pred[2,512]{1,0:T(4,128)(4,1)S(1)} %bitcast.88, ...), kind=kOutput, calls=%fused_computation.5 | convolution fusion | flops 814739456 | bytes 12092416 | tf_op jit(solution)/shard_map/transpose(jvp(phqk,pkhd->pqhd))/dot_general | solution.py:62
  87.6 2.6 fusion.58
  90.2 5.7 %fusion.17 = f32[2,128,8,64]{1,3,2,0:T(8,128)S(1)} fusion(f32[2,512,8,64]{1,3,2,0:T(8,128)S(1)} %copy-done.4, f32[2,8,128,512]{3,2,1,0:T(8,128)S(1)} %get-tuple-element.16, pred[2,8,128,512]{3,2,1,0:T(32,128)(4,1)S(1)} %get-tuple-element.18, f32[2,8,128]{2,1,0:T(8,128)S(1)} %negate_divide_fusion, pred[2,512]{1,0:T(4,128)(4,1)S(1)} %bitcast.90), kind=kOutput, calls=%fused_computation.31 | convolution fusion | flops 809500672 | bytes 7873536 | tf_op jit(solution)/shard_map/transpose(jvp(pqhd,pkhd->phqk))/dot_general | solution.py:54
  95.9 4.7 %fusion.15 = f32[2,512,8,64]{1,3,2,0:T(8,128)} fusion(f32[2,8,128,512]{3,2,1,0:T(8,128)S(1)} %get-tuple-element.16, pred[2,8,128,512]{3,2,1,0:T(32,128)(4,1)S(1)} %get-tuple-element.18, f32[2,8,128]{2,1,0:T(8,128)S(1)} %negate_divide_fusion, pred[2,512]{1,0:T(4,128)(4,1)S(1)} %bitcast.91, f32[2,128,8,64]{1,0,3,2:T(2,128)S(1)} %copy-done.10), kind=kOutput, calls=%fused_computation.26 | convolution fusion | flops 809500672 | bytes 7873536 | tf_op jit(solution)/shard_map/transpose(jvp(pqhd,pkhd->phqk))/dot_general | solution.py:54
  100.6 5.4 %fusion.16 = f32[2,128,8,64]{1,3,2,0:T(8,128)S(1)} fusion(f32[2,512,8,64]{1,3,2,0:T(8,128)S(1)} %copy-done.21, f32[2,8,128]{2,1,0:T(8,128)S(1)} %fusion.39, f32[2,8,128,512]{3,2,1,0:T(8,128)S(1)} %copy-done.2, f32[2,8,128]{2,1,0:T(8,128)S(1)} %get-tuple-element.22, pred[2,512]{1,0:T(4,128)(4,1)S(1)} %bitcast.92), kind=kOutput, calls=%fused_computation.29 | convolution fusion | flops 809500672 | bytes 6833152 | tf_op jit(solution)/shard_map/jvp(phqk,pkhd->pqhd)/dot_general | solution.py:62
  107.4 2.8 fusion.18
  110.2 3.8 %copy.65 = f32[2,512,8,64]{3,2,1,0:T(8,128)} copy(f32[2,512,8,64]{1,3,2,0:T(8,128)} %fusion.14) | data formatting | bytes 4194304 | tf_op jit(solution)/shard_map/transpose(jvp())/reshape | solution.py:50
  114.0 4.8 %reshape.225 = f32[8,128,512]{2,1,0:T(8,128)} reshape(f32[2,512,8,64]{3,2,1,0:T(8,128)} %copy.65) | data formatting | bytes 4194304 | tf_op jit(solution)/shard_map/transpose(jvp())/reshape | solution.py:50
  118.8 3.8 %copy.64 = f32[2,512,8,64]{3,2,1,0:T(8,128)} copy(f32[2,512,8,64]{1,3,2,0:T(8,128)} %fusion.15) | data formatting | bytes 4194304 | tf_op jit(solution)/shard_map/transpose(jvp())/reshape | solution.py:47
  122.6 4.9 %reshape.224 = f32[8,128,512]{2,1,0:T(8,128)} reshape(f32[2,512,8,64]{3,2,1,0:T(8,128)} %copy.64) | data formatting | bytes 4194304 | tf_op jit(solution)/shard_map/transpose(jvp())/reshape | solution.py:47
  130.1 3.3 %scatter_fusion = f32[6,128,512]{2,1,0:T(8,128)S(1)} fusion(f32[6,128,512]{2,1,0:T(8,128)S(1)} %broadcast.104.clone, s32[8]{0:T(128)S(1)} %reshape.186, f32[8,128,512]{2,1,0:T(8,128)} %reshape.224), kind=kCustom, calls=%fused_computation.2 | custom fusion | flops 524288 | bytes 6291488 | tf_op jit(solution)/shard_map/transpose(jvp())/scatter-add | solution.py:47
  134.6 3.8 %fusion.63 = f32[768,512]{1,0:T(8,128)} fusion(f32[768,512]{1,0:T(8,128)S(1)} %bitcast.75, f32[512,512]{1,0:T(8,128)S(1)} %copy-done), kind=kOutput, calls=%fused_computation.93 | convolution fusion | flops 2415919104 | bytes 4194304 | tf_op jit(solution)/shard_map/dot_general | solution.py:33
  138.6 3.6 %scatter_fusion.1 = f32[6,128,512]{2,1,0:T(8,128)S(1)} fusion(f32[6,128,512]{2,1,0:T(8,128)S(1)} %broadcast.104.clone.1, s32[8]{0:T(128)S(1)} %reshape.186, f32[8,128,512]{2,1,0:T(8,128)} %reshape.225), kind=kCustom, calls=%fused_computation.3 | custom fusion | flops 524288 | bytes 6291488 | tf_op jit(solution)/shard_map/transpose(jvp())/scatter-add | solution.py:50
  142.2 5.4 %fusion.41 = f32[512,512]{1,0:T(8,128)} fusion(f32[768,512]{1,0:T(8,128)} %bitcast.76, f32[256,512]{1,0:T(8,128)} %collective-permute-done.1, f32[256,512]{1,0:T(8,128)S(1)} %multiply_multiply_fusion, f32[256,512]{1,0:T(8,128)} %copy-done.6), kind=kOutput, calls=%fused_computation.60 | convolution fusion | flops 2416705536 | bytes 4194304 | tf_op jit(solution)/shard_map/dot_general | solution.py:33
  147.6 4.7 %fusion.40 = f32[512,512]{1,0:T(8,128)} fusion(f32[768,512]{1,0:T(8,128)S(1)} %bitcast.73, f32[256,512]{1,0:T(8,128)} %collective-permute-done.1, f32[256,512]{1,0:T(8,128)S(1)} %multiply_multiply_fusion, f32[256,512]{1,0:T(8,128)S(1)} %copy-done.8), kind=kOutput, calls=%fused_computation.59 | convolution fusion | flops 2416705536 | bytes 4194304 | tf_op jit(solution)/shard_map/dot_general | solution.py:33
  152.4 4.5 %convolution_add_fusion = f32[768,512]{1,0:T(8,128)S(1)} fusion(f32[768,512]{1,0:T(8,128)} %fusion.63, f32[768,512]{1,0:T(8,128)S(1)} %bitcast.74, f32[512,512]{1,0:T(8,128)} %param.13), kind=kOutput, calls=%fused_computation.28 | convolution fusion | flops 2416312320 | bytes 5767168 | tf_op jit(solution)/shard_map/dot_general | solution.py:33
  157.1 4.1 %collective-permute-start.2 = (f32[256,512]{1,0:T(8,128)S(1)}, f32[256,512]{1,0:T(8,128)S(1)}, u32[]{:S(2)}, u32[]{:S(2)}) collective-permute-start(f32[256,512]{1,0:T(8,128)S(1)} %get-tuple-element.20), channel_id=1, source_target_pairs={{0,28},{4,0},{8,4},{12,8},{16,12},{20,16},{24,20},{28,24},{1,29},{... | collective-permute-start | bytes 1572872 | tf_op jit(solution)/shard_map/ppermute | solution.py:29
  163.0 26.3 %collective-permute-done.2 = f32[256,512]{1,0:T(8,128)S(1)} collective-permute-done((f32[256,512]{1,0:T(8,128)S(1)}, f32[256,512]{1,0:T(8,128)S(1)}, u32[]{:S(2)}, u32[]{:S(2)}) %collective-permute-start.2) | collective-permute-done | bytes 524320 | tf_op jit(solution)/shard_map/ppermute | solution.py:29
  191.4 41.4 %psum.35 = f32[512]{0:T(512)} all-reduce(f32[512]{0:T(512)S(1)} %get-tuple-element.7), channel_id=1, replica_groups=mesh['space'=8,'slab'=4] {'space','slab'}, use_global_device_ids=true, to_apply=%region_12.13 | all-reduce | flops 512 | bytes 4096 | tf_op jit(solution)/shard_map/psum | solution.py:112
  234.1 75.2 %all-reduce.4.cloned.1.call-done = (f32[512,512]{1,0:T(8,128)}, f32[512,512]{1,0:T(8,128)}, f32[512,512]{1,0:T(8,128)}, f32[512,512]{1,0:T(8,128)}) async-done(((f32[512,512]{1,0:T(8,128)}, f32[512,512]{1,0:T(8,128)}, f32[512,512]{1,0:T(8,128)}, f32[512,512]{1,0:T(8,128)}), (f32[512,512]{1,0:T(8,128)}, f32[512,512]{1,0:T(8,128)}, f32[512,512]{1,0:T(8,128)}, ...) | async-done | bytes 4194320 | tf_op jit(solution)/shard_map/psum | solution.py:112
  (102 shorter events, 33.4 us)
Async XLA Ops:
  7.2 31.6 %copy-start = (f32[512,512]{1,0:T(8,128)S(1)}, f32[512,512]{1,0:T(8,128)}, u32[]{:S(2)}) copy-start(f32[512,512]{1,0:T(8,128)} %param.12) | copy-start | bytes 3145732
  7.2 10.0 %copy-start.27 = (s32[2,3]{1,0:T(2,128)S(1)}, s32[2,3]{1,0:T(2,128)}, u32[]{:S(2)}) copy-start(s32[2,3]{1,0:T(2,128)} %param.15) | copy-start | bytes 76
  7.2 302.1 %all-reduce.4.cloned.1.call-start = ((), (), s32[]{:S(2)}) async-start(), calls=%async_computation | async-start | bytes 8388608 | tf_op jit(solution)/shard_map/psum | solution.py:112
  9.7 11.7 %copy-start.28 = (s32[2]{0:T(128)S(1)}, s32[2]{0:T(128)}, u32[]{:S(2)}) copy-start(s32[2]{0:T(128)} %param.16) | copy-start | bytes 28
  9.8 12.0 %copy-start.15 = (f32[256,512]{1,0:T(8,128)S(1)}, f32[256,512]{1,0:T(8,128)}, u32[]{:S(2)}) copy-start(f32[256,512]{1,0:T(8,128)} %param.17) | copy-start | bytes 1572868
  11.0 25.4 %collective-permute-start = (f32[256,512]{1,0:T(8,128)S(1)}, f32[256,512]{1,0:T(8,128)S(1)}, u32[]{:S(2)}, u32[]{:S(2)}) collective-permute-start(f32[256,512]{1,0:T(8,128)S(1)} %multiply_multiply_fusion), channel_id=1, source_target_pairs={{0,4},{4,8},{8,12},{12,16},{16,20},{20,24},{24,28},{28,0},{1,5},{5... | collective-permute-start | bytes 1572872 | tf_op jit(solution)/shard_map/ppermute | solution.py:17
  14.0 24.7 %collective-permute-start.1 = (f32[256,512]{1,0:T(8,128)S(1)}, f32[256,512]{1,0:T(8,128)}, u32[]{:S(2)}, u32[]{:S(2)}) collective-permute-start(f32[256,512]{1,0:T(8,128)S(1)} %multiply_multiply_fusion), channel_id=1, source_target_pairs={{4,0},{8,4},{12,8},{16,12},{20,16},{24,20},{28,24},{0,28},{5,1},{9... | collective-permute-start | bytes 1572872 | tf_op jit(solution)/shard_map/ppermute | solution.py:19
  49.1 3.8 %copy-start.9 = (f32[2,128,8,64]{1,0,3,2:T(2,128)S(1)}, f32[2,128,8,64]{1,0,3,2:T(2,128)}, u32[]{:S(2)}) copy-start(f32[2,128,8,64]{1,0,3,2:T(2,128)} %reshape.174) | copy-start | bytes 1572868
  58.6 2.0 copy-start.1
  58.6 2.0 copy-start.7
  58.6 2.5 copy-start.20
  71.2 4.0 %copy-start.25 = (f32[2,128,8,64]{1,0,3,2:T(2,128)S(1)}, f32[2,128,8,64]{1,0,3,2:T(2,128)}, u32[]{:S(2)}) copy-start(f32[2,128,8,64]{1,0,3,2:T(2,128)} %reshape.178) | copy-start | bytes 1572868
  75.2 7.0 %copy-start.2 = (f32[2,8,128,512]{3,2,1,0:T(8,128)S(1)}, f32[2,8,128,512]{3,2,1,0:T(8,128)}, u32[]{:S(2)}) copy-start(f32[2,8,128,512]{3,2,1,0:T(8,128)} %copy-done.1) | copy-start | bytes 12582916
  75.2 7.0 %copy-start.21 = (f32[2,512,8,64]{1,3,2,0:T(8,128)S(1)}, f32[2,512,8,64]{1,3,2,0:T(8,128)}, u32[]{:S(2)}) copy-start(f32[2,512,8,64]{1,3,2,0:T(8,128)} %copy.45) | copy-start | bytes 6291460
  87.6 2.6 copy-start.4
  90.2 5.7 %copy-start.10 = (f32[2,128,8,64]{1,0,3,2:T(2,128)S(1)}, f32[2,128,8,64]{1,0,3,2:T(2,128)}, u32[]{:S(2)}) copy-start(f32[2,128,8,64]{1,0,3,2:T(2,128)} %reshape.174) | copy-start | bytes 1572868
  122.6 5.3 %copy-start.16 = (f32[256,512]{1,0:T(8,128)S(1)}, f32[256,512]{1,0:T(8,128)}, u32[]{:S(2)}) copy-start(f32[256,512]{1,0:T(8,128)} %param.17) | copy-start | bytes 1572868
  127.9 2.0 copy-start.13
  133.4 1.2 copy-start.3
  142.2 5.4 %copy-start.8 = (f32[256,512]{1,0:T(8,128)S(1)}, f32[256,512]{1,0:T(8,128)}, u32[]{:S(2)}) copy-start(f32[256,512]{1,0:T(8,128)} %copy-done.6) | copy-start | bytes 1572868
  152.4 8.8 %copy-start.19 = (f32[512,512]{1,0:T(8,128)S(1)}, f32[512,512]{1,0:T(8,128)}, u32[]{:S(2)}) copy-start(f32[512,512]{1,0:T(8,128)} %param.14) | copy-start | bytes 3145732
  156.9 4.2 %copy-start.5 = (f32[256,512]{1,0:T(8,128)S(1)}, f32[256,512]{1,0:T(8,128)}, u32[]{:S(2)}) copy-start(f32[256,512]{1,0:T(8,128)} %param.9) | copy-start | bytes 1572868
  156.9 4.2 %copy-start.14 = (f32[2,128,8,64]{1,0,3,2:T(2,128)S(1)}, f32[2,128,8,64]{1,0,3,2:T(2,128)}, u32[]{:S(2)}) copy-start(f32[2,128,8,64]{1,0,3,2:T(2,128)} %copy-done.13) | copy-start | bytes 1572868
  156.9 32.4 %copy-start.12 = (f32[2,128,8,64]{1,0,3,2:T(2,128)S(1)}, f32[2,128,8,64]{1,0,3,2:T(2,128)}, u32[]{:S(2)}) copy-start(f32[2,128,8,64]{1,0,3,2:T(2,128)} %copy-done.11) | copy-start | bytes 1572868
  157.0 32.4 %copy-start.18 = (f32[512,512]{1,0:T(8,128)S(1)}, f32[512,512]{1,0:T(8,128)}, u32[]{:S(2)}) copy-start(f32[512,512]{1,0:T(8,128)} %param.11) | copy-start | bytes 3145732
  157.0 32.4 %copy-start.26 = (f32[512]{0:T(512)S(1)}, f32[512]{0:T(512)}, u32[]{:S(2)}) copy-start(f32[512]{0:T(512)} %param.10) | copy-start | bytes 6148
  157.1 32.3 %collective-permute-start.2 = (f32[256,512]{1,0:T(8,128)S(1)}, f32[256,512]{1,0:T(8,128)S(1)}, u32[]{:S(2)}, u32[]{:S(2)}) collective-permute-start(f32[256,512]{1,0:T(8,128)S(1)} %get-tuple-element.20), channel_id=1, source_target_pairs={{0,28},{4,0},{8,4},{12,8},{16,12},{20,16},{24,20},{28,24},{1,29},{... | collective-permute-start | bytes 1572872 | tf_op jit(solution)/shard_map/ppermute | solution.py:29
  161.1 28.2 %collective-permute-start.3 = (f32[256,512]{1,0:T(8,128)S(1)}, f32[256,512]{1,0:T(8,128)S(1)}, u32[]{:S(2)}, u32[]{:S(2)}) collective-permute-start(f32[256,512]{1,0:T(8,128)S(1)} %get-tuple-element.21), channel_id=1, source_target_pairs={{0,4},{4,8},{8,12},{12,16},{16,20},{20,24},{24,28},{28,0},{1,5},{5... | collective-permute-start | bytes 1572872 | tf_op jit(solution)/shard_map/ppermute | solution.py:29
  163.0 70.1 %copy-start.17 = (f32[256,512]{1,0:T(8,128)S(1)}, f32[256,512]{1,0:T(8,128)}, u32[]{:S(2)}) copy-start(f32[256,512]{1,0:T(8,128)} %param.17) | copy-start | bytes 1572868
  309.3 2.4 copy-start.24
  309.3 3.4 %copy-start.23 = (f32[512,512]{1,0:T(8,128)S(1)}, f32[512,512]{1,0:T(8,128)}, u32[]{:S(2)}) copy-start(f32[512,512]{1,0:T(8,128)} %get-tuple-element.31) | copy-start | bytes 3145732
  311.7 1.9 copy-start.22
  (2 other events, 1.6 us)
Sparse Core Ops, SparseCore 0:
  152.5 156.7 all-reduce.3
where the time goes:
time: 328 us; the launch traced here: 322 us
  waiting for transfers between devices  114 us (35%)
  matrix products  73.6 us (22%)
  local copies, waits for them, and re-layouts  51.3 us (16%)
  blocking collectives  41.4 us (13%)
  other arithmetic  15.9 us (5%)
  between operations  14.7 us (4%)
  starting transfers between devices  10.2 us (3%)
    psum x1, waiting for transfers between devices, body(): lax.psum((grad_gain, grad_query, grad_key, grad_value, grad_output), ('sp...  75.2 us
    psum x1, blocking collectives, body(): lax.psum((grad_gain, grad_query, grad_key, grad_value, grad_output), ('sp...  41.4 us
    dot_general x12, matrix products, matmul(): jnp.dot(left, right, precision=lax.Precision.HIGHEST, preferred_element_t...  40 us
    ppermute x2, waiting for transfers between devices, passed_along(): return lax.ppermute(value, axis, pairs)  26.3 us
    dot_general x3, matrix products, attention(): jnp.einsum('phqk,pkhd->pqhd', probability, picked_values, precision=lax.P...  17.7 us
    reshape x4, local copies, waits for them, and re-layouts, attention(): key_win.reshape(-1, PT, model_width)[block_index]  17.1 us
    reshape x4, local copies, waits for them, and re-layouts, attention(): value_win.reshape(-1, PT, model_width)[block_index]  17 us
    dot_general x3, matrix products, attention(): jnp.einsum('pqhd,pkhd->phqk', query_blocks, picked_keys, precision=lax.Pr...  15.9 us
  transfers between devices with their start and end apart: 5, of which 4 were waited for; matrix products, arithmetic and copies ran while one was open for 5% of the time, Pallas kernels for 0%

commit v1 on v0

v1 whole, which is shorter than its diff:
```python
import functools

import jax
import jax.numpy as jnp
from jax import lax
from jax.experimental import pallas as pl
from jax.experimental.pallas import tpu as pltpu
from jax.sharding import PartitionSpec as P

HEADS = 8
PT = 128
HD = 64
PAIRS = HEADS // 2
F32 = jnp.float32
BF16 = jnp.bfloat16
NN = (((1,), (0,)), ((), ()))
NT = (((1,), (1,)), ((), ()))
VMEM = pl.BlockSpec(memory_space=pltpu.VMEM)
SMEM = pl.BlockSpec(memory_space=pltpu.SMEM)


def pair_of(x):
    high = x.astype(BF16)
    return high, (x - high.astype(F32)).astype(BF16)


def dot(left, right, dims=NN):
    return lax.dot_general(left, right, dims, preferred_element_type=F32)


def dot3(left, right, dims=NN):
    return dot(left[0], right[0], dims) + (dot(left[0], right[1], dims) + dot(left[1], right[0], dims))


def load(refs, *index):
    return refs[0][index], refs[1][index]


def store(refs, pair, *index):
    refs[0][index] = pair[0]
    refs[1][index] = pair[1]


def unit_rows(tokens):
    centred = tokens - jnp.mean(tokens, axis=1, keepdims=True)
    variance = jnp.mean(centred * centred, axis=1, keepdims=True)
    rstd = lax.rsqrt(variance + 1e-05)
    return centred * rstd, rstd


def store_stacked(ref, row, rows):
    count = rows.shape[0]
    left_half = lax.broadcasted_iota(jnp.int32, (count, 2 * HD), 1) < HD
    for p in range(PAIRS):
        part = rows[:, p * 2 * HD : (p + 1) * 2 * HD]
        swapped = pltpu.roll(part, HD, 1)
        for a in range(2):
            both = jnp.where(left_half == (a == 0), part, swapped)
            high, low = pair_of(both)
            base = (2 * p + a) * 4 * HD
            ref[pl.ds(row, count), base : base + 2 * HD] = high
            ref[pl.ds(row, count), base + 2 * HD : base + 4 * HD] = low


def pre_kernel(
    tokens, gain, wq, wk, wv, wo, cot,
    xhat, ht_h, ht_l, q_h, q_l, q_stack, k_stack, v_stack, kt_h, kt_l, vt_h, vt_l, dot_out,
    wq_h, wq_l, wk_h, wk_l, wv_h, wv_l, wo_h, wo_l,
):
    for source, high, low in ((wq, wq_h, wq_l), (wk, wk_h, wk_l), (wv, wv_h, wv_l), (wo, wo_h, wo_l)):
        store((high, low), pair_of(source[...]), ...)
    normal, _ = unit_rows(tokens[...])
    xhat[...] = normal
    hidden = normal * gain[...]
    store((ht_h, ht_l), pair_of(hidden.T), ...)
    rows = pair_of(hidden)
    query = dot3(rows, load((wq_h, wq_l), ...)) * HD ** (-0.5)
    store((q_h, q_l), pair_of(query), ...)
    qt_h, qt_l = pair_of(query.T)
    for h in range(HEADS):
        high, low = qt_h[h * HD : (h + 1) * HD], qt_l[h * HD : (h + 1) * HD]
        for i, piece in enumerate((high, low, high, low)):
            q_stack[h * 4 * HD + i * HD : h * 4 * HD + (i + 1) * HD, :] = piece
    key = dot3(rows, load((wk_h, wk_l), ...))
    store_stacked(k_stack, 0, key)
    store((kt_h, kt_l), pair_of(key.T), ...)
    value = dot3(rows, load((wv_h, wv_l), ...))
    store_stacked(v_stack, 0, value)
    store((vt_h, vt_l), pair_of(value.T), ...)
    dot_out[...] = dot3(load((wo_h, wo_l), ...), pair_of(cot[...]), NT)


def main_kernel(
    listed, counts, before, after, gain, tokens, cot,
    xhat, ht_h, ht_l, q_h, q_l, q_stack, k_stack, v_stack, kt_h, kt_l, vt_h, vt_l, dot_out,
    wq_h, wq_l, wk_h, wk_l, wv_h, wv_l, wo_h, wo_l,
    result, dh_own, dh_before, dh_after, grads, d_gain,
    bias, xhat2, ht2_h, ht2_l, k_stack2, v_stack2, kt2_h, kt2_l, vt2_h, vt2_l,
    e_h, e_l, s_h, s_l, mixed_t, dq_t, dk_h, dk_l, dv_h, dv_l,
):
    own = tokens.shape[0]
    halo = 2 * own
    lane = lax.broadcasted_iota(jnp.int32, (1, own), 1)
    for place, w in enumerate((2, 3, 0, 1, 4, 5)):
        level = []
        for p in range(2):
            live = jnp.int32(1 if w == 2 + p else 0)
            for j in range(listed.shape[1]):
                hit = jnp.logical_and(j < counts[0, p], listed[p, j] == w)
                live = jnp.where(hit, 1, live)
            level.append(jnp.where(live == 1, 0.0, -1e30).astype(F32))
        bias[place : place + 1, :] = jnp.where(lane < PT, level[0], level[1])

    for i, rows_ref in enumerate((before, after)):
        normal, _ = unit_rows(rows_ref[...])
        at = slice(i * own, (i + 1) * own)
        xhat2[at, :] = normal
        hidden = normal * gain[...]
        store((ht2_h, ht2_l), pair_of(hidden.T), slice(None), at)
        rows = pair_of(hidden)
        key = dot3(rows, load((wk_h, wk_l), ...))
        store_stacked(k_stack2, i * own, key)
        store((kt2_h, kt2_l), pair_of(key.T), slice(None), at)
        value = dot3(rows, load((wv_h, wv_l), ...))
        store_stacked(v_stack2, i * own, value)
        store((vt2_h, vt2_l), pair_of(value.T), slice(None), at)

    def biased(scores, first):
        return jnp.concatenate(
            [scores[i * PT : (i + 1) * PT] + bias[first + i : first + i + 1, :] for i in range(scores.shape[0] // PT)],
            axis=0,
        )

    def joined(one, two, rows):
        return jnp.concatenate([one[rows, :], two[rows, :]], axis=1)

    left_half = lax.broadcasted_iota(jnp.int32, (own, 2 * HD), 1) < HD

    def masked(pair, a):
        keep = left_half == (a == 0)
        zero = jnp.zeros_like(pair[0])
        return jnp.where(keep, pair[0], zero), jnp.where(keep, pair[1], zero)

    def gathered(left_h, left_l, right):
        one, two = masked(right, 0), masked(right, 1)
        wide = dot(left_h[0], jnp.concatenate(one, axis=1)) + dot(left_h[1], jnp.concatenate(two, axis=1))
        narrow = dot(left_l[0], one[0]) + dot(left_l[1], two[0])
        return wide[:, : 2 * HD] + (wide[:, 2 * HD :] + narrow)

    def one_pair(p, carry):
        scaled = []
        for a in range(2):
            head = pl.ds(pl.multiple_of(p * 2 * HD + a * HD, HD), HD)
            stack = pl.ds(pl.multiple_of((2 * p + a) * 4 * HD, 4 * HD), 4 * HD)
            q_now = q_stack[stack, :]
            s_own = biased(dot(k_stack[:, stack], q_now), 0)
            s_halo = biased(dot(k_stack2[:, stack], q_now), 2)
            top = jnp.maximum(jnp.max(s_own, axis=0, keepdims=True), jnp.max(s_halo, axis=0, keepdims=True))
            e_own, e_halo = jnp.exp(s_own - top), jnp.exp(s_halo - top)
            total = jnp.sum(e_own, axis=0, keepdims=True) + jnp.sum(e_halo, axis=0, keepdims=True)
            e_all = jnp.concatenate([e_own, e_halo], axis=0)
            high, low = pair_of(e_all)
            e_h[a] = high
            e_l[a] = low
            v_high, v_low = joined(vt_h, vt2_h, head), joined(vt_l, vt2_l, head)
            both = dot(jnp.concatenate([v_high, v_low], axis=0), high)
            mixed = both[:HD] + (both[HD:] + dot(v_high, low))
            share = 1.0 / total
            mixed = mixed * share
            mixed_t[head, :] = mixed
            d_mixed = dot_out[head, :] * share
            scaled.append(d_mixed)
            delta = jnp.sum(d_mixed * mixed, axis=0, keepdims=True)
            d_high, d_low = pair_of(d_mixed)
            d_now = jnp.concatenate([d_high, d_low, d_high, d_low], axis=0)
            d_scores = jnp.concatenate([dot(v_stack[:, stack], d_now), dot(v_stack2[:, stack], d_now)], axis=0)
            d_scores = (d_scores - delta) * (e_h[a].astype(F32) + e_l[a].astype(F32))
            high, low = pair_of(d_scores)
            s_h[a] = high
            s_l[a] = low
            k_high, k_low = joined(kt_h, kt2_h, head), joined(kt_l, kt2_l, head)
            both = dot(jnp.concatenate([k_high, k_low], axis=0), high)
            dq_t[head, :] = (both[:HD] + (both[HD:] + dot(k_high, low))) * HD ** (-0.5)
        lanes = pl.ds(pl.multiple_of(p * 2 * HD, 2 * HD), 2 * HD)
        d_rows = pair_of(jnp.concatenate(scaled, axis=0).T)
        store((dv_h, dv_l), pair_of(gathered((e_h[0], e_h[1]), (e_l[0], e_l[1]), d_rows)), slice(None), lanes)
        q_rows = (q_h[:, lanes], q_l[:, lanes])
        store((dk_h, dk_l), pair_of(gathered((s_h[0], s_h[1]), (s_l[0], s_l[1]), q_rows)), slice(None), lanes)
        return carry

    lax.fori_loop(0, PAIRS, one_pair, 0)

    w_q, w_k, w_v, w_o = (load(w, ...) for w in ((wq_h, wq_l), (wk_h, wk_l), (wv_h, wv_l), (wo_h, wo_l)))
    width = tokens.shape[1]
    mixed = mixed_t[...]
    result[...] = dot3(pair_of(mixed.T), w_o) + tokens[...]
    grads[3 * width :, :] = dot3(pair_of(mixed), pair_of(cot[...]))
    d_query = pair_of(dq_t[...].T)
    ht, ht2 = load((ht_h, ht_l), ...), load((ht2_h, ht2_l), ...)
    grads[:width, :] = dot3(ht, d_query)
    first, rest = slice(0, own), slice(own, own + halo)
    for i, pair in ((1, (dk_h, dk_l)), (2, (dv_h, dv_l))):
        grads[i * width : (i + 1) * width, :] = dot3(ht, load(pair, first)) + dot3(ht2, load(pair, rest))
    d_own = (
        dot3(d_query, w_q, NT) + dot3(load((dk_h, dk_l), first), w_k, NT) + dot3(load((dv_h, dv_l), first), w_v, NT)
    )
    dh_own[...] = d_own
    gain_sum = jnp.sum(d_own * xhat[...], axis=0, keepdims=True)
    for i, out in enumerate((dh_before, dh_after)):
        at = slice(own + i * own, 2 * own + i * own)
        d_part = dot3(load((dk_h, dk_l), at), w_k, NT) + dot3(load((dv_h, dv_l), at), w_v, NT)
        out[...] = d_part
        gain_sum = gain_sum + jnp.sum(d_part * xhat2[i * own : (i + 1) * own, :], axis=0, keepdims=True)
    d_gain[...] = gain_sum


def post_kernel(tokens, gain, cot, d_own, d_one, d_two, out):
    normal, rstd = unit_rows(tokens[...])
    d_normal = (d_own[...] + (d_one[...] + d_two[...])) * gain[...]
    inner = jnp.mean(d_normal * normal, axis=1, keepdims=True)
    centre = jnp.mean(d_normal, axis=1, keepdims=True)
    out[...] = (d_normal - centre - normal * inner) * rstd + cot[...]


def shape(*dims, dtype=F32):
    return jax.ShapeDtypeStruct(dims, dtype)


def pairs(*dims):
    return [shape(*dims, dtype=BF16)] * 2


def call(kernel, inputs, outputs, scratch=(), scalars=0, limit=56):
    return pl.pallas_call(
        kernel,
        out_shape=outputs,
        in_specs=[SMEM] * scalars + [VMEM] * (len(inputs) - scalars),
        out_specs=[VMEM] * len(outputs),
        scratch_shapes=[pltpu.VMEM(s.shape, s.dtype) for s in scratch],
        compiler_params=pltpu.CompilerParams(vmem_limit_bytes=limit * 2**20),
    )(*inputs)


def shifted(value, axis, steps):
    count = lax.axis_size(axis)
    return lax.ppermute(value, axis, [(i, (i + steps) % count) for i in range(count)])


def swapped(value, axis, mask):
    return lax.ppermute(value, axis, [(i, i ^ mask) for i in range(lax.axis_size(axis))])


def side(axis, mask):
    return (lax.axis_index(axis) // mask) % 2


def half(value, index):
    rows = value.shape[0] // 2
    return lax.dynamic_slice_in_dim(value, index * rows, rows, 0)


def halved(value, dim):
    mine = side(*dim)
    return half(value, mine) + swapped(half(value, 1 - mine), *dim)


def doubled(value, dim):
    mine = side(*dim)
    other = swapped(value, *dim)
    return jnp.concatenate([jnp.where(mine == 0, value, other), jnp.where(mine == 0, other, value)], axis=0)


def bits(axis):
    return [(axis, 1 << k) for k in range((lax.axis_size(axis) - 1).bit_length())]


def summed(value):
    slab, space = bits("slab"), bits("space")
    first, rest = slab[0], slab[1:] + space
    cross, along, last = rest[0], rest[1], rest[2:]
    orders = [[along, cross, *last], [cross, last[0], along, *last[1:]], [last[0], along, cross, *last[1:]]]
    value = halved(value, first)
    rows = value.shape[0]
    step = 1 << len(rest)
    third = -(-rows // (3 * step)) * step
    parts = [value[:third], value[third : 2 * third], value[2 * third :]]
    for i in range(len(rest)):
        parts = [halved(part, order[i]) for part, order in zip(parts, orders)]
    for i in reversed(range(len(rest))):
        parts = [doubled(part, order[i]) for part, order in zip(parts, orders)]
    return doubled(jnp.concatenate(parts, axis=0), first)


def body(tokens, gain, wq, wk, wv, wo, neighbour_list, neighbour_count, cotangent):
    rows, width = tokens.shape
    before, after = shifted(tokens, "space", 1), shifted(tokens, "space", -1)
    gain_row = gain[None, :]
    mid = call(
        pre_kernel,
        (tokens, gain_row, wq, wk, wv, wo, cotangent),
        [
            shape(rows, width), *pairs(width, rows), *pairs(rows, width),
            shape(HEADS * 4 * HD, rows, dtype=BF16),
            shape(rows, HEADS * 4 * HD, dtype=BF16), shape(rows, HEADS * 4 * HD, dtype=BF16),
            *pairs(width, rows), *pairs(width, rows), shape(width, rows),
            *pairs(width, width), *pairs(width, width), *pairs(width, width), *pairs(width, width),
        ],
    )
    halo, window = 2 * rows, 3 * rows
    result, d_own, d_before, d_after, grads, d_gain = call(
        main_kernel,
        (neighbour_list, neighbour_count[None, :], before, after, gain_row, tokens, cotangent, *mid),
        [shape(rows, width)] * 4 + [shape(4 * width, width), shape(1, width)],
        [
            shape(8, rows), shape(halo, width), *pairs(width, halo),
            shape(halo, HEADS * 4 * HD, dtype=BF16), shape(halo, HEADS * 4 * HD, dtype=BF16),
            *pairs(width, halo), *pairs(width, halo),
            *pairs(2, window, rows), *pairs(2, window, rows),
            shape(width, rows), shape(width, rows), *pairs(window, width), *pairs(window, width),
        ],
        scalars=2,
    )
    from_after, from_before = shifted(d_before, "space", -1), shifted(d_after, "space", 1)
    (d_tokens,) = call(
        post_kernel, (tokens, gain_row, cotangent, d_own, from_after, from_before), [shape(rows, width)]
    )
    grads = summed(grads)
    d_gain = lax.psum(d_gain[0], ("space", "slab"))
    gq, gk, gv, go = (grads[i * width : (i + 1) * width] for i in range(4))
    return (result, d_tokens, d_gain, gq, gk, gv, go)


def solution(mesh):
    tokens = P(("space", "slab"), None)
    return jax.shard_map(
        body,
        mesh=mesh,
        in_specs=(tokens, P(), P(), P(), P(), P(), tokens, P(("space", "slab")), tokens),
        out_specs=(tokens, tokens, P(), P(), P(), P(), P()),
        check_vma=False,
    )
```

time: 328 us -> 199 us (0.61); the launches traced: 322 us -> 199 us
  matrix products: 73.6 us -> 0 us
  waiting for transfers between devices: 114 us -> 59.4 us
  local copies, waits for them, and re-layouts: 51.3 us -> 7.37 us
  Pallas kernels: 0 us -> 38.6 us
  starting transfers between devices: 10.2 us -> 30.5 us
  blocking collectives: 41.4 us -> 57.1 us
  between operations: 14.7 us -> 1.07 us
  other arithmetic: 15.9 us -> 5.1 us
    psum x1 -> x0, waiting for transfers between devices: 75.2 us -> none  [body(): lax.psum((grad_gain, grad_query, grad_key, grad_value, grad_output), ('sp...]
    dot_general x18 -> x0, matrix products: 73.6 us -> none  [the longest x12 40 us: matmul(): jnp.dot(left, right, precision=lax.Precision.HIGHEST, preferred_element_t...]
    pallas_call x0 -> x3, Pallas kernels: none -> 38.6 us  [call(): pl.pallas_call(kernel, out_shape=outputs, in_specs=[SMEM] * scalars + [VM...]
    reshape x10 -> x0, local copies, waits for them, and re-layouts: 36.2 us -> none  [the longest x4 17.1 us: attention(): key_win.reshape(-1, PT, model_width)[block_index]]
    ppermute x4 -> x30, starting transfers between devices: 10.2 us -> 30.5 us  [the longest x26 22.2 us: swapped(): lax.ppermute(value, axis, [(i, i ^ mask) for i in range(lax.axis_size(axi...]
    ppermute x4 -> x30, waiting for transfers between devices: 39.3 us -> 59.4 us  [the longest x26 45.4 us: swapped(): lax.ppermute(value, axis, [(i, i ^ mask) for i in range(lax.axis_size(axi...]
    psum x1, blocking collectives: 41.4 us -> 57.1 us  [body(): d_gain = lax.psum(d_gain[0], ('space', 'slab'))]
    unnamed x64 -> x10, local copies, waits for them, and re-layouts: 9.5 us -> 1.75 us
  transfers between devices with their start and end apart: 5 -> 30, of which waited for: 4 -> 22; matrix products, arithmetic and copies ran while one was open for 5% -> 1% of each run, Pallas kernels for 0% -> 5%
where the time goes in v1:
time: 199 us
  waiting for transfers between devices  59.4 us (30%)
  blocking collectives  57.1 us (29%)
  Pallas kernels  38.6 us (19%)
  starting transfers between devices  30.5 us (15%)
  local copies, waits for them, and re-layouts  7.37 us (4%)
  other arithmetic  5.1 us (3%)
    psum x1, blocking collectives, body(): d_gain = lax.psum(d_gain[0], ('space', 'slab'))  57.1 us
    ppermute x26, waiting for transfers between devices, swapped(): lax.ppermute(value, axis, [(i, i ^ mask) for i in range(lax.axis_size(axi...  45.4 us
    pallas_call x3, Pallas kernels, call(): pl.pallas_call(kernel, out_shape=outputs, in_specs=[SMEM] * scalars + [VM...  38.6 us
    ppermute x26, starting transfers between devices, swapped(): lax.ppermute(value, axis, [(i, i ^ mask) for i in range(lax.axis_size(axi...  22.2 us
    ppermute x4, waiting for transfers between devices, shifted(): lax.ppermute(value, axis, [(i, (i + steps) % count) for i in range(count)])  14.1 us
    ppermute x4, starting transfers between devices, shifted(): lax.ppermute(value, axis, [(i, (i + steps) % count) for i in range(count)])  8.2 us
  transfers between devices with their start and end apart: 30, of which 22 were waited for; matrix products, arithmetic and copies ran while one was open for 1% of the time, Pallas kernels for 5%

profile of v1, /device:TPU:0, one launch (start us, length us, event | category | flops | bytes accessed | tf_op | source)
XLA Modules:
  0.0 199.1 jit_solution(885108865355891199)
XLA Ops:
  0.6 3.0 %collective-permute-start = (f32[256,512]{1,0:T(8,128)}, f32[256,512]{1,0:T(8,128)S(1)}, u32[]{:S(2)}, u32[]{:S(2)}) collective-permute-start(f32[256,512]{1,0:T(8,128)} %tokens.5), channel_id=1, source_target_pairs={{0,4},{4,8},{8,12},{12,16},{16,20},{20,24},{24,28},{28,0},{1,5},{5... | collective-permute-start | bytes 1572872 | tf_op jit(solution)/shard_map/ppermute | solution.py:246
  3.6 3.1 %collective-permute-start.1 = (f32[256,512]{1,0:T(8,128)}, f32[256,512]{1,0:T(8,128)S(1)}, u32[]{:S(2)}, u32[]{:S(2)}) collective-permute-start(f32[256,512]{1,0:T(8,128)} %tokens.5), channel_id=1, source_target_pairs={{0,28},{4,0},{8,4},{12,8},{16,12},{20,16},{24,20},{28,24},{1,29},{... | collective-permute-start | bytes 1572872 | tf_op jit(solution)/shard_map/ppermute | solution.py:246
  6.7 7.6 %shard_map.144 = (f32[256,512]{1,0:T(8,128)}, bf16[512,256]{1,0:T(8,128)(2,1)}, bf16[512,256]{1,0:T(8,128)(2,1)}, bf16[256,512]{1,0:T(8,128)(2,1)}, bf16[256,512...) custom-call(f32[256,512]{1,0:T(8,128)} %tokens.5, ...), custom_call_target="tpu_custom_call" | custom-call | tf_op jit(solution)/shard_map/pallas_call | solution.py:234
  14.4 12.0 %collective-permute-done.before = f32[256,512]{1,0:T(8,128)S(1)} collective-permute-done((f32[256,512]{1,0:T(8,128)}, f32[256,512]{1,0:T(8,128)S(1)}, u32[]{:S(2)}, u32[]{:S(2)}) %collective-permute-start) | collective-permute-done | bytes 524320 | tf_op jit(solution)/shard_map/ppermute | solution.py:246
  26.4 2.1 %collective-permute-done.1.after = f32[256,512]{1,0:T(8,128)S(1)} collective-permute-done((f32[256,512]{1,0:T(8,128)}, f32[256,512]{1,0:T(8,128)S(1)}, u32[]{:S(2)}, u32[]{:S(2)}) %collective-permute-start.1) | collective-permute-done | bytes 524320 | tf_op jit(solution)/shard_map/ppermute | solution.py:246
  29.2 28.2 %shard_map.145 = (f32[256,512]{1,0:T(8,128)}, f32[256,512]{1,0:T(8,128)}, f32[256,512]{1,0:T(8,128)}, f32[256,512]{1,0:T(8,128)}, f32[2048,512]{1,0:T(8,128)}, /*index=5*/f32[1,512]{1,0:T(1,128)}) custom-call(s32[2,3]{1,0:T(2,128)} %listed.1, s32[1,2]{1,0:T(1,128)} %bitcast.7, f32[256,512]{1,0:T(8,128)} %copy-done, f32[256,512]{1,0:T(8,128)} %copy-done.1, ...), custom_call_target="tpu_custom_call" | custom-call | tf_op jit(solution)/shard_map/pallas_call | solution.py:234
  57.4 3.1 %constant_dynamic-slice_fusion.12 = f32[1024,512]{1,0:T(8,128)} fusion(f32[2048,512]{1,0:T(8,128)} %get-tuple-element.60, s32[]{:T(128)S(6)} %select_n.332), kind=kLoop, calls=%fused_computation.60 | loop fusion | bytes 4194308 | tf_op jit(solution)/shard_map/dynamic_slice | solution.py:259
  60.6 4.4 %collective-permute-done.4 = f32[1024,512]{1,0:T(8,128)S(1)} collective-permute-done((f32[1024,512]{1,0:T(8,128)}, f32[1024,512]{1,0:T(8,128)S(1)}, u32[]{:S(2)}, u32[]{:S(2)}) %collective-permute-start.4) | collective-permute-done | bytes 2097184 | tf_op jit(solution)/shard_map/ppermute | solution.py:250
  64.9 2.1 %dynamic-slice_add_fusion = f32[1024,512]{1,0:T(8,128)S(1)} fusion(f32[1024,512]{1,0:T(8,128)S(1)} %collective-permute-done.4, f32[2048,512]{1,0:T(8,128)} %get-tuple-element.60, s32[]{:T(128)S(6)} %select_n.331), kind=kLoop, calls=%fused_computation | loop fusion | flops 524288 | bytes 6291460 | tf_op jit(solution)/shard_map/add | solution.py:264
  67.1 1.3 collective-permute-start.21
  68.6 1.6 collective-permute-start.13
  71.0 5.9 %collective-permute-done.21 = f32[160,512]{1,0:T(8,128)S(1)} collective-permute-done((f32[160,512]{1,0:T(8,128)S(1)}, f32[160,512]{1,0:T(8,128)S(1)}, u32[]{:S(2)}, u32[]{:S(2)}) %collective-permute-start.21) | collective-permute-done | bytes 327712 | tf_op jit(solution)/shard_map/ppermute | solution.py:250
  79.7 1.6 collective-permute-done.5
  81.5 2.2 %collective-permute-done.22 = f32[80,512]{1,0:T(8,128)S(1)} collective-permute-done((f32[80,512]{1,0:T(8,128)S(1)}, f32[80,512]{1,0:T(8,128)S(1)}, u32[]{:S(2)}, u32[]{:S(2)}) %collective-permute-start.22) | collective-permute-done | bytes 163872 | tf_op jit(solution)/shard_map/ppermute | solution.py:250
  85.4 2.5 %collective-permute-done.6 = f32[88,512]{1,0:T(8,128)S(1)} collective-permute-done((f32[88,512]{1,0:T(8,128)S(1)}, f32[88,512]{1,0:T(8,128)S(1)}, u32[]{:S(2)}, u32[]{:S(2)}) %collective-permute-start.6) | collective-permute-done | bytes 180256 | tf_op jit(solution)/shard_map/ppermute | solution.py:250
  88.8 2.7 %collective-permute-start.24 = (f32[20,512]{1,0:T(8,128)S(1)}, f32[20,512]{1,0:T(8,128)S(1)}, u32[]{:S(2)}, u32[]{:S(2)}) collective-permute-start(f32[20,512]{1,0:T(8,128)S(1)} %constant_dynamic-slice_fusion), channel_id=1, source_target_pairs={{0,16},{4,20},{8,24},{12,28},{16,0},{20,4},{24,8},{28,12},{1,17},{... | collective-permute-start | bytes 122888 | tf_op jit(solution)/shard_map/ppermute | solution.py:250
  91.5 2.6 %collective-permute-done.24 = f32[20,512]{1,0:T(8,128)S(1)} collective-permute-done((f32[20,512]{1,0:T(8,128)S(1)}, f32[20,512]{1,0:T(8,128)S(1)}, u32[]{:S(2)}, u32[]{:S(2)}) %collective-permute-start.24) | collective-permute-done | bytes 40992 | tf_op jit(solution)/shard_map/ppermute | solution.py:250
  94.2 2.3 %collective-permute-start.25 = (f32[20,512]{1,0:T(8,128)S(1)}, f32[20,512]{1,0:T(8,128)S(1)}, u32[]{:S(2)}, u32[]{:S(2)}) collective-permute-start(f32[20,512]{1,0:T(8,128)S(1)} %dynamic-slice_add_fusion.10), channel_id=1, source_target_pairs={{0,16},{4,20},{8,24},{12,28},{16,0},{20,4},{24,8},{28,12},{1,17},{... | collective-permute-start | bytes 122888 | tf_op jit(solution)/shard_map/ppermute | solution.py:250
  97.3 2.3 %collective-permute-start.8 = (f32[22,512]{1,0:T(8,128)S(1)}, f32[22,512]{1,0:T(8,128)S(1)}, u32[]{:S(2)}, u32[]{:S(2)}) collective-permute-start(f32[22,512]{1,0:T(8,128)S(1)} %constant_dynamic-slice_fusion.8), channel_id=1, source_target_pairs={{0,16},{4,20},{8,24},{12,28},{16,0},{20,4},{24,8},{28,12},{1,17},{... | collective-permute-start | bytes 135176 | tf_op jit(solution)/shard_map/ppermute | solution.py:250
  100.6 3.2 %collective-permute-done.16 = f32[22,512]{1,0:T(8,128)S(1)} collective-permute-done((f32[22,512]{1,0:T(8,128)S(1)}, f32[22,512]{1,0:T(8,128)S(1)}, u32[]{:S(2)}, u32[]{:S(2)}) %collective-permute-start.16) | collective-permute-done | bytes 45088 | tf_op jit(solution)/shard_map/ppermute | solution.py:250
  104.8 2.0 %collective-permute-start.9 = (f32[22,512]{1,0:T(8,128)S(1)}, f32[22,512]{1,0:T(8,128)S(1)}, u32[]{:S(2)}, u32[]{:S(2)}) collective-permute-start(f32[22,512]{1,0:T(8,128)S(1)} %dynamic-slice_add_fusion.12), channel_id=1, source_target_pairs={{0,16},{4,20},{8,24},{12,28},{16,0},{20,4},{24,8},{28,12},{1,17},{... | collective-permute-start | bytes 135176 | tf_op jit(solution)/shard_map/ppermute | solution.py:250
  106.8 2.2 %collective-permute-done.17 = f32[22,512]{1,0:T(8,128)S(1)} collective-permute-done((f32[22,512]{1,0:T(8,128)S(1)}, f32[22,512]{1,0:T(8,128)S(1)}, u32[]{:S(2)}, u32[]{:S(2)}) %collective-permute-start.17) | collective-permute-done | bytes 45088 | tf_op jit(solution)/shard_map/ppermute | solution.py:250
  110.0 1.3 collective-permute-start.27
  111.3 2.4 %collective-permute-done.18 = f32[44,512]{1,0:T(8,128)S(1)} collective-permute-done((f32[44,512]{1,0:T(8,128)S(1)}, f32[44,512]{1,0:T(8,128)S(1)}, u32[]{:S(2)}, u32[]{:S(2)}) %collective-permute-start.18) | collective-permute-done | bytes 90144 | tf_op jit(solution)/shard_map/ppermute | solution.py:250
  115.5 6.6 %collective-permute-done.11 = f32[88,512]{1,0:T(8,128)S(1)} collective-permute-done((f32[88,512]{1,0:T(8,128)S(1)}, f32[88,512]{1,0:T(8,128)S(1)}, u32[]{:S(2)}, u32[]{:S(2)}) %collective-permute-start.11) | collective-permute-done | bytes 180256 | tf_op jit(solution)/shard_map/ppermute | solution.py:250
  124.3 5.4 %collective-permute-done.12 = f32[176,512]{1,0:T(8,128)S(1)} collective-permute-done((f32[176,512]{1,0:T(8,128)S(1)}, f32[176,512]{1,0:T(8,128)S(1)}, u32[]{:S(2)}, u32[]{:S(2)}) %collective-permute-start.12) | collective-permute-done | bytes 360480 | tf_op jit(solution)/shard_map/ppermute | solution.py:250
  129.8 1.9 collective-permute-done.20
  132.0 2.1 %collective-permute-start.2 = (f32[256,512]{1,0:T(8,128)}, f32[256,512]{1,0:T(8,128)S(1)}, u32[]{:S(2)}, u32[]{:S(2)}) collective-permute-start(f32[256,512]{1,0:T(8,128)} %get-tuple-element.57), channel_id=1, source_target_pairs={{0,28},{4,0},{8,4},{12,8},{16,12},{20,16},{24,20},{28,24},{1,29},{... | collective-permute-start | bytes 1572872 | tf_op jit(solution)/shard_map/ppermute | solution.py:246
  134.1 57.1 %psum.7 = f32[512]{0:T(512)} all-reduce(f32[512]{0:T(512)S(1)} %bitcast.6), channel_id=1, replica_groups=mesh['space'=8,'slab'=4] {'space','slab'}, use_global_device_ids=true, to_apply=%region_0.1 | all-reduce | flops 512 | bytes 4096 | tf_op jit(solution)/shard_map/psum | solution.py:328
  192.1 2.8 %shard_map.146 = f32[256,512]{1,0:T(8,128)} custom-call(f32[256,512]{1,0:T(8,128)} %tokens.5, f32[1,512]{1,0:T(1,128)} %bitcast.5, f32[256,512]{1,0:T(8,128)} %cot.5, f32[256,512]{1,0:T(8,128)} %get-tuple-element.56.d_own, f32[256,512]{1,0:T(8,128)} %copy-done.2, f32[256,512]{1,0:T(8,128)} %copy-done.3), custom_call_target="tpu_custom_call" | custom-call | tf_op jit(solution)/shard_map/pallas_call | solution.py:234
  195.0 2.1 %broadcast_select_fusion = (f32[1024,512]{1,0:T(8,128)S(1)}, f32[1024,512]{1,0:T(8,128)S(1)}) fusion(f32[1024,512]{1,0:T(8,128)} %collective-permute-done.29, f32[1024,512]{1,0:T(8,128)S(1)} %select_dynamic-update-slice_fusion.4, pred[]{:T(512)S(6)} %eq.63), kind=kLoop, calls=%fused_computation.1 | loop fusion | flops 1048576 | bytes 8388609 | tf_op jit(solution)/shard_map/jit(_where)/select_n | solution.py:270
  197.1 2.1 %fusion = (f32[512,512]{1,0:T(8,128)}, f32[512,512]{1,0:T(8,128)}, f32[512,512]{1,0:T(8,128)}, f32[512,512]{1,0:T(8,128)}) fusion(f32[1024,512]{1,0:T(8,128)S(1)} %get-tuple-element.61, f32[1024,512]{1,0:T(8,128)S(1)} %get-tuple-element.62), kind=kLoop, calls=%fused_computation.61 | loop fusion | bytes 8388608 | tf_op jit(solution)/shard_map/slice | solution.py:329
  (96 shorter events, 16.4 us)
Async XLA Ops:
  0.6 25.7 %collective-permute-start = (f32[256,512]{1,0:T(8,128)}, f32[256,512]{1,0:T(8,128)S(1)}, u32[]{:S(2)}, u32[]{:S(2)}) collective-permute-start(f32[256,512]{1,0:T(8,128)} %tokens.5), channel_id=1, source_target_pairs={{0,4},{4,8},{8,12},{12,16},{16,20},{20,24},{24,28},{28,0},{1,5},{5... | collective-permute-start | bytes 1572872 | tf_op jit(solution)/shard_map/ppermute | solution.py:246
  3.6 24.8 %collective-permute-start.1 = (f32[256,512]{1,0:T(8,128)}, f32[256,512]{1,0:T(8,128)S(1)}, u32[]{:S(2)}, u32[]{:S(2)}) collective-permute-start(f32[256,512]{1,0:T(8,128)} %tokens.5), channel_id=1, source_target_pairs={{0,28},{4,0},{8,4},{12,8},{16,12},{20,16},{24,20},{28,24},{1,29},{... | collective-permute-start | bytes 1572872 | tf_op jit(solution)/shard_map/ppermute | solution.py:246
  26.4 2.1 %copy-start = (f32[256,512]{1,0:T(8,128)}, f32[256,512]{1,0:T(8,128)S(1)}, u32[]{:S(2)}) copy-start(f32[256,512]{1,0:T(8,128)S(1)} %collective-permute-done.before) | copy-start | bytes 1572868
  60.6 4.4 %collective-permute-start.4 = (f32[1024,512]{1,0:T(8,128)}, f32[1024,512]{1,0:T(8,128)S(1)}, u32[]{:S(2)}, u32[]{:S(2)}) collective-permute-start(f32[1024,512]{1,0:T(8,128)} %constant_dynamic-slice_fusion.12), channel_id=1, source_target_pairs={{0,1},{1,0},{2,3},{3,2},{4,5},{5,4},{6,7},{7,6},{8,9},{9,8},{10,11... | collective-permute-start | bytes 6291464 | tf_op jit(solution)/shard_map/ppermute | solution.py:250
  67.1 9.8 %collective-permute-start.21 = (f32[160,512]{1,0:T(8,128)S(1)}, f32[160,512]{1,0:T(8,128)S(1)}, u32[]{:S(2)}, u32[]{:S(2)}) collective-permute-start(f32[160,512]{1,0:T(8,128)S(1)} %constant_dynamic-slice_fusion.3), channel_id=1, source_target_pairs={{0,8},{4,12},{8,0},{12,4},{16,24},{20,28},{24,16},{28,20},{1,9},{5... | collective-permute-start | bytes 983048 | tf_op jit(solution)/shard_map/ppermute | solution.py:250
  68.6 10.2 %collective-permute-start.13 = (f32[176,512]{1,0:T(8,128)S(1)}, f32[176,512]{1,0:T(8,128)S(1)}, u32[]{:S(2)}, u32[]{:S(2)}) collective-permute-start(f32[176,512]{1,0:T(8,128)S(1)} %constant_dynamic-slice_fusion.7), channel_id=1, source_target_pairs={{0,2},{1,3},{2,0},{3,1},{4,6},{5,7},{6,4},{7,5},{8,10},{9,11},{10,... | collective-permute-start | bytes 1081352 | tf_op jit(solution)/shard_map/ppermute | solution.py:250
  70.2 11.1 %collective-permute-start.5 = (f32[176,512]{1,0:T(8,128)S(1)}, f32[176,512]{1,0:T(8,128)S(1)}, u32[]{:S(2)}, u32[]{:S(2)}) collective-permute-start(f32[176,512]{1,0:T(8,128)S(1)} %constant_dynamic-slice_fusion.11), channel_id=1, source_target_pairs={{0,4},{4,0},{8,12},{12,8},{16,20},{20,16},{24,28},{28,24},{1,5},{5... | collective-permute-start | bytes 1081352 | tf_op jit(solution)/shard_map/ppermute | solution.py:250
  77.0 6.7 %collective-permute-start.22 = (f32[80,512]{1,0:T(8,128)S(1)}, f32[80,512]{1,0:T(8,128)S(1)}, u32[]{:S(2)}, u32[]{:S(2)}) collective-permute-start(f32[80,512]{1,0:T(8,128)S(1)} %constant_dynamic-slice_fusion.2), channel_id=1, source_target_pairs={{0,4},{4,0},{8,12},{12,8},{16,20},{20,16},{24,28},{28,24},{1,5},{5... | collective-permute-start | bytes 491528 | tf_op jit(solution)/shard_map/ppermute | solution.py:250
  78.9 5.6 %collective-permute-start.14 = (f32[88,512]{1,0:T(8,128)S(1)}, f32[88,512]{1,0:T(8,128)S(1)}, u32[]{:S(2)}, u32[]{:S(2)}) collective-permute-start(f32[88,512]{1,0:T(8,128)S(1)} %constant_dynamic-slice_fusion.6), channel_id=1, source_target_pairs={{0,8},{4,12},{8,0},{12,4},{16,24},{20,28},{24,16},{28,20},{1,9},{5... | collective-permute-start | bytes 540680 | tf_op jit(solution)/shard_map/ppermute | solution.py:250
  81.4 6.4 %collective-permute-start.6 = (f32[88,512]{1,0:T(8,128)S(1)}, f32[88,512]{1,0:T(8,128)S(1)}, u32[]{:S(2)}, u32[]{:S(2)}) collective-permute-start(f32[88,512]{1,0:T(8,128)S(1)} %constant_dynamic-slice_fusion.10), channel_id=1, source_target_pairs={{0,2},{1,3},{2,0},{3,1},{4,6},{5,7},{6,4},{7,5},{8,10},{9,11},{10,... | collective-permute-start | bytes 540680 | tf_op jit(solution)/shard_map/ppermute | solution.py:250
  83.7 5.0 %collective-permute-start.23 = (f32[40,512]{1,0:T(8,128)S(1)}, f32[40,512]{1,0:T(8,128)S(1)}, u32[]{:S(2)}, u32[]{:S(2)}) collective-permute-start(f32[40,512]{1,0:T(8,128)S(1)} %constant_dynamic-slice_fusion.1), channel_id=1, source_target_pairs={{0,2},{1,3},{2,0},{3,1},{4,6},{5,7},{6,4},{7,5},{8,10},{9,11},{10,... | collective-permute-start | bytes 245768 | tf_op jit(solution)/shard_map/ppermute | solution.py:250
  84.5 12.0 %collective-permute-start.15 = (f32[44,512]{1,0:T(8,128)S(1)}, f32[44,512]{1,0:T(8,128)S(1)}, u32[]{:S(2)}, u32[]{:S(2)}) collective-permute-start(f32[44,512]{1,0:T(8,128)S(1)} %constant_dynamic-slice_fusion.5), channel_id=1, source_target_pairs={{0,4},{4,0},{8,12},{12,8},{16,20},{20,16},{24,28},{28,24},{1,5},{5... | collective-permute-start | bytes 270344 | tf_op jit(solution)/shard_map/ppermute | solution.py:250
  88.8 5.4 %collective-permute-start.24 = (f32[20,512]{1,0:T(8,128)S(1)}, f32[20,512]{1,0:T(8,128)S(1)}, u32[]{:S(2)}, u32[]{:S(2)}) collective-permute-start(f32[20,512]{1,0:T(8,128)S(1)} %constant_dynamic-slice_fusion), channel_id=1, source_target_pairs={{0,16},{4,20},{8,24},{12,28},{16,0},{20,4},{24,8},{28,12},{1,17},{... | collective-permute-start | bytes 122888 | tf_op jit(solution)/shard_map/ppermute | solution.py:250
  91.4 5.9 %collective-permute-start.7 = (f32[44,512]{1,0:T(8,128)S(1)}, f32[44,512]{1,0:T(8,128)S(1)}, u32[]{:S(2)}, u32[]{:S(2)}) collective-permute-start(f32[44,512]{1,0:T(8,128)S(1)} %constant_dynamic-slice_fusion.9), channel_id=1, source_target_pairs={{0,8},{4,12},{8,0},{12,4},{16,24},{20,28},{24,16},{28,20},{1,9},{5... | collective-permute-start | bytes 270344 | tf_op jit(solution)/shard_map/ppermute | solution.py:250
  94.2 5.6 %collective-permute-start.25 = (f32[20,512]{1,0:T(8,128)S(1)}, f32[20,512]{1,0:T(8,128)S(1)}, u32[]{:S(2)}, u32[]{:S(2)}) collective-permute-start(f32[20,512]{1,0:T(8,128)S(1)} %dynamic-slice_add_fusion.10), channel_id=1, source_target_pairs={{0,16},{4,20},{8,24},{12,28},{16,0},{20,4},{24,8},{28,12},{1,17},{... | collective-permute-start | bytes 122888 | tf_op jit(solution)/shard_map/ppermute | solution.py:250
  96.6 7.2 %collective-permute-start.16 = (f32[22,512]{1,0:T(8,128)S(1)}, f32[22,512]{1,0:T(8,128)S(1)}, u32[]{:S(2)}, u32[]{:S(2)}) collective-permute-start(f32[22,512]{1,0:T(8,128)S(1)} %constant_dynamic-slice_fusion.4), channel_id=1, source_target_pairs={{0,16},{4,20},{8,24},{12,28},{16,0},{20,4},{24,8},{28,12},{1,17},{... | collective-permute-start | bytes 135176 | tf_op jit(solution)/shard_map/ppermute | solution.py:250
  97.3 7.4 %collective-permute-start.8 = (f32[22,512]{1,0:T(8,128)S(1)}, f32[22,512]{1,0:T(8,128)S(1)}, u32[]{:S(2)}, u32[]{:S(2)}) collective-permute-start(f32[22,512]{1,0:T(8,128)S(1)} %constant_dynamic-slice_fusion.8), channel_id=1, source_target_pairs={{0,16},{4,20},{8,24},{12,28},{16,0},{20,4},{24,8},{28,12},{1,17},{... | collective-permute-start | bytes 135176 | tf_op jit(solution)/shard_map/ppermute | solution.py:250
  99.8 10.1 %collective-permute-start.26 = (f32[40,512]{1,0:T(8,128)S(1)}, f32[40,512]{1,0:T(8,128)S(1)}, u32[]{:S(2)}, u32[]{:S(2)}) collective-permute-start(f32[40,512]{1,0:T(8,128)S(1)} %pad_maximum_fusion.8), channel_id=1, source_target_pairs={{0,2},{1,3},{2,0},{3,1},{4,6},{5,7},{6,4},{7,5},{8,10},{9,11},{10,... | collective-permute-start | bytes 245768 | tf_op jit(solution)/shard_map/ppermute | solution.py:250
  103.7 5.2 %collective-permute-start.17 = (f32[22,512]{1,0:T(8,128)S(1)}, f32[22,512]{1,0:T(8,128)S(1)}, u32[]{:S(2)}, u32[]{:S(2)}) collective-permute-start(f32[22,512]{1,0:T(8,128)S(1)} %dynamic-slice_add_fusion.11), channel_id=1, source_target_pairs={{0,16},{4,20},{8,24},{12,28},{16,0},{20,4},{24,8},{28,12},{1,17},{... | collective-permute-start | bytes 135176 | tf_op jit(solution)/shard_map/ppermute | solution.py:250
  104.8 5.1 %collective-permute-start.9 = (f32[22,512]{1,0:T(8,128)S(1)}, f32[22,512]{1,0:T(8,128)S(1)}, u32[]{:S(2)}, u32[]{:S(2)}) collective-permute-start(f32[22,512]{1,0:T(8,128)S(1)} %dynamic-slice_add_fusion.12), channel_id=1, source_target_pairs={{0,16},{4,20},{8,24},{12,28},{16,0},{20,4},{24,8},{28,12},{1,17},{... | collective-permute-start | bytes 135176 | tf_op jit(solution)/shard_map/ppermute | solution.py:250
  109.0 4.7 %collective-permute-start.18 = (f32[44,512]{1,0:T(8,128)S(1)}, f32[44,512]{1,0:T(8,128)S(1)}, u32[]{:S(2)}, u32[]{:S(2)}) collective-permute-start(f32[44,512]{1,0:T(8,128)S(1)} %pad_maximum_fusion.7), channel_id=1, source_target_pairs={{0,4},{4,0},{8,12},{12,8},{16,20},{20,16},{24,28},{28,24},{1,5},{5... | collective-permute-start | bytes 270344 | tf_op jit(solution)/shard_map/ppermute | solution.py:250
  109.9 4.7 %collective-permute-start.10 = (f32[44,512]{1,0:T(8,128)S(1)}, f32[44,512]{1,0:T(8,128)S(1)}, u32[]{:S(2)}, u32[]{:S(2)}) collective-permute-start(f32[44,512]{1,0:T(8,128)S(1)} %pad_maximum_fusion.6), channel_id=1, source_target_pairs={{0,8},{4,12},{8,0},{12,4},{16,24},{20,28},{24,16},{28,20},{1,9},{5... | collective-permute-start | bytes 270344 | tf_op jit(solution)/shard_map/ppermute | solution.py:250
  110.0 5.4 %collective-permute-start.27 = (f32[80,512]{1,0:T(8,128)S(1)}, f32[80,512]{1,0:T(8,128)S(1)}, u32[]{:S(2)}, u32[]{:S(2)}) collective-permute-start(f32[80,512]{1,0:T(8,128)S(1)} %pad_maximum_fusion.5), channel_id=1, source_target_pairs={{0,4},{4,0},{8,12},{12,8},{16,20},{20,16},{24,28},{28,24},{1,5},{5... | collective-permute-start | bytes 491528 | tf_op jit(solution)/shard_map/ppermute | solution.py:250
  113.7 10.4 %collective-permute-start.19 = (f32[88,512]{1,0:T(8,128)S(1)}, f32[88,512]{1,0:T(8,128)S(1)}, u32[]{:S(2)}, u32[]{:S(2)}) collective-permute-start(f32[88,512]{1,0:T(8,128)S(1)} %pad_maximum_fusion.4), channel_id=1, source_target_pairs={{0,8},{4,12},{8,0},{12,4},{16,24},{20,28},{24,16},{28,20},{1,9},{5... | collective-permute-start | bytes 540680 | tf_op jit(solution)/shard_map/ppermute | solution.py:250
  114.6 7.5 %collective-permute-start.11 = (f32[88,512]{1,0:T(8,128)S(1)}, f32[88,512]{1,0:T(8,128)S(1)}, u32[]{:S(2)}, u32[]{:S(2)}) collective-permute-start(f32[88,512]{1,0:T(8,128)S(1)} %pad_maximum_fusion.3), channel_id=1, source_target_pairs={{0,2},{1,3},{2,0},{3,1},{4,6},{5,7},{6,4},{7,5},{8,10},{9,11},{10,... | collective-permute-start | bytes 540680 | tf_op jit(solution)/shard_map/ppermute | solution.py:250
  122.2 7.5 %collective-permute-start.12 = (f32[176,512]{1,0:T(8,128)S(1)}, f32[176,512]{1,0:T(8,128)S(1)}, u32[]{:S(2)}, u32[]{:S(2)}) collective-permute-start(f32[176,512]{1,0:T(8,128)S(1)} %pad_maximum_fusion), channel_id=1, source_target_pairs={{0,4},{4,0},{8,12},{12,8},{16,20},{20,16},{24,28},{28,24},{1,5},{5... | collective-permute-start | bytes 1081352 | tf_op jit(solution)/shard_map/ppermute | solution.py:250
  123.5 8.3 %collective-permute-start.28 = (f32[160,512]{1,0:T(8,128)S(1)}, f32[160,512]{1,0:T(8,128)S(1)}, u32[]{:S(2)}, u32[]{:S(2)}) collective-permute-start(f32[160,512]{1,0:T(8,128)S(1)} %pad_maximum_fusion.2), channel_id=1, source_target_pairs={{0,8},{4,12},{8,0},{12,4},{16,24},{20,28},{24,16},{28,20},{1,9},{5... | collective-permute-start | bytes 983048 | tf_op jit(solution)/shard_map/ppermute | solution.py:250
  124.2 7.5 %collective-permute-start.20 = (f32[176,512]{1,0:T(8,128)S(1)}, f32[176,512]{1,0:T(8,128)S(1)}, u32[]{:S(2)}, u32[]{:S(2)}) collective-permute-start(f32[176,512]{1,0:T(8,128)S(1)} %pad_maximum_fusion.1), channel_id=1, source_target_pairs={{0,2},{1,3},{2,0},{3,1},{4,6},{5,7},{6,4},{7,5},{8,10},{9,11},{10,... | collective-permute-start | bytes 1081352 | tf_op jit(solution)/shard_map/ppermute | solution.py:250
  129.8 4.3 %copy-start.4 = (f32[1,512]{1,0:T(1,128)S(1)}, f32[1,512]{1,0:T(1,128)}, u32[]{:S(2)}) copy-start(f32[1,512]{1,0:T(1,128)} %get-tuple-element.59) | copy-start | bytes 6148
  131.9 63.1 %collective-permute-start.29 = (f32[1024,512]{1,0:T(8,128)S(1)}, f32[1024,512]{1,0:T(8,128)}, u32[]{:S(2)}, u32[]{:S(2)}) collective-permute-start(f32[1024,512]{1,0:T(8,128)S(1)} %select_dynamic-update-slice_fusion.4), channel_id=1, source_target_pairs={{0,1},{1,0},{2,3},{3,2},{4,5},{5,4},{6,7},{7,6},{8,9},{9,8},{10,11... | collective-permute-start | bytes 6291464 | tf_op jit(solution)/shard_map/ppermute | solution.py:250
  132.0 59.2 %collective-permute-start.2 = (f32[256,512]{1,0:T(8,128)}, f32[256,512]{1,0:T(8,128)S(1)}, u32[]{:S(2)}, u32[]{:S(2)}) collective-permute-start(f32[256,512]{1,0:T(8,128)} %get-tuple-element.57), channel_id=1, source_target_pairs={{0,28},{4,0},{8,4},{12,8},{16,12},{20,16},{24,20},{28,24},{1,29},{... | collective-permute-start | bytes 1572872 | tf_op jit(solution)/shard_map/ppermute | solution.py:246
  134.1 57.1 %collective-permute-start.3 = (f32[256,512]{1,0:T(8,128)}, f32[256,512]{1,0:T(8,128)S(1)}, u32[]{:S(2)}, u32[]{:S(2)}) collective-permute-start(f32[256,512]{1,0:T(8,128)} %get-tuple-element.58), channel_id=1, source_target_pairs={{0,4},{4,8},{8,12},{12,16},{16,20},{20,24},{24,28},{28,0},{1,5},{5... | collective-permute-start | bytes 1572872 | tf_op jit(solution)/shard_map/ppermute | solution.py:246
  (3 other events, 2.5 us)

commit v2 on v1

v2 whole, which is shorter than its diff:
```python
import functools

import jax
import jax.numpy as jnp
from jax import lax
from jax.experimental import pallas as pl
from jax.experimental.pallas import tpu as pltpu
from jax.sharding import PartitionSpec as P

HEADS = 8
PT = 128
HD = 64
PAIRS = HEADS // 2
F32 = jnp.float32
BF16 = jnp.bfloat16
NN = (((1,), (0,)), ((), ()))
NT = (((1,), (1,)), ((), ()))
VMEM = pl.BlockSpec(memory_space=pltpu.VMEM)
SMEM = pl.BlockSpec(memory_space=pltpu.SMEM)


def pair_of(x):
    high = x.astype(BF16)
    return high, (x - high.astype(F32)).astype(BF16)


def dot(left, right, dims=NN):
    return lax.dot_general(left, right, dims, preferred_element_type=F32)


def dot3(left, right, dims=NN):
    return dot(left[0], right[0], dims) + (dot(left[0], right[1], dims) + dot(left[1], right[0], dims))


def load(refs, *index):
    return refs[0][index], refs[1][index]


def store(refs, pair, *index):
    refs[0][index] = pair[0]
    refs[1][index] = pair[1]


def unit_rows(tokens):
    centred = tokens - jnp.mean(tokens, axis=1, keepdims=True)
    variance = jnp.mean(centred * centred, axis=1, keepdims=True)
    rstd = lax.rsqrt(variance + 1e-05)
    return centred * rstd, rstd


def store_stacked(ref, row, rows):
    count = rows.shape[0]
    left_half = lax.broadcasted_iota(jnp.int32, (count, 2 * HD), 1) < HD
    for p in range(PAIRS):
        part = rows[:, p * 2 * HD : (p + 1) * 2 * HD]
        swapped = pltpu.roll(part, HD, 1)
        for a in range(2):
            both = jnp.where(left_half == (a == 0), part, swapped)
            high, low = pair_of(both)
            base = (2 * p + a) * 4 * HD
            ref[pl.ds(row, count), base : base + 2 * HD] = high
            ref[pl.ds(row, count), base + 2 * HD : base + 4 * HD] = low


def store_interleaved(ref, columns):
    high, low = pair_of(columns)
    for h in range(HEADS):
        for i, piece in enumerate((high, low, high, low)):
            at = h * 4 * HD + i * HD
            ref[at : at + HD, :] = piece[h * HD : (h + 1) * HD]


def sums_of(left, right, dims=NN):
    return sum(dot3(a, b, dims) for a, b in zip(left[1:], right[1:], strict=True)) + dot3(left[0], right[0], dims)


def weight_kernel(_me, _parity, wq, wk, wv, wo, wq_h, wq_l, wk_h, wk_l, wv_h, wv_l, wo_h, wo_l):
    for source, high, low in ((wq, wq_h, wq_l), (wk, wk_h, wk_l), (wv, wv_h, wv_l), (wo, wo_h, wo_l)):
        store((high, low), pair_of(source[...]), ...)


def own_kernel(
    _, tokens, gain, cot, wq_h, wq_l, wk_h, wk_l, wv_h, wv_l, wo_h, wo_l,
    xhat, ht_h, ht_l, q_t, q_stack, k_stack, v_stack, kt_h, kt_l, vt_h, vt_l, d_mixed_t, d_stack,
):
    normal, _ = unit_rows(tokens[...])
    xhat[...] = normal
    hidden = normal * gain[...]
    store((ht_h, ht_l), pair_of(hidden.T), ...)
    rows = pair_of(hidden)
    query = dot3(rows, load((wq_h, wq_l), ...)) * HD ** (-0.5)
    q_t[...] = query.T
    store_interleaved(q_stack, q_t[...])
    key = dot3(rows, load((wk_h, wk_l), ...))
    store_stacked(k_stack, 0, key)
    store((kt_h, kt_l), pair_of(key.T), ...)
    value = dot3(rows, load((wv_h, wv_l), ...))
    store_stacked(v_stack, 0, value)
    store((vt_h, vt_l), pair_of(value.T), ...)
    d_mixed = dot3(load((wo_h, wo_l), ...), pair_of(cot[...]), NT)
    d_mixed_t[...] = d_mixed
    store_interleaved(d_stack, d_mixed)


def store_bias(bias, listed, counts, parity, patches):
    queries = bias.shape[1]
    lane = lax.broadcasted_iota(jnp.int32, (1, queries), 1)
    near = jnp.where(parity[0] == 0, 4, 0)
    windows = (2, 3, near, near + 1, 4 - near, 5 - near)
    for place in patches:
        level = []
        for p in range(2):
            live = jnp.int32(1 if place == p else 0)
            for j in range(listed.shape[1]):
                hit = jnp.logical_and(j < counts[0, p], listed[p, j] == windows[place])
                live = jnp.where(hit, 1, live)
            level.append(jnp.where(live == 1, 0.0, -1e30).astype(F32))
        bias[place : place + 1, :] = jnp.where(lane < PT, level[0], level[1])


def biased(scores, bias, first):
    count = scores.shape[0] // PT
    return jnp.concatenate(
        [scores[i * PT : (i + 1) * PT] + bias[first + i : first + i + 1, :] for i in range(count)], axis=0
    )


def key_side(patches, gain, wk, wv, xhat, ht, k_stack, kt, v_stack, vt):
    for i, tokens in enumerate(patches):
        normal, _ = unit_rows(tokens[...])
        at = slice(i * PT, (i + 1) * PT)
        xhat[at, :] = normal
        hidden = normal * gain[...]
        store(ht, pair_of(hidden.T), slice(None), at)
    hidden = pair_of(xhat[...] * gain[...])
    key = dot3(hidden, load(wk, ...))
    store_stacked(k_stack, 0, key)
    store(kt, pair_of(key.T), ...)
    value = dot3(hidden, load(wv, ...))
    store_stacked(v_stack, 0, value)
    store(vt, pair_of(value.T), ...)


def head_rows(h):
    return pl.ds(pl.multiple_of(h * HD, HD), HD)


def head_stack(h):
    return pl.ds(pl.multiple_of(h * 4 * HD, 4 * HD), 4 * HD)


def weighed(highs, lows, rows, right):
    high = jnp.concatenate([r[rows, :] for r in highs], axis=1)
    low = jnp.concatenate([r[rows, :] for r in lows], axis=1)
    both = dot(jnp.concatenate([high, low], axis=0), right[0])
    return both[:HD] + (both[HD:] + dot(high, right[1]))


def near_kernel(
    parity, listed, counts, patch_0, patch_1, gain, q_stack, k_stack, v_stack, vt_h, vt_l, d_stack,
    wk_h, wk_l, wv_h, wv_l,
    xhat, ht_h, ht_l, kt_h, kt_l, e_h, e_l, d_scores, mixed, tops, totals,
    bias, k_near, v_near, vt2_h, vt2_l,
):
    store_bias(bias, listed, counts, parity, range(4))
    key_side(
        (patch_0, patch_1), gain, (wk_h, wk_l), (wv_h, wv_l), xhat, (ht_h, ht_l), k_near, (kt_h, kt_l), v_near,
        (vt2_h, vt2_l),
    )

    def one_head(h, carry):
        stack, rows = head_stack(h), head_rows(h)
        q_now, d_now = q_stack[stack, :], d_stack[stack, :]
        scores = jnp.concatenate(
            [biased(dot(k_stack[:, stack], q_now), bias, 0), biased(dot(k_near[:, stack], q_now), bias, 2)], axis=0
        )
        top = jnp.max(scores, axis=0, keepdims=True)
        weights = jnp.exp(scores - top)
        tops[pl.ds(h, 1), :] = top
        totals[pl.ds(h, 1), :] = jnp.sum(weights, axis=0, keepdims=True)
        pair = pair_of(weights)
        e_h[h] = pair[0]
        e_l[h] = pair[1]
        mixed[rows, :] = weighed((vt_h, vt2_h), (vt_l, vt2_l), rows, pair)
        d_scores[h] = jnp.concatenate([dot(v_stack[:, stack], d_now), dot(v_near[:, stack], d_now)], axis=0)
        return carry

    lax.fori_loop(0, HEADS, one_head, 0, unroll=UNROLL)


def gathered(left_h, left_l, right):
    left_half = lax.broadcasted_iota(jnp.int32, right[0].shape, 1) < HD
    zero = jnp.zeros_like(right[0])
    one = [jnp.where(left_half, x, zero) for x in right]
    two = [jnp.where(left_half, zero, x) for x in right]
    wide = dot(left_h[0], jnp.concatenate(one, axis=1)) + dot(left_h[1], jnp.concatenate(two, axis=1))
    narrow = dot(left_l[0], one[0]) + dot(left_l[1], two[0])
    return wide[:, : 2 * HD] + (wide[:, 2 * HD :] + narrow)


def pair_lanes(p):
    return pl.ds(pl.multiple_of(p * 2 * HD, 2 * HD), 2 * HD)


def kept_and_sent(me, pair, keep, send):
    rows = pair[0].shape[0]

    @pl.when(me[0] % 2 == 0)
    def _():
        keep[:rows, :] = pair[0][...]
        send[:rows, :] = pair[1][...]

    @pl.when(me[0] % 2 == 1)
    def _():
        keep[:rows, :] = pair[1][...]
        send[:rows, :] = pair[0][...]


def far_kernel(
    parity, listed, counts, patch_0, patch_1, gain, q_t, q_stack, d_mixed_t, d_stack, mixed_1, tops, totals,
    wk_h, wk_l, wv_h, wv_l,
    xhat, ht_h, ht_l, kt_h, kt_l, u_h, u_l, mixed_t, deltas, shares, shares_1, dk_h, dk_l, dv_h, dv_l, d_far,
    bias, k_far, v_far, vt_h, vt_l, e_h, e_l,
):
    store_bias(bias, listed, counts, parity, range(4, 6))
    key_side(
        (patch_0, patch_1), gain, (wk_h, wk_l), (wv_h, wv_l), xhat, (ht_h, ht_l), k_far, (kt_h, kt_l), v_far,
        (vt_h, vt_l),
    )

    def one_pair(p, carry):
        d_scaled, q_scaled = [], []
        for a in range(2):
            h = 2 * p + a
            stack, rows, row = head_stack(h), head_rows(h), pl.ds(h, 1)
            scores = biased(dot(k_far[:, stack], q_stack[stack, :]), bias, 4)
            top_1 = tops[row, :]
            top = jnp.maximum(top_1, jnp.max(scores, axis=0, keepdims=True))
            weights = jnp.exp(scores - top)
            shrink = jnp.exp(top_1 - top)
            share = 1.0 / (shrink * totals[row, :] + jnp.sum(weights, axis=0, keepdims=True))
            share_1 = shrink * share
            pair = pair_of(weights)
            e_h[a] = pair[0]
            e_l[a] = pair[1]
            mixed = share_1 * mixed_1[rows, :] + share * weighed((vt_h,), (vt_l,), rows, pair)
            mixed_t[rows, :] = mixed
            d_mixed = d_mixed_t[rows, :]
            delta = jnp.sum(d_mixed * mixed, axis=0, keepdims=True)
            deltas[row, :] = delta
            shares[row, :] = share
            shares_1[row, :] = share_1
            pair = pair_of(weights * (dot(v_far[:, stack], d_stack[stack, :]) - delta))
            u_h[h] = pair[0]
            u_l[h] = pair[1]
            d_scaled.append(d_mixed * share)
            q_scaled.append(q_t[rows, :] * share)
        lanes = pair_lanes(p)
        right = pair_of(jnp.concatenate(d_scaled, axis=0).T)
        d_value = gathered((e_h[0], e_h[1]), (e_l[0], e_l[1]), right)
        store((dv_h, dv_l), pair_of(d_value), slice(None), lanes)
        right = pair_of(jnp.concatenate(q_scaled, axis=0).T)
        d_key = gathered((u_h[2 * p], u_h[2 * p + 1]), (u_l[2 * p], u_l[2 * p + 1]), right)
        store((dk_h, dk_l), pair_of(d_key), slice(None), lanes)
        return carry

    lax.fori_loop(0, PAIRS, one_pair, 0, unroll=UNROLL)
    d_far[...] = sums_of(
        [load((dk_h, dk_l), ...), load((dv_h, dv_l), ...)], [load((wk_h, wk_l), ...), load((wv_h, wv_l), ...)], NT
    )


def mix_kernel(
    me, mixed_t, e_h, e_l, d_mixed_t, shares_1, ht_h, ht_l, ht2_h, ht2_l, ht3_h, ht3_l, dv3_h, dv3_l, tokens, cot,
    wo_h, wo_l,
    result, keep, send, dv_h, dv_l,
    grad_o, grad_v,
):
    own = tokens.shape[0]

    def one_pair(p, carry):
        d_scaled = [
            d_mixed_t[head_rows(2 * p + a), :] * shares_1[pl.ds(2 * p + a, 1), :] for a in range(2)
        ]
        right = pair_of(jnp.concatenate(d_scaled, axis=0).T)
        d_value = gathered((e_h[2 * p], e_h[2 * p + 1]), (e_l[2 * p], e_l[2 * p + 1]), right)
        store((dv_h, dv_l), pair_of(d_value), slice(None), pair_lanes(p))
        return carry

    lax.fori_loop(0, PAIRS, one_pair, 0, unroll=UNROLL)
    mixed = mixed_t[...]
    grad_o[...] = dot3(pair_of(mixed), pair_of(cot[...]))
    turned = [load(t, ...) for t in ((ht_h, ht_l), (ht2_h, ht2_l), (ht3_h, ht3_l))]
    d_values = [load((dv_h, dv_l), slice(0, own)), load((dv_h, dv_l), slice(own, 2 * own)), load((dv3_h, dv3_l), ...)]
    grad_v[...] = sums_of(turned, d_values)
    kept_and_sent(me, (grad_o, grad_v), keep, send)
    result[...] = dot3(pair_of(mixed.T), load((wo_h, wo_l), ...)) + tokens[...]


def back_kernel(
    d_back, q_t, kt_h, kt_l, kt2_h, kt2_l, kt3_h, kt3_l, e_h, e_l, d_scores, u_h, u_l, deltas, shares, shares_1,
    dv_h, dv_l, wk_h, wk_l, wv_h, wv_l,
    d_near, dq_t, dk_h, dk_l,
    s_h, s_l,
):
    own = d_near.shape[0]

    def one_pair(p, carry):
        q_scaled = []
        for a in range(2):
            h = 2 * p + a
            rows, row = head_rows(h), pl.ds(h, 1)
            weights = e_h[h].astype(F32) + e_l[h].astype(F32)
            pair = pair_of(weights * (d_scores[h] - deltas[row, :]))
            s_h[a] = pair[0]
            s_l[a] = pair[1]
            share_1 = shares_1[row, :]
            one = weighed((kt_h, kt2_h), (kt_l, kt2_l), rows, pair)
            two = weighed((kt3_h,), (kt3_l,), rows, (u_h[h], u_l[h]))
            dq_t[rows, :] = (share_1 * one + shares[row, :] * two) * HD ** (-0.5)
            q_scaled.append(q_t[rows, :] * share_1)
        right = pair_of(jnp.concatenate(q_scaled, axis=0).T)
        d_key = gathered((s_h[0], s_h[1]), (s_l[0], s_l[1]), right)
        store((dk_h, dk_l), pair_of(d_key), slice(None), pair_lanes(p))
        return carry

    lax.fori_loop(0, PAIRS, one_pair, 0, unroll=UNROLL)
    near = slice(own, 2 * own)
    d_near[...] = d_back[...] + sums_of(
        [load((dk_h, dk_l), near), load((dv_h, dv_l), near)], [load((wk_h, wk_l), ...), load((wv_h, wv_l), ...)], NT
    )


def grad_kernel(
    me, d_back, ht_h, ht_l, ht2_h, ht2_l, ht3_h, ht3_l, xhat, xhat2, xhat3, dq_t, dk_h, dk_l, dk3_h, dk3_l, dv_h, dv_l,
    d_near, d_far, wq_h, wq_l, wk_h, wk_l, wv_h, wv_l,
    keep, send, d_own,
    grad_q, grad_k,
):
    own, width = d_own.shape
    first, second = slice(0, own), slice(own, 2 * own)
    d_query = pair_of(dq_t[...].T)
    turned = [load(t, ...) for t in ((ht_h, ht_l), (ht2_h, ht2_l), (ht3_h, ht3_l))]
    d_keys = [load((dk_h, dk_l), first), load((dk_h, dk_l), second), load((dk3_h, dk3_l), ...)]
    grad_q[...] = dot3(turned[0], d_query)
    grad_k[...] = sums_of(turned, d_keys)
    w_q, w_k, w_v = load((wq_h, wq_l), ...), load((wk_h, wk_l), ...), load((wv_h, wv_l), ...)
    d_own[...] = sums_of([d_query, d_keys[0], load((dv_h, dv_l), first)], [w_q, w_k, w_v], NT)
    d_gain = jnp.sum(
        d_own[...] * xhat[...] + (d_near[...] - d_back[...]) * xhat2[...] + d_far[...] * xhat3[...],
        axis=0, keepdims=True,
    )
    top = lax.broadcasted_iota(jnp.int32, (TAIL, width), 0) == 0
    for out in (keep, send):
        out[width:, :] = jnp.where(top, d_gain, 0.0)
    kept_and_sent(me, (grad_q, grad_k), keep, send)


TAIL = 8


def half_of(me, mask, mine, rows):
    index = (me[0] // mask) % 2
    return pl.ds(pl.multiple_of((index if mine else 1 - index) * rows, 8), rows)


def add_kernel(a, b, out):
    out[...] = a[...] + b[...]


def last_kernel(a, b, out, tail):
    rows = out.shape[0]
    out[...] = a[:rows, :] + b[:rows, :]
    tail[...] = a[rows : rows + 1, :] + b[rows : rows + 1, :]


def cut_kernel(masks, me, keep_1, other_1, keep_2, other_2, *outs):
    count = keep_1.shape[0]
    sums = outs[-1]
    sums[:count, :] = keep_1[...] + other_1[...]
    sums[count:, :] = keep_2[...] + other_2[...]
    tail = sums[2 * count :, :]
    at = 0
    for i, mask in enumerate(masks):
        keep, send = outs[2 * i], outs[2 * i + 1]
        rows = keep.shape[0] - (TAIL if i == 0 else 0)
        for out, mine in ((keep, True), (send, False)):
            index = (me[0] // mask) % 2
            start = at + (index if mine else 1 - index) * rows
            out[:rows, :] = sums[pl.ds(pl.multiple_of(start, 8), rows), :]
            if i == 0:
                out[rows:, :] = tail
        at += 2 * rows


def halve_kernel(mask, tail, me, keep, other, next_keep, next_send):
    rows = next_keep.shape[0] - tail
    for out, mine in ((next_keep, True), (next_send, False)):
        at = half_of(me, mask, mine, rows)
        out[:rows, :] = keep[at, :] + other[at, :]
        if tail:
            out[rows:, :] = keep[2 * rows :, :] + other[2 * rows :, :]


def join_kernel(mask, me, *refs):
    *ins, keep, send, d_tokens, sums = refs
    at = 0
    for i in range(3):
        rows = ins[2 * i].shape[0] - (TAIL if i == 0 else 0)
        sums[at : at + rows, :] = ins[2 * i][:rows, :] + ins[2 * i + 1][:rows, :]
        at += rows
    tail = ins[0][rows_of(ins[0]) :, :] + ins[1][rows_of(ins[0]) :, :]
    for out, mine in ((keep, True), (send, False)):
        out[: at // 2, :] = sums[half_of(me, mask, mine, at // 2), :]
        out[at // 2 :, :] = tail
    tokens_kernel(*ins[6:], d_tokens)


def rows_of(ref):
    return ref.shape[0] - TAIL


def part_kernel(mask, me, mine, other, *outs):
    *parts, whole = outs
    rows = mine.shape[0]
    whole[half_of(me, mask, True, rows), :] = mine[...]
    whole[half_of(me, mask, False, rows), :] = other[...]
    at = 0
    for out in parts:
        out[...] = whole[at : at + out.shape[0], :]
        at += out.shape[0]


def double_kernel(mask, me, mine, other, out):
    rows = mine.shape[0]
    out[half_of(me, mask, True, rows), :] = mine[...]
    out[half_of(me, mask, False, rows), :] = other[...]


def split_kernel(ranges, me, *refs):
    *ins, one, two = refs
    count = len(ins) // 2
    for bit in range(2):

        @pl.when(me[0] % 2 == bit)
        def _():
            for out, pieces in ((one, ins[:count] if bit == 0 else ins[count:]), (two, ins[count:] if bit == 0 else ins[:count])):
                at = 0
                for piece, (start, stop) in zip(pieces, ranges):
                    out[at : at + stop - start, :] = piece[start:stop, :]
                    at += stop - start


def tokens_kernel(tokens, gain, cot, d_own, d_other, out):
    normal, rstd = unit_rows(tokens[...])
    d_normal = (d_own[...] + d_other[...]) * gain[...]
    inner = jnp.mean(d_normal * normal, axis=1, keepdims=True)
    centre = jnp.mean(d_normal, axis=1, keepdims=True)
    out[...] = (d_normal - centre - normal * inner) * rstd + cot[...]


def shape(*dims, dtype=F32):
    return jax.ShapeDtypeStruct(dims, dtype)


def pairs(*dims):
    return [shape(*dims, dtype=BF16)] * 2


def call(kernel, inputs, outputs, scratch=(), scalars=0, limit=4, us=1):
    return pl.pallas_call(
        kernel,
        out_shape=outputs,
        in_specs=[SMEM] * scalars + [VMEM] * (len(inputs) - scalars),
        out_specs=[VMEM] * len(outputs),
        scratch_shapes=[pltpu.VMEM(s.shape, s.dtype) for s in scratch],
        compiler_params=pltpu.CompilerParams(vmem_limit_bytes=limit * 2**20),
        cost_estimate=pl.CostEstimate(flops=us * 10**9, bytes_accessed=0, transcendentals=0),
    )(*inputs)


def along_space(value, target):
    count = lax.axis_size("space")
    return lax.ppermute(value, "space", [(i, target(i) % count) for i in range(count)])


def across(value):
    return along_space(value, lambda i: i ^ 1)


def onward(value):
    return along_space(value, lambda i: i + 2 - 4 * (i % 2))


def homeward(value):
    return along_space(value, lambda i: i - 2 + 4 * (i % 2))


def devices():
    return lax.axis_size("space") * lax.axis_size("slab")


def swapped(value, mask):
    return lax.ppermute(value, ("space", "slab"), [(i, i ^ mask) for i in range(devices())])


ORDERS = ((4, 2, 8), (2, 8, 4), (8, 4, 2))
LAST = 16


def summed(me, keep_1, other_1, keep_2, send_2, token_side):
    count, width = keep_1.shape
    total = 2 * count
    unit = 8 * 8
    sizes = [total // unit // 3 * unit] * 2
    sizes.append(total - sum(sizes))
    tails = (TAIL, 0, 0)
    halves = [size // 2 for size in sizes]
    parts = call(
        functools.partial(cut_kernel, [order[0] for order in ORDERS]),
        (me, keep_1, other_1, keep_2, swapped(send_2, 1)),
        [shape(half + tail, width) for half, tail in zip(halves, tails) for _ in range(2)],
        [shape(total + TAIL, width)],
        scalars=1, limit=8,
    )
    parts = [[parts[2 * i], swapped(parts[2 * i + 1], ORDERS[i][0])] for i in range(3)]
    for step in (1, 2):
        for i in range(3):
            rows, mask = sizes[i] >> (step + 1), ORDERS[i][step]
            keep, send = call(
                functools.partial(halve_kernel, mask, tails[i]), (me, *parts[i]), [shape(rows + tails[i], width)] * 2,
                scalars=1,
            )
            parts[i] = [keep, swapped(send, mask)]
    joined = total // 8
    keep, send, *d_tokens = call(
        functools.partial(join_kernel, LAST), (me, *parts[0], *parts[1], *parts[2], *token_side),
        [shape(joined // 2 + TAIL, width)] * 2 + [token_side[0]], [shape(joined, width)], scalars=1, limit=8,
    )
    other = swapped(send, LAST)
    mask = 2 * LAST
    while mask < devices():
        (keep,) = call(add_kernel, (keep, other), [keep])
        other = swapped(keep, mask)
        mask *= 2
    mine, d_gain = call(last_kernel, (keep, other), [shape(joined // 2, width), shape(1, width)])
    parts = list(call(
        functools.partial(part_kernel, LAST), (me, mine, swapped(mine, LAST)),
        [shape(size // 8, width) for size in sizes], [shape(joined, width)], scalars=1,
    ))
    for step in (2, 1, 0):
        for i in range(3):
            mask = ORDERS[i][step]
            (parts[i],) = call(
                functools.partial(double_kernel, mask), (me, parts[i], swapped(parts[i], mask)),
                [shape(2 * parts[i].shape[0], width)], scalars=1,
            )
    others = [swapped(part, 1) for part in parts]
    split = count - sizes[0]
    first = call(
        functools.partial(split_kernel, [(0, sizes[0]), (0, split)]), (me, *parts[:2], *others[:2]),
        [shape(count, width)] * 2, scalars=1, limit=8,
    )
    second = call(
        functools.partial(split_kernel, [(split, sizes[1]), (0, sizes[2])]), (me, *parts[1:], *others[1:]),
        [shape(count, width)] * 2, scalars=1, limit=8,
    )
    return first, second, d_gain.reshape(width), d_tokens


def body(tokens, gain, wq, wk, wv, wo, neighbour_list, neighbour_count, cotangent):
    rows, width = tokens.shape
    me = (lax.axis_index("space") * lax.axis_size("slab") + lax.axis_index("slab")).astype(jnp.int32)[None]
    parity = (lax.axis_index("space") % 2).astype(jnp.int32)[None]
    counts = neighbour_count[None, :]
    near = [across(tokens[i * PT : (i + 1) * PT]) for i in range(2)]
    far = [onward(part) for part in near]
    gain_row = gain[None, :]
    stack_rows, stack_columns = shape(HEADS * 4 * HD, rows, dtype=BF16), shape(rows, HEADS * 4 * HD, dtype=BF16)
    turned, square, pair = pairs(width, rows), pairs(width, width), pairs(rows, width)
    whole, whole_t, scalars = shape(rows, width), shape(width, rows), shape(HEADS, rows)
    weights = call(weight_kernel, (me, parity, wq, wk, wv, wo), square * 4, scalars=2, limit=20, us=2)
    wq_h, wq_l, wk_h, wk_l, wv_h, wv_l, wo_h, wo_l = weights
    (
        xhat, ht_h, ht_l, q_t, q_stack, k_stack, v_stack, kt_h, kt_l, vt_h, vt_l, d_mixed_t, d_stack,
    ) = call(
        own_kernel,
        (near[0], tokens, gain_row, cotangent, *weights),
        [whole, *turned, whole_t, stack_rows, stack_columns, stack_columns, *turned, *turned, whole_t, stack_rows],
        limit=LIMITS[0], us=3,
    )
    w_k, w_v = (wk_h, wk_l), (wv_h, wv_l)
    xhat2, ht2_h, ht2_l, kt2_h, kt2_l, e_h, e_l, d_scores, mixed, tops, totals = call(
        near_kernel,
        (
            parity, neighbour_list, counts, *near, gain_row, q_stack, k_stack, v_stack, vt_h, vt_l, d_stack,
            *w_k, *w_v,
        ),
        [
            whole, *turned, *turned, *pairs(HEADS, 2 * rows, rows), shape(HEADS, 2 * rows, rows), whole_t, scalars,
            scalars,
        ],
        [shape(8, rows), stack_columns, stack_columns, *turned],
        scalars=3, limit=LIMITS[1], us=6,
    )
    (
        xhat3, ht3_h, ht3_l, kt3_h, kt3_l, u_h, u_l, mixed_t, deltas, shares, shares_1, dk3_h, dk3_l, dv3_h, dv3_l,
        d_far,
    ) = call(
        far_kernel,
        (
            parity, neighbour_list, counts, *far, gain_row, q_t, q_stack, d_mixed_t, d_stack, mixed, tops, totals,
            *w_k, *w_v,
        ),
        [
            whole, *turned, *turned, *pairs(HEADS, rows, rows), whole_t, scalars, scalars, scalars, *pair, *pair,
            whole,
        ],
        [shape(8, rows), stack_columns, stack_columns, *turned, *pairs(2, rows, rows)],
        scalars=3, limit=LIMITS[2], us=6,
    )
    d_back = homeward(d_far)
    result, keep_1, send_1, dv_h, dv_l = call(
        mix_kernel,
        (
            me, mixed_t, e_h, e_l, d_mixed_t, shares_1, ht_h, ht_l, ht2_h, ht2_l, ht3_h, ht3_l, dv3_h, dv3_l, tokens,
            cotangent, wo_h, wo_l,
        ),
        [whole, shape(width, width), shape(width, width), *pairs(2 * rows, width)],
        [shape(width, width), shape(width, width)],
        scalars=1, limit=LIMITS[3], us=5,
    )
    other_1 = swapped(send_1, 1)
    d_near, dq_t, dk_h, dk_l = call(
        back_kernel,
        (
            d_back, q_t, kt_h, kt_l, kt2_h, kt2_l, kt3_h, kt3_l, e_h, e_l, d_scores, u_h, u_l, deltas, shares, shares_1,
            dv_h, dv_l, *w_k, *w_v,
        ),
        [whole, whole_t, *pairs(2 * rows, width)],
        [*pairs(2, 2 * rows, rows)],
        limit=LIMITS[4], us=5,
    )
    d_other = across(d_near)
    tall = shape(width + TAIL, width)
    keep_2, send_2, d_own = call(
        grad_kernel,
        (
            me, d_back, ht_h, ht_l, ht2_h, ht2_l, ht3_h, ht3_l, xhat, xhat2, xhat3, dq_t, dk_h, dk_l, dk3_h, dk3_l,
            dv_h, dv_l, d_near, d_far, wq_h, wq_l, *w_k, *w_v,
        ),
        [tall, tall, whole],
        [shape(width, width), shape(width, width)],
        scalars=1, limit=LIMITS[5], us=4,
    )
    (grad_o, grad_v), (grad_q, grad_k), d_gain, (d_tokens,) = summed(
        me, keep_1, other_1, keep_2, send_2, (tokens, gain_row, cotangent, d_own, d_other)
    )
    return (result, d_tokens, d_gain, grad_q, grad_k, grad_v, grad_o)


UNROLL = False
LIMITS = (8, 8, 8, 8, 8, 8)


def solution(mesh):
    tokens = P(("space", "slab"), None)
    return jax.shard_map(
        body,
        mesh=mesh,
        in_specs=(tokens, P(), P(), P(), P(), P(), tokens, P(("space", "slab")), tokens),
        out_specs=(tokens, tokens, P(), P(), P(), P(), P()),
        check_vma=False,
    )
```

time: 199 us -> 139 us (0.70)
  blocking collectives: 57.1 us -> 0 us
  other arithmetic: 5.1 us -> 0 us
  waiting for transfers between devices: 59.4 us -> 64.4 us
    psum x1 -> x0, blocking collectives: 57.1 us -> none  [body(): d_gain = lax.psum(d_gain[0], ('space', 'slab'))]
    ppermute x30 -> x31, waiting for transfers between devices: 59.4 us -> 64.4 us  [the longest x25 55.4 us: swapped(): lax.ppermute(value, ('space', 'slab'), [(i, i ^ mask) for i in range(devi...]
    dynamic_slice x13 -> x0, local copies, waits for them, and re-layouts: 3.39 us -> none  [half(): return lax.dynamic_slice_in_dim(value, index * rows, rows, 0)]
    unnamed x10 -> x18, local copies, waits for them, and re-layouts: 1.75 us -> 4.92 us
    add x13 -> x0, other arithmetic: 2.39 us -> none  [halved(): return half(value, mine) + swapped(half(value, 1 - mine), *dim)]
    select_n x10 -> x0, other arithmetic: 2.25 us -> none  [the longest x1 2.09 us: doubled(): jnp.where(mine == 0, other, value)]
    pallas_call x3 -> x28, Pallas kernels: 38.6 us -> 37 us  [call(): pl.pallas_call(kernel, out_shape=outputs, in_specs=[SMEM] * scalars + [VM...]
    ppermute x30 -> x31, starting transfers between devices: 30.5 us -> 30.1 us  [the longest x25 20.8 us: swapped(): lax.ppermute(value, ('space', 'slab'), [(i, i ^ mask) for i in range(devi...]
  transfers between devices with their start and end apart: 30 -> 31, of which waited for: 22 -> 22; matrix products, arithmetic and copies ran while one was open for 1% -> 0% of each run, Pallas kernels for 5% -> 13%
where the time goes in v2:
time: 139 us; the launch traced here: 138 us
  waiting for transfers between devices  64.4 us (46%)
  Pallas kernels  37 us (27%)
  starting transfers between devices  30.1 us (22%)
  local copies, waits for them, and re-layouts  5.99 us (4%)
    ppermute x25, waiting for transfers between devices, swapped(): lax.ppermute(value, ('space', 'slab'), [(i, i ^ mask) for i in range(devi...  55.4 us
    pallas_call x28, Pallas kernels, call(): pl.pallas_call(kernel, out_shape=outputs, in_specs=[SMEM] * scalars + [VM...  37 us
    ppermute x25, starting transfers between devices, swapped(): lax.ppermute(value, ('space', 'slab'), [(i, i ^ mask) for i in range(devi...  20.8 us
    ppermute x6, starting transfers between devices, along_space(): lax.ppermute(value, 'space', [(i, target(i) % count) for i in range(count)])  9.3 us
    ppermute x6, waiting for transfers between devices, along_space(): lax.ppermute(value, 'space', [(i, target(i) % count) for i in range(count)])  8.98 us
    unnamed x18, local copies, waits for them, and re-layouts  4.92 us
  transfers between devices with their start and end apart: 31, of which 22 were waited for; matrix products, arithmetic and copies ran while one was open for 0% of the time, Pallas kernels for 13%

profile of v2, /device:TPU:0, one launch (start us, length us, event | category | flops | bytes accessed | tf_op | source)
XLA Modules:
  0.0 138.4 jit_solution(9764847487022393339)
XLA Ops:
  1.7 3.0 %collective-permute-start = (f32[128,512]{1,0:T(8,128)S(1)}, f32[128,512]{1,0:T(8,128)S(1)}, u32[]{:S(2)}, u32[]{:S(2)}) collective-permute-start(f32[128,512]{1,0:T(8,128)S(1)} %get-tuple-element.188), channel_id=1, source_target_pairs={{0,4},{4,0},{8,12},{12,8},{16,20},{20,16},{24,28},{28,24},{1,5},{5... | collective-permute-start | bytes 786440 | tf_op jit(solution)/shard_map/ppermute | solution.py:484
  11.8 2.1 %collective-permute-start.1 = (f32[128,512]{1,0:T(8,128)S(1)}, f32[128,512]{1,0:T(8,128)S(1)}, u32[]{:S(2)}, u32[]{:S(2)}) collective-permute-start(f32[128,512]{1,0:T(8,128)S(1)} %collective-permute-done._.patch_0), channel_id=1, source_target_pairs={{0,8},{4,28},{8,16},{12,4},{16,24},{20,12},{24,0},{28,20},{1,9},{5... | collective-permute-start | bytes 786440 | tf_op jit(solution)/shard_map/ppermute | solution.py:484
  14.0 2.6 %collective-permute-done.2.patch_1 = f32[128,512]{1,0:T(8,128)S(1)} collective-permute-done((f32[128,512]{1,0:T(8,128)S(1)}, f32[128,512]{1,0:T(8,128)S(1)}, u32[]{:S(2)}, u32[]{:S(2)}) %collective-permute-start.2) | collective-permute-done | bytes 262176 | tf_op jit(solution)/shard_map/ppermute | solution.py:484
  16.6 1.8 %collective-permute-start.3 = (f32[128,512]{1,0:T(8,128)S(1)}, f32[128,512]{1,0:T(8,128)S(1)}, u32[]{:S(2)}, u32[]{:S(2)}) collective-permute-start(f32[128,512]{1,0:T(8,128)S(1)} %collective-permute-done.2.patch_1), channel_id=1, source_target_pairs={{0,8},{4,28},{8,16},{12,4},{16,24},{20,12},{24,0},{28,20},{1,9},{5... | collective-permute-start | bytes 786440 | tf_op jit(solution)/shard_map/ppermute | solution.py:484
  18.5 2.3 %shard_map.145 = (f32[256,512]{1,0:T(8,128)S(1)}, bf16[512,256]{1,0:T(8,128)(2,1)S(1)}, bf16[512,256]{1,0:T(8,128)(2,1)S(1)}, f32[512,256]{1,0:T(8,128)S(1)}, bf...) custom-call(f32[128,512]{1,0:T(8,128)S(1)} %collective-permute-done., ...), custom_call_target="tpu_custom_call" | custom-call | flops 3000000000 | tf_op jit(solution)/shard_map/pallas_call | solution.py:471
  20.8 7.1 %shard_map.146 = (f32[256,512]{1,0:T(8,128)S(1)}, bf16[512,256]{1,0:T(8,128)(2,1)S(1)}, bf16[512,256]{1,0:T(8,128)(2,1)S(1)}, bf16[512,256]{1,0:T(8,128)(2,1)S(1...) custom-call(s32[1]{0:T(128)} %bitcast.1._parity.parity, ...), custom_call_target="tpu_custom_call" | custom-call | flops 6000000000 | tf_op jit(solution)/shard_map/pallas_call | solution.py:471
  27.9 7.8 %shard_map.147 = (f32[256,512]{1,0:T(8,128)S(1)}, bf16[512,256]{1,0:T(8,128)(2,1)S(1)}, bf16[512,256]{1,0:T(8,128)(2,1)S(1)}, bf16[512,256]{1,0:T(8,128)(2,1)S(1...) custom-call(s32[1]{0:T(128)} %bitcast.1._parity.parity, ...), custom_call_target="tpu_custom_call" | custom-call | flops 6000000000 | tf_op jit(solution)/shard_map/pallas_call | solution.py:471
  35.8 2.1 %collective-permute-start.5 = (f32[256,512]{1,0:T(8,128)S(1)}, f32[256,512]{1,0:T(8,128)S(1)}, u32[]{:S(2)}, u32[]{:S(2)}) collective-permute-start(f32[256,512]{1,0:T(8,128)S(1)} %get-tuple-element.131.d_far), channel_id=1, source_target_pairs={{0,24},{4,12},{8,0},{12,20},{16,8},{20,28},{24,16},{28,4},{1,25},{... | collective-permute-start | bytes 1572872 | tf_op jit(solution)/shard_map/ppermute | solution.py:484
  37.9 5.7 %shard_map.148 = (f32[256,512]{1,0:T(8,128)}, f32[512,512]{1,0:T(8,128)S(1)}, f32[512,512]{1,0:T(8,128)S(1)}, bf16[512,512]{1,0:T(8,128)(2,1)S(1)}, bf16[512,512]{1,0:T(8,128)(2,1)S(1)}) custom-call(s32[1]{0:T(128)} %bitcast._me.me, f32[512,256]{1,0:T(8,128)S(1)} %get-tuple-element.116.mixed_t, bf16[8,512,256]{2,1,0:T(8,128)(2,1)S(1)} %get-tuple-element.117.e_h, ...), custom_call_target="tpu_custom_call" | custom-call | flops 5000000000 | tf_op jit(solution)/shard_map/pallas_call | solution.py:471
  43.5 4.8 %collective-permute-done.5.d_back = f32[256,512]{1,0:T(8,128)S(1)} collective-permute-done((f32[256,512]{1,0:T(8,128)S(1)}, f32[256,512]{1,0:T(8,128)S(1)}, u32[]{:S(2)}, u32[]{:S(2)}) %collective-permute-start.5) | collective-permute-done | bytes 524320 | tf_op jit(solution)/shard_map/ppermute | solution.py:484
  48.3 4.3 %shard_map.149 = (f32[256,512]{1,0:T(8,128)S(1)}, f32[512,256]{1,0:T(8,128)S(1)}, bf16[512,512]{1,0:T(8,128)(2,1)S(1)}, bf16[512,512]{1,0:T(8,128)(2,1)S(1)}) custom-call(f32[256,512]{1,0:T(8,128)S(1)} %collective-permute-done.5.d_back, f32[512,256]{1,0:T(8,128)S(1)} %get-tuple-element.105.q_t, bf16[512,256]{1,0:T(8,128)(2,1)S(1)} %get-tuple-element.135.kt_h, ...), custom_call_target="tpu_custom_call" | custom-call | flops 5000000000 | tf_op jit(solution)/shard_map/pallas_call | solution.py:471
  52.7 3.5 %shard_map.150 = (f32[520,512]{1,0:T(8,128)S(1)}, f32[520,512]{1,0:T(8,128)S(1)}, f32[256,512]{1,0:T(8,128)S(1)}) custom-call(s32[1]{0:T(128)} %bitcast._me.me, f32[256,512]{1,0:T(8,128)S(1)} %collective-permute-done.5.d_back, bf16[512,256]{1,0:T(8,128)(2,1)S(1)} %get-tuple-element.120.ht_h, bf16[512,256]{1,0:T(8,128)(2,1)S(1)} %get-tuple-element.121.ht_l, ...), custom_call_target="tpu_custom_call" | custom-call | flops 4000000000 | tf_op jit(solution)/shard_map/pallas_call | solution.py:471
  56.7 3.7 %collective-permute-done.4.other_1 = f32[512,512]{1,0:T(8,128)S(1)} collective-permute-done((f32[512,512]{1,0:T(8,128)S(1)}, f32[512,512]{1,0:T(8,128)S(1)}, u32[]{:S(2)}, u32[]{:S(2)}) %collective-permute-start.4) | collective-permute-done | bytes 1048608 | tf_op jit(solution)/shard_map/ppermute | solution.py:504
  60.8 5.4 %collective-permute-start.7 = (f32[168,512]{1,0:T(8,128)S(1)}, f32[168,512]{1,0:T(8,128)S(1)}, u32[]{:S(2)}, u32[]{:S(2)}) collective-permute-start(f32[168,512]{1,0:T(8,128)S(1)} %get-tuple-element.157), channel_id=1, source_target_pairs={{0,4},{1,5},{2,6},{3,7},{4,0},{5,1},{6,2},{7,3},{8,12},{9,13},{10,... | collective-permute-start | bytes 1032200 | tf_op jit(solution)/shard_map/ppermute | solution.py:504
  67.8 7.2 %collective-permute-done.7.other = f32[168,512]{1,0:T(8,128)S(1)} collective-permute-done((f32[168,512]{1,0:T(8,128)S(1)}, f32[168,512]{1,0:T(8,128)S(1)}, u32[]{:S(2)}, u32[]{:S(2)}) %collective-permute-start.7) | collective-permute-done | bytes 344096 | tf_op jit(solution)/shard_map/ppermute | solution.py:504
  75.0 1.6 %collective-permute-start.8 = (f32[88,512]{1,0:T(8,128)S(1)}, f32[88,512]{1,0:T(8,128)S(1)}, u32[]{:S(2)}, u32[]{:S(2)}) collective-permute-start(f32[88,512]{1,0:T(8,128)S(1)} %get-tuple-element.159), channel_id=1, source_target_pairs={{0,2},{1,3},{2,0},{3,1},{4,6},{5,7},{6,4},{7,5},{8,10},{9,11},{10,... | collective-permute-start | bytes 540680 | tf_op jit(solution)/shard_map/ppermute | solution.py:504
  77.1 1.7 %collective-permute-start.14 = (f32[96,512]{1,0:T(8,128)S(1)}, f32[96,512]{1,0:T(8,128)S(1)}, u32[]{:S(2)}, u32[]{:S(2)}) collective-permute-start(f32[96,512]{1,0:T(8,128)S(1)} %get-tuple-element.171), channel_id=1, source_target_pairs={{0,4},{1,5},{2,6},{3,7},{4,0},{5,1},{6,2},{7,3},{8,12},{9,13},{10,... | collective-permute-start | bytes 589832 | tf_op jit(solution)/shard_map/ppermute | solution.py:504
  78.9 1.8 %collective-permute-done.8.other = f32[88,512]{1,0:T(8,128)S(1)} collective-permute-done((f32[88,512]{1,0:T(8,128)S(1)}, f32[88,512]{1,0:T(8,128)S(1)}, u32[]{:S(2)}, u32[]{:S(2)}) %collective-permute-start.8) | collective-permute-done | bytes 180256 | tf_op jit(solution)/shard_map/ppermute | solution.py:504
  81.3 8.6 %collective-permute-done.14.other = f32[96,512]{1,0:T(8,128)S(1)} collective-permute-done((f32[96,512]{1,0:T(8,128)S(1)}, f32[96,512]{1,0:T(8,128)S(1)}, u32[]{:S(2)}, u32[]{:S(2)}) %collective-permute-start.14) | collective-permute-done | bytes 196640 | tf_op jit(solution)/shard_map/ppermute | solution.py:504
  90.0 1.6 %collective-permute-start.15 = (f32[48,512]{1,0:T(8,128)S(1)}, f32[48,512]{1,0:T(8,128)S(1)}, u32[]{:S(2)}, u32[]{:S(2)}) collective-permute-start(f32[48,512]{1,0:T(8,128)S(1)} %get-tuple-element.173), channel_id=1, source_target_pairs={{0,2},{1,3},{2,0},{3,1},{4,6},{5,7},{6,4},{7,5},{8,10},{9,11},{10,... | collective-permute-start | bytes 294920 | tf_op jit(solution)/shard_map/ppermute | solution.py:504
  91.6 1.8 %collective-permute-start.12 = (f32[40,512]{1,0:T(8,128)S(1)}, f32[40,512]{1,0:T(8,128)S(1)}, u32[]{:S(2)}, u32[]{:S(2)}) collective-permute-start(f32[40,512]{1,0:T(8,128)S(1)} %get-tuple-element.167), channel_id=1, source_target_pairs={{0,4},{1,5},{2,6},{3,7},{4,0},{5,1},{6,2},{7,3},{8,12},{9,13},{10,... | collective-permute-start | bytes 245768 | tf_op jit(solution)/shard_map/ppermute | solution.py:504
  93.4 2.7 %collective-permute-done.12.refs_3_ = f32[40,512]{1,0:T(8,128)S(1)} collective-permute-done((f32[40,512]{1,0:T(8,128)S(1)}, f32[40,512]{1,0:T(8,128)S(1)}, u32[]{:S(2)}, u32[]{:S(2)}) %collective-permute-start.12) | collective-permute-done | bytes 81952 | tf_op jit(solution)/shard_map/ppermute | solution.py:504
  97.3 6.7 %collective-permute-done.17.b = f32[72,512]{1,0:T(8,128)S(1)} collective-permute-done((f32[72,512]{1,0:T(8,128)S(1)}, f32[72,512]{1,0:T(8,128)S(1)}, u32[]{:S(2)}, u32[]{:S(2)}) %collective-permute-start.17) | collective-permute-done | bytes 147488 | tf_op jit(solution)/shard_map/ppermute | solution.py:504
  104.6 7.1 %collective-permute-done.18.other = f32[64,512]{1,0:T(8,128)S(1)} collective-permute-done((f32[64,512]{1,0:T(8,128)S(1)}, f32[64,512]{1,0:T(8,128)S(1)}, u32[]{:S(2)}, u32[]{:S(2)}) %collective-permute-start.18) | collective-permute-done | bytes 131104 | tf_op jit(solution)/shard_map/ppermute | solution.py:504
  111.8 1.7 %collective-permute-start.19 = (f32[40,512]{1,0:T(8,128)S(1)}, f32[40,512]{1,0:T(8,128)S(1)}, u32[]{:S(2)}, u32[]{:S(2)}) collective-permute-start(f32[40,512]{1,0:T(8,128)S(1)} %get-tuple-element.180.mine), channel_id=1, source_target_pairs={{0,4},{1,5},{2,6},{3,7},{4,0},{5,1},{6,2},{7,3},{8,12},{9,13},{10,... | collective-permute-start | bytes 245768 | tf_op jit(solution)/shard_map/ppermute | solution.py:504
  113.7 2.6 %collective-permute-done.19.other = f32[40,512]{1,0:T(8,128)S(1)} collective-permute-done((f32[40,512]{1,0:T(8,128)S(1)}, f32[40,512]{1,0:T(8,128)S(1)}, u32[]{:S(2)}, u32[]{:S(2)}) %collective-permute-start.19) | collective-permute-done | bytes 81952 | tf_op jit(solution)/shard_map/ppermute | solution.py:504
  116.4 1.7 %collective-permute-done.22.other = f32[48,512]{1,0:T(8,128)S(1)} collective-permute-done((f32[48,512]{1,0:T(8,128)S(1)}, f32[48,512]{1,0:T(8,128)S(1)}, u32[]{:S(2)}, u32[]{:S(2)}) %collective-permute-start.22) | collective-permute-done | bytes 98336 | tf_op jit(solution)/shard_map/ppermute | solution.py:504
  120.0 1.7 %collective-permute-done.20.other = f32[80,512]{1,0:T(8,128)S(1)} collective-permute-done((f32[80,512]{1,0:T(8,128)S(1)}, f32[80,512]{1,0:T(8,128)S(1)}, u32[]{:S(2)}, u32[]{:S(2)}) %collective-permute-start.20) | collective-permute-done | bytes 163872 | tf_op jit(solution)/shard_map/ppermute | solution.py:504
  121.8 2.0 %collective-permute-done.23.other = f32[96,512]{1,0:T(8,128)S(1)} collective-permute-done((f32[96,512]{1,0:T(8,128)S(1)}, f32[96,512]{1,0:T(8,128)S(1)}, u32[]{:S(2)}, u32[]{:S(2)}) %collective-permute-start.23) | collective-permute-done | bytes 196640 | tf_op jit(solution)/shard_map/ppermute | solution.py:504
  124.3 1.6 %collective-permute-done.28.other = f32[80,512]{1,0:T(8,128)S(1)} collective-permute-done((f32[80,512]{1,0:T(8,128)S(1)}, f32[80,512]{1,0:T(8,128)S(1)}, u32[]{:S(2)}, u32[]{:S(2)}) %collective-permute-start.28) | collective-permute-done | bytes 163872 | tf_op jit(solution)/shard_map/ppermute | solution.py:504
  127.5 3.7 %collective-permute-done.21.other = f32[160,512]{1,0:T(8,128)S(1)} collective-permute-done((f32[160,512]{1,0:T(8,128)S(1)}, f32[160,512]{1,0:T(8,128)S(1)}, u32[]{:S(2)}, u32[]{:S(2)}) %collective-permute-start.21) | collective-permute-done | bytes 327712 | tf_op jit(solution)/shard_map/ppermute | solution.py:504
  133.4 2.1 %collective-permute-done.30.refs_2_ = f32[320,512]{1,0:T(8,128)S(1)} collective-permute-done((f32[320,512]{1,0:T(8,128)S(1)}, f32[320,512]{1,0:T(8,128)S(1)}, u32[]{:S(2)}, u32[]{:S(2)}) %collective-permute-start.30) | collective-permute-done | bytes 655392 | tf_op jit(solution)/shard_map/ppermute | solution.py:504
  (77 shorter events, 23.4 us)
Async XLA Ops:
  1.7 10.1 %collective-permute-start = (f32[128,512]{1,0:T(8,128)S(1)}, f32[128,512]{1,0:T(8,128)S(1)}, u32[]{:S(2)}, u32[]{:S(2)}) collective-permute-start(f32[128,512]{1,0:T(8,128)S(1)} %get-tuple-element.188), channel_id=1, source_target_pairs={{0,4},{4,0},{8,12},{12,8},{16,20},{20,16},{24,28},{28,24},{1,5},{5... | collective-permute-start | bytes 786440 | tf_op jit(solution)/shard_map/ppermute | solution.py:484
  4.7 11.9 %collective-permute-start.2 = (f32[128,512]{1,0:T(8,128)S(1)}, f32[128,512]{1,0:T(8,128)S(1)}, u32[]{:S(2)}, u32[]{:S(2)}) collective-permute-start(f32[128,512]{1,0:T(8,128)S(1)} %get-tuple-element.187), channel_id=1, source_target_pairs={{0,4},{4,0},{8,12},{12,8},{16,20},{20,16},{24,28},{28,24},{1,5},{5... | collective-permute-start | bytes 786440 | tf_op jit(solution)/shard_map/ppermute | solution.py:484
  9.7 8.8 %copy-start.6 = (f32[512]{0:T(512)S(1)}, f32[512]{0:T(512)}, u32[]{:S(2)}) copy-start(f32[512]{0:T(512)} %param.10) | copy-start | bytes 6148
  11.8 16.1 %collective-permute-start.1 = (f32[128,512]{1,0:T(8,128)S(1)}, f32[128,512]{1,0:T(8,128)S(1)}, u32[]{:S(2)}, u32[]{:S(2)}) collective-permute-start(f32[128,512]{1,0:T(8,128)S(1)} %collective-permute-done._.patch_0), channel_id=1, source_target_pairs={{0,8},{4,28},{8,16},{12,4},{16,24},{20,12},{24,0},{28,20},{1,9},{5... | collective-permute-start | bytes 786440 | tf_op jit(solution)/shard_map/ppermute | solution.py:484
  16.6 11.3 %collective-permute-start.3 = (f32[128,512]{1,0:T(8,128)S(1)}, f32[128,512]{1,0:T(8,128)S(1)}, u32[]{:S(2)}, u32[]{:S(2)}) collective-permute-start(f32[128,512]{1,0:T(8,128)S(1)} %collective-permute-done.2.patch_1), channel_id=1, source_target_pairs={{0,8},{4,28},{8,16},{12,4},{16,24},{20,12},{24,0},{28,20},{1,9},{5... | collective-permute-start | bytes 786440 | tf_op jit(solution)/shard_map/ppermute | solution.py:484
  35.8 12.6 %collective-permute-start.5 = (f32[256,512]{1,0:T(8,128)S(1)}, f32[256,512]{1,0:T(8,128)S(1)}, u32[]{:S(2)}, u32[]{:S(2)}) collective-permute-start(f32[256,512]{1,0:T(8,128)S(1)} %get-tuple-element.131.d_far), channel_id=1, source_target_pairs={{0,24},{4,12},{8,0},{12,20},{16,8},{20,28},{24,16},{28,4},{1,25},{... | collective-permute-start | bytes 1572872 | tf_op jit(solution)/shard_map/ppermute | solution.py:484
  56.2 4.3 %collective-permute-start.6 = (f32[520,512]{1,0:T(8,128)S(1)}, f32[520,512]{1,0:T(8,128)S(1)}, u32[]{:S(2)}, u32[]{:S(2)}) collective-permute-start(f32[520,512]{1,0:T(8,128)S(1)} %get-tuple-element.155), channel_id=1, source_target_pairs={{0,1},{1,0},{2,3},{3,2},{4,5},{5,4},{6,7},{7,6},{8,9},{9,8},{10,11... | collective-permute-start | bytes 3194888 | tf_op jit(solution)/shard_map/ppermute | solution.py:504
  56.2 4.2 %collective-permute-start.4 = (f32[512,512]{1,0:T(8,128)S(1)}, f32[512,512]{1,0:T(8,128)S(1)}, u32[]{:S(2)}, u32[]{:S(2)}) collective-permute-start(f32[512,512]{1,0:T(8,128)S(1)} %get-tuple-element.130), channel_id=1, source_target_pairs={{0,1},{1,0},{2,3},{3,2},{4,5},{5,4},{6,7},{7,6},{8,9},{9,8},{10,11... | collective-permute-start | bytes 3145736 | tf_op jit(solution)/shard_map/ppermute | solution.py:504
  60.8 14.2 %collective-permute-start.7 = (f32[168,512]{1,0:T(8,128)S(1)}, f32[168,512]{1,0:T(8,128)S(1)}, u32[]{:S(2)}, u32[]{:S(2)}) collective-permute-start(f32[168,512]{1,0:T(8,128)S(1)} %get-tuple-element.157), channel_id=1, source_target_pairs={{0,4},{1,5},{2,6},{3,7},{4,0},{5,1},{6,2},{7,3},{8,12},{9,13},{10,... | collective-permute-start | bytes 1032200 | tf_op jit(solution)/shard_map/ppermute | solution.py:504
  66.1 10.9 %collective-permute-start.13 = (f32[192,512]{1,0:T(8,128)S(1)}, f32[192,512]{1,0:T(8,128)S(1)}, u32[]{:S(2)}, u32[]{:S(2)}) collective-permute-start(f32[192,512]{1,0:T(8,128)S(1)} %get-tuple-element.169), channel_id=1, source_target_pairs={{0,8},{1,9},{2,10},{3,11},{4,12},{5,13},{6,14},{7,15},{8,0},{9,1},... | collective-permute-start | bytes 1179656 | tf_op jit(solution)/shard_map/ppermute | solution.py:504
  66.2 12.7 %collective-permute-start.10 = (f32[160,512]{1,0:T(8,128)S(1)}, f32[160,512]{1,0:T(8,128)S(1)}, u32[]{:S(2)}, u32[]{:S(2)}) collective-permute-start(f32[160,512]{1,0:T(8,128)S(1)} %get-tuple-element.163), channel_id=1, source_target_pairs={{0,2},{1,3},{2,0},{3,1},{4,6},{5,7},{6,4},{7,5},{8,10},{9,11},{10,... | collective-permute-start | bytes 983048 | tf_op jit(solution)/shard_map/ppermute | solution.py:504
  67.7 25.7 %collective-permute-start.16 = (f32[256,512]{1,0:T(8,128)S(1)}, f32[256,512]{1,0:T(8,128)S(1)}, u32[]{:S(2)}, u32[]{:S(2)}) collective-permute-start(f32[256,512]{1,0:T(8,128)S(1)} %get-tuple-element.153.d_near), channel_id=1, source_target_pairs={{0,4},{4,0},{8,12},{12,8},{16,20},{20,16},{24,28},{28,24},{1,5},{5... | collective-permute-start | bytes 1572872 | tf_op jit(solution)/shard_map/ppermute | solution.py:484
  75.0 5.7 %collective-permute-start.8 = (f32[88,512]{1,0:T(8,128)S(1)}, f32[88,512]{1,0:T(8,128)S(1)}, u32[]{:S(2)}, u32[]{:S(2)}) collective-permute-start(f32[88,512]{1,0:T(8,128)S(1)} %get-tuple-element.159), channel_id=1, source_target_pairs={{0,2},{1,3},{2,0},{3,1},{4,6},{5,7},{6,4},{7,5},{8,10},{9,11},{10,... | collective-permute-start | bytes 540680 | tf_op jit(solution)/shard_map/ppermute | solution.py:504
  77.1 12.9 %collective-permute-start.14 = (f32[96,512]{1,0:T(8,128)S(1)}, f32[96,512]{1,0:T(8,128)S(1)}, u32[]{:S(2)}, u32[]{:S(2)}) collective-permute-start(f32[96,512]{1,0:T(8,128)S(1)} %get-tuple-element.171), channel_id=1, source_target_pairs={{0,4},{1,5},{2,6},{3,7},{4,0},{5,1},{6,2},{7,3},{8,12},{9,13},{10,... | collective-permute-start | bytes 589832 | tf_op jit(solution)/shard_map/ppermute | solution.py:504
  78.8 12.7 %collective-permute-start.11 = (f32[80,512]{1,0:T(8,128)S(1)}, f32[80,512]{1,0:T(8,128)S(1)}, u32[]{:S(2)}, u32[]{:S(2)}) collective-permute-start(f32[80,512]{1,0:T(8,128)S(1)} %get-tuple-element.165), channel_id=1, source_target_pairs={{0,8},{1,9},{2,10},{3,11},{4,12},{5,13},{6,14},{7,15},{8,0},{9,1},... | collective-permute-start | bytes 491528 | tf_op jit(solution)/shard_map/ppermute | solution.py:504
  80.7 15.4 %collective-permute-start.9 = (f32[48,512]{1,0:T(8,128)S(1)}, f32[48,512]{1,0:T(8,128)S(1)}, u32[]{:S(2)}, u32[]{:S(2)}) collective-permute-start(f32[48,512]{1,0:T(8,128)S(1)} %get-tuple-element.161), channel_id=1, source_target_pairs={{0,8},{1,9},{2,10},{3,11},{4,12},{5,13},{6,14},{7,15},{8,0},{9,1},... | collective-permute-start | bytes 294920 | tf_op jit(solution)/shard_map/ppermute | solution.py:504
  90.0 6.1 %collective-permute-start.15 = (f32[48,512]{1,0:T(8,128)S(1)}, f32[48,512]{1,0:T(8,128)S(1)}, u32[]{:S(2)}, u32[]{:S(2)}) collective-permute-start(f32[48,512]{1,0:T(8,128)S(1)} %get-tuple-element.173), channel_id=1, source_target_pairs={{0,2},{1,3},{2,0},{3,1},{4,6},{5,7},{6,4},{7,5},{8,10},{9,11},{10,... | collective-permute-start | bytes 294920 | tf_op jit(solution)/shard_map/ppermute | solution.py:504
  91.6 4.5 %collective-permute-start.12 = (f32[40,512]{1,0:T(8,128)S(1)}, f32[40,512]{1,0:T(8,128)S(1)}, u32[]{:S(2)}, u32[]{:S(2)}) collective-permute-start(f32[40,512]{1,0:T(8,128)S(1)} %get-tuple-element.167), channel_id=1, source_target_pairs={{0,4},{1,5},{2,6},{3,7},{4,0},{5,1},{6,2},{7,3},{8,12},{9,13},{10,... | collective-permute-start | bytes 245768 | tf_op jit(solution)/shard_map/ppermute | solution.py:504
  97.3 6.7 %collective-permute-start.17 = (f32[72,512]{1,0:T(8,128)S(1)}, f32[72,512]{1,0:T(8,128)S(1)}, u32[]{:S(2)}, u32[]{:S(2)}) collective-permute-start(f32[72,512]{1,0:T(8,128)S(1)} %get-tuple-element.177), channel_id=1, source_target_pairs={{0,16},{1,17},{2,18},{3,19},{4,20},{5,21},{6,22},{7,23},{8,24},{9,... | collective-permute-start | bytes 442376 | tf_op jit(solution)/shard_map/ppermute | solution.py:504
  104.6 7.1 %collective-permute-start.18 = (f32[64,512]{1,0:T(8,128)S(1)}, f32[64,512]{1,0:T(8,128)S(1)}, u32[]{:S(2)}, u32[]{:S(2)}) collective-permute-start(f32[64,512]{1,0:T(8,128)S(1)} %get-tuple-element.179.mine), channel_id=1, source_target_pairs={{0,16},{1,17},{2,18},{3,19},{4,20},{5,21},{6,22},{7,23},{8,24},{9,... | collective-permute-start | bytes 393224 | tf_op jit(solution)/shard_map/ppermute | solution.py:504
  111.8 4.5 %collective-permute-start.19 = (f32[40,512]{1,0:T(8,128)S(1)}, f32[40,512]{1,0:T(8,128)S(1)}, u32[]{:S(2)}, u32[]{:S(2)}) collective-permute-start(f32[40,512]{1,0:T(8,128)S(1)} %get-tuple-element.180.mine), channel_id=1, source_target_pairs={{0,4},{1,5},{2,6},{3,7},{4,0},{5,1},{6,2},{7,3},{8,12},{9,13},{10,... | collective-permute-start | bytes 245768 | tf_op jit(solution)/shard_map/ppermute | solution.py:504
  113.4 4.6 %collective-permute-start.22 = (f32[48,512]{1,0:T(8,128)S(1)}, f32[48,512]{1,0:T(8,128)S(1)}, u32[]{:S(2)}, u32[]{:S(2)}) collective-permute-start(f32[48,512]{1,0:T(8,128)S(1)} %get-tuple-element.181.mine), channel_id=1, source_target_pairs={{0,2},{1,3},{2,0},{3,1},{4,6},{5,7},{6,4},{7,5},{8,10},{9,11},{10,... | collective-permute-start | bytes 294920 | tf_op jit(solution)/shard_map/ppermute | solution.py:504
  113.7 5.1 %collective-permute-start.27 = (f32[40,512]{1,0:T(8,128)S(1)}, f32[40,512]{1,0:T(8,128)S(1)}, u32[]{:S(2)}, u32[]{:S(2)}) collective-permute-start(f32[40,512]{1,0:T(8,128)S(1)} %get-tuple-element.184.mine), channel_id=1, source_target_pairs={{0,8},{1,9},{2,10},{3,11},{4,12},{5,13},{6,14},{7,15},{8,0},{9,1},... | collective-permute-start | bytes 245768 | tf_op jit(solution)/shard_map/ppermute | solution.py:504
  116.3 5.4 %collective-permute-start.20 = (f32[80,512]{1,0:T(8,128)S(1)}, f32[80,512]{1,0:T(8,128)S(1)}, u32[]{:S(2)}, u32[]{:S(2)}) collective-permute-start(f32[80,512]{1,0:T(8,128)S(1)} %shard_map.161.mine), channel_id=1, source_target_pairs={{0,8},{1,9},{2,10},{3,11},{4,12},{5,13},{6,14},{7,15},{8,0},{9,1},... | collective-permute-start | bytes 491528 | tf_op jit(solution)/shard_map/ppermute | solution.py:504
  118.1 5.7 %collective-permute-start.23 = (f32[96,512]{1,0:T(8,128)S(1)}, f32[96,512]{1,0:T(8,128)S(1)}, u32[]{:S(2)}, u32[]{:S(2)}) collective-permute-start(f32[96,512]{1,0:T(8,128)S(1)} %shard_map.164.mine), channel_id=1, source_target_pairs={{0,4},{1,5},{2,6},{3,7},{4,0},{5,1},{6,2},{7,3},{8,12},{9,13},{10,... | collective-permute-start | bytes 589832 | tf_op jit(solution)/shard_map/ppermute | solution.py:504
  118.8 7.1 %collective-permute-start.28 = (f32[80,512]{1,0:T(8,128)S(1)}, f32[80,512]{1,0:T(8,128)S(1)}, u32[]{:S(2)}, u32[]{:S(2)}) collective-permute-start(f32[80,512]{1,0:T(8,128)S(1)} %shard_map.168.mine), channel_id=1, source_target_pairs={{0,2},{1,3},{2,0},{3,1},{4,6},{5,7},{6,4},{7,5},{8,10},{9,11},{10,... | collective-permute-start | bytes 491528 | tf_op jit(solution)/shard_map/ppermute | solution.py:504
  121.7 9.4 %collective-permute-start.21 = (f32[160,512]{1,0:T(8,128)S(1)}, f32[160,512]{1,0:T(8,128)S(1)}, u32[]{:S(2)}, u32[]{:S(2)}) collective-permute-start(f32[160,512]{1,0:T(8,128)S(1)} %shard_map.162.mine), channel_id=1, source_target_pairs={{0,2},{1,3},{2,0},{3,1},{4,6},{5,7},{6,4},{7,5},{8,10},{9,11},{10,... | collective-permute-start | bytes 983048 | tf_op jit(solution)/shard_map/ppermute | solution.py:504
  123.9 7.8 %collective-permute-start.24 = (f32[192,512]{1,0:T(8,128)S(1)}, f32[192,512]{1,0:T(8,128)S(1)}, u32[]{:S(2)}, u32[]{:S(2)}) collective-permute-start(f32[192,512]{1,0:T(8,128)S(1)} %shard_map.165.mine), channel_id=1, source_target_pairs={{0,8},{1,9},{2,10},{3,11},{4,12},{5,13},{6,14},{7,15},{8,0},{9,1},... | collective-permute-start | bytes 1179656 | tf_op jit(solution)/shard_map/ppermute | solution.py:504
  126.0 7.1 %collective-permute-start.29 = (f32[160,512]{1,0:T(8,128)S(1)}, f32[160,512]{1,0:T(8,128)S(1)}, u32[]{:S(2)}, u32[]{:S(2)}) collective-permute-start(f32[160,512]{1,0:T(8,128)S(1)} %shard_map.169.mine), channel_id=1, source_target_pairs={{0,4},{1,5},{2,6},{3,7},{4,0},{5,1},{6,2},{7,3},{8,12},{9,13},{10,... | collective-permute-start | bytes 983048 | tf_op jit(solution)/shard_map/ppermute | solution.py:504
  131.2 2.2 %collective-permute-start.25 = (f32[320,512]{1,0:T(8,128)S(1)}, f32[320,512]{1,0:T(8,128)S(1)}, u32[]{:S(2)}, u32[]{:S(2)}) collective-permute-start(f32[320,512]{1,0:T(8,128)S(1)} %shard_map.163.refs_0_.refs_1_), channel_id=1, source_target_pairs={{0,1},{1,0},{2,3},{3,2},{4,5},{5,4},{6,7},{7,6},{8,9},{9,8},{10,11... | collective-permute-start | bytes 1966088 | tf_op jit(solution)/shard_map/ppermute | solution.py:504
  131.8 5.1 %collective-permute-start.26 = (f32[384,512]{1,0:T(8,128)S(1)}, f32[384,512]{1,0:T(8,128)S(1)}, u32[]{:S(2)}, u32[]{:S(2)}) collective-permute-start(f32[384,512]{1,0:T(8,128)S(1)} %shard_map.166.refs_1_), channel_id=1, source_target_pairs={{0,1},{1,0},{2,3},{3,2},{4,5},{5,4},{6,7},{7,6},{8,9},{9,8},{10,11... | collective-permute-start | bytes 2359304 | tf_op jit(solution)/shard_map/ppermute | solution.py:504
  133.2 2.3 %collective-permute-start.30 = (f32[320,512]{1,0:T(8,128)S(1)}, f32[320,512]{1,0:T(8,128)S(1)}, u32[]{:S(2)}, u32[]{:S(2)}) collective-permute-start(f32[320,512]{1,0:T(8,128)S(1)} %shard_map.170.refs_0_), channel_id=1, source_target_pairs={{0,1},{1,0},{2,3},{3,2},{4,5},{5,4},{6,7},{7,6},{8,9},{9,8},{10,11... | collective-permute-start | bytes 1966088 | tf_op jit(solution)/shard_map/ppermute | solution.py:504
  (8 other events, 27.0 us)

commit v3 on v2

--- a/solution.py
+++ b/solution.py
@@ -156,17 +156,22 @@
     return both[:HD] + (both[HD:] + dot(high, right[1]))
 
 
+def near_side_kernel(
+    patch_0, patch_1, gain, wk_h, wk_l, wv_h, wv_l,
+    xhat, ht_h, ht_l, kt_h, kt_l, k_stack, v_stack, vt_h, vt_l,
+):
+    key_side(
+        (patch_0, patch_1), gain, (wk_h, wk_l), (wv_h, wv_l), xhat, (ht_h, ht_l), k_stack, (kt_h, kt_l), v_stack,
+        (vt_h, vt_l),
+    )
+
+
 def near_kernel(
-    parity, listed, counts, patch_0, patch_1, gain, q_stack, k_stack, v_stack, vt_h, vt_l, d_stack,
-    wk_h, wk_l, wv_h, wv_l,
-    xhat, ht_h, ht_l, kt_h, kt_l, e_h, e_l, d_scores, mixed, tops, totals,
-    bias, k_near, v_near, vt2_h, vt2_l,
+    parity, listed, counts, _, q_stack, k_stack, v_stack, vt_h, vt_l, d_stack, k_near, v_near, vt2_h, vt2_l,
+    e_h, e_l, d_scores, mixed, tops, totals,
+    bias,
 ):
     store_bias(bias, listed, counts, parity, range(4))
-    key_side(
-        (patch_0, patch_1), gain, (wk_h, wk_l), (wv_h, wv_l), xhat, (ht_h, ht_l), k_near, (kt_h, kt_l), v_near,
-        (vt2_h, vt2_l),
-    )
 
     def one_head(h, carry):
         stack, rows = head_stack(h), head_rows(h)
@@ -270,43 +275,16 @@
     )
 
 
-def mix_kernel(
-    me, mixed_t, e_h, e_l, d_mixed_t, shares_1, ht_h, ht_l, ht2_h, ht2_l, ht3_h, ht3_l, dv3_h, dv3_l, tokens, cot,
-    wo_h, wo_l,
-    result, keep, send, dv_h, dv_l,
-    grad_o, grad_v,
-):
-    own = tokens.shape[0]
-
-    def one_pair(p, carry):
-        d_scaled = [
-            d_mixed_t[head_rows(2 * p + a), :] * shares_1[pl.ds(2 * p + a, 1), :] for a in range(2)
-        ]
-        right = pair_of(jnp.concatenate(d_scaled, axis=0).T)
-        d_value = gathered((e_h[2 * p], e_h[2 * p + 1]), (e_l[2 * p], e_l[2 * p + 1]), right)
-        store((dv_h, dv_l), pair_of(d_value), slice(None), pair_lanes(p))
-        return carry
-
-    lax.fori_loop(0, PAIRS, one_pair, 0, unroll=UNROLL)
-    mixed = mixed_t[...]
-    grad_o[...] = dot3(pair_of(mixed), pair_of(cot[...]))
-    turned = [load(t, ...) for t in ((ht_h, ht_l), (ht2_h, ht2_l), (ht3_h, ht3_l))]
-    d_values = [load((dv_h, dv_l), slice(0, own)), load((dv_h, dv_l), slice(own, 2 * own)), load((dv3_h, dv3_l), ...)]
-    grad_v[...] = sums_of(turned, d_values)
-    kept_and_sent(me, (grad_o, grad_v), keep, send)
-    result[...] = dot3(pair_of(mixed.T), load((wo_h, wo_l), ...)) + tokens[...]
-
-
 def back_kernel(
-    d_back, q_t, kt_h, kt_l, kt2_h, kt2_l, kt3_h, kt3_l, e_h, e_l, d_scores, u_h, u_l, deltas, shares, shares_1,
-    dv_h, dv_l, wk_h, wk_l, wv_h, wv_l,
-    d_near, dq_t, dk_h, dk_l,
+    q_t, d_mixed_t, kt_h, kt_l, kt2_h, kt2_l, kt3_h, kt3_l, e_h, e_l, d_scores, u_h, u_l, deltas, shares, shares_1,
+    wk_h, wk_l, wv_h, wv_l,
+    d_near, dq_t, dk_h, dk_l, dv_h, dv_l,
     s_h, s_l,
 ):
     own = d_near.shape[0]
 
     def one_pair(p, carry):
-        q_scaled = []
+        q_scaled, d_scaled = [], []
         for a in range(2):
             h = 2 * p + a
             rows, row = head_rows(h), pl.ds(h, 1)
@@ -319,23 +297,45 @@
             two = weighed((kt3_h,), (kt3_l,), rows, (u_h[h], u_l[h]))
             dq_t[rows, :] = (share_1 * one + shares[row, :] * two) * HD ** (-0.5)
             q_scaled.append(q_t[rows, :] * share_1)
+            d_scaled.append(d_mixed_t[rows, :] * share_1)
+        lanes = pair_lanes(p)
         right = pair_of(jnp.concatenate(q_scaled, axis=0).T)
         d_key = gathered((s_h[0], s_h[1]), (s_l[0], s_l[1]), right)
-        store((dk_h, dk_l), pair_of(d_key), slice(None), pair_lanes(p))
+        store((dk_h, dk_l), pair_of(d_key), slice(None), lanes)
+        right = pair_of(jnp.concatenate(d_scaled, axis=0).T)
+        d_value = gathered((e_h[2 * p], e_h[2 * p + 1]), (e_l[2 * p], e_l[2 * p + 1]), right)
+        store((dv_h, dv_l), pair_of(d_value), slice(None), lanes)
         return carry
 
     lax.fori_loop(0, PAIRS, one_pair, 0, unroll=UNROLL)
     near = slice(own, 2 * own)
-    d_near[...] = d_back[...] + sums_of(
+    d_near[...] = sums_of(
         [load((dk_h, dk_l), near), load((dv_h, dv_l), near)], [load((wk_h, wk_l), ...), load((wv_h, wv_l), ...)], NT
     )
 
 
+def mix_kernel(
+    me, mixed_t, ht_h, ht_l, ht2_h, ht2_l, ht3_h, ht3_l, dv_h, dv_l, dv3_h, dv3_l, cot,
+    keep, send,
+    grad_o, grad_v,
+):
+    own = cot.shape[0]
+    grad_o[...] = dot3(pair_of(mixed_t[...]), pair_of(cot[...]))
+    turned = [load(t, ...) for t in ((ht_h, ht_l), (ht2_h, ht2_l), (ht3_h, ht3_l))]
+    d_values = [load((dv_h, dv_l), slice(0, own)), load((dv_h, dv_l), slice(own, 2 * own)), load((dv3_h, dv3_l), ...)]
+    grad_v[...] = sums_of(turned, d_values)
+    kept_and_sent(me, (grad_o, grad_v), keep, send)
+
+
+def result_kernel(_, mixed_t, tokens, wo_h, wo_l, result, mark):
+    mark[...] = jnp.zeros_like(mark)
+    result[...] = dot3(pair_of(mixed_t[...].T), load((wo_h, wo_l), ...)) + tokens[...]
+
+
 def grad_kernel(
-    me, d_back, ht_h, ht_l, ht2_h, ht2_l, ht3_h, ht3_l, xhat, xhat2, xhat3, dq_t, dk_h, dk_l, dk3_h, dk3_l, dv_h, dv_l,
+    ht_h, ht_l, ht2_h, ht2_l, ht3_h, ht3_l, xhat, xhat2, xhat3, dq_t, dk_h, dk_l, dk3_h, dk3_l, dv_h, dv_l,
     d_near, d_far, wq_h, wq_l, wk_h, wk_l, wv_h, wv_l,
-    keep, send, d_own,
-    grad_q, grad_k,
+    grad_q, grad_k, d_own, gain_sum,
 ):
     own, width = d_own.shape
     first, second = slice(0, own), slice(own, 2 * own)
@@ -346,13 +346,17 @@
     grad_k[...] = sums_of(turned, d_keys)
     w_q, w_k, w_v = load((wq_h, wq_l), ...), load((wk_h, wk_l), ...), load((wv_h, wv_l), ...)
     d_own[...] = sums_of([d_query, d_keys[0], load((dv_h, dv_l), first)], [w_q, w_k, w_v], NT)
-    d_gain = jnp.sum(
-        d_own[...] * xhat[...] + (d_near[...] - d_back[...]) * xhat2[...] + d_far[...] * xhat3[...],
-        axis=0, keepdims=True,
-    )
+    gain_sum[...] = jnp.sum(
+        d_own[...] * xhat[...] + d_near[...] * xhat2[...] + d_far[...] * xhat3[...], axis=0, keepdims=True
+    )
+
+
+def core_kernel(me, grad_q, grad_k, gain_sum, d_near, d_back, _, keep, send, d_given):
+    d_given[...] = d_near[...] + d_back[...]
+    width = grad_q.shape[1]
     top = lax.broadcasted_iota(jnp.int32, (TAIL, width), 0) == 0
     for out in (keep, send):
-        out[width:, :] = jnp.where(top, d_gain, 0.0)
+        out[width:, :] = jnp.where(top, gain_sum[...], 0.0)
     kept_and_sent(me, (grad_q, grad_k), keep, send)
 
 
@@ -368,15 +372,9 @@
     out[...] = a[...] + b[...]
 
 
-def last_kernel(a, b, out, tail):
-    rows = out.shape[0]
-    out[...] = a[:rows, :] + b[:rows, :]
-    tail[...] = a[rows : rows + 1, :] + b[rows : rows + 1, :]
-
-
 def cut_kernel(masks, me, keep_1, other_1, keep_2, other_2, *outs):
     count = keep_1.shape[0]
-    sums = outs[-1]
+    *outs, sums = outs
     sums[:count, :] = keep_1[...] + other_1[...]
     sums[count:, :] = keep_2[...] + other_2[...]
     tail = sums[2 * count :, :]
@@ -402,56 +400,57 @@
             out[rows:, :] = keep[2 * rows :, :] + other[2 * rows :, :]
 
 
-def join_kernel(mask, me, *refs):
-    *ins, keep, send, d_tokens, sums = refs
+def join_kernel(*refs):
+    *ins, d_given, sums, d_going = refs
     at = 0
     for i in range(3):
         rows = ins[2 * i].shape[0] - (TAIL if i == 0 else 0)
         sums[at : at + rows, :] = ins[2 * i][:rows, :] + ins[2 * i + 1][:rows, :]
         at += rows
-    tail = ins[0][rows_of(ins[0]) :, :] + ins[1][rows_of(ins[0]) :, :]
-    for out, mine in ((keep, True), (send, False)):
-        out[: at // 2, :] = sums[half_of(me, mask, mine, at // 2), :]
-        out[at // 2 :, :] = tail
-    tokens_kernel(*ins[6:], d_tokens)
+    sums[at:, :] = ins[0][rows_of(ins[0]) :, :] + ins[1][rows_of(ins[0]) :, :]
+    d_going[...] = d_given[...]
 
 
 def rows_of(ref):
     return ref.shape[0] - TAIL
 
 
-def part_kernel(mask, me, mine, other, *outs):
-    *parts, whole = outs
-    rows = mine.shape[0]
-    whole[half_of(me, mask, True, rows), :] = mine[...]
-    whole[half_of(me, mask, False, rows), :] = other[...]
+def part_kernel(a, b, _mark, _other, *outs):
     at = 0
-    for out in parts:
-        out[...] = whole[at : at + out.shape[0], :]
-        at += out.shape[0]
-
-
-def double_kernel(mask, me, mine, other, out):
+    for out in outs:
+        rows = out.shape[0]
+        out[...] = a[at : at + rows, :] + b[at : at + rows, :]
+        at += rows
+
+
+def double_kernel(mask, me, mine, other, *rest):
+    out = rest[-1]
     rows = mine.shape[0]
     out[half_of(me, mask, True, rows), :] = mine[...]
     out[half_of(me, mask, False, rows), :] = other[...]
 
 
 def split_kernel(ranges, me, *refs):
-    *ins, one, two = refs
-    count = len(ins) // 2
+    count = len(refs) - 5
+    ins, outs, sent = refs[:count], refs[count:-1], refs[-1]
     for bit in range(2):
 
         @pl.when(me[0] % 2 == bit)
         def _():
-            for out, pieces in ((one, ins[:count] if bit == 0 else ins[count:]), (two, ins[count:] if bit == 0 else ins[:count])):
-                at = 0
-                for piece, (start, stop) in zip(pieces, ranges):
-                    out[at : at + stop - start, :] = piece[start:stop, :]
-                    at += stop - start
-
-
-def tokens_kernel(tokens, gain, cot, d_own, d_other, out):
+            copies = []
+            for core in range(2):
+                for part, first, rows, exchange, to in ranges:
+                    source = ins[part + core * (count // 2)].at[pl.ds(first, rows)]
+                    target = outs[2 * exchange + (bit + core) % 2].at[pl.ds(to, rows)]
+                    copies.append(pltpu.make_async_copy(source, target, sent.at[len(copies)]))
+            for copy in copies:
+                copy.start()
+            for copy in copies:
+                copy.wait()
+
+
+def tokens_kernel(_, tokens, gain, cot, d_own, d_other, out, mark):
+    mark[...] = jnp.zeros_like(mark)
     normal, rstd = unit_rows(tokens[...])
     d_normal = (d_own[...] + d_other[...]) * gain[...]
     inner = jnp.mean(d_normal * normal, axis=1, keepdims=True)
@@ -479,6 +478,9 @@
     )(*inputs)
 
 
+MARK = shape(8, 128)
+
+
 def along_space(value, target):
     count = lax.axis_size("space")
     return lax.ppermute(value, "space", [(i, target(i) % count) for i in range(count)])
@@ -508,7 +510,7 @@
 LAST = 16
 
 
-def summed(me, keep_1, other_1, keep_2, send_2, token_side):
+def summed(me, keep_1, other_1, keep_2, send_2, d_given, token_side, result_of):
     count, width = keep_1.shape
     total = 2 * count
     unit = 8 * 8
@@ -533,39 +535,49 @@
             )
             parts[i] = [keep, swapped(send, mask)]
     joined = total // 8
-    keep, send, *d_tokens = call(
-        functools.partial(join_kernel, LAST), (me, *parts[0], *parts[1], *parts[2], *token_side),
-        [shape(joined // 2 + TAIL, width)] * 2 + [token_side[0]], [shape(joined, width)], scalars=1, limit=8,
-    )
-    other = swapped(send, LAST)
+    sums, d_going = call(
+        join_kernel, (*parts[0], *parts[1], *parts[2], d_given), [shape(joined + TAIL, width), d_given],
+        limit=8,
+    )
+    other = swapped(sums, LAST)
+    result, mark = result_of(sums)
+    d_other = across(d_going)
     mask = 2 * LAST
     while mask < devices():
-        (keep,) = call(add_kernel, (keep, other), [keep])
-        other = swapped(keep, mask)
+        (sums,) = call(add_kernel, (sums, other), [sums])
+        other = swapped(sums, mask)
         mask *= 2
-    mine, d_gain = call(last_kernel, (keep, other), [shape(joined // 2, width), shape(1, width)])
-    parts = list(call(
-        functools.partial(part_kernel, LAST), (me, mine, swapped(mine, LAST)),
-        [shape(size // 8, width) for size in sizes], [shape(joined, width)], scalars=1,
-    ))
+    *parts, d_gain = call(
+        part_kernel, (sums, other, mark, d_other), [shape(size // 8, width) for size in sizes] + [shape(1, width)],
+    )
     for step in (2, 1, 0):
         for i in range(3):
             mask = ORDERS[i][step]
+            place = (mark,) if step == 0 and i == 2 else ()
             (parts[i],) = call(
-                functools.partial(double_kernel, mask), (me, parts[i], swapped(parts[i], mask)),
+                functools.partial(double_kernel, mask), (me, parts[i], swapped(parts[i], mask), *place),
                 [shape(2 * parts[i].shape[0], width)], scalars=1,
             )
+        if step == 1:
+            d_tokens, mark = call(tokens_kernel, (parts[0], *token_side, d_other), [d_given, MARK])
     others = [swapped(part, 1) for part in parts]
-    split = count - sizes[0]
-    first = call(
-        functools.partial(split_kernel, [(0, sizes[0]), (0, split)]), (me, *parts[:2], *others[:2]),
-        [shape(count, width)] * 2, scalars=1, limit=8,
-    )
-    second = call(
-        functools.partial(split_kernel, [(split, sizes[1]), (0, sizes[2])]), (me, *parts[1:], *others[1:]),
-        [shape(count, width)] * 2, scalars=1, limit=8,
-    )
-    return first, second, d_gain.reshape(width), d_tokens
+    ranges, at = [], 0
+    for i, size in enumerate(sizes):
+        for exchange in range(2):
+            start, stop = max(at, exchange * count), min(at + size, (exchange + 1) * count)
+            if start < stop:
+                ranges.append((i, start - at, stop - start, exchange, start - exchange * count))
+        at += size
+    outputs = pl.pallas_call(
+        functools.partial(split_kernel, ranges),
+        out_shape=[shape(count, width)] * 4,
+        in_specs=[SMEM] + [VMEM] * 6,
+        out_specs=[pl.BlockSpec(memory_space=pl.ANY)] * 4,
+        scratch_shapes=[pltpu.SemaphoreType.DMA((2 * len(ranges),))],
+        compiler_params=pltpu.CompilerParams(vmem_limit_bytes=2**23),
+    )(me, *parts, *others)
+    first, second = outputs[:2], outputs[2:]
+    return first, second, d_gain.reshape(width), d_tokens, result
 
 
 def body(tokens, gain, wq, wk, wv, wo, neighbour_list, neighbour_count, cotangent):
@@ -574,12 +586,12 @@
     parity = (lax.axis_index("space") % 2).astype(jnp.int32)[None]
     counts = neighbour_count[None, :]
     near = [across(tokens[i * PT : (i + 1) * PT]) for i in range(2)]
-    far = [onward(part) for part in near]
+    far = [onward(near[0])]
     gain_row = gain[None, :]
     stack_rows, stack_columns = shape(HEADS * 4 * HD, rows, dtype=BF16), shape(rows, HEADS * 4 * HD, dtype=BF16)
     turned, square, pair = pairs(width, rows), pairs(width, width), pairs(rows, width)
     whole, whole_t, scalars = shape(rows, width), shape(width, rows), shape(HEADS, rows)
-    weights = call(weight_kernel, (me, parity, wq, wk, wv, wo), square * 4, scalars=2, limit=20, us=2)
+    weights = call(weight_kernel, (me, parity, wq, wk, wv, wo), square * 4, scalars=2, limit=20)
     wq_h, wq_l, wk_h, wk_l, wv_h, wv_l, wo_h, wo_l = weights
     (
         xhat, ht_h, ht_l, q_t, q_stack, k_stack, v_stack, kt_h, kt_l, vt_h, vt_l, d_mixed_t, d_stack,
@@ -587,21 +599,26 @@
         own_kernel,
         (near[0], tokens, gain_row, cotangent, *weights),
         [whole, *turned, whole_t, stack_rows, stack_columns, stack_columns, *turned, *turned, whole_t, stack_rows],
-        limit=LIMITS[0], us=3,
-    )
+        limit=LIMITS[0], us=1,
+    )
+    near[1], q_stack = lax.optimization_barrier((near[1], q_stack))
+    far.append(onward(near[1]))
     w_k, w_v = (wk_h, wk_l), (wv_h, wv_l)
-    xhat2, ht2_h, ht2_l, kt2_h, kt2_l, e_h, e_l, d_scores, mixed, tops, totals = call(
+    xhat2, ht2_h, ht2_l, kt2_h, kt2_l, k_near, v_near, vt2_h, vt2_l = call(
+        near_side_kernel,
+        (*near, gain_row, *w_k, *w_v),
+        [whole, *turned, *turned, stack_columns, stack_columns, *turned],
+        limit=LIMITS[1], us=1,
+    )
+    e_h, e_l, d_scores, mixed, tops, totals = call(
         near_kernel,
         (
-            parity, neighbour_list, counts, *near, gain_row, q_stack, k_stack, v_stack, vt_h, vt_l, d_stack,
-            *w_k, *w_v,
+            parity, neighbour_list, counts, far[0], q_stack, k_stack, v_stack, vt_h, vt_l, d_stack, k_near, v_near,
+            vt2_h, vt2_l,
         ),
-        [
-            whole, *turned, *turned, *pairs(HEADS, 2 * rows, rows), shape(HEADS, 2 * rows, rows), whole_t, scalars,
-            scalars,
-        ],
-        [shape(8, rows), stack_columns, stack_columns, *turned],
-        scalars=3, limit=LIMITS[1], us=6,
+        [*pairs(HEADS, 2 * rows, rows), shape(HEADS, 2 * rows, rows), whole_t, scalars, scalars],
+        [shape(8, rows)],
+        scalars=3, limit=LIMITS[1], us=1,
     )
     (
         xhat3, ht3_h, ht3_l, kt3_h, kt3_l, u_h, u_l, mixed_t, deltas, shares, shares_1, dk3_h, dk3_l, dv3_h, dv3_l,
@@ -617,49 +634,51 @@
             whole,
         ],
         [shape(8, rows), stack_columns, stack_columns, *turned, *pairs(2, rows, rows)],
-        scalars=3, limit=LIMITS[2], us=6,
+        scalars=3, limit=LIMITS[2], us=1,
     )
     d_back = homeward(d_far)
-    result, keep_1, send_1, dv_h, dv_l = call(
-        mix_kernel,
-        (
-            me, mixed_t, e_h, e_l, d_mixed_t, shares_1, ht_h, ht_l, ht2_h, ht2_l, ht3_h, ht3_l, dv3_h, dv3_l, tokens,
-            cotangent, wo_h, wo_l,
-        ),
-        [whole, shape(width, width), shape(width, width), *pairs(2 * rows, width)],
-        [shape(width, width), shape(width, width)],
-        scalars=1, limit=LIMITS[3], us=5,
-    )
-    other_1 = swapped(send_1, 1)
-    d_near, dq_t, dk_h, dk_l = call(
+    d_near, dq_t, dk_h, dk_l, dv_h, dv_l = call(
         back_kernel,
         (
-            d_back, q_t, kt_h, kt_l, kt2_h, kt2_l, kt3_h, kt3_l, e_h, e_l, d_scores, u_h, u_l, deltas, shares, shares_1,
-            dv_h, dv_l, *w_k, *w_v,
+            q_t, d_mixed_t, kt_h, kt_l, kt2_h, kt2_l, kt3_h, kt3_l, e_h, e_l, d_scores, u_h, u_l, deltas, shares,
+            shares_1, *w_k, *w_v,
         ),
-        [whole, whole_t, *pairs(2 * rows, width)],
+        [whole, whole_t, *pairs(2 * rows, width), *pairs(2 * rows, width)],
         [*pairs(2, 2 * rows, rows)],
-        limit=LIMITS[4], us=5,
-    )
-    d_other = across(d_near)
+        limit=LIMITS[4], us=1,
+    )
+    keep_1, send_1 = call(
+        mix_kernel,
+        (me, mixed_t, ht_h, ht_l, ht2_h, ht2_l, ht3_h, ht3_l, dv_h, dv_l, dv3_h, dv3_l, cotangent),
+        [shape(width, width), shape(width, width)],
+        [shape(width, width), shape(width, width)],
+        scalars=1, limit=LIMITS[3], us=1,
+    )
+    other_1 = swapped(send_1, 1)
     tall = shape(width + TAIL, width)
-    keep_2, send_2, d_own = call(
+    grad_q, grad_k, d_own, gain_sum = call(
         grad_kernel,
         (
-            me, d_back, ht_h, ht_l, ht2_h, ht2_l, ht3_h, ht3_l, xhat, xhat2, xhat3, dq_t, dk_h, dk_l, dk3_h, dk3_l,
+            ht_h, ht_l, ht2_h, ht2_l, ht3_h, ht3_l, xhat, xhat2, xhat3, dq_t, dk_h, dk_l, dk3_h, dk3_l,
             dv_h, dv_l, d_near, d_far, wq_h, wq_l, *w_k, *w_v,
         ),
-        [tall, tall, whole],
-        [shape(width, width), shape(width, width)],
-        scalars=1, limit=LIMITS[5], us=4,
-    )
-    (grad_o, grad_v), (grad_q, grad_k), d_gain, (d_tokens,) = summed(
-        me, keep_1, other_1, keep_2, send_2, (tokens, gain_row, cotangent, d_own, d_other)
+        [shape(width, width), shape(width, width), whole, shape(1, width)],
+        limit=LIMITS[5], us=1,
+    )
+    keep_2, send_2, d_given = call(
+        core_kernel, (me, grad_q, grad_k, gain_sum, d_near, d_back, keep_1), [tall, tall, whole], scalars=1, limit=8
+    )
+
+    def result_of(place):
+        return call(result_kernel, (place, mixed_t, tokens, wo_h, wo_l), [whole, MARK], limit=LIMITS[3], us=1)
+
+    (grad_o, grad_v), (grad_q, grad_k), d_gain, d_tokens, result = summed(
+        me, keep_1, other_1, keep_2, send_2, d_given, (tokens, gain_row, cotangent, d_own), result_of
     )
     return (result, d_tokens, d_gain, grad_q, grad_k, grad_v, grad_o)
 
 
-UNROLL = False
+UNROLL = True
 LIMITS = (8, 8, 8, 8, 8, 8)
 
 

time: 139 us -> 119 us (0.86)
  waiting for transfers between devices: 64.4 us -> 47.3 us
  Pallas kernels: 37 us -> 32.4 us
  starting transfers between devices: 30.1 us -> 32 us
    ppermute x25 -> x24, waiting for transfers between devices: 55.4 us -> 43.8 us  [swapped(): lax.ppermute(value, ('space', 'slab'), [(i, i ^ mask) for i in range(devi...]
    pallas_call x28 -> x29, Pallas kernels: 37 us -> 30.3 us  [call(): pl.pallas_call(kernel, out_shape=outputs, in_specs=[SMEM] * scalars + [VM...]
    ppermute x6, waiting for transfers between devices: 8.98 us -> 3.46 us  [along_space(): lax.ppermute(value, 'space', [(i, target(i) % count) for i in range(count)])]
    pallas_call x0 -> x1, Pallas kernels: none -> 2.07 us  [summed(): pl.pallas_call(functools.partial(split_kernel, ranges), out_shape=[shape(...]
    ppermute x25 -> x24, starting transfers between devices: 20.8 us -> 21.5 us  [swapped(): lax.ppermute(value, ('space', 'slab'), [(i, i ^ mask) for i in range(devi...]
  transfers between devices with their start and end apart: 31 -> 30, of which waited for: 22 -> 21; matrix products, arithmetic and copies ran while one was open for 0% -> 0% of each run, Pallas kernels for 13% -> 19%
where the time goes in v3:
time: 119 us
  waiting for transfers between devices  47.3 us (40%)
  Pallas kernels  32.4 us (27%)
  starting transfers between devices  32 us (27%)
  local copies, waits for them, and re-layouts  5.99 us (5%)
    ppermute x24, waiting for transfers between devices, swapped(): lax.ppermute(value, ('space', 'slab'), [(i, i ^ mask) for i in range(devi...  43.8 us
    pallas_call x29, Pallas kernels, call(): pl.pallas_call(kernel, out_shape=outputs, in_specs=[SMEM] * scalars + [VM...  30.3 us
    ppermute x24, starting transfers between devices, swapped(): lax.ppermute(value, ('space', 'slab'), [(i, i ^ mask) for i in range(devi...  21.5 us
    ppermute x6, starting transfers between devices, along_space(): lax.ppermute(value, 'space', [(i, target(i) % count) for i in range(count)])  10.5 us
    unnamed x18, local copies, waits for them, and re-layouts  4.92 us
    ppermute x6, waiting for transfers between devices, along_space(): lax.ppermute(value, 'space', [(i, target(i) % count) for i in range(count)])  3.46 us
  transfers between devices with their start and end apart: 30, of which 21 were waited for; matrix products, arithmetic and copies ran while one was open for 0% of the time, Pallas kernels for 19%

profile of v3, /device:TPU:0, one launch (start us, length us, event | category | flops | bytes accessed | tf_op | source)
XLA Modules:
  0.0 118.7 jit_solution(7428063164514130141)
XLA Ops:
  1.7 3.0 %collective-permute-start = (f32[128,512]{1,0:T(8,128)S(1)}, f32[128,512]{1,0:T(8,128)S(1)}, u32[]{:S(2)}, u32[]{:S(2)}) collective-permute-start(f32[128,512]{1,0:T(8,128)S(1)} %get-tuple-element.210), channel_id=1, source_target_pairs={{0,4},{4,0},{8,12},{12,8},{16,20},{20,16},{24,28},{28,24},{1,5},{5... | collective-permute-start | bytes 786440 | tf_op jit(solution)/shard_map/ppermute | solution.py:486
  10.3 1.5 %collective-permute-done._.patch_0 = f32[128,512]{1,0:T(8,128)S(1)} collective-permute-done((f32[128,512]{1,0:T(8,128)S(1)}, f32[128,512]{1,0:T(8,128)S(1)}, u32[]{:S(2)}, u32[]{:S(2)}) %collective-permute-start) | collective-permute-done | bytes 262176 | tf_op jit(solution)/shard_map/ppermute | solution.py:486
  11.8 2.1 %collective-permute-start.1 = (f32[128,512]{1,0:T(8,128)S(1)}, f32[128,512]{1,0:T(8,128)S(1)}, u32[]{:S(2)}, u32[]{:S(2)}) collective-permute-start(f32[128,512]{1,0:T(8,128)S(1)} %collective-permute-done._.patch_0), channel_id=1, source_target_pairs={{0,8},{4,28},{8,16},{12,4},{16,24},{20,12},{24,0},{28,20},{1,9},{5... | collective-permute-start | bytes 786440 | tf_op jit(solution)/shard_map/ppermute | solution.py:486
  14.0 2.2 %shard_map.145 = (f32[256,512]{1,0:T(8,128)S(1)}, bf16[512,256]{1,0:T(8,128)(2,1)S(1)}, bf16[512,256]{1,0:T(8,128)(2,1)S(1)}, f32[512,256]{1,0:T(8,128)S(1)}, bf...) custom-call(f32[128,512]{1,0:T(8,128)S(1)} %collective-permute-done., ...), custom_call_target="tpu_custom_call" | custom-call | flops 1000000000 | tf_op jit(solution)/shard_map/pallas_call | solution.py:470
  16.6 1.8 %collective-permute-start.3 = (f32[128,512]{1,0:T(8,128)S(1)}, f32[128,512]{1,0:T(8,128)S(1)}, u32[]{:S(2)}, u32[]{:S(2)}) collective-permute-start(f32[128,512]{1,0:T(8,128)S(1)} %collective-permute-done.2.patch_1), channel_id=1, source_target_pairs={{0,8},{4,28},{8,16},{12,4},{16,24},{20,12},{24,0},{28,20},{1,9},{5... | collective-permute-start | bytes 786440 | tf_op jit(solution)/shard_map/ppermute | solution.py:486
  18.5 1.6 %shard_map.146 = (f32[256,512]{1,0:T(8,128)S(1)}, bf16[512,256]{1,0:T(8,128)(2,1)S(1)}, bf16[512,256]{1,0:T(8,128)(2,1)S(1)}, bf16[512,256]{1,0:T(8,128)(2,1)S(1...) custom-call(f32[128,512]{1,0:T(8,128)S(1)} %collective-permute-done., ...), custom_call_target="tpu_custom_call" | custom-call | flops 1000000000 | tf_op jit(solution)/shard_map/pallas_call | solution.py:470
  20.4 4.6 %shard_map.147 = (bf16[8,512,256]{2,1,0:T(8,128)(2,1)S(1)}, bf16[8,512,256]{2,1,0:T(8,128)(2,1)S(1)}, f32[8,512,256]{2,1,0:T(8,128)S(1)}, f32[512,256]{1,0:T(8,1...) custom-call(s32[1]{0:T(128)} %bitcast.1._parity.parity, s32[2,3]{1,0:T(2,128)S(1)} %copy-done.7, s32[1,2]{1,0:T(1,128)S(1)} %bitcast.9, ...), custom_call_target="tpu_custom_call" | custom-call | flops 1000000000 | tf_op jit(solution)/shard_map/pallas_call | solution.py:470
  26.0 6.9 %shard_map.148 = (f32[256,512]{1,0:T(8,128)S(1)}, bf16[512,256]{1,0:T(8,128)(2,1)S(1)}, bf16[512,256]{1,0:T(8,128)(2,1)S(1)}, bf16[512,256]{1,0:T(8,128)(2,1)S(1...) custom-call(s32[1]{0:T(128)} %bitcast.1._parity.parity, ...), custom_call_target="tpu_custom_call" | custom-call | flops 1000000000 | tf_op jit(solution)/shard_map/pallas_call | solution.py:470
  32.9 2.3 %collective-permute-start.5 = (f32[256,512]{1,0:T(8,128)S(1)}, f32[256,512]{1,0:T(8,128)S(1)}, u32[]{:S(2)}, u32[]{:S(2)}) collective-permute-start(f32[256,512]{1,0:T(8,128)S(1)} %get-tuple-element.169.d_far), channel_id=1, source_target_pairs={{0,24},{4,12},{8,0},{12,20},{16,8},{20,28},{24,16},{28,4},{1,25},{... | collective-permute-start | bytes 1572872 | tf_op jit(solution)/shard_map/ppermute | solution.py:486
  35.2 4.7 %shard_map.149 = (f32[256,512]{1,0:T(8,128)S(1)}, f32[512,256]{1,0:T(8,128)S(1)}, bf16[512,512]{1,0:T(8,128)(2,1)S(1)}, bf16[512,512]{1,0:T(8,128)(2,1)S(1)}, bf...) custom-call(f32[512,256]{1,0:T(8,128)S(1)} %get-tuple-element.118.q_t, ...), custom_call_target="tpu_custom_call" | custom-call | flops 1000000000 | tf_op jit(solution)/shard_map/pallas_call | solution.py:470
  39.9 1.9 %shard_map.150 = (f32[512,512]{1,0:T(8,128)S(1)}, f32[512,512]{1,0:T(8,128)S(1)}) custom-call(s32[1]{0:T(128)} %bitcast._me.me, f32[512,256]{1,0:T(8,128)S(1)} %get-tuple-element.133.mixed_t, bf16[512,256]{1,0:T(8,128)(2,1)S(1)} %get-tuple-element.134.ht_h, bf16[512,256]{1,0:T(8,128)(2,1)S(1)} %get-tuple-element.135.ht_l, ...), custom_call_target="tpu_custom_call" | custom-call | flops 1000000000 | tf_op jit(solution)/shard_map/pallas_call | solution.py:470
  41.9 3.3 %shard_map.151 = (f32[512,512]{1,0:T(8,128)S(1)}, f32[512,512]{1,0:T(8,128)S(1)}, f32[256,512]{1,0:T(8,128)S(1)}, f32[1,512]{1,0:T(1,128)S(1)}) custom-call(bf16[512,256]{1,0:T(8,128)(2,1)S(1)} %get-tuple-element.134.ht_h, bf16[512,256]{1,0:T(8,128)(2,1)S(1)} %get-tuple-element.135.ht_l, bf16[512,256]{1,0:T(8,128)(2,1)S(1)} %get-tuple-element.136.ht2_h, ...), custom_call_target="tpu_custom_call" | custom-call | flops 1000000000 | tf_op jit(solution)/shard_map/pallas_call | solution.py:470
  46.2 3.7 %collective-permute-done.4.other_1 = f32[512,512]{1,0:T(8,128)S(1)} collective-permute-done((f32[512,512]{1,0:T(8,128)S(1)}, f32[512,512]{1,0:T(8,128)S(1)}, u32[]{:S(2)}, u32[]{:S(2)}) %collective-permute-start.4) | collective-permute-done | bytes 1048608 | tf_op jit(solution)/shard_map/ppermute | solution.py:506
  50.2 4.5 %collective-permute-start.7 = (f32[168,512]{1,0:T(8,128)S(1)}, f32[168,512]{1,0:T(8,128)S(1)}, u32[]{:S(2)}, u32[]{:S(2)}) collective-permute-start(f32[168,512]{1,0:T(8,128)S(1)} %get-tuple-element.176), channel_id=1, source_target_pairs={{0,4},{1,5},{2,6},{3,7},{4,0},{5,1},{6,2},{7,3},{8,12},{9,13},{10,... | collective-permute-start | bytes 1032200 | tf_op jit(solution)/shard_map/ppermute | solution.py:506
  54.7 1.5 %collective-permute-start.10 = (f32[160,512]{1,0:T(8,128)S(1)}, f32[160,512]{1,0:T(8,128)S(1)}, u32[]{:S(2)}, u32[]{:S(2)}) collective-permute-start(f32[160,512]{1,0:T(8,128)S(1)} %get-tuple-element.182), channel_id=1, source_target_pairs={{0,2},{1,3},{2,0},{3,1},{4,6},{5,7},{6,4},{7,5},{8,10},{9,11},{10,... | collective-permute-start | bytes 983048 | tf_op jit(solution)/shard_map/ppermute | solution.py:506
  56.2 6.8 %collective-permute-done.7.other = f32[168,512]{1,0:T(8,128)S(1)} collective-permute-done((f32[168,512]{1,0:T(8,128)S(1)}, f32[168,512]{1,0:T(8,128)S(1)}, u32[]{:S(2)}, u32[]{:S(2)}) %collective-permute-start.7) | collective-permute-done | bytes 344096 | tf_op jit(solution)/shard_map/ppermute | solution.py:506
  63.1 1.6 %collective-permute-start.8 = (f32[88,512]{1,0:T(8,128)S(1)}, f32[88,512]{1,0:T(8,128)S(1)}, u32[]{:S(2)}, u32[]{:S(2)}) collective-permute-start(f32[88,512]{1,0:T(8,128)S(1)} %get-tuple-element.178), channel_id=1, source_target_pairs={{0,2},{1,3},{2,0},{3,1},{4,6},{5,7},{6,4},{7,5},{8,10},{9,11},{10,... | collective-permute-start | bytes 540680 | tf_op jit(solution)/shard_map/ppermute | solution.py:506
  67.5 1.8 %collective-permute-done.8.other = f32[88,512]{1,0:T(8,128)S(1)} collective-permute-done((f32[88,512]{1,0:T(8,128)S(1)}, f32[88,512]{1,0:T(8,128)S(1)}, u32[]{:S(2)}, u32[]{:S(2)}) %collective-permute-start.8) | collective-permute-done | bytes 180256 | tf_op jit(solution)/shard_map/ppermute | solution.py:506
  69.9 1.6 %collective-permute-done.14.other = f32[96,512]{1,0:T(8,128)S(1)} collective-permute-done((f32[96,512]{1,0:T(8,128)S(1)}, f32[96,512]{1,0:T(8,128)S(1)}, u32[]{:S(2)}, u32[]{:S(2)}) %collective-permute-start.14) | collective-permute-done | bytes 196640 | tf_op jit(solution)/shard_map/ppermute | solution.py:506
  71.5 1.6 %collective-permute-start.15 = (f32[48,512]{1,0:T(8,128)S(1)}, f32[48,512]{1,0:T(8,128)S(1)}, u32[]{:S(2)}, u32[]{:S(2)}) collective-permute-start(f32[48,512]{1,0:T(8,128)S(1)} %get-tuple-element.192), channel_id=1, source_target_pairs={{0,2},{1,3},{2,0},{3,1},{4,6},{5,7},{6,4},{7,5},{8,10},{9,11},{10,... | collective-permute-start | bytes 294920 | tf_op jit(solution)/shard_map/ppermute | solution.py:506
  74.3 4.0 %collective-permute-done.12.refs_3_ = f32[40,512]{1,0:T(8,128)S(1)} collective-permute-done((f32[40,512]{1,0:T(8,128)S(1)}, f32[40,512]{1,0:T(8,128)S(1)}, u32[]{:S(2)}, u32[]{:S(2)}) %collective-permute-start.12) | collective-permute-done | bytes 81952 | tf_op jit(solution)/shard_map/ppermute | solution.py:506
  79.5 1.4 %shard_map.161 = (f32[256,512]{1,0:T(8,128)}, f32[8,128]{1,0:T(8,128)S(1)}) custom-call(f32[136,512]{1,0:T(8,128)S(1)} %get-tuple-element.194._.a, f32[512,256]{1,0:T(8,128)S(1)} %get-tuple-element.133.mixed_t, f32[256,512]{1,0:T(8,128)S(1)} %copy-done.1, bf16[512,512]{1,0:T(8,128)(2,1)S(1)} %get-tuple-element.114.wo_h, ...), custom_call_target="tpu_custom_call" | custom-call | flops 1000000000 | tf_op jit(solution)/shard_map/pallas_call | solution.py:470
  80.9 9.9 %collective-permute-done.16.b = f32[136,512]{1,0:T(8,128)S(1)} collective-permute-done((f32[136,512]{1,0:T(8,128)S(1)}, f32[136,512]{1,0:T(8,128)S(1)}, u32[]{:S(2)}, u32[]{:S(2)}) %collective-permute-start.16) | collective-permute-done | bytes 278560 | tf_op jit(solution)/shard_map/ppermute | solution.py:506
  93.0 3.0 %collective-permute-done.24.other = f32[48,512]{1,0:T(8,128)S(1)} collective-permute-done((f32[48,512]{1,0:T(8,128)S(1)}, f32[48,512]{1,0:T(8,128)S(1)}, u32[]{:S(2)}, u32[]{:S(2)}) %collective-permute-start.24) | collective-permute-done | bytes 98336 | tf_op jit(solution)/shard_map/ppermute | solution.py:506
  97.0 2.1 %collective-permute-start.22 = (f32[80,512]{1,0:T(8,128)S(1)}, f32[80,512]{1,0:T(8,128)S(1)}, u32[]{:S(2)}, u32[]{:S(2)}) collective-permute-start(f32[80,512]{1,0:T(8,128)S(1)} %shard_map.167.mine), channel_id=1, source_target_pairs={{0,8},{1,9},{2,10},{3,11},{4,12},{5,13},{6,14},{7,15},{8,0},{9,1},... | collective-permute-start | bytes 491528 | tf_op jit(solution)/shard_map/ppermute | solution.py:506
  99.0 2.5 %collective-permute-done.18.other = f32[40,512]{1,0:T(8,128)S(1)} collective-permute-done((f32[40,512]{1,0:T(8,128)S(1)}, f32[40,512]{1,0:T(8,128)S(1)}, u32[]{:S(2)}, u32[]{:S(2)}) %collective-permute-start.18) | collective-permute-done | bytes 81952 | tf_op jit(solution)/shard_map/ppermute | solution.py:506
  102.6 2.5 %collective-permute-done.22.other = f32[80,512]{1,0:T(8,128)S(1)} collective-permute-done((f32[80,512]{1,0:T(8,128)S(1)}, f32[80,512]{1,0:T(8,128)S(1)}, u32[]{:S(2)}, u32[]{:S(2)}) %collective-permute-start.22) | collective-permute-done | bytes 163872 | tf_op jit(solution)/shard_map/ppermute | solution.py:506
  107.0 1.8 %collective-permute-start.20 = (f32[160,512]{1,0:T(8,128)S(1)}, f32[160,512]{1,0:T(8,128)S(1)}, u32[]{:S(2)}, u32[]{:S(2)}) collective-permute-start(f32[160,512]{1,0:T(8,128)S(1)} %shard_map.164._.mine), channel_id=1, source_target_pairs={{0,4},{1,5},{2,6},{3,7},{4,0},{5,1},{6,2},{7,3},{8,12},{9,13},{10,... | collective-permute-start | bytes 983048 | tf_op jit(solution)/shard_map/ppermute | solution.py:506
  110.0 1.6 %collective-permute-done.26.other = f32[192,512]{1,0:T(8,128)S(1)} collective-permute-done((f32[192,512]{1,0:T(8,128)S(1)}, f32[192,512]{1,0:T(8,128)S(1)}, u32[]{:S(2)}, u32[]{:S(2)}) %collective-permute-start.26) | collective-permute-done | bytes 393248 | tf_op jit(solution)/shard_map/ppermute | solution.py:506
  112.4 1.8 %collective-permute-done.20.other = f32[160,512]{1,0:T(8,128)S(1)} collective-permute-done((f32[160,512]{1,0:T(8,128)S(1)}, f32[160,512]{1,0:T(8,128)S(1)}, u32[]{:S(2)}, u32[]{:S(2)}) %collective-permute-start.20) | collective-permute-done | bytes 327712 | tf_op jit(solution)/shard_map/ppermute | solution.py:506
  114.9 1.5 %collective-permute-done.27.refs_3_ = f32[320,512]{1,0:T(8,128)S(1)} collective-permute-done((f32[320,512]{1,0:T(8,128)S(1)}, f32[320,512]{1,0:T(8,128)S(1)}, u32[]{:S(2)}, u32[]{:S(2)}) %collective-permute-start.27) | collective-permute-done | bytes 655392 | tf_op jit(solution)/shard_map/ppermute | solution.py:506
  116.4 2.1 %shard_map.173 = (f32[512,512]{1,0:T(8,128)}, f32[512,512]{1,0:T(8,128)}, f32[512,512]{1,0:T(8,128)}, f32[512,512]{1,0:T(8,128)}) custom-call(s32[1]{0:T(128)} %bitcast._me.me, f32[320,512]{1,0:T(8,128)S(1)} %shard_map.166.refs_0_, f32[320,512]{1,0:T(8,128)S(1)} %shard_map.169.refs_1_, f32[384,512]{1,0:T(8,128)S(1)} %shard_map.172.refs_2_, ...), custom_call_target="tpu_custom_call" | custom-call | tf_op jit(solution)/shard_map/pallas_call | solution.py:571
  (77 shorter events, 24.4 us)
Async XLA Ops:
  1.7 10.1 %collective-permute-start = (f32[128,512]{1,0:T(8,128)S(1)}, f32[128,512]{1,0:T(8,128)S(1)}, u32[]{:S(2)}, u32[]{:S(2)}) collective-permute-start(f32[128,512]{1,0:T(8,128)S(1)} %get-tuple-element.210), channel_id=1, source_target_pairs={{0,4},{4,0},{8,12},{12,8},{16,20},{20,16},{24,28},{28,24},{1,5},{5... | collective-permute-start | bytes 786440 | tf_op jit(solution)/shard_map/ppermute | solution.py:486
  4.7 11.9 %collective-permute-start.2 = (f32[128,512]{1,0:T(8,128)S(1)}, f32[128,512]{1,0:T(8,128)S(1)}, u32[]{:S(2)}, u32[]{:S(2)}) collective-permute-start(f32[128,512]{1,0:T(8,128)S(1)} %get-tuple-element.209), channel_id=1, source_target_pairs={{0,4},{4,0},{8,12},{12,8},{16,20},{20,16},{24,28},{28,24},{1,5},{5... | collective-permute-start | bytes 786440 | tf_op jit(solution)/shard_map/ppermute | solution.py:486
  9.7 4.3 %copy-start.1 = (f32[256,512]{1,0:T(8,128)S(1)}, f32[256,512]{1,0:T(8,128)}, u32[]{:S(2)}) copy-start(f32[256,512]{1,0:T(8,128)} %tokens.5) | copy-start | bytes 1572868
  9.7 4.3 %copy-start.6 = (f32[512]{0:T(512)S(1)}, f32[512]{0:T(512)}, u32[]{:S(2)}) copy-start(f32[512]{0:T(512)} %param.10) | copy-start | bytes 6148
  11.8 8.5 %collective-permute-start.1 = (f32[128,512]{1,0:T(8,128)S(1)}, f32[128,512]{1,0:T(8,128)S(1)}, u32[]{:S(2)}, u32[]{:S(2)}) collective-permute-start(f32[128,512]{1,0:T(8,128)S(1)} %collective-permute-done._.patch_0), channel_id=1, source_target_pairs={{0,8},{4,28},{8,16},{12,4},{16,24},{20,12},{24,0},{28,20},{1,9},{5... | collective-permute-start | bytes 786440 | tf_op jit(solution)/shard_map/ppermute | solution.py:486
  16.6 9.3 %collective-permute-start.3 = (f32[128,512]{1,0:T(8,128)S(1)}, f32[128,512]{1,0:T(8,128)S(1)}, u32[]{:S(2)}, u32[]{:S(2)}) collective-permute-start(f32[128,512]{1,0:T(8,128)S(1)} %collective-permute-done.2.patch_1), channel_id=1, source_target_pairs={{0,8},{4,28},{8,16},{12,4},{16,24},{20,12},{24,0},{28,20},{1,9},{5... | collective-permute-start | bytes 786440 | tf_op jit(solution)/shard_map/ppermute | solution.py:486
  32.9 12.5 %collective-permute-start.5 = (f32[256,512]{1,0:T(8,128)S(1)}, f32[256,512]{1,0:T(8,128)S(1)}, u32[]{:S(2)}, u32[]{:S(2)}) collective-permute-start(f32[256,512]{1,0:T(8,128)S(1)} %get-tuple-element.169.d_far), channel_id=1, source_target_pairs={{0,24},{4,12},{8,0},{12,20},{16,8},{20,28},{24,16},{28,4},{1,25},{... | collective-permute-start | bytes 1572872 | tf_op jit(solution)/shard_map/ppermute | solution.py:486
  45.6 4.3 %collective-permute-start.6 = (f32[520,512]{1,0:T(8,128)S(1)}, f32[520,512]{1,0:T(8,128)S(1)}, u32[]{:S(2)}, u32[]{:S(2)}) collective-permute-start(f32[520,512]{1,0:T(8,128)S(1)} %get-tuple-element.174), channel_id=1, source_target_pairs={{0,1},{1,0},{2,3},{3,2},{4,5},{5,4},{6,7},{7,6},{8,9},{9,8},{10,11... | collective-permute-start | bytes 3194888 | tf_op jit(solution)/shard_map/ppermute | solution.py:506
  45.7 4.2 %collective-permute-start.4 = (f32[512,512]{1,0:T(8,128)S(1)}, f32[512,512]{1,0:T(8,128)S(1)}, u32[]{:S(2)}, u32[]{:S(2)}) collective-permute-start(f32[512,512]{1,0:T(8,128)S(1)} %get-tuple-element.159), channel_id=1, source_target_pairs={{0,1},{1,0},{2,3},{3,2},{4,5},{5,4},{6,7},{7,6},{8,9},{9,8},{10,11... | collective-permute-start | bytes 3145736 | tf_op jit(solution)/shard_map/ppermute | solution.py:506
  50.2 12.9 %collective-permute-start.7 = (f32[168,512]{1,0:T(8,128)S(1)}, f32[168,512]{1,0:T(8,128)S(1)}, u32[]{:S(2)}, u32[]{:S(2)}) collective-permute-start(f32[168,512]{1,0:T(8,128)S(1)} %get-tuple-element.176), channel_id=1, source_target_pairs={{0,4},{1,5},{2,6},{3,7},{4,0},{5,1},{6,2},{7,3},{8,12},{9,13},{10,... | collective-permute-start | bytes 1032200 | tf_op jit(solution)/shard_map/ppermute | solution.py:506
  54.7 10.9 %collective-permute-start.13 = (f32[192,512]{1,0:T(8,128)S(1)}, f32[192,512]{1,0:T(8,128)S(1)}, u32[]{:S(2)}, u32[]{:S(2)}) collective-permute-start(f32[192,512]{1,0:T(8,128)S(1)} %get-tuple-element.188), channel_id=1, source_target_pairs={{0,8},{1,9},{2,10},{3,11},{4,12},{5,13},{6,14},{7,15},{8,0},{9,1},... | collective-permute-start | bytes 1179656 | tf_op jit(solution)/shard_map/ppermute | solution.py:506
  54.7 11.9 %collective-permute-start.10 = (f32[160,512]{1,0:T(8,128)S(1)}, f32[160,512]{1,0:T(8,128)S(1)}, u32[]{:S(2)}, u32[]{:S(2)}) collective-permute-start(f32[160,512]{1,0:T(8,128)S(1)} %get-tuple-element.182), channel_id=1, source_target_pairs={{0,2},{1,3},{2,0},{3,1},{4,6},{5,7},{6,4},{7,5},{8,10},{9,11},{10,... | collective-permute-start | bytes 983048 | tf_op jit(solution)/shard_map/ppermute | solution.py:506
  63.1 6.1 %collective-permute-start.8 = (f32[88,512]{1,0:T(8,128)S(1)}, f32[88,512]{1,0:T(8,128)S(1)}, u32[]{:S(2)}, u32[]{:S(2)}) collective-permute-start(f32[88,512]{1,0:T(8,128)S(1)} %get-tuple-element.178), channel_id=1, source_target_pairs={{0,2},{1,3},{2,0},{3,1},{4,6},{5,7},{6,4},{7,5},{8,10},{9,11},{10,... | collective-permute-start | bytes 540680 | tf_op jit(solution)/shard_map/ppermute | solution.py:506
  65.6 5.9 %collective-permute-start.14 = (f32[96,512]{1,0:T(8,128)S(1)}, f32[96,512]{1,0:T(8,128)S(1)}, u32[]{:S(2)}, u32[]{:S(2)}) collective-permute-start(f32[96,512]{1,0:T(8,128)S(1)} %get-tuple-element.190), channel_id=1, source_target_pairs={{0,4},{1,5},{2,6},{3,7},{4,0},{5,1},{6,2},{7,3},{8,12},{9,13},{10,... | collective-permute-start | bytes 589832 | tf_op jit(solution)/shard_map/ppermute | solution.py:506
  66.6 6.5 %collective-permute-start.11 = (f32[80,512]{1,0:T(8,128)S(1)}, f32[80,512]{1,0:T(8,128)S(1)}, u32[]{:S(2)}, u32[]{:S(2)}) collective-permute-start(f32[80,512]{1,0:T(8,128)S(1)} %get-tuple-element.184), channel_id=1, source_target_pairs={{0,8},{1,9},{2,10},{3,11},{4,12},{5,13},{6,14},{7,15},{8,0},{9,1},... | collective-permute-start | bytes 491528 | tf_op jit(solution)/shard_map/ppermute | solution.py:506
  69.3 9.0 %collective-permute-start.9 = (f32[48,512]{1,0:T(8,128)S(1)}, f32[48,512]{1,0:T(8,128)S(1)}, u32[]{:S(2)}, u32[]{:S(2)}) collective-permute-start(f32[48,512]{1,0:T(8,128)S(1)} %get-tuple-element.180), channel_id=1, source_target_pairs={{0,8},{1,9},{2,10},{3,11},{4,12},{5,13},{6,14},{7,15},{8,0},{9,1},... | collective-permute-start | bytes 294920 | tf_op jit(solution)/shard_map/ppermute | solution.py:506
  71.5 6.7 %collective-permute-start.15 = (f32[48,512]{1,0:T(8,128)S(1)}, f32[48,512]{1,0:T(8,128)S(1)}, u32[]{:S(2)}, u32[]{:S(2)}) collective-permute-start(f32[48,512]{1,0:T(8,128)S(1)} %get-tuple-element.192), channel_id=1, source_target_pairs={{0,2},{1,3},{2,0},{3,1},{4,6},{5,7},{6,4},{7,5},{8,10},{9,11},{10,... | collective-permute-start | bytes 294920 | tf_op jit(solution)/shard_map/ppermute | solution.py:506
  73.1 5.1 %collective-permute-start.12 = (f32[40,512]{1,0:T(8,128)S(1)}, f32[40,512]{1,0:T(8,128)S(1)}, u32[]{:S(2)}, u32[]{:S(2)}) collective-permute-start(f32[40,512]{1,0:T(8,128)S(1)} %get-tuple-element.186), channel_id=1, source_target_pairs={{0,4},{1,5},{2,6},{3,7},{4,0},{5,1},{6,2},{7,3},{8,12},{9,13},{10,... | collective-permute-start | bytes 245768 | tf_op jit(solution)/shard_map/ppermute | solution.py:506
  78.3 12.5 %collective-permute-start.17 = (f32[256,512]{1,0:T(8,128)S(1)}, f32[256,512]{1,0:T(8,128)S(1)}, u32[]{:S(2)}, u32[]{:S(2)}) collective-permute-start(f32[256,512]{1,0:T(8,128)S(1)} %get-tuple-element.197), channel_id=1, source_target_pairs={{0,4},{4,0},{8,12},{12,8},{16,20},{20,16},{24,28},{28,24},{1,5},{5... | collective-permute-start | bytes 1572872 | tf_op jit(solution)/shard_map/ppermute | solution.py:486
  79.5 11.3 %collective-permute-start.16 = (f32[136,512]{1,0:T(8,128)S(1)}, f32[136,512]{1,0:T(8,128)S(1)}, u32[]{:S(2)}, u32[]{:S(2)}) collective-permute-start(f32[136,512]{1,0:T(8,128)S(1)} %get-tuple-element.194._.a), channel_id=1, source_target_pairs={{0,16},{1,17},{2,18},{3,19},{4,20},{5,21},{6,22},{7,23},{8,24},{9,... | collective-permute-start | bytes 835592 | tf_op jit(solution)/shard_map/ppermute | solution.py:506
  91.4 4.6 %collective-permute-start.24 = (f32[48,512]{1,0:T(8,128)S(1)}, f32[48,512]{1,0:T(8,128)S(1)}, u32[]{:S(2)}, u32[]{:S(2)}) collective-permute-start(f32[48,512]{1,0:T(8,128)S(1)} %get-tuple-element.203.mine), channel_id=1, source_target_pairs={{0,2},{1,3},{2,0},{3,1},{4,6},{5,7},{6,4},{7,5},{8,10},{9,11},{10,... | collective-permute-start | bytes 294920 | tf_op jit(solution)/shard_map/ppermute | solution.py:506
  92.1 4.8 %collective-permute-start.21 = (f32[40,512]{1,0:T(8,128)S(1)}, f32[40,512]{1,0:T(8,128)S(1)}, u32[]{:S(2)}, u32[]{:S(2)}) collective-permute-start(f32[40,512]{1,0:T(8,128)S(1)} %get-tuple-element.202.mine), channel_id=1, source_target_pairs={{0,4},{1,5},{2,6},{3,7},{4,0},{5,1},{6,2},{7,3},{8,12},{9,13},{10,... | collective-permute-start | bytes 245768 | tf_op jit(solution)/shard_map/ppermute | solution.py:506
  96.1 6.4 %collective-permute-start.25 = (f32[96,512]{1,0:T(8,128)S(1)}, f32[96,512]{1,0:T(8,128)S(1)}, u32[]{:S(2)}, u32[]{:S(2)}) collective-permute-start(f32[96,512]{1,0:T(8,128)S(1)} %shard_map.170.mine), channel_id=1, source_target_pairs={{0,4},{1,5},{2,6},{3,7},{4,0},{5,1},{6,2},{7,3},{8,12},{9,13},{10,... | collective-permute-start | bytes 589832 | tf_op jit(solution)/shard_map/ppermute | solution.py:506
  96.9 4.7 %collective-permute-start.18 = (f32[40,512]{1,0:T(8,128)S(1)}, f32[40,512]{1,0:T(8,128)S(1)}, u32[]{:S(2)}, u32[]{:S(2)}) collective-permute-start(f32[40,512]{1,0:T(8,128)S(1)} %get-tuple-element.198.mine), channel_id=1, source_target_pairs={{0,8},{1,9},{2,10},{3,11},{4,12},{5,13},{6,14},{7,15},{8,0},{9,1},... | collective-permute-start | bytes 245768 | tf_op jit(solution)/shard_map/ppermute | solution.py:506
  97.0 8.1 %collective-permute-start.22 = (f32[80,512]{1,0:T(8,128)S(1)}, f32[80,512]{1,0:T(8,128)S(1)}, u32[]{:S(2)}, u32[]{:S(2)}) collective-permute-start(f32[80,512]{1,0:T(8,128)S(1)} %shard_map.167.mine), channel_id=1, source_target_pairs={{0,8},{1,9},{2,10},{3,11},{4,12},{5,13},{6,14},{7,15},{8,0},{9,1},... | collective-permute-start | bytes 491528 | tf_op jit(solution)/shard_map/ppermute | solution.py:506
  101.6 5.4 %collective-permute-start.19 = (f32[80,512]{1,0:T(8,128)S(1)}, f32[80,512]{1,0:T(8,128)S(1)}, u32[]{:S(2)}, u32[]{:S(2)}) collective-permute-start(f32[80,512]{1,0:T(8,128)S(1)} %shard_map.163.mine), channel_id=1, source_target_pairs={{0,2},{1,3},{2,0},{3,1},{4,6},{5,7},{6,4},{7,5},{8,10},{9,11},{10,... | collective-permute-start | bytes 491528 | tf_op jit(solution)/shard_map/ppermute | solution.py:506
  102.5 9.0 %collective-permute-start.26 = (f32[192,512]{1,0:T(8,128)S(1)}, f32[192,512]{1,0:T(8,128)S(1)}, u32[]{:S(2)}, u32[]{:S(2)}) collective-permute-start(f32[192,512]{1,0:T(8,128)S(1)} %shard_map.171.mine), channel_id=1, source_target_pairs={{0,8},{1,9},{2,10},{3,11},{4,12},{5,13},{6,14},{7,15},{8,0},{9,1},... | collective-permute-start | bytes 1179656 | tf_op jit(solution)/shard_map/ppermute | solution.py:506
  105.1 7.1 %collective-permute-start.23 = (f32[160,512]{1,0:T(8,128)S(1)}, f32[160,512]{1,0:T(8,128)S(1)}, u32[]{:S(2)}, u32[]{:S(2)}) collective-permute-start(f32[160,512]{1,0:T(8,128)S(1)} %shard_map.168.mine), channel_id=1, source_target_pairs={{0,2},{1,3},{2,0},{3,1},{4,6},{5,7},{6,4},{7,5},{8,10},{9,11},{10,... | collective-permute-start | bytes 983048 | tf_op jit(solution)/shard_map/ppermute | solution.py:506
  107.0 7.1 %collective-permute-start.20 = (f32[160,512]{1,0:T(8,128)S(1)}, f32[160,512]{1,0:T(8,128)S(1)}, u32[]{:S(2)}, u32[]{:S(2)}) collective-permute-start(f32[160,512]{1,0:T(8,128)S(1)} %shard_map.164._.mine), channel_id=1, source_target_pairs={{0,4},{1,5},{2,6},{3,7},{4,0},{5,1},{6,2},{7,3},{8,12},{9,13},{10,... | collective-permute-start | bytes 983048 | tf_op jit(solution)/shard_map/ppermute | solution.py:506
  111.6 4.8 %collective-permute-start.29 = (f32[384,512]{1,0:T(8,128)S(1)}, f32[384,512]{1,0:T(8,128)S(1)}, u32[]{:S(2)}, u32[]{:S(2)}) collective-permute-start(f32[384,512]{1,0:T(8,128)S(1)} %shard_map.172.refs_2_), channel_id=1, source_target_pairs={{0,1},{1,0},{2,3},{3,2},{4,5},{5,4},{6,7},{7,6},{8,9},{9,8},{10,11... | collective-permute-start | bytes 2359304 | tf_op jit(solution)/shard_map/ppermute | solution.py:506
  112.3 2.6 %collective-permute-start.28 = (f32[320,512]{1,0:T(8,128)S(1)}, f32[320,512]{1,0:T(8,128)S(1)}, u32[]{:S(2)}, u32[]{:S(2)}) collective-permute-start(f32[320,512]{1,0:T(8,128)S(1)} %shard_map.169.refs_1_), channel_id=1, source_target_pairs={{0,1},{1,0},{2,3},{3,2},{4,5},{5,4},{6,7},{7,6},{8,9},{9,8},{10,11... | collective-permute-start | bytes 1966088 | tf_op jit(solution)/shard_map/ppermute | solution.py:506
  114.2 2.2 %collective-permute-start.27 = (f32[320,512]{1,0:T(8,128)S(1)}, f32[320,512]{1,0:T(8,128)S(1)}, u32[]{:S(2)}, u32[]{:S(2)}) collective-permute-start(f32[320,512]{1,0:T(8,128)S(1)} %shard_map.166.refs_0_), channel_id=1, source_target_pairs={{0,1},{1,0},{2,3},{3,2},{4,5},{5,4},{6,7},{7,6},{8,9},{9,8},{10,11... | collective-permute-start | bytes 1966088 | tf_op jit(solution)/shard_map/ppermute | solution.py:506
  (7 other events, 17.6 us)

commit v4 on v3

--- a/solution.py
+++ b/solution.py
@@ -277,12 +277,9 @@
 
 def back_kernel(
     q_t, d_mixed_t, kt_h, kt_l, kt2_h, kt2_l, kt3_h, kt3_l, e_h, e_l, d_scores, u_h, u_l, deltas, shares, shares_1,
-    wk_h, wk_l, wv_h, wv_l,
-    d_near, dq_t, dk_h, dk_l, dv_h, dv_l,
+    dq_t, dk_h, dk_l, dv_h, dv_l,
     s_h, s_l,
 ):
-    own = d_near.shape[0]
-
     def one_pair(p, carry):
         q_scaled, d_scaled = [], []
         for a in range(2):
@@ -308,10 +305,6 @@
         return carry
 
     lax.fori_loop(0, PAIRS, one_pair, 0, unroll=UNROLL)
-    near = slice(own, 2 * own)
-    d_near[...] = sums_of(
-        [load((dk_h, dk_l), near), load((dv_h, dv_l), near)], [load((wk_h, wk_l), ...), load((wv_h, wv_l), ...)], NT
-    )
 
 
 def mix_kernel(
@@ -333,34 +326,36 @@
 
 
 def grad_kernel(
-    ht_h, ht_l, ht2_h, ht2_l, ht3_h, ht3_l, xhat, xhat2, xhat3, dq_t, dk_h, dk_l, dk3_h, dk3_l, dv_h, dv_l,
-    d_near, d_far, wq_h, wq_l, wk_h, wk_l, wv_h, wv_l,
-    grad_q, grad_k, d_own, gain_sum,
-):
-    own, width = d_own.shape
-    first, second = slice(0, own), slice(own, 2 * own)
+    ht_h, ht_l, ht2_h, ht2_l, ht3_h, ht3_l, dq_t, dk_h, dk_l, dk3_h, dk3_l,
+    grad_q, grad_k, dq_h, dq_l,
+):
+    own = dq_h.shape[0]
     d_query = pair_of(dq_t[...].T)
+    store((dq_h, dq_l), d_query, ...)
     turned = [load(t, ...) for t in ((ht_h, ht_l), (ht2_h, ht2_l), (ht3_h, ht3_l))]
-    d_keys = [load((dk_h, dk_l), first), load((dk_h, dk_l), second), load((dk3_h, dk3_l), ...)]
+    d_keys = [load((dk_h, dk_l), slice(0, own)), load((dk_h, dk_l), slice(own, 2 * own)), load((dk3_h, dk3_l), ...)]
     grad_q[...] = dot3(turned[0], d_query)
     grad_k[...] = sums_of(turned, d_keys)
+
+
+def core_kernel(me, grad_q, grad_k, _back, _keep, keep, send):
+    kept_and_sent(me, (grad_q, grad_k), keep, send)
+
+
+def side_kernel(
+    _, d_back, dq_h, dq_l, dk_h, dk_l, dv_h, dv_l, wq_h, wq_l, wk_h, wk_l, wv_h, wv_l,
+    d_given, d_own, mark,
+):
+    mark[...] = jnp.zeros_like(mark)
+    own = d_own.shape[0]
+    first, near = slice(0, own), slice(own, 2 * own)
     w_q, w_k, w_v = load((wq_h, wq_l), ...), load((wk_h, wk_l), ...), load((wv_h, wv_l), ...)
-    d_own[...] = sums_of([d_query, d_keys[0], load((dv_h, dv_l), first)], [w_q, w_k, w_v], NT)
-    gain_sum[...] = jnp.sum(
-        d_own[...] * xhat[...] + d_near[...] * xhat2[...] + d_far[...] * xhat3[...], axis=0, keepdims=True
-    )
-
-
-def core_kernel(me, grad_q, grad_k, gain_sum, d_near, d_back, _, keep, send, d_given):
-    d_given[...] = d_near[...] + d_back[...]
-    width = grad_q.shape[1]
-    top = lax.broadcasted_iota(jnp.int32, (TAIL, width), 0) == 0
-    for out in (keep, send):
-        out[width:, :] = jnp.where(top, gain_sum[...], 0.0)
-    kept_and_sent(me, (grad_q, grad_k), keep, send)
-
-
-TAIL = 8
+    d_given[...] = d_back[...] + sums_of(
+        [load((dk_h, dk_l), near), load((dv_h, dv_l), near)], [w_k, w_v], NT
+    )
+    d_own[...] = sums_of(
+        [load((dq_h, dq_l), ...), load((dk_h, dk_l), first), load((dv_h, dv_l), first)], [w_q, w_k, w_v], NT
+    )
 
 
 def half_of(me, mask, mine, rows):
@@ -368,7 +363,7 @@
     return pl.ds(pl.multiple_of((index if mine else 1 - index) * rows, 8), rows)
 
 
-def add_kernel(a, b, out):
+def add_kernel(a, b, out, *_):
     out[...] = a[...] + b[...]
 
 
@@ -377,50 +372,31 @@
     *outs, sums = outs
     sums[:count, :] = keep_1[...] + other_1[...]
     sums[count:, :] = keep_2[...] + other_2[...]
-    tail = sums[2 * count :, :]
     at = 0
     for i, mask in enumerate(masks):
-        keep, send = outs[2 * i], outs[2 * i + 1]
-        rows = keep.shape[0] - (TAIL if i == 0 else 0)
-        for out, mine in ((keep, True), (send, False)):
+        rows = outs[2 * i].shape[0]
+        for out, mine in ((outs[2 * i], True), (outs[2 * i + 1], False)):
             index = (me[0] // mask) % 2
             start = at + (index if mine else 1 - index) * rows
-            out[:rows, :] = sums[pl.ds(pl.multiple_of(start, 8), rows), :]
-            if i == 0:
-                out[rows:, :] = tail
+            out[...] = sums[pl.ds(pl.multiple_of(start, 8), rows), :]
         at += 2 * rows
 
 
-def halve_kernel(mask, tail, me, keep, other, next_keep, next_send):
-    rows = next_keep.shape[0] - tail
+def halve_kernel(mask, me, keep, other, *rest):
+    next_keep, next_send = rest[-2:]
+    rows = next_keep.shape[0]
     for out, mine in ((next_keep, True), (next_send, False)):
         at = half_of(me, mask, mine, rows)
-        out[:rows, :] = keep[at, :] + other[at, :]
-        if tail:
-            out[rows:, :] = keep[2 * rows :, :] + other[2 * rows :, :]
-
-
-def join_kernel(*refs):
-    *ins, d_given, sums, d_going = refs
-    at = 0
-    for i in range(3):
-        rows = ins[2 * i].shape[0] - (TAIL if i == 0 else 0)
-        sums[at : at + rows, :] = ins[2 * i][:rows, :] + ins[2 * i + 1][:rows, :]
-        at += rows
-    sums[at:, :] = ins[0][rows_of(ins[0]) :, :] + ins[1][rows_of(ins[0]) :, :]
+        out[...] = keep[at, :] + other[at, :]
+
+
+def first_kernel(a, b, d_given, out, d_going):
+    out[...] = a[...] + b[...]
     d_going[...] = d_given[...]
 
 
-def rows_of(ref):
-    return ref.shape[0] - TAIL
-
-
-def part_kernel(a, b, _mark, _other, *outs):
-    at = 0
-    for out in outs:
-        rows = out.shape[0]
-        out[...] = a[at : at + rows, :] + b[at : at + rows, :]
-        at += rows
+def last_kernel(a, b, *rest):
+    rest[-1][...] = a[...] + b[...]
 
 
 def double_kernel(mask, me, mine, other, *rest):
@@ -430,23 +406,37 @@
     out[half_of(me, mask, False, rows), :] = other[...]
 
 
-def split_kernel(ranges, me, *refs):
-    count = len(refs) - 5
-    ins, outs, sent = refs[:count], refs[count:-1], refs[-1]
+def write_kernel(ranges, me, gain, wv_h, wv_l, wq_h, wq_l, wk_h, wk_l, *refs):
+    mine, other, outs, d_gain, (partial, sent) = refs[:3], refs[3:6], refs[6:10], refs[10], refs[11:]
+    weights = (None, (wv_h, wv_l), (wq_h, wq_l), (wk_h, wk_l))
+    lanes = partial.shape[1]
+    partial[...] = jnp.zeros_like(partial)
     for bit in range(2):
 
         @pl.when(me[0] % 2 == bit)
         def _():
-            copies = []
-            for core in range(2):
-                for part, first, rows, exchange, to in ranges:
-                    source = ins[part + core * (count // 2)].at[pl.ds(first, rows)]
-                    target = outs[2 * exchange + (bit + core) % 2].at[pl.ds(to, rows)]
-                    copies.append(pltpu.make_async_copy(source, target, sent.at[len(copies)]))
+            pieces = [
+                (parts[i].at[pl.ds(first, rows)], 2 * exchange + (bit + core) % 2, to, rows)
+                for core, parts in enumerate((mine, other))
+                for i, first, rows, exchange, to in ranges
+            ]
+            copies = [
+                pltpu.make_async_copy(piece, outs[matrix].at[pl.ds(to, rows)], sent.at[n])
+                for n, (piece, matrix, to, rows) in enumerate(pieces)
+            ]
             for copy in copies:
                 copy.start()
+            for piece, matrix, to, rows in pieces:
+                if matrix:
+                    high, low = weights[matrix]
+                    for lane in range(0, piece.shape[1], lanes):
+                        at = (slice(to, to + rows), slice(lane, lane + lanes))
+                        weight = high[at].astype(F32) + low[at].astype(F32)
+                        partial[to : to + rows, :] += weight * piece[:, lane : lane + lanes]
             for copy in copies:
                 copy.wait()
+
+    d_gain[...] = jnp.sum(partial[...].T, axis=0, keepdims=True) / gain[...]
 
 
 def tokens_kernel(_, tokens, gain, cot, d_own, d_other, out, mark):
@@ -510,46 +500,43 @@
 LAST = 16
 
 
-def summed(me, keep_1, other_1, keep_2, send_2, d_given, token_side, result_of):
+def summed(me, keep_1, other_1, keep_2, send_2, weights, gain, result_of, side_of, tokens_of):
     count, width = keep_1.shape
     total = 2 * count
     unit = 8 * 8
     sizes = [total // unit // 3 * unit] * 2
     sizes.append(total - sum(sizes))
-    tails = (TAIL, 0, 0)
-    halves = [size // 2 for size in sizes]
     parts = call(
         functools.partial(cut_kernel, [order[0] for order in ORDERS]),
         (me, keep_1, other_1, keep_2, swapped(send_2, 1)),
-        [shape(half + tail, width) for half, tail in zip(halves, tails) for _ in range(2)],
-        [shape(total + TAIL, width)],
+        [shape(size // 2, width) for size in sizes for _ in range(2)],
+        [shape(total, width)],
         scalars=1, limit=8,
     )
+    d_given, d_own, mark = side_of(parts[0])
     parts = [[parts[2 * i], swapped(parts[2 * i + 1], ORDERS[i][0])] for i in range(3)]
     for step in (1, 2):
         for i in range(3):
-            rows, mask = sizes[i] >> (step + 1), ORDERS[i][step]
+            half, mask = shape(sizes[i] >> (step + 1), width), ORDERS[i][step]
+            place = (mark,) if step == 1 and i == 0 else ()
             keep, send = call(
-                functools.partial(halve_kernel, mask, tails[i]), (me, *parts[i]), [shape(rows + tails[i], width)] * 2,
-                scalars=1,
+                functools.partial(halve_kernel, mask), (me, *parts[i], *place), [half, half], scalars=1
             )
             parts[i] = [keep, swapped(send, mask)]
-    joined = total // 8
-    sums, d_going = call(
-        join_kernel, (*parts[0], *parts[1], *parts[2], d_given), [shape(joined + TAIL, width), d_given],
-        limit=8,
-    )
-    other = swapped(sums, LAST)
-    result, mark = result_of(sums)
-    d_other = across(d_going)
-    mask = 2 * LAST
-    while mask < devices():
-        (sums,) = call(add_kernel, (sums, other), [sums])
-        other = swapped(sums, mask)
-        mask *= 2
-    *parts, d_gain = call(
-        part_kernel, (sums, other, mark, d_other), [shape(size // 8, width) for size in sizes] + [shape(1, width)],
-    )
+    for i in (0, 2, 1):
+        if i == 0:
+            part, d_going = call(first_kernel, (*parts[i], d_given), [parts[i][0], d_given])
+            d_other = across(d_going)
+            result, mark = result_of(part)
+        else:
+            (part,) = call(add_kernel, parts[i], [parts[i][0]])
+        mask, other = LAST, swapped(part, LAST)
+        while 2 * mask < devices():
+            (part,) = call(add_kernel, (part, other), [part])
+            mask *= 2
+            other = swapped(part, mask)
+        place = (d_other, mark) if i == 1 else ()
+        (parts[i],) = call(last_kernel, (part, other, *place), [part])
     for step in (2, 1, 0):
         for i in range(3):
             mask = ORDERS[i][step]
@@ -559,7 +546,7 @@
                 [shape(2 * parts[i].shape[0], width)], scalars=1,
             )
         if step == 1:
-            d_tokens, mark = call(tokens_kernel, (parts[0], *token_side, d_other), [d_given, MARK])
+            d_tokens, mark = tokens_of(parts[0], d_own, d_other)
     others = [swapped(part, 1) for part in parts]
     ranges, at = [], 0
     for i, size in enumerate(sizes):
@@ -568,16 +555,15 @@
             if start < stop:
                 ranges.append((i, start - at, stop - start, exchange, start - exchange * count))
         at += size
-    outputs = pl.pallas_call(
-        functools.partial(split_kernel, ranges),
-        out_shape=[shape(count, width)] * 4,
-        in_specs=[SMEM] + [VMEM] * 6,
-        out_specs=[pl.BlockSpec(memory_space=pl.ANY)] * 4,
-        scratch_shapes=[pltpu.SemaphoreType.DMA((2 * len(ranges),))],
+    *gradients, d_gain = pl.pallas_call(
+        functools.partial(write_kernel, ranges),
+        out_shape=[shape(count, width)] * 4 + [shape(1, width)],
+        in_specs=[SMEM] + [VMEM] * 13,
+        out_specs=[pl.BlockSpec(memory_space=pl.ANY)] * 4 + [VMEM],
+        scratch_shapes=[pltpu.VMEM((count, 128), F32), pltpu.SemaphoreType.DMA((2 * len(ranges),))],
         compiler_params=pltpu.CompilerParams(vmem_limit_bytes=2**23),
-    )(me, *parts, *others)
-    first, second = outputs[:2], outputs[2:]
-    return first, second, d_gain.reshape(width), d_tokens, result
+    )(me, gain, *weights, *parts, *others)
+    return gradients, d_gain.reshape(width), d_tokens, result
 
 
 def body(tokens, gain, wq, wk, wv, wo, neighbour_list, neighbour_count, cotangent):
@@ -637,13 +623,13 @@
         scalars=3, limit=LIMITS[2], us=1,
     )
     d_back = homeward(d_far)
-    d_near, dq_t, dk_h, dk_l, dv_h, dv_l = call(
+    dq_t, dk_h, dk_l, dv_h, dv_l = call(
         back_kernel,
         (
             q_t, d_mixed_t, kt_h, kt_l, kt2_h, kt2_l, kt3_h, kt3_l, e_h, e_l, d_scores, u_h, u_l, deltas, shares,
-            shares_1, *w_k, *w_v,
+            shares_1,
         ),
-        [whole, whole_t, *pairs(2 * rows, width), *pairs(2 * rows, width)],
+        [whole_t, *pairs(2 * rows, width), *pairs(2 * rows, width)],
         [*pairs(2, 2 * rows, rows)],
         limit=LIMITS[4], us=1,
     )
@@ -655,25 +641,29 @@
         scalars=1, limit=LIMITS[3], us=1,
     )
     other_1 = swapped(send_1, 1)
-    tall = shape(width + TAIL, width)
-    grad_q, grad_k, d_own, gain_sum = call(
+    grad_q, grad_k, dq_h, dq_l = call(
         grad_kernel,
-        (
-            ht_h, ht_l, ht2_h, ht2_l, ht3_h, ht3_l, xhat, xhat2, xhat3, dq_t, dk_h, dk_l, dk3_h, dk3_l,
-            dv_h, dv_l, d_near, d_far, wq_h, wq_l, *w_k, *w_v,
-        ),
-        [shape(width, width), shape(width, width), whole, shape(1, width)],
+        (ht_h, ht_l, ht2_h, ht2_l, ht3_h, ht3_l, dq_t, dk_h, dk_l, dk3_h, dk3_l),
+        [shape(width, width), shape(width, width), *pair],
         limit=LIMITS[5], us=1,
     )
-    keep_2, send_2, d_given = call(
-        core_kernel, (me, grad_q, grad_k, gain_sum, d_near, d_back, keep_1), [tall, tall, whole], scalars=1, limit=8
+    keep_2, send_2 = call(
+        core_kernel, (me, grad_q, grad_k, d_back, keep_1), [shape(width, width)] * 2, scalars=1, limit=8
     )
 
     def result_of(place):
         return call(result_kernel, (place, mixed_t, tokens, wo_h, wo_l), [whole, MARK], limit=LIMITS[3], us=1)
 
-    (grad_o, grad_v), (grad_q, grad_k), d_gain, d_tokens, result = summed(
-        me, keep_1, other_1, keep_2, send_2, d_given, (tokens, gain_row, cotangent, d_own), result_of
+    def side_of(place):
+        inputs = (place, d_back, dq_h, dq_l, dk_h, dk_l, dv_h, dv_l, wq_h, wq_l, *w_k, *w_v)
+        return call(side_kernel, inputs, [whole, whole, MARK], limit=LIMITS[3], us=1)
+
+    def tokens_of(place, d_own, d_other):
+        inputs = (place, tokens, gain_row, cotangent, d_own, d_other)
+        return call(tokens_kernel, inputs, [whole, MARK], limit=8)
+
+    (grad_o, grad_v, grad_q, grad_k), d_gain, d_tokens, result = summed(
+        me, keep_1, other_1, keep_2, send_2, (wv_h, wv_l, wq_h, wq_l, *w_k), gain_row, result_of, side_of, tokens_of
     )
     return (result, d_tokens, d_gain, grad_q, grad_k, grad_v, grad_o)
 

time: 119 us -> 115 us (0.966)
  waiting for transfers between devices: 47.3 us -> 41.5 us
  Pallas kernels: 32.4 us -> 33.8 us
    ppermute x24 -> x26, waiting for transfers between devices: 43.8 us -> 36.7 us  [swapped(): lax.ppermute(value, ('space', 'slab'), [(i, i ^ mask) for i in range(devi...]
    ppermute x24 -> x26, starting transfers between devices: 21.5 us -> 23 us  [swapped(): lax.ppermute(value, ('space', 'slab'), [(i, i ^ mask) for i in range(devi...]
    ppermute x6, waiting for transfers between devices: 3.46 us -> 4.82 us  [along_space(): lax.ppermute(value, 'space', [(i, target(i) % count) for i in range(count)])]
    pallas_call x29 -> x34, Pallas kernels: 30.3 us -> 31 us  [call(): pl.pallas_call(kernel, out_shape=outputs, in_specs=[SMEM] * scalars + [VM...]
  transfers between devices with their start and end apart: 30 -> 32, of which waited for: 21 -> 20; matrix products, arithmetic and copies ran while one was open for 0% -> 0% of each run, Pallas kernels for 19% -> 20%
where the time goes in v4:
time: 115 us
  waiting for transfers between devices  41.5 us (36%)
  Pallas kernels  33.8 us (29%)
  starting transfers between devices  32.6 us (28%)
  local copies, waits for them, and re-layouts  5.98 us (5%)
    ppermute x26, waiting for transfers between devices, swapped(): lax.ppermute(value, ('space', 'slab'), [(i, i ^ mask) for i in range(devi...  36.7 us
    pallas_call x34, Pallas kernels, call(): pl.pallas_call(kernel, out_shape=outputs, in_specs=[SMEM] * scalars + [VM...  31 us
    ppermute x26, starting transfers between devices, swapped(): lax.ppermute(value, ('space', 'slab'), [(i, i ^ mask) for i in range(devi...  23 us
    ppermute x6, starting transfers between devices, along_space(): lax.ppermute(value, 'space', [(i, target(i) % count) for i in range(count)])  9.61 us
    unnamed x18, local copies, waits for them, and re-layouts  4.92 us
    ppermute x6, waiting for transfers between devices, along_space(): lax.ppermute(value, 'space', [(i, target(i) % count) for i in range(count)])  4.82 us
    pallas_call x1, Pallas kernels, summed(): pl.pallas_call(functools.partial(write_kernel, ranges), out_shape=[shape(...  2.81 us
  transfers between devices with their start and end apart: 32, of which 20 were waited for; matrix products, arithmetic and copies ran while one was open for 0% of the time, Pallas kernels for 20%

profile of v4, /device:TPU:0, one launch (start us, length us, event | category | flops | bytes accessed | tf_op | source)
XLA Modules:
  0.0 115.0 jit_solution(4437915495129031867)
XLA Ops:
  1.7 3.0 %collective-permute-start = (f32[128,512]{1,0:T(8,128)S(1)}, f32[128,512]{1,0:T(8,128)S(1)}, u32[]{:S(2)}, u32[]{:S(2)}) collective-permute-start(f32[128,512]{1,0:T(8,128)S(1)} %get-tuple-element.200), channel_id=1, source_target_pairs={{0,4},{4,0},{8,12},{12,8},{16,20},{20,16},{24,28},{28,24},{1,5},{5... | collective-permute-start | bytes 786440 | tf_op jit(solution)/shard_map/ppermute | solution.py:476
  11.8 2.1 %collective-permute-start.1 = (f32[128,512]{1,0:T(8,128)S(1)}, f32[128,512]{1,0:T(8,128)S(1)}, u32[]{:S(2)}, u32[]{:S(2)}) collective-permute-start(f32[128,512]{1,0:T(8,128)S(1)} %collective-permute-done._.patch_0), channel_id=1, source_target_pairs={{0,8},{4,28},{8,16},{12,4},{16,24},{20,12},{24,0},{28,20},{1,9},{5... | collective-permute-start | bytes 786440 | tf_op jit(solution)/shard_map/ppermute | solution.py:476
  14.0 2.9 %shard_map.145 = (f32[256,512]{1,0:T(8,128)}, bf16[512,256]{1,0:T(8,128)(2,1)S(1)}, bf16[512,256]{1,0:T(8,128)(2,1)S(1)}, f32[512,256]{1,0:T(8,128)S(1)}, bf16[2...) custom-call(f32[128,512]{1,0:T(8,128)S(1)} %collective-permute-done., ...), custom_call_target="tpu_custom_call" | custom-call | flops 1000000000 | tf_op jit(solution)/shard_map/pallas_call | solution.py:460
  16.9 1.6 %collective-permute-start.3 = (f32[128,512]{1,0:T(8,128)S(1)}, f32[128,512]{1,0:T(8,128)S(1)}, u32[]{:S(2)}, u32[]{:S(2)}) collective-permute-start(f32[128,512]{1,0:T(8,128)S(1)} %collective-permute-done.2.patch_1), channel_id=1, source_target_pairs={{0,8},{4,28},{8,16},{12,4},{16,24},{20,12},{24,0},{28,20},{1,9},{5... | collective-permute-start | bytes 786440 | tf_op jit(solution)/shard_map/ppermute | solution.py:476
  18.5 1.6 %shard_map.146 = (f32[256,512]{1,0:T(8,128)}, bf16[512,256]{1,0:T(8,128)(2,1)S(1)}, bf16[512,256]{1,0:T(8,128)(2,1)S(1)}, bf16[512,256]{1,0:T(8,128)(2,1)S(1)}, ...) custom-call(f32[128,512]{1,0:T(8,128)S(1)} %collective-permute-done., ...), custom_call_target="tpu_custom_call" | custom-call | flops 1000000000 | tf_op jit(solution)/shard_map/pallas_call | solution.py:460
  20.4 4.7 %shard_map.147 = (bf16[8,512,256]{2,1,0:T(8,128)(2,1)S(1)}, bf16[8,512,256]{2,1,0:T(8,128)(2,1)S(1)}, f32[8,512,256]{2,1,0:T(8,128)S(1)}, f32[512,256]{1,0:T(8,1...) custom-call(s32[1]{0:T(128)} %bitcast.1._parity.parity, s32[2,3]{1,0:T(2,128)S(1)} %copy-done.7, ...), custom_call_target="tpu_custom_call" | custom-call | flops 1000000000 | tf_op jit(solution)/shard_map/pallas_call | solution.py:460
  26.0 7.5 %shard_map.148 = (f32[256,512]{1,0:T(8,128)}, bf16[512,256]{1,0:T(8,128)(2,1)S(1)}, bf16[512,256]{1,0:T(8,128)(2,1)S(1)}, bf16[512,256]{1,0:T(8,128)(2,1)S(1)}, ...) custom-call(s32[1]{0:T(128)} %bitcast.1._parity.parity, ...), custom_call_target="tpu_custom_call" | custom-call | flops 1000000000 | tf_op jit(solution)/shard_map/pallas_call | solution.py:460
  33.5 2.0 %collective-permute-start.5 = (f32[256,512]{1,0:T(8,128)S(1)}, f32[256,512]{1,0:T(8,128)S(1)}, u32[]{:S(2)}, u32[]{:S(2)}) collective-permute-start(f32[256,512]{1,0:T(8,128)S(1)} %get-tuple-element.162), channel_id=1, source_target_pairs={{0,24},{4,12},{8,0},{12,20},{16,8},{20,28},{24,16},{28,4},{1,25},{... | collective-permute-start | bytes 1572872 | tf_op jit(solution)/shard_map/ppermute | solution.py:476
  35.5 3.9 %shard_map.149 = (f32[512,256]{1,0:T(8,128)S(1)}, bf16[512,512]{1,0:T(8,128)(2,1)S(1)}, bf16[512,512]{1,0:T(8,128)(2,1)S(1)}, bf16[512,512]{1,0:T(8,128)(2,1)S(1)}, bf16[512,512]{1,0:T(8,128)(2,1)S(1)}) custom-call(f32[512,256]{1,0:T(8,128)S(1)} %get-tuple-element.113.q_t, f32[512,256]{1,0:T(8,128)S(1)} %get-tuple-element.115.d_mixed_t, ...), custom_call_target="tpu_custom_call" | custom-call | flops 1000000000 | tf_op jit(solution)/shard_map/pallas_call | solution.py:460
  39.4 1.9 %shard_map.150 = (f32[512,512]{1,0:T(8,128)S(1)}, f32[512,512]{1,0:T(8,128)S(1)}) custom-call(s32[1]{0:T(128)} %bitcast._me.me, f32[512,256]{1,0:T(8,128)S(1)} %get-tuple-element.128.mixed_t, bf16[512,256]{1,0:T(8,128)(2,1)S(1)} %get-tuple-element.129.ht_h, bf16[512,256]{1,0:T(8,128)(2,1)S(1)} %get-tuple-element.130.ht_l, ...), custom_call_target="tpu_custom_call" | custom-call | flops 1000000000 | tf_op jit(solution)/shard_map/pallas_call | solution.py:460
  41.4 2.0 %shard_map.151 = (f32[512,512]{1,0:T(8,128)S(1)}, f32[512,512]{1,0:T(8,128)S(1)}, bf16[256,512]{1,0:T(8,128)(2,1)S(1)}, bf16[256,512]{1,0:T(8,128)(2,1)S(1)}) custom-call(bf16[512,256]{1,0:T(8,128)(2,1)S(1)} %get-tuple-element.129.ht_h, bf16[512,256]{1,0:T(8,128)(2,1)S(1)} %get-tuple-element.130.ht_l, bf16[512,256]{1,0:T(8,128)(2,1)S(1)} %get-tuple-element.131.ht2_h, ...), custom_call_target="tpu_custom_call" | custom-call | flops 1000000000 | tf_op jit(solution)/shard_map/pallas_call | solution.py:460
  43.4 2.0 %collective-permute-done.5._back.d_back = f32[256,512]{1,0:T(8,128)S(1)} collective-permute-done((f32[256,512]{1,0:T(8,128)S(1)}, f32[256,512]{1,0:T(8,128)S(1)}, u32[]{:S(2)}, u32[]{:S(2)}) %collective-permute-start.5) | collective-permute-done | bytes 524320 | tf_op jit(solution)/shard_map/ppermute | solution.py:476
  45.7 2.6 %collective-permute-done.6.other_2 = f32[512,512]{1,0:T(8,128)S(1)} collective-permute-done((f32[512,512]{1,0:T(8,128)S(1)}, f32[512,512]{1,0:T(8,128)S(1)}, u32[]{:S(2)}, u32[]{:S(2)}) %collective-permute-start.6) | collective-permute-done | bytes 1048608 | tf_op jit(solution)/shard_map/ppermute | solution.py:496
  48.7 4.8 %collective-permute-start.7 = (f32[160,512]{1,0:T(8,128)S(1)}, f32[160,512]{1,0:T(8,128)S(1)}, u32[]{:S(2)}, u32[]{:S(2)}) collective-permute-start(f32[160,512]{1,0:T(8,128)S(1)} %get-tuple-element.166), channel_id=1, source_target_pairs={{0,4},{1,5},{2,6},{3,7},{4,0},{5,1},{6,2},{7,3},{8,12},{9,13},{10,... | collective-permute-start | bytes 983048 | tf_op jit(solution)/shard_map/ppermute | solution.py:496
  55.0 2.2 %shard_map.154 = (f32[256,512]{1,0:T(8,128)S(1)}, f32[256,512]{1,0:T(8,128)S(1)}, f32[8,128]{1,0:T(8,128)S(1)}) custom-call(f32[160,512]{1,0:T(8,128)S(1)} %get-tuple-element.165._.keep, f32[256,512]{1,0:T(8,128)S(1)} %collective-permute-done.5._back.d_back, bf16[256,512]{1,0:T(8,128)(2,1)S(1)} %get-tuple-element.167.dq_h, ...), custom_call_target="tpu_custom_call" | custom-call | flops 1000000000 | tf_op jit(solution)/shard_map/pallas_call | solution.py:460
  57.2 4.3 %collective-permute-done.7.other = f32[160,512]{1,0:T(8,128)S(1)} collective-permute-done((f32[160,512]{1,0:T(8,128)S(1)}, f32[160,512]{1,0:T(8,128)S(1)}, u32[]{:S(2)}, u32[]{:S(2)}) %collective-permute-start.7) | collective-permute-done | bytes 327712 | tf_op jit(solution)/shard_map/ppermute | solution.py:496
  61.5 1.6 %collective-permute-start.8 = (f32[80,512]{1,0:T(8,128)S(1)}, f32[80,512]{1,0:T(8,128)S(1)}, u32[]{:S(2)}, u32[]{:S(2)}) collective-permute-start(f32[80,512]{1,0:T(8,128)S(1)} %get-tuple-element.171), channel_id=1, source_target_pairs={{0,2},{1,3},{2,0},{3,1},{4,6},{5,7},{6,4},{7,5},{8,10},{9,11},{10,... | collective-permute-start | bytes 491528 | tf_op jit(solution)/shard_map/ppermute | solution.py:496
  64.9 2.4 %collective-permute-done.8.other = f32[80,512]{1,0:T(8,128)S(1)} collective-permute-done((f32[80,512]{1,0:T(8,128)S(1)}, f32[80,512]{1,0:T(8,128)S(1)}, u32[]{:S(2)}, u32[]{:S(2)}) %collective-permute-start.8) | collective-permute-done | bytes 163872 | tf_op jit(solution)/shard_map/ppermute | solution.py:496
  68.3 2.0 %collective-permute-done.23.other = f32[96,512]{1,0:T(8,128)S(1)} collective-permute-done((f32[96,512]{1,0:T(8,128)S(1)}, f32[96,512]{1,0:T(8,128)S(1)}, u32[]{:S(2)}, u32[]{:S(2)}) %collective-permute-start.23) | collective-permute-done | bytes 196640 | tf_op jit(solution)/shard_map/ppermute | solution.py:496
  70.3 1.6 %collective-permute-start.24 = (f32[48,512]{1,0:T(8,128)S(1)}, f32[48,512]{1,0:T(8,128)S(1)}, u32[]{:S(2)}, u32[]{:S(2)}) collective-permute-start(f32[48,512]{1,0:T(8,128)S(1)} %get-tuple-element.192), channel_id=1, source_target_pairs={{0,2},{1,3},{2,0},{3,1},{4,6},{5,7},{6,4},{7,5},{8,10},{9,11},{10,... | collective-permute-start | bytes 294920 | tf_op jit(solution)/shard_map/ppermute | solution.py:496
  73.4 1.6 %collective-permute-done.24.b = f32[48,512]{1,0:T(8,128)S(1)} collective-permute-done((f32[48,512]{1,0:T(8,128)S(1)}, f32[48,512]{1,0:T(8,128)S(1)}, u32[]{:S(2)}, u32[]{:S(2)}) %collective-permute-start.24) | collective-permute-done | bytes 98336 | tf_op jit(solution)/shard_map/ppermute | solution.py:496
  75.0 3.3 %collective-permute-done.16.other = f32[80,512]{1,0:T(8,128)S(1)} collective-permute-done((f32[80,512]{1,0:T(8,128)S(1)}, f32[80,512]{1,0:T(8,128)S(1)}, u32[]{:S(2)}, u32[]{:S(2)}) %collective-permute-start.16) | collective-permute-done | bytes 163872 | tf_op jit(solution)/shard_map/ppermute | solution.py:496
  80.5 1.8 %collective-permute-done.25.b = f32[48,512]{1,0:T(8,128)S(1)} collective-permute-done((f32[48,512]{1,0:T(8,128)S(1)}, f32[48,512]{1,0:T(8,128)S(1)}, u32[]{:S(2)}, u32[]{:S(2)}) %collective-permute-start.25) | collective-permute-done | bytes 98336 | tf_op jit(solution)/shard_map/ppermute | solution.py:496
  83.3 2.8 %collective-permute-done.17.b = f32[40,512]{1,0:T(8,128)S(1)} collective-permute-done((f32[40,512]{1,0:T(8,128)S(1)}, f32[40,512]{1,0:T(8,128)S(1)}, u32[]{:S(2)}, u32[]{:S(2)}) %collective-permute-start.17) | collective-permute-done | bytes 81952 | tf_op jit(solution)/shard_map/ppermute | solution.py:496
  88.5 3.9 %collective-permute-done.18.b = f32[40,512]{1,0:T(8,128)S(1)} collective-permute-done((f32[40,512]{1,0:T(8,128)S(1)}, f32[40,512]{1,0:T(8,128)S(1)}, u32[]{:S(2)}, u32[]{:S(2)}) %collective-permute-start.18) | collective-permute-done | bytes 81952 | tf_op jit(solution)/shard_map/ppermute | solution.py:496
  94.5 2.7 %collective-permute-done.19.other = f32[40,512]{1,0:T(8,128)S(1)} collective-permute-done((f32[40,512]{1,0:T(8,128)S(1)}, f32[40,512]{1,0:T(8,128)S(1)}, u32[]{:S(2)}, u32[]{:S(2)}) %collective-permute-start.19) | collective-permute-done | bytes 81952 | tf_op jit(solution)/shard_map/ppermute | solution.py:496
  97.7 1.8 %collective-permute-start.28 = (f32[192,512]{1,0:T(8,128)S(1)}, f32[192,512]{1,0:T(8,128)S(1)}, u32[]{:S(2)}, u32[]{:S(2)}) collective-permute-start(f32[192,512]{1,0:T(8,128)S(1)} %shard_map.176.mine), channel_id=1, source_target_pairs={{0,8},{1,9},{2,10},{3,11},{4,12},{5,13},{6,14},{7,15},{8,0},{9,1},... | collective-permute-start | bytes 1179656 | tf_op jit(solution)/shard_map/ppermute | solution.py:496
  100.3 2.4 %collective-permute-done.20.other = f32[80,512]{1,0:T(8,128)S(1)} collective-permute-done((f32[80,512]{1,0:T(8,128)S(1)}, f32[80,512]{1,0:T(8,128)S(1)}, u32[]{:S(2)}, u32[]{:S(2)}) %collective-permute-start.20) | collective-permute-done | bytes 163872 | tf_op jit(solution)/shard_map/ppermute | solution.py:496
  102.7 1.6 %collective-permute-start.21 = (f32[160,512]{1,0:T(8,128)S(1)}, f32[160,512]{1,0:T(8,128)S(1)}, u32[]{:S(2)}, u32[]{:S(2)}) collective-permute-start(f32[160,512]{1,0:T(8,128)S(1)} %shard_map.169.mine), channel_id=1, source_target_pairs={{0,2},{1,3},{2,0},{3,1},{4,6},{5,7},{6,4},{7,5},{8,10},{9,11},{10,... | collective-permute-start | bytes 983048 | tf_op jit(solution)/shard_map/ppermute | solution.py:496
  107.6 2.2 %collective-permute-done.21.other = f32[160,512]{1,0:T(8,128)S(1)} collective-permute-done((f32[160,512]{1,0:T(8,128)S(1)}, f32[160,512]{1,0:T(8,128)S(1)}, u32[]{:S(2)}, u32[]{:S(2)}) %collective-permute-start.21) | collective-permute-done | bytes 327712 | tf_op jit(solution)/shard_map/ppermute | solution.py:496
  110.2 1.8 %collective-permute-done.30.refs_4_ = f32[320,512]{1,0:T(8,128)S(1)} collective-permute-done((f32[320,512]{1,0:T(8,128)S(1)}, f32[320,512]{1,0:T(8,128)S(1)}, u32[]{:S(2)}, u32[]{:S(2)}) %collective-permute-start.30) | collective-permute-done | bytes 655392 | tf_op jit(solution)/shard_map/ppermute | solution.py:496
  112.1 2.8 %shard_map.178 = (f32[512,512]{1,0:T(8,128)}, f32[512,512]{1,0:T(8,128)}, f32[512,512]{1,0:T(8,128)}, f32[512,512]{1,0:T(8,128)}, f32[1,512]{1,0:T(1,128)}) custom-call(s32[1]{0:T(128)} %bitcast._me.me, f32[1,512]{1,0:T(1,128)S(1)} %bitcast.9, bf16[512,512]{1,0:T(8,128)(2,1)S(1)} %get-tuple-element.107.wv_h, bf16[512,512]{1,0:T(8,128)(2,1)S(1)} %get-tuple-element.108.wv_l, ...), custom_call_target="tpu_custom_call" | custom-call | tf_op jit(solution)/shard_map/pallas_call | solution.py:558
  (86 shorter events, 28.6 us)
Async XLA Ops:
  1.7 10.1 %collective-permute-start = (f32[128,512]{1,0:T(8,128)S(1)}, f32[128,512]{1,0:T(8,128)S(1)}, u32[]{:S(2)}, u32[]{:S(2)}) collective-permute-start(f32[128,512]{1,0:T(8,128)S(1)} %get-tuple-element.200), channel_id=1, source_target_pairs={{0,4},{4,0},{8,12},{12,8},{16,20},{20,16},{24,28},{28,24},{1,5},{5... | collective-permute-start | bytes 786440 | tf_op jit(solution)/shard_map/ppermute | solution.py:476
  4.7 12.2 %collective-permute-start.2 = (f32[128,512]{1,0:T(8,128)S(1)}, f32[128,512]{1,0:T(8,128)S(1)}, u32[]{:S(2)}, u32[]{:S(2)}) collective-permute-start(f32[128,512]{1,0:T(8,128)S(1)} %get-tuple-element.199), channel_id=1, source_target_pairs={{0,4},{4,0},{8,12},{12,8},{16,20},{20,16},{24,28},{28,24},{1,5},{5... | collective-permute-start | bytes 786440 | tf_op jit(solution)/shard_map/ppermute | solution.py:476
  11.8 8.5 %collective-permute-start.1 = (f32[128,512]{1,0:T(8,128)S(1)}, f32[128,512]{1,0:T(8,128)S(1)}, u32[]{:S(2)}, u32[]{:S(2)}) collective-permute-start(f32[128,512]{1,0:T(8,128)S(1)} %collective-permute-done._.patch_0), channel_id=1, source_target_pairs={{0,8},{4,28},{8,16},{12,4},{16,24},{20,12},{24,0},{28,20},{1,9},{5... | collective-permute-start | bytes 786440 | tf_op jit(solution)/shard_map/ppermute | solution.py:476
  16.9 9.1 %collective-permute-start.3 = (f32[128,512]{1,0:T(8,128)S(1)}, f32[128,512]{1,0:T(8,128)S(1)}, u32[]{:S(2)}, u32[]{:S(2)}) collective-permute-start(f32[128,512]{1,0:T(8,128)S(1)} %collective-permute-done.2.patch_1), channel_id=1, source_target_pairs={{0,8},{4,28},{8,16},{12,4},{16,24},{20,12},{24,0},{28,20},{1,9},{5... | collective-permute-start | bytes 786440 | tf_op jit(solution)/shard_map/ppermute | solution.py:476
  33.5 12.0 %collective-permute-start.5 = (f32[256,512]{1,0:T(8,128)S(1)}, f32[256,512]{1,0:T(8,128)S(1)}, u32[]{:S(2)}, u32[]{:S(2)}) collective-permute-start(f32[256,512]{1,0:T(8,128)S(1)} %get-tuple-element.162), channel_id=1, source_target_pairs={{0,24},{4,12},{8,0},{12,20},{16,8},{20,28},{24,16},{28,4},{1,25},{... | collective-permute-start | bytes 1572872 | tf_op jit(solution)/shard_map/ppermute | solution.py:476
  41.3 4.3 %collective-permute-start.4 = (f32[512,512]{1,0:T(8,128)S(1)}, f32[512,512]{1,0:T(8,128)S(1)}, u32[]{:S(2)}, u32[]{:S(2)}) collective-permute-start(f32[512,512]{1,0:T(8,128)S(1)} %get-tuple-element.154), channel_id=1, source_target_pairs={{0,1},{1,0},{2,3},{3,2},{4,5},{5,4},{6,7},{7,6},{8,9},{9,8},{10,11... | collective-permute-start | bytes 3145736 | tf_op jit(solution)/shard_map/ppermute | solution.py:496
  45.6 2.7 %collective-permute-start.6 = (f32[512,512]{1,0:T(8,128)S(1)}, f32[512,512]{1,0:T(8,128)S(1)}, u32[]{:S(2)}, u32[]{:S(2)}) collective-permute-start(f32[512,512]{1,0:T(8,128)S(1)} %get-tuple-element.164), channel_id=1, source_target_pairs={{0,1},{1,0},{2,3},{3,2},{4,5},{5,4},{6,7},{7,6},{8,9},{9,8},{10,11... | collective-permute-start | bytes 3145736 | tf_op jit(solution)/shard_map/ppermute | solution.py:496
  48.7 12.8 %collective-permute-start.7 = (f32[160,512]{1,0:T(8,128)S(1)}, f32[160,512]{1,0:T(8,128)S(1)}, u32[]{:S(2)}, u32[]{:S(2)}) collective-permute-start(f32[160,512]{1,0:T(8,128)S(1)} %get-tuple-element.166), channel_id=1, source_target_pairs={{0,4},{1,5},{2,6},{3,7},{4,0},{5,1},{6,2},{7,3},{8,12},{9,13},{10,... | collective-permute-start | bytes 983048 | tf_op jit(solution)/shard_map/ppermute | solution.py:496
  53.5 10.9 %collective-permute-start.22 = (f32[192,512]{1,0:T(8,128)S(1)}, f32[192,512]{1,0:T(8,128)S(1)}, u32[]{:S(2)}, u32[]{:S(2)}) collective-permute-start(f32[192,512]{1,0:T(8,128)S(1)} %get-tuple-element.188), channel_id=1, source_target_pairs={{0,8},{1,9},{2,10},{3,11},{4,12},{5,13},{6,14},{7,15},{8,0},{9,1},... | collective-permute-start | bytes 1179656 | tf_op jit(solution)/shard_map/ppermute | solution.py:496
  53.5 18.4 %collective-permute-start.15 = (f32[160,512]{1,0:T(8,128)S(1)}, f32[160,512]{1,0:T(8,128)S(1)}, u32[]{:S(2)}, u32[]{:S(2)}) collective-permute-start(f32[160,512]{1,0:T(8,128)S(1)} %get-tuple-element.181), channel_id=1, source_target_pairs={{0,2},{1,3},{2,0},{3,1},{4,6},{5,7},{6,4},{7,5},{8,10},{9,11},{10,... | collective-permute-start | bytes 983048 | tf_op jit(solution)/shard_map/ppermute | solution.py:496
  61.5 5.8 %collective-permute-start.8 = (f32[80,512]{1,0:T(8,128)S(1)}, f32[80,512]{1,0:T(8,128)S(1)}, u32[]{:S(2)}, u32[]{:S(2)}) collective-permute-start(f32[80,512]{1,0:T(8,128)S(1)} %get-tuple-element.171), channel_id=1, source_target_pairs={{0,2},{1,3},{2,0},{3,1},{4,6},{5,7},{6,4},{7,5},{8,10},{9,11},{10,... | collective-permute-start | bytes 491528 | tf_op jit(solution)/shard_map/ppermute | solution.py:496
  64.4 5.9 %collective-permute-start.23 = (f32[96,512]{1,0:T(8,128)S(1)}, f32[96,512]{1,0:T(8,128)S(1)}, u32[]{:S(2)}, u32[]{:S(2)}) collective-permute-start(f32[96,512]{1,0:T(8,128)S(1)} %get-tuple-element.190), channel_id=1, source_target_pairs={{0,4},{1,5},{2,6},{3,7},{4,0},{5,1},{6,2},{7,3},{8,12},{9,13},{10,... | collective-permute-start | bytes 589832 | tf_op jit(solution)/shard_map/ppermute | solution.py:496
  67.3 5.2 %collective-permute-start.9 = (f32[40,512]{1,0:T(8,128)S(1)}, f32[40,512]{1,0:T(8,128)S(1)}, u32[]{:S(2)}, u32[]{:S(2)}) collective-permute-start(f32[40,512]{1,0:T(8,128)S(1)} %get-tuple-element.173), channel_id=1, source_target_pairs={{0,8},{1,9},{2,10},{3,11},{4,12},{5,13},{6,14},{7,15},{8,0},{9,1},... | collective-permute-start | bytes 245768 | tf_op jit(solution)/shard_map/ppermute | solution.py:496
  70.3 4.7 %collective-permute-start.24 = (f32[48,512]{1,0:T(8,128)S(1)}, f32[48,512]{1,0:T(8,128)S(1)}, u32[]{:S(2)}, u32[]{:S(2)}) collective-permute-start(f32[48,512]{1,0:T(8,128)S(1)} %get-tuple-element.192), channel_id=1, source_target_pairs={{0,2},{1,3},{2,0},{3,1},{4,6},{5,7},{6,4},{7,5},{8,10},{9,11},{10,... | collective-permute-start | bytes 294920 | tf_op jit(solution)/shard_map/ppermute | solution.py:496
  71.9 6.4 %collective-permute-start.16 = (f32[80,512]{1,0:T(8,128)S(1)}, f32[80,512]{1,0:T(8,128)S(1)}, u32[]{:S(2)}, u32[]{:S(2)}) collective-permute-start(f32[80,512]{1,0:T(8,128)S(1)} %get-tuple-element.183), channel_id=1, source_target_pairs={{0,8},{1,9},{2,10},{3,11},{4,12},{5,13},{6,14},{7,15},{8,0},{9,1},... | collective-permute-start | bytes 491528 | tf_op jit(solution)/shard_map/ppermute | solution.py:496
  72.6 19.8 %collective-permute-start.13 = (f32[256,512]{1,0:T(8,128)S(1)}, f32[256,512]{1,0:T(8,128)S(1)}, u32[]{:S(2)}, u32[]{:S(2)}) collective-permute-start(f32[256,512]{1,0:T(8,128)S(1)} %get-tuple-element.178), channel_id=1, source_target_pairs={{0,4},{4,0},{8,12},{12,8},{16,20},{20,16},{24,28},{28,24},{1,5},{5... | collective-permute-start | bytes 1572872 | tf_op jit(solution)/shard_map/ppermute | solution.py:476
  75.0 7.4 %collective-permute-start.25 = (f32[48,512]{1,0:T(8,128)S(1)}, f32[48,512]{1,0:T(8,128)S(1)}, u32[]{:S(2)}, u32[]{:S(2)}) collective-permute-start(f32[48,512]{1,0:T(8,128)S(1)} %shard_map.173.a), channel_id=1, source_target_pairs={{0,16},{1,17},{2,18},{3,19},{4,20},{5,21},{6,22},{7,23},{8,24},{9,... | collective-permute-start | bytes 294920 | tf_op jit(solution)/shard_map/ppermute | solution.py:496
  78.3 7.7 %collective-permute-start.17 = (f32[40,512]{1,0:T(8,128)S(1)}, f32[40,512]{1,0:T(8,128)S(1)}, u32[]{:S(2)}, u32[]{:S(2)}) collective-permute-start(f32[40,512]{1,0:T(8,128)S(1)} %get-tuple-element.185), channel_id=1, source_target_pairs={{0,4},{1,5},{2,6},{3,7},{4,0},{5,1},{6,2},{7,3},{8,12},{9,13},{10,... | collective-permute-start | bytes 245768 | tf_op jit(solution)/shard_map/ppermute | solution.py:496
  79.1 7.6 %collective-permute-start.10 = (f32[40,512]{1,0:T(8,128)S(1)}, f32[40,512]{1,0:T(8,128)S(1)}, u32[]{:S(2)}, u32[]{:S(2)}) collective-permute-start(f32[40,512]{1,0:T(8,128)S(1)} %get-tuple-element.175._.a), channel_id=1, source_target_pairs={{0,16},{1,17},{2,18},{3,19},{4,20},{5,21},{6,22},{7,23},{8,24},{9,... | collective-permute-start | bytes 245768 | tf_op jit(solution)/shard_map/ppermute | solution.py:496
  82.4 5.3 %collective-permute-start.26 = (f32[48,512]{1,0:T(8,128)S(1)}, f32[48,512]{1,0:T(8,128)S(1)}, u32[]{:S(2)}, u32[]{:S(2)}) collective-permute-start(f32[48,512]{1,0:T(8,128)S(1)} %shard_map.174.mine), channel_id=1, source_target_pairs={{0,2},{1,3},{2,0},{3,1},{4,6},{5,7},{6,4},{7,5},{8,10},{9,11},{10,... | collective-permute-start | bytes 294920 | tf_op jit(solution)/shard_map/ppermute | solution.py:496
  86.1 6.3 %collective-permute-start.18 = (f32[40,512]{1,0:T(8,128)S(1)}, f32[40,512]{1,0:T(8,128)S(1)}, u32[]{:S(2)}, u32[]{:S(2)}) collective-permute-start(f32[40,512]{1,0:T(8,128)S(1)} %shard_map.166.a), channel_id=1, source_target_pairs={{0,16},{1,17},{2,18},{3,19},{4,20},{5,21},{6,22},{7,23},{8,24},{9,... | collective-permute-start | bytes 245768 | tf_op jit(solution)/shard_map/ppermute | solution.py:496
  86.7 6.8 %collective-permute-start.11 = (f32[40,512]{1,0:T(8,128)S(1)}, f32[40,512]{1,0:T(8,128)S(1)}, u32[]{:S(2)}, u32[]{:S(2)}) collective-permute-start(f32[40,512]{1,0:T(8,128)S(1)} %shard_map.159.mine), channel_id=1, source_target_pairs={{0,8},{1,9},{2,10},{3,11},{4,12},{5,13},{6,14},{7,15},{8,0},{9,1},... | collective-permute-start | bytes 245768 | tf_op jit(solution)/shard_map/ppermute | solution.py:496
  87.7 9.9 %collective-permute-start.27 = (f32[96,512]{1,0:T(8,128)S(1)}, f32[96,512]{1,0:T(8,128)S(1)}, u32[]{:S(2)}, u32[]{:S(2)}) collective-permute-start(f32[96,512]{1,0:T(8,128)S(1)} %shard_map.175.mine), channel_id=1, source_target_pairs={{0,4},{1,5},{2,6},{3,7},{4,0},{5,1},{6,2},{7,3},{8,12},{9,13},{10,... | collective-permute-start | bytes 589832 | tf_op jit(solution)/shard_map/ppermute | solution.py:496
  92.4 4.8 %collective-permute-start.19 = (f32[40,512]{1,0:T(8,128)S(1)}, f32[40,512]{1,0:T(8,128)S(1)}, u32[]{:S(2)}, u32[]{:S(2)}) collective-permute-start(f32[40,512]{1,0:T(8,128)S(1)} %shard_map.167.mine), channel_id=1, source_target_pairs={{0,4},{1,5},{2,6},{3,7},{4,0},{5,1},{6,2},{7,3},{8,12},{9,13},{10,... | collective-permute-start | bytes 245768 | tf_op jit(solution)/shard_map/ppermute | solution.py:496
  93.5 5.9 %collective-permute-start.12 = (f32[80,512]{1,0:T(8,128)S(1)}, f32[80,512]{1,0:T(8,128)S(1)}, u32[]{:S(2)}, u32[]{:S(2)}) collective-permute-start(f32[80,512]{1,0:T(8,128)S(1)} %shard_map.160.mine), channel_id=1, source_target_pairs={{0,2},{1,3},{2,0},{3,1},{4,6},{5,7},{6,4},{7,5},{8,10},{9,11},{10,... | collective-permute-start | bytes 491528 | tf_op jit(solution)/shard_map/ppermute | solution.py:496
  97.2 5.4 %collective-permute-start.20 = (f32[80,512]{1,0:T(8,128)S(1)}, f32[80,512]{1,0:T(8,128)S(1)}, u32[]{:S(2)}, u32[]{:S(2)}) collective-permute-start(f32[80,512]{1,0:T(8,128)S(1)} %shard_map.168.mine), channel_id=1, source_target_pairs={{0,8},{1,9},{2,10},{3,11},{4,12},{5,13},{6,14},{7,15},{8,0},{9,1},... | collective-permute-start | bytes 491528 | tf_op jit(solution)/shard_map/ppermute | solution.py:496
  97.7 9.2 %collective-permute-start.28 = (f32[192,512]{1,0:T(8,128)S(1)}, f32[192,512]{1,0:T(8,128)S(1)}, u32[]{:S(2)}, u32[]{:S(2)}) collective-permute-start(f32[192,512]{1,0:T(8,128)S(1)} %shard_map.176.mine), channel_id=1, source_target_pairs={{0,8},{1,9},{2,10},{3,11},{4,12},{5,13},{6,14},{7,15},{8,0},{9,1},... | collective-permute-start | bytes 1179656 | tf_op jit(solution)/shard_map/ppermute | solution.py:496
  99.5 7.5 %collective-permute-start.14 = (f32[160,512]{1,0:T(8,128)S(1)}, f32[160,512]{1,0:T(8,128)S(1)}, u32[]{:S(2)}, u32[]{:S(2)}) collective-permute-start(f32[160,512]{1,0:T(8,128)S(1)} %shard_map.161._.mine), channel_id=1, source_target_pairs={{0,4},{1,5},{2,6},{3,7},{4,0},{5,1},{6,2},{7,3},{8,12},{9,13},{10,... | collective-permute-start | bytes 983048 | tf_op jit(solution)/shard_map/ppermute | solution.py:496
  102.7 7.1 %collective-permute-start.21 = (f32[160,512]{1,0:T(8,128)S(1)}, f32[160,512]{1,0:T(8,128)S(1)}, u32[]{:S(2)}, u32[]{:S(2)}) collective-permute-start(f32[160,512]{1,0:T(8,128)S(1)} %shard_map.169.mine), channel_id=1, source_target_pairs={{0,2},{1,3},{2,0},{3,1},{4,6},{5,7},{6,4},{7,5},{8,10},{9,11},{10,... | collective-permute-start | bytes 983048 | tf_op jit(solution)/shard_map/ppermute | solution.py:496
  106.9 3.3 %collective-permute-start.31 = (f32[384,512]{1,0:T(8,128)S(1)}, f32[384,512]{1,0:T(8,128)S(1)}, u32[]{:S(2)}, u32[]{:S(2)}) collective-permute-start(f32[384,512]{1,0:T(8,128)S(1)} %shard_map.177.refs_2_), channel_id=1, source_target_pairs={{0,1},{1,0},{2,3},{3,2},{4,5},{5,4},{6,7},{7,6},{8,9},{9,8},{10,11... | collective-permute-start | bytes 2359304 | tf_op jit(solution)/shard_map/ppermute | solution.py:496
  107.1 3.1 %collective-permute-start.29 = (f32[320,512]{1,0:T(8,128)S(1)}, f32[320,512]{1,0:T(8,128)S(1)}, u32[]{:S(2)}, u32[]{:S(2)}) collective-permute-start(f32[320,512]{1,0:T(8,128)S(1)} %shard_map.163.refs_0_), channel_id=1, source_target_pairs={{0,1},{1,0},{2,3},{3,2},{4,5},{5,4},{6,7},{7,6},{8,9},{9,8},{10,11... | collective-permute-start | bytes 1966088 | tf_op jit(solution)/shard_map/ppermute | solution.py:496
  109.9 2.2 %collective-permute-start.30 = (f32[320,512]{1,0:T(8,128)S(1)}, f32[320,512]{1,0:T(8,128)S(1)}, u32[]{:S(2)}, u32[]{:S(2)}) collective-permute-start(f32[320,512]{1,0:T(8,128)S(1)} %shard_map.170.refs_1_), channel_id=1, source_target_pairs={{0,1},{1,0},{2,3},{3,2},{4,5},{5,4},{6,7},{7,6},{8,9},{9,8},{10,11... | collective-permute-start | bytes 1966088 | tf_op jit(solution)/shard_map/ppermute | solution.py:496
  (9 other events, 24.8 us)

commit v5 on v4

--- a/solution.py
+++ b/solution.py
@@ -81,11 +81,9 @@
 
 def own_kernel(
     _, tokens, gain, cot, wq_h, wq_l, wk_h, wk_l, wv_h, wv_l, wo_h, wo_l,
-    xhat, ht_h, ht_l, q_t, q_stack, k_stack, v_stack, kt_h, kt_l, vt_h, vt_l, d_mixed_t, d_stack,
-):
-    normal, _ = unit_rows(tokens[...])
-    xhat[...] = normal
-    hidden = normal * gain[...]
+    ht_h, ht_l, q_t, q_stack, k_stack, v_stack, kt_h, kt_l, vt_h, vt_l, d_mixed_t, d_stack,
+):
+    hidden = unit_rows(tokens[...])[0] * gain[...]
     store((ht_h, ht_l), pair_of(hidden.T), ...)
     rows = pair_of(hidden)
     query = dot3(rows, load((wq_h, wq_l), ...)) * HD ** (-0.5)
@@ -125,20 +123,15 @@
     )
 
 
-def key_side(patches, gain, wk, wv, xhat, ht, k_stack, kt, v_stack, vt):
-    for i, tokens in enumerate(patches):
-        normal, _ = unit_rows(tokens[...])
-        at = slice(i * PT, (i + 1) * PT)
-        xhat[at, :] = normal
-        hidden = normal * gain[...]
-        store(ht, pair_of(hidden.T), slice(None), at)
-    hidden = pair_of(xhat[...] * gain[...])
-    key = dot3(hidden, load(wk, ...))
+def key_side(patches, gain, wk, wv, k_stack, v_stack, vt):
+    hidden = jnp.concatenate([unit_rows(tokens[...])[0] * gain[...] for tokens in patches], axis=0)
+    rows = pair_of(hidden)
+    key = dot3(rows, load(wk, ...))
     store_stacked(k_stack, 0, key)
-    store(kt, pair_of(key.T), ...)
-    value = dot3(hidden, load(wv, ...))
+    value = dot3(rows, load(wv, ...))
     store_stacked(v_stack, 0, value)
     store(vt, pair_of(value.T), ...)
+    return hidden, key
 
 
 def head_rows(h):
@@ -152,18 +145,18 @@
 def weighed(highs, lows, rows, right):
     high = jnp.concatenate([r[rows, :] for r in highs], axis=1)
     low = jnp.concatenate([r[rows, :] for r in lows], axis=1)
-    both = dot(jnp.concatenate([high, low], axis=0), right[0])
-    return both[:HD] + (both[HD:] + dot(high, right[1]))
+    left = jnp.concatenate([high, low], axis=0)
+    both = dot(left, right[0]) + dot(left, right[1])
+    return both[:HD] + both[HD:]
 
 
 def near_side_kernel(
     patch_0, patch_1, gain, wk_h, wk_l, wv_h, wv_l,
-    xhat, ht_h, ht_l, kt_h, kt_l, k_stack, v_stack, vt_h, vt_l,
-):
-    key_side(
-        (patch_0, patch_1), gain, (wk_h, wk_l), (wv_h, wv_l), xhat, (ht_h, ht_l), k_stack, (kt_h, kt_l), v_stack,
-        (vt_h, vt_l),
-    )
+    ht_h, ht_l, kt_h, kt_l, k_stack, v_stack, vt_h, vt_l,
+):
+    hidden, key = key_side((patch_0, patch_1), gain, (wk_h, wk_l), (wv_h, wv_l), k_stack, v_stack, (vt_h, vt_l))
+    store((ht_h, ht_l), pair_of(hidden.T), ...)
+    store((kt_h, kt_l), pair_of(key.T), ...)
 
 
 def near_kernel(
@@ -198,39 +191,35 @@
     zero = jnp.zeros_like(right[0])
     one = [jnp.where(left_half, x, zero) for x in right]
     two = [jnp.where(left_half, zero, x) for x in right]
-    wide = dot(left_h[0], jnp.concatenate(one, axis=1)) + dot(left_h[1], jnp.concatenate(two, axis=1))
-    narrow = dot(left_l[0], one[0]) + dot(left_l[1], two[0])
-    return wide[:, : 2 * HD] + (wide[:, 2 * HD :] + narrow)
+    one, two = jnp.concatenate(one, axis=1), jnp.concatenate(two, axis=1)
+    wide = (dot(left_h[0], one) + dot(left_h[1], two)) + (dot(left_l[0], one) + dot(left_l[1], two))
+    return wide[:, : 2 * HD] + wide[:, 2 * HD :]
 
 
 def pair_lanes(p):
     return pl.ds(pl.multiple_of(p * 2 * HD, 2 * HD), 2 * HD)
 
 
-def kept_and_sent(me, pair, keep, send):
-    rows = pair[0].shape[0]
-
-    @pl.when(me[0] % 2 == 0)
-    def _():
-        keep[:rows, :] = pair[0][...]
-        send[:rows, :] = pair[1][...]
-
-    @pl.when(me[0] % 2 == 1)
-    def _():
-        keep[:rows, :] = pair[1][...]
-        send[:rows, :] = pair[0][...]
+def kept_and_sent(me, pair, keep, sends):
+    rows = sends[0].shape[0]
+    for bit in range(2):
+
+        @pl.when(me[0] % 2 == bit)
+        def _():
+            keep[...] = pair[bit][...]
+            for i, send in enumerate(sends):
+                send[...] = pair[1 - bit][i * rows : (i + 1) * rows, :]
 
 
 def far_kernel(
     parity, listed, counts, patch_0, patch_1, gain, q_t, q_stack, d_mixed_t, d_stack, mixed_1, tops, totals,
     wk_h, wk_l, wv_h, wv_l,
-    xhat, ht_h, ht_l, kt_h, kt_l, u_h, u_l, mixed_t, deltas, shares, shares_1, dk_h, dk_l, dv_h, dv_l, d_far,
+    hidden, key, u_h, u_l, mixed_t, deltas, shares, shares_1, dk_h, dk_l, dv_h, dv_l, d_far,
     bias, k_far, v_far, vt_h, vt_l, e_h, e_l,
 ):
     store_bias(bias, listed, counts, parity, range(4, 6))
-    key_side(
-        (patch_0, patch_1), gain, (wk_h, wk_l), (wv_h, wv_l), xhat, (ht_h, ht_l), k_far, (kt_h, kt_l), v_far,
-        (vt_h, vt_l),
+    hidden[...], key[...] = key_side(
+        (patch_0, patch_1), gain, (wk_h, wk_l), (wv_h, wv_l), k_far, v_far, (vt_h, vt_l)
     )
 
     def one_pair(p, carry):
@@ -276,10 +265,12 @@
 
 
 def back_kernel(
-    q_t, d_mixed_t, kt_h, kt_l, kt2_h, kt2_l, kt3_h, kt3_l, e_h, e_l, d_scores, u_h, u_l, deltas, shares, shares_1,
+    q_t, d_mixed_t, kt_h, kt_l, kt2_h, kt2_l, key3, e_h, e_l, d_scores, u_h, u_l, deltas, shares, shares_1,
     dq_t, dk_h, dk_l, dv_h, dv_l,
-    s_h, s_l,
-):
+    s_h, s_l, kt3_h, kt3_l,
+):
+    store((kt3_h, kt3_l), pair_of(key3[...].T), ...)
+
     def one_pair(p, carry):
         q_scaled, d_scaled = [], []
         for a in range(2):
@@ -308,16 +299,16 @@
 
 
 def mix_kernel(
-    me, mixed_t, ht_h, ht_l, ht2_h, ht2_l, ht3_h, ht3_l, dv_h, dv_l, dv3_h, dv3_l, cot,
-    keep, send,
-    grad_o, grad_v,
-):
+    me, mixed_t, ht_h, ht_l, ht2_h, ht2_l, hidden3, dv_h, dv_l, dv3_h, dv3_l, cot, ht3_h, ht3_l, keep, *refs
+):
+    *sends, grad_o, grad_v = refs
     own = cot.shape[0]
+    store((ht3_h, ht3_l), pair_of(hidden3[...].T), ...)
     grad_o[...] = dot3(pair_of(mixed_t[...]), pair_of(cot[...]))
     turned = [load(t, ...) for t in ((ht_h, ht_l), (ht2_h, ht2_l), (ht3_h, ht3_l))]
     d_values = [load((dv_h, dv_l), slice(0, own)), load((dv_h, dv_l), slice(own, 2 * own)), load((dv3_h, dv3_l), ...)]
     grad_v[...] = sums_of(turned, d_values)
-    kept_and_sent(me, (grad_o, grad_v), keep, send)
+    kept_and_sent(me, (grad_o, grad_v), keep, sends)
 
 
 def result_kernel(_, mixed_t, tokens, wo_h, wo_l, result, mark):
@@ -338,8 +329,8 @@
     grad_k[...] = sums_of(turned, d_keys)
 
 
-def core_kernel(me, grad_q, grad_k, _back, _keep, keep, send):
-    kept_and_sent(me, (grad_q, grad_k), keep, send)
+def core_kernel(me, grad_q, grad_k, _keep, _back, keep, *sends):
+    kept_and_sent(me, (grad_q, grad_k), keep, sends)
 
 
 def side_kernel(
@@ -367,11 +358,13 @@
     out[...] = a[...] + b[...]
 
 
-def cut_kernel(masks, me, keep_1, other_1, keep_2, other_2, *outs):
-    count = keep_1.shape[0]
-    *outs, sums = outs
-    sums[:count, :] = keep_1[...] + other_1[...]
-    sums[count:, :] = keep_2[...] + other_2[...]
+def cut_kernel(masks, me, keep_1, keep_2, *refs):
+    others, outs, sums = refs[: 2 * PIECES], refs[2 * PIECES : -1], refs[-1]
+    rows = others[0].shape[0]
+    for i, other in enumerate(others):
+        keep = (keep_1, keep_2)[i // PIECES]
+        first = i % PIECES * rows
+        sums[i * rows : (i + 1) * rows, :] = keep[first : first + rows, :] + other[...]
     at = 0
     for i, mask in enumerate(masks):
         rows = outs[2 * i].shape[0]
@@ -406,18 +399,20 @@
     out[half_of(me, mask, False, rows), :] = other[...]
 
 
-def write_kernel(ranges, me, gain, wv_h, wv_l, wq_h, wq_l, wk_h, wk_l, *refs):
-    mine, other, outs, d_gain, (partial, sent) = refs[:3], refs[3:6], refs[6:10], refs[10], refs[11:]
+def write_kernel(ranges, core, me, gain, wv_h, wv_l, wq_h, wq_l, wk_h, wk_l, *refs):
+    parts, refs = refs[:3], refs[3:]
+    before = refs[4] if core else None
+    refs = refs[5 * core :]
+    outs, last, (partial, total, sent) = refs[:4], refs[4], refs[5:] if core else (refs[4], None, refs[5])
     weights = (None, (wv_h, wv_l), (wq_h, wq_l), (wk_h, wk_l))
     lanes = partial.shape[1]
-    partial[...] = jnp.zeros_like(partial)
+    partial[...] = before[...] if core else jnp.zeros_like(partial)
     for bit in range(2):
 
         @pl.when(me[0] % 2 == bit)
         def _():
             pieces = [
                 (parts[i].at[pl.ds(first, rows)], 2 * exchange + (bit + core) % 2, to, rows)
-                for core, parts in enumerate((mine, other))
                 for i, first, rows, exchange, to in ranges
             ]
             copies = [
@@ -433,10 +428,29 @@
                         at = (slice(to, to + rows), slice(lane, lane + lanes))
                         weight = high[at].astype(F32) + low[at].astype(F32)
                         partial[to : to + rows, :] += weight * piece[:, lane : lane + lanes]
+            if core:
+                total[...] = jnp.sum(partial[...].T, axis=0, keepdims=True) / gain[...]
+                copies.append(pltpu.make_async_copy(total, last, sent.at[len(copies)]))
+                copies[-1].start()
             for copy in copies:
                 copy.wait()
 
-    d_gain[...] = jnp.sum(partial[...].T, axis=0, keepdims=True) / gain[...]
+
+def written(me, gain, weights, parts, ranges, count, core, held=()):
+    width = parts[0].shape[1]
+    anywhere = pl.BlockSpec(memory_space=pl.ANY)
+    partial = shape(count, 128)
+    semaphores = pltpu.SemaphoreType.DMA((len(ranges) + core,))
+    return pl.pallas_call(
+        functools.partial(write_kernel, ranges, core),
+        out_shape=[shape(count, width)] * 4 + [shape(1, width) if core else partial],
+        in_specs=[SMEM] + [VMEM] * 10 + ([anywhere] * 4 + [VMEM] if core else []),
+        out_specs=[anywhere] * 4 + [anywhere if core else VMEM],
+        scratch_shapes=([pltpu.VMEM(partial.shape, F32), pltpu.VMEM((1, width), F32)] if core else []) + [semaphores],
+        input_output_aliases={11 + i: i for i in range(4)} if core else {},
+        compiler_params=pltpu.CompilerParams(vmem_limit_bytes=2**23),
+        cost_estimate=pl.CostEstimate(flops=10**9, bytes_accessed=0, transcendentals=0),
+    )(me, gain, *weights, *parts, *held)
 
 
 def tokens_kernel(_, tokens, gain, cot, d_own, d_other, out, mark):
@@ -464,7 +478,7 @@
         out_specs=[VMEM] * len(outputs),
         scratch_shapes=[pltpu.VMEM(s.shape, s.dtype) for s in scratch],
         compiler_params=pltpu.CompilerParams(vmem_limit_bytes=limit * 2**20),
-        cost_estimate=pl.CostEstimate(flops=us * 10**9, bytes_accessed=0, transcendentals=0),
+        cost_estimate=pl.CostEstimate(flops=int(us * 10**9), bytes_accessed=0, transcendentals=0),
     )(*inputs)
 
 
@@ -500,7 +514,7 @@
 LAST = 16
 
 
-def summed(me, keep_1, other_1, keep_2, send_2, weights, gain, result_of, side_of, tokens_of):
+def summed(me, keep_1, others_1, keep_2, others_2, weights, gain, result_of, side_of, tokens_of):
     count, width = keep_1.shape
     total = 2 * count
     unit = 8 * 8
@@ -508,7 +522,7 @@
     sizes.append(total - sum(sizes))
     parts = call(
         functools.partial(cut_kernel, [order[0] for order in ORDERS]),
-        (me, keep_1, other_1, keep_2, swapped(send_2, 1)),
+        (me, keep_1, keep_2, *others_1, *others_2),
         [shape(size // 2, width) for size in sizes for _ in range(2)],
         [shape(total, width)],
         scalars=1, limit=8,
@@ -518,29 +532,30 @@
     for step in (1, 2):
         for i in range(3):
             half, mask = shape(sizes[i] >> (step + 1), width), ORDERS[i][step]
-            place = (mark,) if step == 1 and i == 0 else ()
+            place = (mark,) if step == 1 else ()
             keep, send = call(
                 functools.partial(halve_kernel, mask), (me, *parts[i], *place), [half, half], scalars=1
             )
             parts[i] = [keep, swapped(send, mask)]
     for i in (0, 2, 1):
-        if i == 0:
+        if i == 1:
             part, d_going = call(first_kernel, (*parts[i], d_given), [parts[i][0], d_given])
             d_other = across(d_going)
-            result, mark = result_of(part)
         else:
             (part,) = call(add_kernel, parts[i], [parts[i][0]])
+        if i == 0:
+            result, mark = result_of(part)
         mask, other = LAST, swapped(part, LAST)
         while 2 * mask < devices():
             (part,) = call(add_kernel, (part, other), [part])
             mask *= 2
             other = swapped(part, mask)
-        place = (d_other, mark) if i == 1 else ()
+        place = (mark,) if i == 1 else ()
         (parts[i],) = call(last_kernel, (part, other, *place), [part])
     for step in (2, 1, 0):
         for i in range(3):
             mask = ORDERS[i][step]
-            place = (mark,) if step == 0 and i == 2 else ()
+            place = {(2, 1): (d_other,), (0, 2): (mark,)}.get((step, i), ())
             (parts[i],) = call(
                 functools.partial(double_kernel, mask), (me, parts[i], swapped(parts[i], mask), *place),
                 [shape(2 * parts[i].shape[0], width)], scalars=1,
@@ -555,14 +570,8 @@
             if start < stop:
                 ranges.append((i, start - at, stop - start, exchange, start - exchange * count))
         at += size
-    *gradients, d_gain = pl.pallas_call(
-        functools.partial(write_kernel, ranges),
-        out_shape=[shape(count, width)] * 4 + [shape(1, width)],
-        in_specs=[SMEM] + [VMEM] * 13,
-        out_specs=[pl.BlockSpec(memory_space=pl.ANY)] * 4 + [VMEM],
-        scratch_shapes=[pltpu.VMEM((count, 128), F32), pltpu.SemaphoreType.DMA((2 * len(ranges),))],
-        compiler_params=pltpu.CompilerParams(vmem_limit_bytes=2**23),
-    )(me, gain, *weights, *parts, *others)
+    held = written(me, gain, weights, parts, ranges, count, 0)
+    *gradients, d_gain = written(me, gain, weights, others, ranges, count, 1, held)
     return gradients, d_gain.reshape(width), d_tokens, result
 
 
@@ -580,20 +589,20 @@
     weights = call(weight_kernel, (me, parity, wq, wk, wv, wo), square * 4, scalars=2, limit=20)
     wq_h, wq_l, wk_h, wk_l, wv_h, wv_l, wo_h, wo_l = weights
     (
-        xhat, ht_h, ht_l, q_t, q_stack, k_stack, v_stack, kt_h, kt_l, vt_h, vt_l, d_mixed_t, d_stack,
+        ht_h, ht_l, q_t, q_stack, k_stack, v_stack, kt_h, kt_l, vt_h, vt_l, d_mixed_t, d_stack,
     ) = call(
         own_kernel,
         (near[0], tokens, gain_row, cotangent, *weights),
-        [whole, *turned, whole_t, stack_rows, stack_columns, stack_columns, *turned, *turned, whole_t, stack_rows],
+        [*turned, whole_t, stack_rows, stack_columns, stack_columns, *turned, *turned, whole_t, stack_rows],
         limit=LIMITS[0], us=1,
     )
     near[1], q_stack = lax.optimization_barrier((near[1], q_stack))
     far.append(onward(near[1]))
     w_k, w_v = (wk_h, wk_l), (wv_h, wv_l)
-    xhat2, ht2_h, ht2_l, kt2_h, kt2_l, k_near, v_near, vt2_h, vt2_l = call(
+    ht2_h, ht2_l, kt2_h, kt2_l, k_near, v_near, vt2_h, vt2_l = call(
         near_side_kernel,
         (*near, gain_row, *w_k, *w_v),
-        [whole, *turned, *turned, stack_columns, stack_columns, *turned],
+        [*turned, *turned, stack_columns, stack_columns, *turned],
         limit=LIMITS[1], us=1,
     )
     e_h, e_l, d_scores, mixed, tops, totals = call(
@@ -607,7 +616,7 @@
         scalars=3, limit=LIMITS[1], us=1,
     )
     (
-        xhat3, ht3_h, ht3_l, kt3_h, kt3_l, u_h, u_l, mixed_t, deltas, shares, shares_1, dk3_h, dk3_l, dv3_h, dv3_l,
+        hidden3, key3, u_h, u_l, mixed_t, deltas, shares, shares_1, dk3_h, dk3_l, dv3_h, dv3_l,
         d_far,
     ) = call(
         far_kernel,
@@ -616,7 +625,7 @@
             *w_k, *w_v,
         ),
         [
-            whole, *turned, *turned, *pairs(HEADS, rows, rows), whole_t, scalars, scalars, scalars, *pair, *pair,
+            whole, whole, *pairs(HEADS, rows, rows), whole_t, scalars, scalars, scalars, *pair, *pair,
             whole,
         ],
         [shape(8, rows), stack_columns, stack_columns, *turned, *pairs(2, rows, rows)],
@@ -626,30 +635,32 @@
     dq_t, dk_h, dk_l, dv_h, dv_l = call(
         back_kernel,
         (
-            q_t, d_mixed_t, kt_h, kt_l, kt2_h, kt2_l, kt3_h, kt3_l, e_h, e_l, d_scores, u_h, u_l, deltas, shares,
+            q_t, d_mixed_t, kt_h, kt_l, kt2_h, kt2_l, key3, e_h, e_l, d_scores, u_h, u_l, deltas, shares,
             shares_1,
         ),
         [whole_t, *pairs(2 * rows, width), *pairs(2 * rows, width)],
-        [*pairs(2, 2 * rows, rows)],
+        [*pairs(2, 2 * rows, rows), *turned],
         limit=LIMITS[4], us=1,
     )
-    keep_1, send_1 = call(
+    pieces = [shape(width // PIECES, width)] * PIECES
+    ht3_h, ht3_l, keep_1, *sends_1 = call(
         mix_kernel,
-        (me, mixed_t, ht_h, ht_l, ht2_h, ht2_l, ht3_h, ht3_l, dv_h, dv_l, dv3_h, dv3_l, cotangent),
-        [shape(width, width), shape(width, width)],
+        (me, mixed_t, ht_h, ht_l, ht2_h, ht2_l, hidden3, dv_h, dv_l, dv3_h, dv3_l, cotangent),
+        [*turned, shape(width, width), *pieces],
         [shape(width, width), shape(width, width)],
         scalars=1, limit=LIMITS[3], us=1,
     )
-    other_1 = swapped(send_1, 1)
+    others_1 = [swapped(send, 1) for send in sends_1]
     grad_q, grad_k, dq_h, dq_l = call(
         grad_kernel,
         (ht_h, ht_l, ht2_h, ht2_l, ht3_h, ht3_l, dq_t, dk_h, dk_l, dk3_h, dk3_l),
         [shape(width, width), shape(width, width), *pair],
         limit=LIMITS[5], us=1,
     )
-    keep_2, send_2 = call(
-        core_kernel, (me, grad_q, grad_k, d_back, keep_1), [shape(width, width)] * 2, scalars=1, limit=8
-    )
+    keep_2, *sends_2 = call(
+        core_kernel, (me, grad_q, grad_k, keep_1, d_back), [shape(width, width), *pieces], scalars=1, limit=8, us=1
+    )
+    others_2 = [swapped(send, 1) for send in sends_2]
 
     def result_of(place):
         return call(result_kernel, (place, mixed_t, tokens, wo_h, wo_l), [whole, MARK], limit=LIMITS[3], us=1)
@@ -663,12 +674,13 @@
         return call(tokens_kernel, inputs, [whole, MARK], limit=8)
 
     (grad_o, grad_v, grad_q, grad_k), d_gain, d_tokens, result = summed(
-        me, keep_1, other_1, keep_2, send_2, (wv_h, wv_l, wq_h, wq_l, *w_k), gain_row, result_of, side_of, tokens_of
+        me, keep_1, others_1, keep_2, others_2, (wv_h, wv_l, wq_h, wq_l, *w_k), gain_row, result_of, side_of, tokens_of
     )
     return (result, d_tokens, d_gain, grad_q, grad_k, grad_v, grad_o)
 
 
 UNROLL = True
+PIECES = 1
 LIMITS = (8, 8, 8, 8, 8, 8)
 
 

time: 115 us -> 113 us (0.983)
  waiting for transfers between devices: 41.5 us -> 32.3 us
  starting transfers between devices: 32.6 us -> 40.2 us
    ppermute x26, waiting for transfers between devices: 36.7 us -> 26.9 us  [swapped(): lax.ppermute(value, ('space', 'slab'), [(i, i ^ mask) for i in range(devi...]
    ppermute x26, starting transfers between devices: 23 us -> 29.1 us  [swapped(): lax.ppermute(value, ('space', 'slab'), [(i, i ^ mask) for i in range(devi...]
    ppermute x6, starting transfers between devices: 9.61 us -> 11.1 us  [along_space(): lax.ppermute(value, 'space', [(i, target(i) % count) for i in range(count)])]
    pallas_call x1 -> x2, Pallas kernels: 2.81 us -> 2.73 us  [written(): pl.pallas_call(functools.partial(write_kernel, ranges, core), out_shape=[...]
  transfers between devices with their start and end apart: 32 -> 32, of which waited for: 20 -> 19; matrix products, arithmetic and copies ran while one was open for 0% -> 0% of each run, Pallas kernels for 20% -> 21%
where the time goes in v5:
time: 113 us; the launch traced here: 112 us
  starting transfers between devices  40.2 us (36%)
  Pallas kernels  32.8 us (29%)
  waiting for transfers between devices  32.3 us (29%)
  local copies, waits for them, and re-layouts  5.99 us (5%)
    pallas_call x34, Pallas kernels, call(): pl.pallas_call(kernel, out_shape=outputs, in_specs=[SMEM] * scalars + [VM...  30.1 us
    ppermute x26, starting transfers between devices, swapped(): lax.ppermute(value, ('space', 'slab'), [(i, i ^ mask) for i in range(devi...  29.1 us
    ppermute x26, waiting for transfers between devices, swapped(): lax.ppermute(value, ('space', 'slab'), [(i, i ^ mask) for i in range(devi...  26.9 us
    ppermute x6, starting transfers between devices, along_space(): lax.ppermute(value, 'space', [(i, target(i) % count) for i in range(count)])  11.1 us
    ppermute x6, waiting for transfers between devices, along_space(): lax.ppermute(value, 'space', [(i, target(i) % count) for i in range(count)])  5.4 us
    unnamed x18, local copies, waits for them, and re-layouts  4.92 us
    pallas_call x2, Pallas kernels, written(): pl.pallas_call(functools.partial(write_kernel, ranges, core), out_shape=[...  2.73 us
  transfers between devices with their start and end apart: 32, of which 19 were waited for; matrix products, arithmetic and copies ran while one was open for 0% of the time, Pallas kernels for 21%

profile of v5, /device:TPU:0, one launch (start us, length us, event | category | flops | bytes accessed | tf_op | source)
XLA Modules:
  0.0 112.5 jit_solution(14224656315847139384)
XLA Ops:
  1.7 3.0 %collective-permute-start = (f32[128,512]{1,0:T(8,128)S(1)}, f32[128,512]{1,0:T(8,128)S(1)}, u32[]{:S(2)}, u32[]{:S(2)}) collective-permute-start(f32[128,512]{1,0:T(8,128)S(1)} %get-tuple-element.210), channel_id=1, source_target_pairs={{0,4},{4,0},{8,12},{12,8},{16,20},{20,16},{24,28},{28,24},{1,5},{5... | collective-permute-start | bytes 786440 | tf_op jit(solution)/shard_map/ppermute | solution.py:490
  10.3 1.5 %collective-permute-done._.patch_0 = f32[128,512]{1,0:T(8,128)S(1)} collective-permute-done((f32[128,512]{1,0:T(8,128)S(1)}, f32[128,512]{1,0:T(8,128)S(1)}, u32[]{:S(2)}, u32[]{:S(2)}) %collective-permute-start) | collective-permute-done | bytes 262176 | tf_op jit(solution)/shard_map/ppermute | solution.py:490
  11.8 2.1 %collective-permute-start.1 = (f32[128,512]{1,0:T(8,128)S(1)}, f32[128,512]{1,0:T(8,128)S(1)}, u32[]{:S(2)}, u32[]{:S(2)}) collective-permute-start(f32[128,512]{1,0:T(8,128)S(1)} %collective-permute-done._.patch_0), channel_id=1, source_target_pairs={{0,8},{4,28},{8,16},{12,4},{16,24},{20,12},{24,0},{28,20},{1,9},{5... | collective-permute-start | bytes 786440 | tf_op jit(solution)/shard_map/ppermute | solution.py:490
  14.0 2.1 %shard_map.145 = (bf16[512,256]{1,0:T(8,128)(2,1)S(1)}, bf16[512,256]{1,0:T(8,128)(2,1)S(1)}, f32[512,256]{1,0:T(8,128)S(1)}, bf16[2048,256]{1,0:T(8,128)(2,1)S(...) custom-call(f32[128,512]{1,0:T(8,128)S(1)} %collective-permute-done., ...), custom_call_target="tpu_custom_call" | custom-call | flops 1000000000 | tf_op jit(solution)/shard_map/pallas_call | solution.py:474
  16.6 1.8 %collective-permute-start.3 = (f32[128,512]{1,0:T(8,128)S(1)}, f32[128,512]{1,0:T(8,128)S(1)}, u32[]{:S(2)}, u32[]{:S(2)}) collective-permute-start(f32[128,512]{1,0:T(8,128)S(1)} %collective-permute-done.2.patch_1), channel_id=1, source_target_pairs={{0,8},{4,28},{8,16},{12,4},{16,24},{20,12},{24,0},{28,20},{1,9},{5... | collective-permute-start | bytes 786440 | tf_op jit(solution)/shard_map/ppermute | solution.py:490
  18.5 1.6 %shard_map.146 = (bf16[512,256]{1,0:T(8,128)(2,1)S(1)}, bf16[512,256]{1,0:T(8,128)(2,1)S(1)}, bf16[512,256]{1,0:T(8,128)(2,1)S(1)}, bf16[512,256]{1,0:T(8,128)(2...) custom-call(f32[128,512]{1,0:T(8,128)S(1)} %collective-permute-done., ...), custom_call_target="tpu_custom_call" | custom-call | flops 1000000000 | tf_op jit(solution)/shard_map/pallas_call | solution.py:474
  20.4 4.7 %shard_map.147 = (bf16[8,512,256]{2,1,0:T(8,128)(2,1)S(1)}, bf16[8,512,256]{2,1,0:T(8,128)(2,1)S(1)}, f32[8,512,256]{2,1,0:T(8,128)S(1)}, f32[512,256]{1,0:T(8,1...) custom-call(s32[1]{0:T(128)} %bitcast.1._parity.parity, s32[2,3]{1,0:T(2,128)S(1)} %copy-done.7, ...), custom_call_target="tpu_custom_call" | custom-call | flops 1000000000 | tf_op jit(solution)/shard_map/pallas_call | solution.py:474
  26.0 7.2 %shard_map.148 = (f32[256,512]{1,0:T(8,128)S(1)}, f32[256,512]{1,0:T(8,128)S(1)}, bf16[8,256,256]{2,1,0:T(8,128)(2,1)S(1)}, bf16[8,256,256]{2,1,0:T(8,128)(2,1)S...) custom-call(s32[1]{0:T(128)} %bitcast.1._parity.parity, ...), custom_call_target="tpu_custom_call" | custom-call | flops 1000000000 | tf_op jit(solution)/shard_map/pallas_call | solution.py:474
  33.1 2.3 %collective-permute-start.4 = (f32[256,512]{1,0:T(8,128)S(1)}, f32[256,512]{1,0:T(8,128)S(1)}, u32[]{:S(2)}, u32[]{:S(2)}) collective-permute-start(f32[256,512]{1,0:T(8,128)S(1)} %get-tuple-element.166), channel_id=1, source_target_pairs={{0,24},{4,12},{8,0},{12,20},{16,8},{20,28},{24,16},{28,4},{1,25},{... | collective-permute-start | bytes 1572872 | tf_op jit(solution)/shard_map/ppermute | solution.py:490
  35.4 4.0 %shard_map.149 = (f32[512,256]{1,0:T(8,128)S(1)}, bf16[512,512]{1,0:T(8,128)(2,1)S(1)}, bf16[512,512]{1,0:T(8,128)(2,1)S(1)}, bf16[512,512]{1,0:T(8,128)(2,1)S(1)}, bf16[512,512]{1,0:T(8,128)(2,1)S(1)}) custom-call(f32[512,256]{1,0:T(8,128)S(1)} %get-tuple-element.118.q_t, f32[512,256]{1,0:T(8,128)S(1)} %get-tuple-element.120.d_mixed_t, ...), custom_call_target="tpu_custom_call" | custom-call | flops 1000000000 | tf_op jit(solution)/shard_map/pallas_call | solution.py:474
  39.5 2.0 %shard_map.150 = (bf16[512,256]{1,0:T(8,128)(2,1)S(1)}, bf16[512,256]{1,0:T(8,128)(2,1)S(1)}, f32[512,512]{1,0:T(8,128)S(1)}, f32[512,512]{1,0:T(8,128)S(1)}) custom-call(s32[1]{0:T(128)} %bitcast._me.me, f32[512,256]{1,0:T(8,128)S(1)} %get-tuple-element.133.mixed_t, bf16[512,256]{1,0:T(8,128)(2,1)S(1)} %get-tuple-element.134.ht_h, ...), custom_call_target="tpu_custom_call" | custom-call | flops 1000000000 | tf_op jit(solution)/shard_map/pallas_call | solution.py:474
  41.5 2.0 %shard_map.151 = (f32[512,512]{1,0:T(8,128)S(1)}, f32[512,512]{1,0:T(8,128)S(1)}, bf16[256,512]{1,0:T(8,128)(2,1)S(1)}, bf16[256,512]{1,0:T(8,128)(2,1)S(1)}) custom-call(bf16[512,256]{1,0:T(8,128)(2,1)S(1)} %get-tuple-element.134.ht_h, bf16[512,256]{1,0:T(8,128)(2,1)S(1)} %get-tuple-element.135.ht_l, bf16[512,256]{1,0:T(8,128)(2,1)S(1)} %get-tuple-element.136.ht2_h, ...), custom_call_target="tpu_custom_call" | custom-call | flops 1000000000 | tf_op jit(solution)/shard_map/pallas_call | solution.py:474
  43.5 2.2 %collective-permute-done.4._back.d_back = f32[256,512]{1,0:T(8,128)S(1)} collective-permute-done((f32[256,512]{1,0:T(8,128)S(1)}, f32[256,512]{1,0:T(8,128)S(1)}, u32[]{:S(2)}, u32[]{:S(2)}) %collective-permute-start.4) | collective-permute-done | bytes 524320 | tf_op jit(solution)/shard_map/ppermute | solution.py:490
  45.9 2.6 %collective-permute-done.6.refs_1_ = f32[512,512]{1,0:T(8,128)S(1)} collective-permute-done((f32[512,512]{1,0:T(8,128)S(1)}, f32[512,512]{1,0:T(8,128)S(1)}, u32[]{:S(2)}, u32[]{:S(2)}) %collective-permute-start.6) | collective-permute-done | bytes 1048608 | tf_op jit(solution)/shard_map/ppermute | solution.py:510
  49.6 3.8 %collective-permute-start.7 = (f32[160,512]{1,0:T(8,128)S(1)}, f32[160,512]{1,0:T(8,128)S(1)}, u32[]{:S(2)}, u32[]{:S(2)}) collective-permute-start(f32[160,512]{1,0:T(8,128)S(1)} %get-tuple-element.171), channel_id=1, source_target_pairs={{0,4},{1,5},{2,6},{3,7},{4,0},{5,1},{6,2},{7,3},{8,12},{9,13},{10,... | collective-permute-start | bytes 983048 | tf_op jit(solution)/shard_map/ppermute | solution.py:510
  53.5 1.5 %collective-permute-start.13 = (f32[160,512]{1,0:T(8,128)S(1)}, f32[160,512]{1,0:T(8,128)S(1)}, u32[]{:S(2)}, u32[]{:S(2)}) collective-permute-start(f32[160,512]{1,0:T(8,128)S(1)} %get-tuple-element.182), channel_id=1, source_target_pairs={{0,2},{1,3},{2,0},{3,1},{4,6},{5,7},{6,4},{7,5},{8,10},{9,11},{10,... | collective-permute-start | bytes 983048 | tf_op jit(solution)/shard_map/ppermute | solution.py:510
  55.0 2.2 %shard_map.154 = (f32[256,512]{1,0:T(8,128)S(1)}, f32[256,512]{1,0:T(8,128)S(1)}, f32[8,128]{1,0:T(8,128)S(1)}) custom-call(f32[160,512]{1,0:T(8,128)S(1)} %get-tuple-element.170._.keep, f32[256,512]{1,0:T(8,128)S(1)} %collective-permute-done.4._back.d_back, bf16[256,512]{1,0:T(8,128)(2,1)S(1)} %get-tuple-element.172.dq_h, ...), custom_call_target="tpu_custom_call" | custom-call | flops 1000000000 | tf_op jit(solution)/shard_map/pallas_call | solution.py:474
  57.2 2.9 %collective-permute-done.24.other = f32[192,512]{1,0:T(8,128)S(1)} collective-permute-done((f32[192,512]{1,0:T(8,128)S(1)}, f32[192,512]{1,0:T(8,128)S(1)}, u32[]{:S(2)}, u32[]{:S(2)}) %collective-permute-start.24) | collective-permute-done | bytes 393248 | tf_op jit(solution)/shard_map/ppermute | solution.py:510
  60.1 4.5 %collective-permute-start.25 = (f32[96,512]{1,0:T(8,128)S(1)}, f32[96,512]{1,0:T(8,128)S(1)}, u32[]{:S(2)}, u32[]{:S(2)}) collective-permute-start(f32[96,512]{1,0:T(8,128)S(1)} %get-tuple-element.195), channel_id=1, source_target_pairs={{0,4},{1,5},{2,6},{3,7},{4,0},{5,1},{6,2},{7,3},{8,12},{9,13},{10,... | collective-permute-start | bytes 589832 | tf_op jit(solution)/shard_map/ppermute | solution.py:510
  64.7 1.6 %collective-permute-start.8 = (f32[80,512]{1,0:T(8,128)S(1)}, f32[80,512]{1,0:T(8,128)S(1)}, u32[]{:S(2)}, u32[]{:S(2)}) collective-permute-start(f32[80,512]{1,0:T(8,128)S(1)} %get-tuple-element.176), channel_id=1, source_target_pairs={{0,2},{1,3},{2,0},{3,1},{4,6},{5,7},{6,4},{7,5},{8,10},{9,11},{10,... | collective-permute-start | bytes 491528 | tf_op jit(solution)/shard_map/ppermute | solution.py:510
  66.7 2.3 %collective-permute-done.25.other = f32[96,512]{1,0:T(8,128)S(1)} collective-permute-done((f32[96,512]{1,0:T(8,128)S(1)}, f32[96,512]{1,0:T(8,128)S(1)}, u32[]{:S(2)}, u32[]{:S(2)}) %collective-permute-start.25) | collective-permute-done | bytes 196640 | tf_op jit(solution)/shard_map/ppermute | solution.py:510
  69.1 1.6 %collective-permute-start.26 = (f32[48,512]{1,0:T(8,128)S(1)}, f32[48,512]{1,0:T(8,128)S(1)}, u32[]{:S(2)}, u32[]{:S(2)}) collective-permute-start(f32[48,512]{1,0:T(8,128)S(1)} %get-tuple-element.197), channel_id=1, source_target_pairs={{0,2},{1,3},{2,0},{3,1},{4,6},{5,7},{6,4},{7,5},{8,10},{9,11},{10,... | collective-permute-start | bytes 294920 | tf_op jit(solution)/shard_map/ppermute | solution.py:510
  75.2 1.6 %collective-permute-start.10 = (f32[40,512]{1,0:T(8,128)S(1)}, f32[40,512]{1,0:T(8,128)S(1)}, u32[]{:S(2)}, u32[]{:S(2)}) collective-permute-start(f32[40,512]{1,0:T(8,128)S(1)} %shard_map.157._.a), channel_id=1, source_target_pairs={{0,16},{1,17},{2,18},{3,19},{4,20},{5,21},{6,22},{7,23},{8,24},{9,... | collective-permute-start | bytes 245768 | tf_op jit(solution)/shard_map/ppermute | solution.py:510
  76.9 1.8 %collective-permute-start.16 = (f32[256,512]{1,0:T(8,128)S(1)}, f32[256,512]{1,0:T(8,128)S(1)}, u32[]{:S(2)}, u32[]{:S(2)}) collective-permute-start(f32[256,512]{1,0:T(8,128)S(1)} %get-tuple-element.188), channel_id=1, source_target_pairs={{0,4},{4,0},{8,12},{12,8},{16,20},{20,16},{24,28},{28,24},{1,5},{5... | collective-permute-start | bytes 1572872 | tf_op jit(solution)/shard_map/ppermute | solution.py:490
  78.7 3.3 %collective-permute-done.27.b = f32[48,512]{1,0:T(8,128)S(1)} collective-permute-done((f32[48,512]{1,0:T(8,128)S(1)}, f32[48,512]{1,0:T(8,128)S(1)}, u32[]{:S(2)}, u32[]{:S(2)}) %collective-permute-start.27) | collective-permute-done | bytes 98336 | tf_op jit(solution)/shard_map/ppermute | solution.py:510
  82.0 2.2 %collective-permute-start.28 = (f32[48,512]{1,0:T(8,128)S(1)}, f32[48,512]{1,0:T(8,128)S(1)}, u32[]{:S(2)}, u32[]{:S(2)}) collective-permute-start(f32[48,512]{1,0:T(8,128)S(1)} %shard_map.174.mine), channel_id=1, source_target_pairs={{0,2},{1,3},{2,0},{3,1},{4,6},{5,7},{6,4},{7,5},{8,10},{9,11},{10,... | collective-permute-start | bytes 294920 | tf_op jit(solution)/shard_map/ppermute | solution.py:510
  88.3 2.7 %collective-permute-done.19.b = f32[40,512]{1,0:T(8,128)S(1)} collective-permute-done((f32[40,512]{1,0:T(8,128)S(1)}, f32[40,512]{1,0:T(8,128)S(1)}, u32[]{:S(2)}, u32[]{:S(2)}) %collective-permute-start.19) | collective-permute-done | bytes 81952 | tf_op jit(solution)/shard_map/ppermute | solution.py:510
  92.6 3.5 %collective-permute-done.20.other = f32[40,512]{1,0:T(8,128)S(1)} collective-permute-done((f32[40,512]{1,0:T(8,128)S(1)}, f32[40,512]{1,0:T(8,128)S(1)}, u32[]{:S(2)}, u32[]{:S(2)}) %collective-permute-start.20) | collective-permute-done | bytes 81952 | tf_op jit(solution)/shard_map/ppermute | solution.py:510
  96.3 2.1 %collective-permute-start.30 = (f32[192,512]{1,0:T(8,128)S(1)}, f32[192,512]{1,0:T(8,128)S(1)}, u32[]{:S(2)}, u32[]{:S(2)}) collective-permute-start(f32[192,512]{1,0:T(8,128)S(1)} %shard_map.176.mine), channel_id=1, source_target_pairs={{0,8},{1,9},{2,10},{3,11},{4,12},{5,13},{6,14},{7,15},{8,0},{9,1},... | collective-permute-start | bytes 1179656 | tf_op jit(solution)/shard_map/ppermute | solution.py:510
  98.4 1.7 %collective-permute-start.17 = (f32[160,512]{1,0:T(8,128)S(1)}, f32[160,512]{1,0:T(8,128)S(1)}, u32[]{:S(2)}, u32[]{:S(2)}) collective-permute-start(f32[160,512]{1,0:T(8,128)S(1)} %shard_map.161._.mine), channel_id=1, source_target_pairs={{0,4},{1,5},{2,6},{3,7},{4,0},{5,1},{6,2},{7,3},{8,12},{9,13},{10,... | collective-permute-start | bytes 983048 | tf_op jit(solution)/shard_map/ppermute | solution.py:510
  103.6 2.2 %collective-permute-done.30.other = f32[192,512]{1,0:T(8,128)S(1)} collective-permute-done((f32[192,512]{1,0:T(8,128)S(1)}, f32[192,512]{1,0:T(8,128)S(1)}, u32[]{:S(2)}, u32[]{:S(2)}) %collective-permute-start.30) | collective-permute-done | bytes 393248 | tf_op jit(solution)/shard_map/ppermute | solution.py:510
  106.5 2.2 %collective-permute-done.22.other = f32[160,512]{1,0:T(8,128)S(1)} collective-permute-done((f32[160,512]{1,0:T(8,128)S(1)}, f32[160,512]{1,0:T(8,128)S(1)}, u32[]{:S(2)}, u32[]{:S(2)}) %collective-permute-start.22) | collective-permute-done | bytes 327712 | tf_op jit(solution)/shard_map/ppermute | solution.py:510
  (87 shorter events, 28.6 us)
Async XLA Ops:
  1.7 10.1 %collective-permute-start = (f32[128,512]{1,0:T(8,128)S(1)}, f32[128,512]{1,0:T(8,128)S(1)}, u32[]{:S(2)}, u32[]{:S(2)}) collective-permute-start(f32[128,512]{1,0:T(8,128)S(1)} %get-tuple-element.210), channel_id=1, source_target_pairs={{0,4},{4,0},{8,12},{12,8},{16,20},{20,16},{24,28},{28,24},{1,5},{5... | collective-permute-start | bytes 786440 | tf_op jit(solution)/shard_map/ppermute | solution.py:490
  4.7 11.9 %collective-permute-start.2 = (f32[128,512]{1,0:T(8,128)S(1)}, f32[128,512]{1,0:T(8,128)S(1)}, u32[]{:S(2)}, u32[]{:S(2)}) collective-permute-start(f32[128,512]{1,0:T(8,128)S(1)} %get-tuple-element.209), channel_id=1, source_target_pairs={{0,4},{4,0},{8,12},{12,8},{16,20},{20,16},{24,28},{28,24},{1,5},{5... | collective-permute-start | bytes 786440 | tf_op jit(solution)/shard_map/ppermute | solution.py:490
  11.8 8.5 %collective-permute-start.1 = (f32[128,512]{1,0:T(8,128)S(1)}, f32[128,512]{1,0:T(8,128)S(1)}, u32[]{:S(2)}, u32[]{:S(2)}) collective-permute-start(f32[128,512]{1,0:T(8,128)S(1)} %collective-permute-done._.patch_0), channel_id=1, source_target_pairs={{0,8},{4,28},{8,16},{12,4},{16,24},{20,12},{24,0},{28,20},{1,9},{5... | collective-permute-start | bytes 786440 | tf_op jit(solution)/shard_map/ppermute | solution.py:490
  16.6 9.3 %collective-permute-start.3 = (f32[128,512]{1,0:T(8,128)S(1)}, f32[128,512]{1,0:T(8,128)S(1)}, u32[]{:S(2)}, u32[]{:S(2)}) collective-permute-start(f32[128,512]{1,0:T(8,128)S(1)} %collective-permute-done.2.patch_1), channel_id=1, source_target_pairs={{0,8},{4,28},{8,16},{12,4},{16,24},{20,12},{24,0},{28,20},{1,9},{5... | collective-permute-start | bytes 786440 | tf_op jit(solution)/shard_map/ppermute | solution.py:490
  33.1 12.5 %collective-permute-start.4 = (f32[256,512]{1,0:T(8,128)S(1)}, f32[256,512]{1,0:T(8,128)S(1)}, u32[]{:S(2)}, u32[]{:S(2)}) collective-permute-start(f32[256,512]{1,0:T(8,128)S(1)} %get-tuple-element.166), channel_id=1, source_target_pairs={{0,24},{4,12},{8,0},{12,20},{16,8},{20,28},{24,16},{28,4},{1,25},{... | collective-permute-start | bytes 1572872 | tf_op jit(solution)/shard_map/ppermute | solution.py:490
  41.4 4.4 %collective-permute-start.5 = (f32[512,512]{1,0:T(8,128)S(1)}, f32[512,512]{1,0:T(8,128)S(1)}, u32[]{:S(2)}, u32[]{:S(2)}) collective-permute-start(f32[512,512]{1,0:T(8,128)S(1)} %get-tuple-element.168), channel_id=1, source_target_pairs={{0,1},{1,0},{2,3},{3,2},{4,5},{5,4},{6,7},{7,6},{8,9},{9,8},{10,11... | collective-permute-start | bytes 3145736 | tf_op jit(solution)/shard_map/ppermute | solution.py:510
  45.8 2.7 %collective-permute-start.6 = (f32[512,512]{1,0:T(8,128)S(1)}, f32[512,512]{1,0:T(8,128)S(1)}, u32[]{:S(2)}, u32[]{:S(2)}) collective-permute-start(f32[512,512]{1,0:T(8,128)S(1)} %get-tuple-element.169), channel_id=1, source_target_pairs={{0,1},{1,0},{2,3},{3,2},{4,5},{5,4},{6,7},{7,6},{8,9},{9,8},{10,11... | collective-permute-start | bytes 3145736 | tf_op jit(solution)/shard_map/ppermute | solution.py:510
  48.8 11.2 %collective-permute-start.24 = (f32[192,512]{1,0:T(8,128)S(1)}, f32[192,512]{1,0:T(8,128)S(1)}, u32[]{:S(2)}, u32[]{:S(2)}) collective-permute-start(f32[192,512]{1,0:T(8,128)S(1)} %get-tuple-element.193), channel_id=1, source_target_pairs={{0,8},{1,9},{2,10},{3,11},{4,12},{5,13},{6,14},{7,15},{8,0},{9,1},... | collective-permute-start | bytes 1179656 | tf_op jit(solution)/shard_map/ppermute | solution.py:510
  49.6 15.0 %collective-permute-start.7 = (f32[160,512]{1,0:T(8,128)S(1)}, f32[160,512]{1,0:T(8,128)S(1)}, u32[]{:S(2)}, u32[]{:S(2)}) collective-permute-start(f32[160,512]{1,0:T(8,128)S(1)} %get-tuple-element.171), channel_id=1, source_target_pairs={{0,4},{1,5},{2,6},{3,7},{4,0},{5,1},{6,2},{7,3},{8,12},{9,13},{10,... | collective-permute-start | bytes 983048 | tf_op jit(solution)/shard_map/ppermute | solution.py:510
  53.5 12.8 %collective-permute-start.13 = (f32[160,512]{1,0:T(8,128)S(1)}, f32[160,512]{1,0:T(8,128)S(1)}, u32[]{:S(2)}, u32[]{:S(2)}) collective-permute-start(f32[160,512]{1,0:T(8,128)S(1)} %get-tuple-element.182), channel_id=1, source_target_pairs={{0,2},{1,3},{2,0},{3,1},{4,6},{5,7},{6,4},{7,5},{8,10},{9,11},{10,... | collective-permute-start | bytes 983048 | tf_op jit(solution)/shard_map/ppermute | solution.py:510
  60.1 8.9 %collective-permute-start.25 = (f32[96,512]{1,0:T(8,128)S(1)}, f32[96,512]{1,0:T(8,128)S(1)}, u32[]{:S(2)}, u32[]{:S(2)}) collective-permute-start(f32[96,512]{1,0:T(8,128)S(1)} %get-tuple-element.195), channel_id=1, source_target_pairs={{0,4},{1,5},{2,6},{3,7},{4,0},{5,1},{6,2},{7,3},{8,12},{9,13},{10,... | collective-permute-start | bytes 589832 | tf_op jit(solution)/shard_map/ppermute | solution.py:510
  64.7 6.0 %collective-permute-start.8 = (f32[80,512]{1,0:T(8,128)S(1)}, f32[80,512]{1,0:T(8,128)S(1)}, u32[]{:S(2)}, u32[]{:S(2)}) collective-permute-start(f32[80,512]{1,0:T(8,128)S(1)} %get-tuple-element.176), channel_id=1, source_target_pairs={{0,2},{1,3},{2,0},{3,1},{4,6},{5,7},{6,4},{7,5},{8,10},{9,11},{10,... | collective-permute-start | bytes 491528 | tf_op jit(solution)/shard_map/ppermute | solution.py:510
  66.3 5.4 %collective-permute-start.14 = (f32[80,512]{1,0:T(8,128)S(1)}, f32[80,512]{1,0:T(8,128)S(1)}, u32[]{:S(2)}, u32[]{:S(2)}) collective-permute-start(f32[80,512]{1,0:T(8,128)S(1)} %get-tuple-element.184), channel_id=1, source_target_pairs={{0,8},{1,9},{2,10},{3,11},{4,12},{5,13},{6,14},{7,15},{8,0},{9,1},... | collective-permute-start | bytes 491528 | tf_op jit(solution)/shard_map/ppermute | solution.py:510
  69.1 4.7 %collective-permute-start.26 = (f32[48,512]{1,0:T(8,128)S(1)}, f32[48,512]{1,0:T(8,128)S(1)}, u32[]{:S(2)}, u32[]{:S(2)}) collective-permute-start(f32[48,512]{1,0:T(8,128)S(1)} %get-tuple-element.197), channel_id=1, source_target_pairs={{0,2},{1,3},{2,0},{3,1},{4,6},{5,7},{6,4},{7,5},{8,10},{9,11},{10,... | collective-permute-start | bytes 294920 | tf_op jit(solution)/shard_map/ppermute | solution.py:510
  70.7 4.5 %collective-permute-start.9 = (f32[40,512]{1,0:T(8,128)S(1)}, f32[40,512]{1,0:T(8,128)S(1)}, u32[]{:S(2)}, u32[]{:S(2)}) collective-permute-start(f32[40,512]{1,0:T(8,128)S(1)} %get-tuple-element.178), channel_id=1, source_target_pairs={{0,8},{1,9},{2,10},{3,11},{4,12},{5,13},{6,14},{7,15},{8,0},{9,1},... | collective-permute-start | bytes 245768 | tf_op jit(solution)/shard_map/ppermute | solution.py:510
  71.8 5.1 %collective-permute-start.15 = (f32[40,512]{1,0:T(8,128)S(1)}, f32[40,512]{1,0:T(8,128)S(1)}, u32[]{:S(2)}, u32[]{:S(2)}) collective-permute-start(f32[40,512]{1,0:T(8,128)S(1)} %get-tuple-element.186), channel_id=1, source_target_pairs={{0,4},{1,5},{2,6},{3,7},{4,0},{5,1},{6,2},{7,3},{8,12},{9,13},{10,... | collective-permute-start | bytes 245768 | tf_op jit(solution)/shard_map/ppermute | solution.py:510
  73.8 8.2 %collective-permute-start.27 = (f32[48,512]{1,0:T(8,128)S(1)}, f32[48,512]{1,0:T(8,128)S(1)}, u32[]{:S(2)}, u32[]{:S(2)}) collective-permute-start(f32[48,512]{1,0:T(8,128)S(1)} %shard_map.173.a), channel_id=1, source_target_pairs={{0,16},{1,17},{2,18},{3,19},{4,20},{5,21},{6,22},{7,23},{8,24},{9,... | collective-permute-start | bytes 294920 | tf_op jit(solution)/shard_map/ppermute | solution.py:510
  75.2 10.4 %collective-permute-start.10 = (f32[40,512]{1,0:T(8,128)S(1)}, f32[40,512]{1,0:T(8,128)S(1)}, u32[]{:S(2)}, u32[]{:S(2)}) collective-permute-start(f32[40,512]{1,0:T(8,128)S(1)} %shard_map.157._.a), channel_id=1, source_target_pairs={{0,16},{1,17},{2,18},{3,19},{4,20},{5,21},{6,22},{7,23},{8,24},{9,... | collective-permute-start | bytes 245768 | tf_op jit(solution)/shard_map/ppermute | solution.py:510
  76.9 19.2 %collective-permute-start.16 = (f32[256,512]{1,0:T(8,128)S(1)}, f32[256,512]{1,0:T(8,128)S(1)}, u32[]{:S(2)}, u32[]{:S(2)}) collective-permute-start(f32[256,512]{1,0:T(8,128)S(1)} %get-tuple-element.188), channel_id=1, source_target_pairs={{0,4},{4,0},{8,12},{12,8},{16,20},{20,16},{24,28},{28,24},{1,5},{5... | collective-permute-start | bytes 1572872 | tf_op jit(solution)/shard_map/ppermute | solution.py:490
  82.0 4.8 %collective-permute-start.28 = (f32[48,512]{1,0:T(8,128)S(1)}, f32[48,512]{1,0:T(8,128)S(1)}, u32[]{:S(2)}, u32[]{:S(2)}) collective-permute-start(f32[48,512]{1,0:T(8,128)S(1)} %shard_map.174.mine), channel_id=1, source_target_pairs={{0,2},{1,3},{2,0},{3,1},{4,6},{5,7},{6,4},{7,5},{8,10},{9,11},{10,... | collective-permute-start | bytes 294920 | tf_op jit(solution)/shard_map/ppermute | solution.py:510
  85.6 5.4 %collective-permute-start.19 = (f32[40,512]{1,0:T(8,128)S(1)}, f32[40,512]{1,0:T(8,128)S(1)}, u32[]{:S(2)}, u32[]{:S(2)}) collective-permute-start(f32[40,512]{1,0:T(8,128)S(1)} %get-tuple-element.190.a), channel_id=1, source_target_pairs={{0,16},{1,17},{2,18},{3,19},{4,20},{5,21},{6,22},{7,23},{8,24},{9,... | collective-permute-start | bytes 245768 | tf_op jit(solution)/shard_map/ppermute | solution.py:510
  85.6 6.9 %collective-permute-start.11 = (f32[40,512]{1,0:T(8,128)S(1)}, f32[40,512]{1,0:T(8,128)S(1)}, u32[]{:S(2)}, u32[]{:S(2)}) collective-permute-start(f32[40,512]{1,0:T(8,128)S(1)} %shard_map.159.mine), channel_id=1, source_target_pairs={{0,8},{1,9},{2,10},{3,11},{4,12},{5,13},{6,14},{7,15},{8,0},{9,1},... | collective-permute-start | bytes 245768 | tf_op jit(solution)/shard_map/ppermute | solution.py:510
  86.8 9.4 %collective-permute-start.29 = (f32[96,512]{1,0:T(8,128)S(1)}, f32[96,512]{1,0:T(8,128)S(1)}, u32[]{:S(2)}, u32[]{:S(2)}) collective-permute-start(f32[96,512]{1,0:T(8,128)S(1)} %shard_map.175.mine), channel_id=1, source_target_pairs={{0,4},{1,5},{2,6},{3,7},{4,0},{5,1},{6,2},{7,3},{8,12},{9,13},{10,... | collective-permute-start | bytes 589832 | tf_op jit(solution)/shard_map/ppermute | solution.py:510
  91.0 5.1 %collective-permute-start.20 = (f32[40,512]{1,0:T(8,128)S(1)}, f32[40,512]{1,0:T(8,128)S(1)}, u32[]{:S(2)}, u32[]{:S(2)}) collective-permute-start(f32[40,512]{1,0:T(8,128)S(1)} %shard_map.167.mine), channel_id=1, source_target_pairs={{0,4},{1,5},{2,6},{3,7},{4,0},{5,1},{6,2},{7,3},{8,12},{9,13},{10,... | collective-permute-start | bytes 245768 | tf_op jit(solution)/shard_map/ppermute | solution.py:510
  92.6 5.8 %collective-permute-start.12 = (f32[80,512]{1,0:T(8,128)S(1)}, f32[80,512]{1,0:T(8,128)S(1)}, u32[]{:S(2)}, u32[]{:S(2)}) collective-permute-start(f32[80,512]{1,0:T(8,128)S(1)} %shard_map.160.mine), channel_id=1, source_target_pairs={{0,2},{1,3},{2,0},{3,1},{4,6},{5,7},{6,4},{7,5},{8,10},{9,11},{10,... | collective-permute-start | bytes 491528 | tf_op jit(solution)/shard_map/ppermute | solution.py:510
  96.1 5.4 %collective-permute-start.21 = (f32[80,512]{1,0:T(8,128)S(1)}, f32[80,512]{1,0:T(8,128)S(1)}, u32[]{:S(2)}, u32[]{:S(2)}) collective-permute-start(f32[80,512]{1,0:T(8,128)S(1)} %shard_map.168.mine), channel_id=1, source_target_pairs={{0,8},{1,9},{2,10},{3,11},{4,12},{5,13},{6,14},{7,15},{8,0},{9,1},... | collective-permute-start | bytes 491528 | tf_op jit(solution)/shard_map/ppermute | solution.py:510
  96.3 9.5 %collective-permute-start.30 = (f32[192,512]{1,0:T(8,128)S(1)}, f32[192,512]{1,0:T(8,128)S(1)}, u32[]{:S(2)}, u32[]{:S(2)}) collective-permute-start(f32[192,512]{1,0:T(8,128)S(1)} %shard_map.176.mine), channel_id=1, source_target_pairs={{0,8},{1,9},{2,10},{3,11},{4,12},{5,13},{6,14},{7,15},{8,0},{9,1},... | collective-permute-start | bytes 1179656 | tf_op jit(solution)/shard_map/ppermute | solution.py:510
  98.4 7.5 %collective-permute-start.17 = (f32[160,512]{1,0:T(8,128)S(1)}, f32[160,512]{1,0:T(8,128)S(1)}, u32[]{:S(2)}, u32[]{:S(2)}) collective-permute-start(f32[160,512]{1,0:T(8,128)S(1)} %shard_map.161._.mine), channel_id=1, source_target_pairs={{0,4},{1,5},{2,6},{3,7},{4,0},{5,1},{6,2},{7,3},{8,12},{9,13},{10,... | collective-permute-start | bytes 983048 | tf_op jit(solution)/shard_map/ppermute | solution.py:510
  101.6 7.1 %collective-permute-start.22 = (f32[160,512]{1,0:T(8,128)S(1)}, f32[160,512]{1,0:T(8,128)S(1)}, u32[]{:S(2)}, u32[]{:S(2)}) collective-permute-start(f32[160,512]{1,0:T(8,128)S(1)} %shard_map.169.mine), channel_id=1, source_target_pairs={{0,2},{1,3},{2,0},{3,1},{4,6},{5,7},{6,4},{7,5},{8,10},{9,11},{10,... | collective-permute-start | bytes 983048 | tf_op jit(solution)/shard_map/ppermute | solution.py:510
  105.8 5.1 %collective-permute-start.31 = (f32[384,512]{1,0:T(8,128)S(1)}, f32[384,512]{1,0:T(8,128)S(1)}, u32[]{:S(2)}, u32[]{:S(2)}) collective-permute-start(f32[384,512]{1,0:T(8,128)S(1)} %shard_map.177.refs_2_), channel_id=1, source_target_pairs={{0,1},{1,0},{2,3},{3,2},{4,5},{5,4},{6,7},{7,6},{8,9},{9,8},{10,11... | collective-permute-start | bytes 2359304 | tf_op jit(solution)/shard_map/ppermute | solution.py:510
  106.0 4.3 %collective-permute-start.18 = (f32[320,512]{1,0:T(8,128)S(1)}, f32[320,512]{1,0:T(8,128)S(1)}, u32[]{:S(2)}, u32[]{:S(2)}) collective-permute-start(f32[320,512]{1,0:T(8,128)S(1)} %shard_map.166.refs_0_), channel_id=1, source_target_pairs={{0,1},{1,0},{2,3},{3,2},{4,5},{5,4},{6,7},{7,6},{8,9},{9,8},{10,11... | collective-permute-start | bytes 1966088 | tf_op jit(solution)/shard_map/ppermute | solution.py:510
  108.8 2.2 %collective-permute-start.23 = (f32[320,512]{1,0:T(8,128)S(1)}, f32[320,512]{1,0:T(8,128)S(1)}, u32[]{:S(2)}, u32[]{:S(2)}) collective-permute-start(f32[320,512]{1,0:T(8,128)S(1)} %shard_map.170.refs_1_), channel_id=1, source_target_pairs={{0,1},{1,0},{2,3},{3,2},{4,5},{5,4},{6,7},{7,6},{8,9},{9,8},{10,11... | collective-permute-start | bytes 1966088 | tf_op jit(solution)/shard_map/ppermute | solution.py:510
  (9 other events, 26.2 us)

commit v6 on v5

--- a/solution.py
+++ b/solution.py
@@ -329,8 +329,13 @@
     grad_k[...] = sums_of(turned, d_keys)
 
 
-def core_kernel(me, grad_q, grad_k, _keep, _back, keep, *sends):
+def core_kernel(me, grad_q, grad_k, _keep, keep, *sends):
     kept_and_sent(me, (grad_q, grad_k), keep, sends)
+
+
+def arrive_kernel(a, out, mark):
+    mark[...] = jnp.zeros_like(mark)
+    out[...] = a[...]
 
 
 def side_kernel(
@@ -358,7 +363,7 @@
     out[...] = a[...] + b[...]
 
 
-def cut_kernel(masks, me, keep_1, keep_2, *refs):
+def cut_kernel(masks, me, keep_1, keep_2, _, *refs):
     others, outs, sums = refs[: 2 * PIECES], refs[2 * PIECES : -1], refs[-1]
     rows = others[0].shape[0]
     for i, other in enumerate(others):
@@ -514,7 +519,7 @@
 LAST = 16
 
 
-def summed(me, keep_1, others_1, keep_2, others_2, weights, gain, result_of, side_of, tokens_of):
+def summed(me, keep_1, others_1, keep_2, others_2, mark, weights, gain, result_of, side_of, tokens_of):
     count, width = keep_1.shape
     total = 2 * count
     unit = 8 * 8
@@ -522,7 +527,7 @@
     sizes.append(total - sum(sizes))
     parts = call(
         functools.partial(cut_kernel, [order[0] for order in ORDERS]),
-        (me, keep_1, keep_2, *others_1, *others_2),
+        (me, keep_1, keep_2, mark, *others_1, *others_2),
         [shape(size // 2, width) for size in sizes for _ in range(2)],
         [shape(total, width)],
         scalars=1, limit=8,
@@ -640,7 +645,7 @@
         ),
         [whole_t, *pairs(2 * rows, width), *pairs(2 * rows, width)],
         [*pairs(2, 2 * rows, rows), *turned],
-        limit=LIMITS[4], us=1,
+        limit=LIMITS[4], us=0.001,
     )
     pieces = [shape(width // PIECES, width)] * PIECES
     ht3_h, ht3_l, keep_1, *sends_1 = call(
@@ -648,19 +653,20 @@
         (me, mixed_t, ht_h, ht_l, ht2_h, ht2_l, hidden3, dv_h, dv_l, dv3_h, dv3_l, cotangent),
         [*turned, shape(width, width), *pieces],
         [shape(width, width), shape(width, width)],
-        scalars=1, limit=LIMITS[3], us=1,
+        scalars=1, limit=LIMITS[3], us=0.001,
     )
     others_1 = [swapped(send, 1) for send in sends_1]
     grad_q, grad_k, dq_h, dq_l = call(
         grad_kernel,
         (ht_h, ht_l, ht2_h, ht2_l, ht3_h, ht3_l, dq_t, dk_h, dk_l, dk3_h, dk3_l),
         [shape(width, width), shape(width, width), *pair],
-        limit=LIMITS[5], us=1,
+        limit=LIMITS[5], us=0.001,
     )
     keep_2, *sends_2 = call(
-        core_kernel, (me, grad_q, grad_k, keep_1, d_back), [shape(width, width), *pieces], scalars=1, limit=8, us=1
+        core_kernel, (me, grad_q, grad_k, keep_1), [shape(width, width), *pieces], scalars=1, limit=8, us=0.001
     )
     others_2 = [swapped(send, 1) for send in sends_2]
+    d_back, mark = call(arrive_kernel, (d_back,), [whole, MARK], us=20)
 
     def result_of(place):
         return call(result_kernel, (place, mixed_t, tokens, wo_h, wo_l), [whole, MARK], limit=LIMITS[3], us=1)
@@ -674,7 +680,7 @@
         return call(tokens_kernel, inputs, [whole, MARK], limit=8)
 
     (grad_o, grad_v, grad_q, grad_k), d_gain, d_tokens, result = summed(
-        me, keep_1, others_1, keep_2, others_2, (wv_h, wv_l, wq_h, wq_l, *w_k), gain_row, result_of, side_of, tokens_of
+        me, keep_1, others_1, keep_2, others_2, mark, (wv_h, wv_l, wq_h, wq_l, *w_k), gain_row, result_of, side_of, tokens_of
     )
     return (result, d_tokens, d_gain, grad_q, grad_k, grad_v, grad_o)
 

time: 113 us -> 109 us (0.965)
  waiting for transfers between devices: 32.3 us -> 29.3 us
    ppermute x26, waiting for transfers between devices: 26.9 us -> 24.5 us  [swapped(): lax.ppermute(value, ('space', 'slab'), [(i, i ^ mask) for i in range(devi...]
    pallas_call x34 -> x35, Pallas kernels: 30.1 us -> 30.2 us  [call(): pl.pallas_call(kernel, out_shape=outputs, in_specs=[SMEM] * scalars + [VM...]
  transfers between devices with their start and end apart: 32 -> 32, of which waited for: 19 -> 16; matrix products, arithmetic and copies ran while one was open for 0% -> 0% of each run, Pallas kernels for 21% -> 22%
where the time goes in v6:
time: 109 us
  starting transfers between devices  39.9 us (37%)
  Pallas kernels  32.9 us (30%)
  waiting for transfers between devices  29.3 us (27%)
  local copies, waits for them, and re-layouts  5.99 us (5%)
    pallas_call x35, Pallas kernels, call(): pl.pallas_call(kernel, out_shape=outputs, in_specs=[SMEM] * scalars + [VM...  30.2 us
    ppermute x26, starting transfers between devices, swapped(): lax.ppermute(value, ('space', 'slab'), [(i, i ^ mask) for i in range(devi...  28.9 us
    ppermute x26, waiting for transfers between devices, swapped(): lax.ppermute(value, ('space', 'slab'), [(i, i ^ mask) for i in range(devi...  24.5 us
    ppermute x6, starting transfers between devices, along_space(): lax.ppermute(value, 'space', [(i, target(i) % count) for i in range(count)])  11 us
    unnamed x18, local copies, waits for them, and re-layouts  4.92 us
    ppermute x6, waiting for transfers between devices, along_space(): lax.ppermute(value, 'space', [(i, target(i) % count) for i in range(count)])  4.74 us
    pallas_call x2, Pallas kernels, written(): pl.pallas_call(functools.partial(write_kernel, ranges, core), out_shape=[...  2.73 us
  transfers between devices with their start and end apart: 32, of which 16 were waited for; matrix products, arithmetic and copies ran while one was open for 0% of the time, Pallas kernels for 22%

profile of v6, /device:TPU:0, one launch (start us, length us, event | category | flops | bytes accessed | tf_op | source)
XLA Modules:
  0.0 109.1 jit_solution(2214714045574677028)
XLA Ops:
  1.7 3.0 %collective-permute-start = (f32[128,512]{1,0:T(8,128)S(1)}, f32[128,512]{1,0:T(8,128)S(1)}, u32[]{:S(2)}, u32[]{:S(2)}) collective-permute-start(f32[128,512]{1,0:T(8,128)S(1)} %get-tuple-element.214), channel_id=1, source_target_pairs={{0,4},{4,0},{8,12},{12,8},{16,20},{20,16},{24,28},{28,24},{1,5},{5... | collective-permute-start | bytes 786440 | tf_op jit(solution)/shard_map/ppermute | solution.py:495
  10.3 1.5 %collective-permute-done._.patch_0 = f32[128,512]{1,0:T(8,128)S(1)} collective-permute-done((f32[128,512]{1,0:T(8,128)S(1)}, f32[128,512]{1,0:T(8,128)S(1)}, u32[]{:S(2)}, u32[]{:S(2)}) %collective-permute-start) | collective-permute-done | bytes 262176 | tf_op jit(solution)/shard_map/ppermute | solution.py:495
  11.8 2.1 %collective-permute-start.1 = (f32[128,512]{1,0:T(8,128)S(1)}, f32[128,512]{1,0:T(8,128)S(1)}, u32[]{:S(2)}, u32[]{:S(2)}) collective-permute-start(f32[128,512]{1,0:T(8,128)S(1)} %collective-permute-done._.patch_0), channel_id=1, source_target_pairs={{0,8},{4,28},{8,16},{12,4},{16,24},{20,12},{24,0},{28,20},{1,9},{5... | collective-permute-start | bytes 786440 | tf_op jit(solution)/shard_map/ppermute | solution.py:495
  14.0 2.1 %shard_map.145 = (bf16[512,256]{1,0:T(8,128)(2,1)S(1)}, bf16[512,256]{1,0:T(8,128)(2,1)S(1)}, f32[512,256]{1,0:T(8,128)S(1)}, bf16[2048,256]{1,0:T(8,128)(2,1)S(...) custom-call(f32[128,512]{1,0:T(8,128)S(1)} %collective-permute-done., ...), custom_call_target="tpu_custom_call" | custom-call | flops 1000000000 | tf_op jit(solution)/shard_map/pallas_call | solution.py:479
  16.6 1.8 %collective-permute-start.3 = (f32[128,512]{1,0:T(8,128)S(1)}, f32[128,512]{1,0:T(8,128)S(1)}, u32[]{:S(2)}, u32[]{:S(2)}) collective-permute-start(f32[128,512]{1,0:T(8,128)S(1)} %collective-permute-done.2.patch_1), channel_id=1, source_target_pairs={{0,8},{4,28},{8,16},{12,4},{16,24},{20,12},{24,0},{28,20},{1,9},{5... | collective-permute-start | bytes 786440 | tf_op jit(solution)/shard_map/ppermute | solution.py:495
  18.5 1.6 %shard_map.146 = (bf16[512,256]{1,0:T(8,128)(2,1)S(1)}, bf16[512,256]{1,0:T(8,128)(2,1)S(1)}, bf16[512,256]{1,0:T(8,128)(2,1)S(1)}, bf16[512,256]{1,0:T(8,128)(2...) custom-call(f32[128,512]{1,0:T(8,128)S(1)} %collective-permute-done., ...), custom_call_target="tpu_custom_call" | custom-call | flops 1000000000 | tf_op jit(solution)/shard_map/pallas_call | solution.py:479
  20.4 4.7 %shard_map.147 = (bf16[8,512,256]{2,1,0:T(8,128)(2,1)S(1)}, bf16[8,512,256]{2,1,0:T(8,128)(2,1)S(1)}, f32[8,512,256]{2,1,0:T(8,128)S(1)}, f32[512,256]{1,0:T(8,1...) custom-call(s32[1]{0:T(128)} %bitcast.1._parity.parity, s32[2,3]{1,0:T(2,128)S(1)} %copy-done.7, ...), custom_call_target="tpu_custom_call" | custom-call | flops 1000000000 | tf_op jit(solution)/shard_map/pallas_call | solution.py:479
  26.0 7.2 %shard_map.148 = (f32[256,512]{1,0:T(8,128)S(1)}, f32[256,512]{1,0:T(8,128)S(1)}, bf16[8,256,256]{2,1,0:T(8,128)(2,1)S(1)}, bf16[8,256,256]{2,1,0:T(8,128)(2,1)S...) custom-call(s32[1]{0:T(128)} %bitcast.1._parity.parity, ...), custom_call_target="tpu_custom_call" | custom-call | flops 1000000000 | tf_op jit(solution)/shard_map/pallas_call | solution.py:479
  33.2 2.3 %collective-permute-start.4 = (f32[256,512]{1,0:T(8,128)S(1)}, f32[256,512]{1,0:T(8,128)S(1)}, u32[]{:S(2)}, u32[]{:S(2)}) collective-permute-start(f32[256,512]{1,0:T(8,128)S(1)} %get-tuple-element.169), channel_id=1, source_target_pairs={{0,24},{4,12},{8,0},{12,20},{16,8},{20,28},{24,16},{28,4},{1,25},{... | collective-permute-start | bytes 1572872 | tf_op jit(solution)/shard_map/ppermute | solution.py:495
  35.5 4.0 %shard_map.149 = (f32[512,256]{1,0:T(8,128)S(1)}, bf16[512,512]{1,0:T(8,128)(2,1)S(1)}, bf16[512,512]{1,0:T(8,128)(2,1)S(1)}, bf16[512,512]{1,0:T(8,128)(2,1)S(1)}, bf16[512,512]{1,0:T(8,128)(2,1)S(1)}) custom-call(f32[512,256]{1,0:T(8,128)S(1)} %get-tuple-element.120.q_t, f32[512,256]{1,0:T(8,128)S(1)} %get-tuple-element.122.d_mixed_t, ...), custom_call_target="tpu_custom_call" | custom-call | flops 1000000 | tf_op jit(solution)/shard_map/pallas_call | solution.py:479
  39.5 1.9 %shard_map.150 = (bf16[512,256]{1,0:T(8,128)(2,1)S(1)}, bf16[512,256]{1,0:T(8,128)(2,1)S(1)}, f32[512,512]{1,0:T(8,128)S(1)}, f32[512,512]{1,0:T(8,128)S(1)}) custom-call(s32[1]{0:T(128)} %bitcast._me.me, f32[512,256]{1,0:T(8,128)S(1)} %get-tuple-element.135.mixed_t, bf16[512,256]{1,0:T(8,128)(2,1)S(1)} %get-tuple-element.136.ht_h, ...), custom_call_target="tpu_custom_call" | custom-call | flops 1000000 | tf_op jit(solution)/shard_map/pallas_call | solution.py:479
  41.4 2.0 %shard_map.151 = (f32[512,512]{1,0:T(8,128)S(1)}, f32[512,512]{1,0:T(8,128)S(1)}, bf16[256,512]{1,0:T(8,128)(2,1)S(1)}, bf16[256,512]{1,0:T(8,128)(2,1)S(1)}) custom-call(bf16[512,256]{1,0:T(8,128)(2,1)S(1)} %get-tuple-element.136.ht_h, bf16[512,256]{1,0:T(8,128)(2,1)S(1)} %get-tuple-element.137.ht_l, bf16[512,256]{1,0:T(8,128)(2,1)S(1)} %get-tuple-element.138.ht2_h, ...), custom_call_target="tpu_custom_call" | custom-call | flops 1000000 | tf_op jit(solution)/shard_map/pallas_call | solution.py:479
  46.3 1.5 %collective-permute-done.5.refs_0_ = f32[512,512]{1,0:T(8,128)S(1)} collective-permute-done((f32[512,512]{1,0:T(8,128)S(1)}, f32[512,512]{1,0:T(8,128)S(1)}, u32[]{:S(2)}, u32[]{:S(2)}) %collective-permute-start.5) | collective-permute-done | bytes 1048608 | tf_op jit(solution)/shard_map/ppermute | solution.py:515
  48.3 2.4 %collective-permute-start.7 = (f32[160,512]{1,0:T(8,128)S(1)}, f32[160,512]{1,0:T(8,128)S(1)}, u32[]{:S(2)}, u32[]{:S(2)}) collective-permute-start(f32[160,512]{1,0:T(8,128)S(1)} %get-tuple-element.174), channel_id=1, source_target_pairs={{0,4},{1,5},{2,6},{3,7},{4,0},{5,1},{6,2},{7,3},{8,12},{9,13},{10,... | collective-permute-start | bytes 983048 | tf_op jit(solution)/shard_map/ppermute | solution.py:515
  50.7 1.5 %collective-permute-start.13 = (f32[160,512]{1,0:T(8,128)S(1)}, f32[160,512]{1,0:T(8,128)S(1)}, u32[]{:S(2)}, u32[]{:S(2)}) collective-permute-start(f32[160,512]{1,0:T(8,128)S(1)} %get-tuple-element.186), channel_id=1, source_target_pairs={{0,2},{1,3},{2,0},{3,1},{4,6},{5,7},{6,4},{7,5},{8,10},{9,11},{10,... | collective-permute-start | bytes 983048 | tf_op jit(solution)/shard_map/ppermute | solution.py:515
  52.2 2.2 %shard_map.155 = (f32[256,512]{1,0:T(8,128)S(1)}, f32[256,512]{1,0:T(8,128)S(1)}, f32[8,128]{1,0:T(8,128)S(1)}) custom-call(f32[160,512]{1,0:T(8,128)S(1)} %get-tuple-element.173._.keep, f32[256,512]{1,0:T(8,128)S(1)} %get-tuple-element.175.d_back, bf16[256,512]{1,0:T(8,128)(2,1)S(1)} %get-tuple-element.176.dq_h, ...), custom_call_target="tpu_custom_call" | custom-call | flops 1000000000 | tf_op jit(solution)/shard_map/pallas_call | solution.py:479
  54.5 5.0 %collective-permute-done.24.other = f32[192,512]{1,0:T(8,128)S(1)} collective-permute-done((f32[192,512]{1,0:T(8,128)S(1)}, f32[192,512]{1,0:T(8,128)S(1)}, u32[]{:S(2)}, u32[]{:S(2)}) %collective-permute-start.24) | collective-permute-done | bytes 393248 | tf_op jit(solution)/shard_map/ppermute | solution.py:515
  59.9 1.6 %collective-permute-start.8 = (f32[80,512]{1,0:T(8,128)S(1)}, f32[80,512]{1,0:T(8,128)S(1)}, u32[]{:S(2)}, u32[]{:S(2)}) collective-permute-start(f32[80,512]{1,0:T(8,128)S(1)} %get-tuple-element.180), channel_id=1, source_target_pairs={{0,2},{1,3},{2,0},{3,1},{4,6},{5,7},{6,4},{7,5},{8,10},{9,11},{10,... | collective-permute-start | bytes 491528 | tf_op jit(solution)/shard_map/ppermute | solution.py:515
  62.3 3.3 %collective-permute-done.25.other = f32[96,512]{1,0:T(8,128)S(1)} collective-permute-done((f32[96,512]{1,0:T(8,128)S(1)}, f32[96,512]{1,0:T(8,128)S(1)}, u32[]{:S(2)}, u32[]{:S(2)}) %collective-permute-start.25) | collective-permute-done | bytes 196640 | tf_op jit(solution)/shard_map/ppermute | solution.py:515
  65.7 1.6 %collective-permute-start.26 = (f32[48,512]{1,0:T(8,128)S(1)}, f32[48,512]{1,0:T(8,128)S(1)}, u32[]{:S(2)}, u32[]{:S(2)}) collective-permute-start(f32[48,512]{1,0:T(8,128)S(1)} %get-tuple-element.201), channel_id=1, source_target_pairs={{0,2},{1,3},{2,0},{3,1},{4,6},{5,7},{6,4},{7,5},{8,10},{9,11},{10,... | collective-permute-start | bytes 294920 | tf_op jit(solution)/shard_map/ppermute | solution.py:515
  70.4 2.2 %collective-permute-start.27 = (f32[48,512]{1,0:T(8,128)S(1)}, f32[48,512]{1,0:T(8,128)S(1)}, u32[]{:S(2)}, u32[]{:S(2)}) collective-permute-start(f32[48,512]{1,0:T(8,128)S(1)} %shard_map.174.a), channel_id=1, source_target_pairs={{0,16},{1,17},{2,18},{3,19},{4,20},{5,21},{6,22},{7,23},{8,24},{9,... | collective-permute-start | bytes 294920 | tf_op jit(solution)/shard_map/ppermute | solution.py:515
  72.6 1.6 %collective-permute-start.10 = (f32[40,512]{1,0:T(8,128)S(1)}, f32[40,512]{1,0:T(8,128)S(1)}, u32[]{:S(2)}, u32[]{:S(2)}) collective-permute-start(f32[40,512]{1,0:T(8,128)S(1)} %shard_map.158._.a), channel_id=1, source_target_pairs={{0,16},{1,17},{2,18},{3,19},{4,20},{5,21},{6,22},{7,23},{8,24},{9,... | collective-permute-start | bytes 245768 | tf_op jit(solution)/shard_map/ppermute | solution.py:515
  74.2 1.7 %collective-permute-start.16 = (f32[256,512]{1,0:T(8,128)S(1)}, f32[256,512]{1,0:T(8,128)S(1)}, u32[]{:S(2)}, u32[]{:S(2)}) collective-permute-start(f32[256,512]{1,0:T(8,128)S(1)} %get-tuple-element.192), channel_id=1, source_target_pairs={{0,4},{4,0},{8,12},{12,8},{16,20},{20,16},{24,28},{28,24},{1,5},{5... | collective-permute-start | bytes 1572872 | tf_op jit(solution)/shard_map/ppermute | solution.py:495
  75.8 2.6 %collective-permute-done.27.b = f32[48,512]{1,0:T(8,128)S(1)} collective-permute-done((f32[48,512]{1,0:T(8,128)S(1)}, f32[48,512]{1,0:T(8,128)S(1)}, u32[]{:S(2)}, u32[]{:S(2)}) %collective-permute-start.27) | collective-permute-done | bytes 98336 | tf_op jit(solution)/shard_map/ppermute | solution.py:515
  81.2 3.2 %collective-permute-start.11 = (f32[40,512]{1,0:T(8,128)S(1)}, f32[40,512]{1,0:T(8,128)S(1)}, u32[]{:S(2)}, u32[]{:S(2)}) collective-permute-start(f32[40,512]{1,0:T(8,128)S(1)} %shard_map.160.mine), channel_id=1, source_target_pairs={{0,8},{1,9},{2,10},{3,11},{4,12},{5,13},{6,14},{7,15},{8,0},{9,1},... | collective-permute-start | bytes 245768 | tf_op jit(solution)/shard_map/ppermute | solution.py:515
  84.4 2.5 %collective-permute-start.29 = (f32[96,512]{1,0:T(8,128)S(1)}, f32[96,512]{1,0:T(8,128)S(1)}, u32[]{:S(2)}, u32[]{:S(2)}) collective-permute-start(f32[96,512]{1,0:T(8,128)S(1)} %shard_map.176.mine), channel_id=1, source_target_pairs={{0,4},{1,5},{2,6},{3,7},{4,0},{5,1},{6,2},{7,3},{8,12},{9,13},{10,... | collective-permute-start | bytes 589832 | tf_op jit(solution)/shard_map/ppermute | solution.py:515
  88.6 2.9 %collective-permute-done.20.other = f32[40,512]{1,0:T(8,128)S(1)} collective-permute-done((f32[40,512]{1,0:T(8,128)S(1)}, f32[40,512]{1,0:T(8,128)S(1)}, u32[]{:S(2)}, u32[]{:S(2)}) %collective-permute-start.20) | collective-permute-done | bytes 81952 | tf_op jit(solution)/shard_map/ppermute | solution.py:515
  91.9 1.8 %collective-permute-start.30 = (f32[192,512]{1,0:T(8,128)S(1)}, f32[192,512]{1,0:T(8,128)S(1)}, u32[]{:S(2)}, u32[]{:S(2)}) collective-permute-start(f32[192,512]{1,0:T(8,128)S(1)} %shard_map.177.mine), channel_id=1, source_target_pairs={{0,8},{1,9},{2,10},{3,11},{4,12},{5,13},{6,14},{7,15},{8,0},{9,1},... | collective-permute-start | bytes 1179656 | tf_op jit(solution)/shard_map/ppermute | solution.py:515
  93.7 2.1 %collective-permute-start.17 = (f32[160,512]{1,0:T(8,128)S(1)}, f32[160,512]{1,0:T(8,128)S(1)}, u32[]{:S(2)}, u32[]{:S(2)}) collective-permute-start(f32[160,512]{1,0:T(8,128)S(1)} %shard_map.162._.mine), channel_id=1, source_target_pairs={{0,4},{1,5},{2,6},{3,7},{4,0},{5,1},{6,2},{7,3},{8,12},{9,13},{10,... | collective-permute-start | bytes 983048 | tf_op jit(solution)/shard_map/ppermute | solution.py:515
  95.8 2.3 %collective-permute-done.21.other = f32[80,512]{1,0:T(8,128)S(1)} collective-permute-done((f32[80,512]{1,0:T(8,128)S(1)}, f32[80,512]{1,0:T(8,128)S(1)}, u32[]{:S(2)}, u32[]{:S(2)}) %collective-permute-start.21) | collective-permute-done | bytes 163872 | tf_op jit(solution)/shard_map/ppermute | solution.py:515
  100.3 2.1 %collective-permute-done.30.other = f32[192,512]{1,0:T(8,128)S(1)} collective-permute-done((f32[192,512]{1,0:T(8,128)S(1)}, f32[192,512]{1,0:T(8,128)S(1)}, u32[]{:S(2)}, u32[]{:S(2)}) %collective-permute-start.30) | collective-permute-done | bytes 393248 | tf_op jit(solution)/shard_map/ppermute | solution.py:515
  103.1 2.2 %collective-permute-done.22.other = f32[160,512]{1,0:T(8,128)S(1)} collective-permute-done((f32[160,512]{1,0:T(8,128)S(1)}, f32[160,512]{1,0:T(8,128)S(1)}, u32[]{:S(2)}, u32[]{:S(2)}) %collective-permute-start.22) | collective-permute-done | bytes 327712 | tf_op jit(solution)/shard_map/ppermute | solution.py:515
  (88 shorter events, 27.6 us)
Async XLA Ops:
  1.7 10.1 %collective-permute-start = (f32[128,512]{1,0:T(8,128)S(1)}, f32[128,512]{1,0:T(8,128)S(1)}, u32[]{:S(2)}, u32[]{:S(2)}) collective-permute-start(f32[128,512]{1,0:T(8,128)S(1)} %get-tuple-element.214), channel_id=1, source_target_pairs={{0,4},{4,0},{8,12},{12,8},{16,20},{20,16},{24,28},{28,24},{1,5},{5... | collective-permute-start | bytes 786440 | tf_op jit(solution)/shard_map/ppermute | solution.py:495
  4.7 11.9 %collective-permute-start.2 = (f32[128,512]{1,0:T(8,128)S(1)}, f32[128,512]{1,0:T(8,128)S(1)}, u32[]{:S(2)}, u32[]{:S(2)}) collective-permute-start(f32[128,512]{1,0:T(8,128)S(1)} %get-tuple-element.213), channel_id=1, source_target_pairs={{0,4},{4,0},{8,12},{12,8},{16,20},{20,16},{24,28},{28,24},{1,5},{5... | collective-permute-start | bytes 786440 | tf_op jit(solution)/shard_map/ppermute | solution.py:495
  11.8 8.5 %collective-permute-start.1 = (f32[128,512]{1,0:T(8,128)S(1)}, f32[128,512]{1,0:T(8,128)S(1)}, u32[]{:S(2)}, u32[]{:S(2)}) collective-permute-start(f32[128,512]{1,0:T(8,128)S(1)} %collective-permute-done._.patch_0), channel_id=1, source_target_pairs={{0,8},{4,28},{8,16},{12,4},{16,24},{20,12},{24,0},{28,20},{1,9},{5... | collective-permute-start | bytes 786440 | tf_op jit(solution)/shard_map/ppermute | solution.py:495
  16.6 9.3 %collective-permute-start.3 = (f32[128,512]{1,0:T(8,128)S(1)}, f32[128,512]{1,0:T(8,128)S(1)}, u32[]{:S(2)}, u32[]{:S(2)}) collective-permute-start(f32[128,512]{1,0:T(8,128)S(1)} %collective-permute-done.2.patch_1), channel_id=1, source_target_pairs={{0,8},{4,28},{8,16},{12,4},{16,24},{20,12},{24,0},{28,20},{1,9},{5... | collective-permute-start | bytes 786440 | tf_op jit(solution)/shard_map/ppermute | solution.py:495
  33.2 12.5 %collective-permute-start.4 = (f32[256,512]{1,0:T(8,128)S(1)}, f32[256,512]{1,0:T(8,128)S(1)}, u32[]{:S(2)}, u32[]{:S(2)}) collective-permute-start(f32[256,512]{1,0:T(8,128)S(1)} %get-tuple-element.169), channel_id=1, source_target_pairs={{0,24},{4,12},{8,0},{12,20},{16,8},{20,28},{24,16},{28,4},{1,25},{... | collective-permute-start | bytes 1572872 | tf_op jit(solution)/shard_map/ppermute | solution.py:495
  43.6 2.7 %collective-permute-start.6 = (f32[512,512]{1,0:T(8,128)S(1)}, f32[512,512]{1,0:T(8,128)S(1)}, u32[]{:S(2)}, u32[]{:S(2)}) collective-permute-start(f32[512,512]{1,0:T(8,128)S(1)} %get-tuple-element.172), channel_id=1, source_target_pairs={{0,1},{1,0},{2,3},{3,2},{4,5},{5,4},{6,7},{7,6},{8,9},{9,8},{10,11... | collective-permute-start | bytes 3145736 | tf_op jit(solution)/shard_map/ppermute | solution.py:515
  43.6 4.1 %collective-permute-start.5 = (f32[512,512]{1,0:T(8,128)S(1)}, f32[512,512]{1,0:T(8,128)S(1)}, u32[]{:S(2)}, u32[]{:S(2)}) collective-permute-start(f32[512,512]{1,0:T(8,128)S(1)} %get-tuple-element.171), channel_id=1, source_target_pairs={{0,1},{1,0},{2,3},{3,2},{4,5},{5,4},{6,7},{7,6},{8,9},{9,8},{10,11... | collective-permute-start | bytes 3145736 | tf_op jit(solution)/shard_map/ppermute | solution.py:515
  48.2 11.2 %collective-permute-start.24 = (f32[192,512]{1,0:T(8,128)S(1)}, f32[192,512]{1,0:T(8,128)S(1)}, u32[]{:S(2)}, u32[]{:S(2)}) collective-permute-start(f32[192,512]{1,0:T(8,128)S(1)} %get-tuple-element.197), channel_id=1, source_target_pairs={{0,8},{1,9},{2,10},{3,11},{4,12},{5,13},{6,14},{7,15},{8,0},{9,1},... | collective-permute-start | bytes 1179656 | tf_op jit(solution)/shard_map/ppermute | solution.py:515
  48.3 11.6 %collective-permute-start.7 = (f32[160,512]{1,0:T(8,128)S(1)}, f32[160,512]{1,0:T(8,128)S(1)}, u32[]{:S(2)}, u32[]{:S(2)}) collective-permute-start(f32[160,512]{1,0:T(8,128)S(1)} %get-tuple-element.174), channel_id=1, source_target_pairs={{0,4},{1,5},{2,6},{3,7},{4,0},{5,1},{6,2},{7,3},{8,12},{9,13},{10,... | collective-permute-start | bytes 983048 | tf_op jit(solution)/shard_map/ppermute | solution.py:515
  50.7 10.8 %collective-permute-start.13 = (f32[160,512]{1,0:T(8,128)S(1)}, f32[160,512]{1,0:T(8,128)S(1)}, u32[]{:S(2)}, u32[]{:S(2)}) collective-permute-start(f32[160,512]{1,0:T(8,128)S(1)} %get-tuple-element.186), channel_id=1, source_target_pairs={{0,2},{1,3},{2,0},{3,1},{4,6},{5,7},{6,4},{7,5},{8,10},{9,11},{10,... | collective-permute-start | bytes 983048 | tf_op jit(solution)/shard_map/ppermute | solution.py:515
  59.5 6.2 %collective-permute-start.25 = (f32[96,512]{1,0:T(8,128)S(1)}, f32[96,512]{1,0:T(8,128)S(1)}, u32[]{:S(2)}, u32[]{:S(2)}) collective-permute-start(f32[96,512]{1,0:T(8,128)S(1)} %get-tuple-element.199), channel_id=1, source_target_pairs={{0,4},{1,5},{2,6},{3,7},{4,0},{5,1},{6,2},{7,3},{8,12},{9,13},{10,... | collective-permute-start | bytes 589832 | tf_op jit(solution)/shard_map/ppermute | solution.py:515
  59.9 7.3 %collective-permute-start.8 = (f32[80,512]{1,0:T(8,128)S(1)}, f32[80,512]{1,0:T(8,128)S(1)}, u32[]{:S(2)}, u32[]{:S(2)}) collective-permute-start(f32[80,512]{1,0:T(8,128)S(1)} %get-tuple-element.180), channel_id=1, source_target_pairs={{0,2},{1,3},{2,0},{3,1},{4,6},{5,7},{6,4},{7,5},{8,10},{9,11},{10,... | collective-permute-start | bytes 491528 | tf_op jit(solution)/shard_map/ppermute | solution.py:515
  61.5 6.1 %collective-permute-start.14 = (f32[80,512]{1,0:T(8,128)S(1)}, f32[80,512]{1,0:T(8,128)S(1)}, u32[]{:S(2)}, u32[]{:S(2)}) collective-permute-start(f32[80,512]{1,0:T(8,128)S(1)} %get-tuple-element.188), channel_id=1, source_target_pairs={{0,8},{1,9},{2,10},{3,11},{4,12},{5,13},{6,14},{7,15},{8,0},{9,1},... | collective-permute-start | bytes 491528 | tf_op jit(solution)/shard_map/ppermute | solution.py:515
  65.7 4.7 %collective-permute-start.26 = (f32[48,512]{1,0:T(8,128)S(1)}, f32[48,512]{1,0:T(8,128)S(1)}, u32[]{:S(2)}, u32[]{:S(2)}) collective-permute-start(f32[48,512]{1,0:T(8,128)S(1)} %get-tuple-element.201), channel_id=1, source_target_pairs={{0,2},{1,3},{2,0},{3,1},{4,6},{5,7},{6,4},{7,5},{8,10},{9,11},{10,... | collective-permute-start | bytes 294920 | tf_op jit(solution)/shard_map/ppermute | solution.py:515
  67.3 5.3 %collective-permute-start.9 = (f32[40,512]{1,0:T(8,128)S(1)}, f32[40,512]{1,0:T(8,128)S(1)}, u32[]{:S(2)}, u32[]{:S(2)}) collective-permute-start(f32[40,512]{1,0:T(8,128)S(1)} %get-tuple-element.182), channel_id=1, source_target_pairs={{0,8},{1,9},{2,10},{3,11},{4,12},{5,13},{6,14},{7,15},{8,0},{9,1},... | collective-permute-start | bytes 245768 | tf_op jit(solution)/shard_map/ppermute | solution.py:515
  67.7 6.4 %collective-permute-start.15 = (f32[40,512]{1,0:T(8,128)S(1)}, f32[40,512]{1,0:T(8,128)S(1)}, u32[]{:S(2)}, u32[]{:S(2)}) collective-permute-start(f32[40,512]{1,0:T(8,128)S(1)} %get-tuple-element.190), channel_id=1, source_target_pairs={{0,4},{1,5},{2,6},{3,7},{4,0},{5,1},{6,2},{7,3},{8,12},{9,13},{10,... | collective-permute-start | bytes 245768 | tf_op jit(solution)/shard_map/ppermute | solution.py:515
  70.4 8.0 %collective-permute-start.27 = (f32[48,512]{1,0:T(8,128)S(1)}, f32[48,512]{1,0:T(8,128)S(1)}, u32[]{:S(2)}, u32[]{:S(2)}) collective-permute-start(f32[48,512]{1,0:T(8,128)S(1)} %shard_map.174.a), channel_id=1, source_target_pairs={{0,16},{1,17},{2,18},{3,19},{4,20},{5,21},{6,22},{7,23},{8,24},{9,... | collective-permute-start | bytes 294920 | tf_op jit(solution)/shard_map/ppermute | solution.py:515
  72.6 8.6 %collective-permute-start.10 = (f32[40,512]{1,0:T(8,128)S(1)}, f32[40,512]{1,0:T(8,128)S(1)}, u32[]{:S(2)}, u32[]{:S(2)}) collective-permute-start(f32[40,512]{1,0:T(8,128)S(1)} %shard_map.158._.a), channel_id=1, source_target_pairs={{0,16},{1,17},{2,18},{3,19},{4,20},{5,21},{6,22},{7,23},{8,24},{9,... | collective-permute-start | bytes 245768 | tf_op jit(solution)/shard_map/ppermute | solution.py:515
  74.2 17.3 %collective-permute-start.16 = (f32[256,512]{1,0:T(8,128)S(1)}, f32[256,512]{1,0:T(8,128)S(1)}, u32[]{:S(2)}, u32[]{:S(2)}) collective-permute-start(f32[256,512]{1,0:T(8,128)S(1)} %get-tuple-element.192), channel_id=1, source_target_pairs={{0,4},{4,0},{8,12},{12,8},{16,20},{20,16},{24,28},{28,24},{1,5},{5... | collective-permute-start | bytes 1572872 | tf_op jit(solution)/shard_map/ppermute | solution.py:495
  78.4 6.0 %collective-permute-start.28 = (f32[48,512]{1,0:T(8,128)S(1)}, f32[48,512]{1,0:T(8,128)S(1)}, u32[]{:S(2)}, u32[]{:S(2)}) collective-permute-start(f32[48,512]{1,0:T(8,128)S(1)} %shard_map.175.mine), channel_id=1, source_target_pairs={{0,2},{1,3},{2,0},{3,1},{4,6},{5,7},{6,4},{7,5},{8,10},{9,11},{10,... | collective-permute-start | bytes 294920 | tf_op jit(solution)/shard_map/ppermute | solution.py:515
  80.3 6.7 %collective-permute-start.19 = (f32[40,512]{1,0:T(8,128)S(1)}, f32[40,512]{1,0:T(8,128)S(1)}, u32[]{:S(2)}, u32[]{:S(2)}) collective-permute-start(f32[40,512]{1,0:T(8,128)S(1)} %get-tuple-element.194.a), channel_id=1, source_target_pairs={{0,16},{1,17},{2,18},{3,19},{4,20},{5,21},{6,22},{7,23},{8,24},{9,... | collective-permute-start | bytes 245768 | tf_op jit(solution)/shard_map/ppermute | solution.py:515
  81.2 5.9 %collective-permute-start.11 = (f32[40,512]{1,0:T(8,128)S(1)}, f32[40,512]{1,0:T(8,128)S(1)}, u32[]{:S(2)}, u32[]{:S(2)}) collective-permute-start(f32[40,512]{1,0:T(8,128)S(1)} %shard_map.160.mine), channel_id=1, source_target_pairs={{0,8},{1,9},{2,10},{3,11},{4,12},{5,13},{6,14},{7,15},{8,0},{9,1},... | collective-permute-start | bytes 245768 | tf_op jit(solution)/shard_map/ppermute | solution.py:515
  84.4 7.4 %collective-permute-start.29 = (f32[96,512]{1,0:T(8,128)S(1)}, f32[96,512]{1,0:T(8,128)S(1)}, u32[]{:S(2)}, u32[]{:S(2)}) collective-permute-start(f32[96,512]{1,0:T(8,128)S(1)} %shard_map.176.mine), channel_id=1, source_target_pairs={{0,4},{1,5},{2,6},{3,7},{4,0},{5,1},{6,2},{7,3},{8,12},{9,13},{10,... | collective-permute-start | bytes 589832 | tf_op jit(solution)/shard_map/ppermute | solution.py:515
  86.9 4.5 %collective-permute-start.20 = (f32[40,512]{1,0:T(8,128)S(1)}, f32[40,512]{1,0:T(8,128)S(1)}, u32[]{:S(2)}, u32[]{:S(2)}) collective-permute-start(f32[40,512]{1,0:T(8,128)S(1)} %shard_map.168.mine), channel_id=1, source_target_pairs={{0,4},{1,5},{2,6},{3,7},{4,0},{5,1},{6,2},{7,3},{8,12},{9,13},{10,... | collective-permute-start | bytes 245768 | tf_op jit(solution)/shard_map/ppermute | solution.py:515
  87.2 6.5 %collective-permute-start.12 = (f32[80,512]{1,0:T(8,128)S(1)}, f32[80,512]{1,0:T(8,128)S(1)}, u32[]{:S(2)}, u32[]{:S(2)}) collective-permute-start(f32[80,512]{1,0:T(8,128)S(1)} %shard_map.161.mine), channel_id=1, source_target_pairs={{0,2},{1,3},{2,0},{3,1},{4,6},{5,7},{6,4},{7,5},{8,10},{9,11},{10,... | collective-permute-start | bytes 491528 | tf_op jit(solution)/shard_map/ppermute | solution.py:515
  91.5 6.6 %collective-permute-start.21 = (f32[80,512]{1,0:T(8,128)S(1)}, f32[80,512]{1,0:T(8,128)S(1)}, u32[]{:S(2)}, u32[]{:S(2)}) collective-permute-start(f32[80,512]{1,0:T(8,128)S(1)} %shard_map.169.mine), channel_id=1, source_target_pairs={{0,8},{1,9},{2,10},{3,11},{4,12},{5,13},{6,14},{7,15},{8,0},{9,1},... | collective-permute-start | bytes 491528 | tf_op jit(solution)/shard_map/ppermute | solution.py:515
  91.9 10.4 %collective-permute-start.30 = (f32[192,512]{1,0:T(8,128)S(1)}, f32[192,512]{1,0:T(8,128)S(1)}, u32[]{:S(2)}, u32[]{:S(2)}) collective-permute-start(f32[192,512]{1,0:T(8,128)S(1)} %shard_map.177.mine), channel_id=1, source_target_pairs={{0,8},{1,9},{2,10},{3,11},{4,12},{5,13},{6,14},{7,15},{8,0},{9,1},... | collective-permute-start | bytes 1179656 | tf_op jit(solution)/shard_map/ppermute | solution.py:515
  93.7 8.8 %collective-permute-start.17 = (f32[160,512]{1,0:T(8,128)S(1)}, f32[160,512]{1,0:T(8,128)S(1)}, u32[]{:S(2)}, u32[]{:S(2)}) collective-permute-start(f32[160,512]{1,0:T(8,128)S(1)} %shard_map.162._.mine), channel_id=1, source_target_pairs={{0,4},{1,5},{2,6},{3,7},{4,0},{5,1},{6,2},{7,3},{8,12},{9,13},{10,... | collective-permute-start | bytes 983048 | tf_op jit(solution)/shard_map/ppermute | solution.py:515
  98.2 7.1 %collective-permute-start.22 = (f32[160,512]{1,0:T(8,128)S(1)}, f32[160,512]{1,0:T(8,128)S(1)}, u32[]{:S(2)}, u32[]{:S(2)}) collective-permute-start(f32[160,512]{1,0:T(8,128)S(1)} %shard_map.170.mine), channel_id=1, source_target_pairs={{0,2},{1,3},{2,0},{3,1},{4,6},{5,7},{6,4},{7,5},{8,10},{9,11},{10,... | collective-permute-start | bytes 983048 | tf_op jit(solution)/shard_map/ppermute | solution.py:515
  102.4 5.1 %collective-permute-start.31 = (f32[384,512]{1,0:T(8,128)S(1)}, f32[384,512]{1,0:T(8,128)S(1)}, u32[]{:S(2)}, u32[]{:S(2)}) collective-permute-start(f32[384,512]{1,0:T(8,128)S(1)} %shard_map.178.refs_2_), channel_id=1, source_target_pairs={{0,1},{1,0},{2,3},{3,2},{4,5},{5,4},{6,7},{7,6},{8,9},{9,8},{10,11... | collective-permute-start | bytes 2359304 | tf_op jit(solution)/shard_map/ppermute | solution.py:515
  102.6 4.3 %collective-permute-start.18 = (f32[320,512]{1,0:T(8,128)S(1)}, f32[320,512]{1,0:T(8,128)S(1)}, u32[]{:S(2)}, u32[]{:S(2)}) collective-permute-start(f32[320,512]{1,0:T(8,128)S(1)} %shard_map.167.refs_0_), channel_id=1, source_target_pairs={{0,1},{1,0},{2,3},{3,2},{4,5},{5,4},{6,7},{7,6},{8,9},{9,8},{10,11... | collective-permute-start | bytes 1966088 | tf_op jit(solution)/shard_map/ppermute | solution.py:515
  105.4 2.2 %collective-permute-start.23 = (f32[320,512]{1,0:T(8,128)S(1)}, f32[320,512]{1,0:T(8,128)S(1)}, u32[]{:S(2)}, u32[]{:S(2)}) collective-permute-start(f32[320,512]{1,0:T(8,128)S(1)} %shard_map.171.refs_1_), channel_id=1, source_target_pairs={{0,1},{1,0},{2,3},{3,2},{4,5},{5,4},{6,7},{7,6},{8,9},{9,8},{10,11... | collective-permute-start | bytes 1966088 | tf_op jit(solution)/shard_map/ppermute | solution.py:515
  (9 other events, 26.2 us)

commit v7 on v6

--- a/solution.py
+++ b/solution.py
@@ -211,23 +211,34 @@
                 send[...] = pair[1 - bit][i * rows : (i + 1) * rows, :]
 
 
+def far_side_kernel(
+    _, patch, gain, wk_h, wk_l, wv_h, wv_l,
+    hidden, key, k_stack, v_stack, vt_h, vt_l,
+):
+    hidden[...], key[...] = key_side((patch,), gain, (wk_h, wk_l), (wv_h, wv_l), k_stack, v_stack, (vt_h, vt_l))
+
+
 def far_kernel(
-    parity, listed, counts, patch_0, patch_1, gain, q_t, q_stack, d_mixed_t, d_stack, mixed_1, tops, totals,
+    parity, listed, counts, hidden_0, key_0, k_far_0, v_far_0, vt_0_h, vt_0_l, patch_1, gain, q_t, q_stack, d_mixed_t, d_stack, mixed_1, tops, totals,
     wk_h, wk_l, wv_h, wv_l,
     hidden, key, u_h, u_l, mixed_t, deltas, shares, shares_1, dk_h, dk_l, dv_h, dv_l, d_far,
     bias, k_far, v_far, vt_h, vt_l, e_h, e_l,
 ):
     store_bias(bias, listed, counts, parity, range(4, 6))
-    hidden[...], key[...] = key_side(
-        (patch_0, patch_1), gain, (wk_h, wk_l), (wv_h, wv_l), k_far, v_far, (vt_h, vt_l)
-    )
+    hidden[:PT, :], key[:PT, :] = hidden_0[...], key_0[...]
+    hidden[PT:, :], key[PT:, :] = key_side(
+        (patch_1,), gain, (wk_h, wk_l), (wv_h, wv_l), k_far, v_far, (vt_h, vt_l)
+    )
+
+    def both_patches(one, two, stack, right):
+        return jnp.concatenate([dot(one[:, stack], right), dot(two[:, stack], right)], axis=0)
 
     def one_pair(p, carry):
         d_scaled, q_scaled = [], []
         for a in range(2):
             h = 2 * p + a
             stack, rows, row = head_stack(h), head_rows(h), pl.ds(h, 1)
-            scores = biased(dot(k_far[:, stack], q_stack[stack, :]), bias, 4)
+            scores = biased(both_patches(k_far_0, k_far, stack, q_stack[stack, :]), bias, 4)
             top_1 = tops[row, :]
             top = jnp.maximum(top_1, jnp.max(scores, axis=0, keepdims=True))
             weights = jnp.exp(scores - top)
@@ -237,14 +248,14 @@
             pair = pair_of(weights)
             e_h[a] = pair[0]
             e_l[a] = pair[1]
-            mixed = share_1 * mixed_1[rows, :] + share * weighed((vt_h,), (vt_l,), rows, pair)
+            mixed = share_1 * mixed_1[rows, :] + share * weighed((vt_0_h, vt_h), (vt_0_l, vt_l), rows, pair)
             mixed_t[rows, :] = mixed
             d_mixed = d_mixed_t[rows, :]
             delta = jnp.sum(d_mixed * mixed, axis=0, keepdims=True)
             deltas[row, :] = delta
             shares[row, :] = share
             shares_1[row, :] = share_1
-            pair = pair_of(weights * (dot(v_far[:, stack], d_stack[stack, :]) - delta))
+            pair = pair_of(weights * (both_patches(v_far_0, v_far, stack, d_stack[stack, :]) - delta))
             u_h[h] = pair[0]
             u_l[h] = pair[1]
             d_scaled.append(d_mixed * share)
@@ -533,11 +544,12 @@
         scalars=1, limit=8,
     )
     d_given, d_own, mark = side_of(parts[0])
+    result, mark_2 = result_of(parts[0])
     parts = [[parts[2 * i], swapped(parts[2 * i + 1], ORDERS[i][0])] for i in range(3)]
     for step in (1, 2):
         for i in range(3):
             half, mask = shape(sizes[i] >> (step + 1), width), ORDERS[i][step]
-            place = (mark,) if step == 1 else ()
+            place = (mark, mark_2) if step == 1 else ()
             keep, send = call(
                 functools.partial(halve_kernel, mask), (me, *parts[i], *place), [half, half], scalars=1
             )
@@ -548,15 +560,12 @@
             d_other = across(d_going)
         else:
             (part,) = call(add_kernel, parts[i], [parts[i][0]])
-        if i == 0:
-            result, mark = result_of(part)
         mask, other = LAST, swapped(part, LAST)
         while 2 * mask < devices():
             (part,) = call(add_kernel, (part, other), [part])
             mask *= 2
             other = swapped(part, mask)
-        place = (mark,) if i == 1 else ()
-        (parts[i],) = call(last_kernel, (part, other, *place), [part])
+        (parts[i],) = call(last_kernel, (part, other), [part])
     for step in (2, 1, 0):
         for i in range(3):
             mask = ORDERS[i][step]
@@ -586,12 +595,13 @@
     parity = (lax.axis_index("space") % 2).astype(jnp.int32)[None]
     counts = neighbour_count[None, :]
     near = [across(tokens[i * PT : (i + 1) * PT]) for i in range(2)]
-    far = [onward(near[0])]
     gain_row = gain[None, :]
     stack_rows, stack_columns = shape(HEADS * 4 * HD, rows, dtype=BF16), shape(rows, HEADS * 4 * HD, dtype=BF16)
     turned, square, pair = pairs(width, rows), pairs(width, width), pairs(rows, width)
     whole, whole_t, scalars = shape(rows, width), shape(width, rows), shape(HEADS, rows)
     weights = call(weight_kernel, (me, parity, wq, wk, wv, wo), square * 4, scalars=2, limit=20)
+    near[0], *weights = lax.optimization_barrier((near[0], *weights))
+    far = [onward(near[0])]
     wq_h, wq_l, wk_h, wk_l, wv_h, wv_l, wo_h, wo_l = weights
     (
         ht_h, ht_l, q_t, q_stack, k_stack, v_stack, kt_h, kt_l, vt_h, vt_l, d_mixed_t, d_stack,
@@ -620,20 +630,27 @@
         [shape(8, rows)],
         scalars=3, limit=LIMITS[1], us=1,
     )
+    half_stack, half_t = shape(PT, HEADS * 4 * HD, dtype=BF16), pairs(width, PT)
+    first = call(
+        far_side_kernel,
+        (tops, far[0], gain_row, *w_k, *w_v),
+        [shape(PT, width), shape(PT, width), half_stack, half_stack, *half_t],
+        limit=LIMITS[1], us=1,
+    )
     (
         hidden3, key3, u_h, u_l, mixed_t, deltas, shares, shares_1, dk3_h, dk3_l, dv3_h, dv3_l,
         d_far,
     ) = call(
         far_kernel,
         (
-            parity, neighbour_list, counts, *far, gain_row, q_t, q_stack, d_mixed_t, d_stack, mixed, tops, totals,
+            parity, neighbour_list, counts, *first, far[1], gain_row, q_t, q_stack, d_mixed_t, d_stack, mixed, tops, totals,
             *w_k, *w_v,
         ),
         [
             whole, whole, *pairs(HEADS, rows, rows), whole_t, scalars, scalars, scalars, *pair, *pair,
             whole,
         ],
-        [shape(8, rows), stack_columns, stack_columns, *turned, *pairs(2, rows, rows)],
+        [shape(8, rows), half_stack, half_stack, *half_t, *pairs(2, rows, rows)],
         scalars=3, limit=LIMITS[2], us=1,
     )
     d_back = homeward(d_far)

time: 109 us -> 109 us (level)
  waiting for transfers between devices: 29.3 us -> 25.8 us
  starting transfers between devices: 39.9 us -> 42.5 us
    ppermute x26, starting transfers between devices: 28.9 us -> 31.4 us  [swapped(): lax.ppermute(value, ('space', 'slab'), [(i, i ^ mask) for i in range(devi...]
    ppermute x26, waiting for transfers between devices: 24.5 us -> 22.2 us  [swapped(): lax.ppermute(value, ('space', 'slab'), [(i, i ^ mask) for i in range(devi...]
    ppermute x6, waiting for transfers between devices: 4.74 us -> 3.59 us  [along_space(): lax.ppermute(value, 'space', [(i, target(i) % count) for i in range(count)])]
    pallas_call x35 -> x36, Pallas kernels: 30.2 us -> 30.6 us  [call(): pl.pallas_call(kernel, out_shape=outputs, in_specs=[SMEM] * scalars + [VM...]
  transfers between devices with their start and end apart: 32 -> 32, of which waited for: 16 -> 20; matrix products, arithmetic and copies ran while one was open for 0% -> 0% of each run, Pallas kernels for 22% -> 23%
where the time goes in v7:
time: 109 us
  starting transfers between devices  42.5 us (39%)
  Pallas kernels  33.3 us (31%)
  waiting for transfers between devices  25.8 us (24%)
  local copies, waits for them, and re-layouts  5.99 us (5%)
  between operations  1.1 us (1%)
    ppermute x26, starting transfers between devices, swapped(): lax.ppermute(value, ('space', 'slab'), [(i, i ^ mask) for i in range(devi...  31.4 us
    pallas_call x36, Pallas kernels, call(): pl.pallas_call(kernel, out_shape=outputs, in_specs=[SMEM] * scalars + [VM...  30.6 us
    ppermute x26, waiting for transfers between devices, swapped(): lax.ppermute(value, ('space', 'slab'), [(i, i ^ mask) for i in range(devi...  22.2 us
    ppermute x6, starting transfers between devices, along_space(): lax.ppermute(value, 'space', [(i, target(i) % count) for i in range(count)])  11.1 us
    unnamed x18, local copies, waits for them, and re-layouts  4.92 us
    ppermute x6, waiting for transfers between devices, along_space(): lax.ppermute(value, 'space', [(i, target(i) % count) for i in range(count)])  3.59 us
    pallas_call x2, Pallas kernels, written(): pl.pallas_call(functools.partial(write_kernel, ranges, core), out_shape=[...  2.73 us
  transfers between devices with their start and end apart: 32, of which 20 were waited for; matrix products, arithmetic and copies ran while one was open for 0% of the time, Pallas kernels for 23%

profile of v7, /device:TPU:0, one launch (start us, length us, event | category | flops | bytes accessed | tf_op | source)
XLA Modules:
  0.0 108.7 jit_solution(1670897183041024953)
XLA Ops:
  1.7 3.0 %collective-permute-start = (f32[128,512]{1,0:T(8,128)S(1)}, f32[128,512]{1,0:T(8,128)S(1)}, u32[]{:S(2)}, u32[]{:S(2)}) collective-permute-start(f32[128,512]{1,0:T(8,128)S(1)} %get-tuple-element.244), channel_id=1, source_target_pairs={{0,4},{4,0},{8,12},{12,8},{16,20},{20,16},{24,28},{28,24},{1,5},{5... | collective-permute-start | bytes 786440 | tf_op jit(solution)/shard_map/ppermute | solution.py:506
  10.3 1.5 %collective-permute-done._.patch_0 = f32[128,512]{1,0:T(8,128)S(1)} collective-permute-done((f32[128,512]{1,0:T(8,128)S(1)}, f32[128,512]{1,0:T(8,128)S(1)}, u32[]{:S(2)}, u32[]{:S(2)}) %collective-permute-start) | collective-permute-done | bytes 262176 | tf_op jit(solution)/shard_map/ppermute | solution.py:506
  11.8 2.1 %collective-permute-start.1 = (f32[128,512]{1,0:T(8,128)S(1)}, f32[128,512]{1,0:T(8,128)S(1)}, u32[]{:S(2)}, u32[]{:S(2)}) collective-permute-start(f32[128,512]{1,0:T(8,128)S(1)} %collective-permute-done._.patch_0), channel_id=1, source_target_pairs={{0,8},{4,28},{8,16},{12,4},{16,24},{20,12},{24,0},{28,20},{1,9},{5... | collective-permute-start | bytes 786440 | tf_op jit(solution)/shard_map/ppermute | solution.py:506
  14.0 2.1 %shard_map.145 = (bf16[512,256]{1,0:T(8,128)(2,1)S(1)}, bf16[512,256]{1,0:T(8,128)(2,1)S(1)}, f32[512,256]{1,0:T(8,128)S(1)}, bf16[2048,256]{1,0:T(8,128)(2,1)S(...) custom-call(f32[128,512]{1,0:T(8,128)S(1)} %collective-permute-done., ...), custom_call_target="tpu_custom_call" | custom-call | flops 1000000000 | tf_op jit(solution)/shard_map/pallas_call | solution.py:490
  16.6 1.8 %collective-permute-start.3 = (f32[128,512]{1,0:T(8,128)S(1)}, f32[128,512]{1,0:T(8,128)S(1)}, u32[]{:S(2)}, u32[]{:S(2)}) collective-permute-start(f32[128,512]{1,0:T(8,128)S(1)} %collective-permute-done.2.patch_1), channel_id=1, source_target_pairs={{0,8},{4,28},{8,16},{12,4},{16,24},{20,12},{24,0},{28,20},{1,9},{5... | collective-permute-start | bytes 786440 | tf_op jit(solution)/shard_map/ppermute | solution.py:506
  18.5 1.6 %shard_map.146 = (bf16[512,256]{1,0:T(8,128)(2,1)S(1)}, bf16[512,256]{1,0:T(8,128)(2,1)S(1)}, bf16[512,256]{1,0:T(8,128)(2,1)S(1)}, bf16[512,256]{1,0:T(8,128)(2...) custom-call(f32[128,512]{1,0:T(8,128)S(1)} %collective-permute-done., ...), custom_call_target="tpu_custom_call" | custom-call | flops 1000000000 | tf_op jit(solution)/shard_map/pallas_call | solution.py:490
  20.4 4.7 %shard_map.147 = (bf16[8,512,256]{2,1,0:T(8,128)(2,1)S(1)}, bf16[8,512,256]{2,1,0:T(8,128)(2,1)S(1)}, f32[8,512,256]{2,1,0:T(8,128)S(1)}, f32[512,256]{1,0:T(8,1...) custom-call(s32[1]{0:T(128)} %bitcast.1._parity.parity, s32[2,3]{1,0:T(2,128)S(1)} %copy-done.7, ...), custom_call_target="tpu_custom_call" | custom-call | flops 1000000000 | tf_op jit(solution)/shard_map/pallas_call | solution.py:490
  26.0 6.6 %shard_map.149 = (f32[256,512]{1,0:T(8,128)S(1)}, f32[256,512]{1,0:T(8,128)S(1)}, bf16[8,256,256]{2,1,0:T(8,128)(2,1)S(1)}, bf16[8,256,256]{2,1,0:T(8,128)(2,1)S...) custom-call(s32[1]{0:T(128)} %bitcast.1._parity.parity, ...), custom_call_target="tpu_custom_call" | custom-call | flops 1000000000 | tf_op jit(solution)/shard_map/pallas_call | solution.py:490
  32.6 2.6 %collective-permute-start.4 = (f32[256,512]{1,0:T(8,128)S(1)}, f32[256,512]{1,0:T(8,128)S(1)}, u32[]{:S(2)}, u32[]{:S(2)}) collective-permute-start(f32[256,512]{1,0:T(8,128)S(1)} %get-tuple-element.199), channel_id=1, source_target_pairs={{0,24},{4,12},{8,0},{12,20},{16,8},{20,28},{24,16},{28,4},{1,25},{... | collective-permute-start | bytes 1572872 | tf_op jit(solution)/shard_map/ppermute | solution.py:506
  35.2 4.0 %shard_map.150 = (f32[512,256]{1,0:T(8,128)S(1)}, bf16[512,512]{1,0:T(8,128)(2,1)S(1)}, bf16[512,512]{1,0:T(8,128)(2,1)S(1)}, bf16[512,512]{1,0:T(8,128)(2,1)S(1)}, bf16[512,512]{1,0:T(8,128)(2,1)S(1)}) custom-call(f32[512,256]{1,0:T(8,128)S(1)} %get-tuple-element.161.q_t, f32[512,256]{1,0:T(8,128)S(1)} %get-tuple-element.162.d_mixed_t, ...), custom_call_target="tpu_custom_call" | custom-call | flops 1000000 | tf_op jit(solution)/shard_map/pallas_call | solution.py:490
  39.2 1.9 %shard_map.151 = (bf16[512,256]{1,0:T(8,128)(2,1)S(1)}, bf16[512,256]{1,0:T(8,128)(2,1)S(1)}, f32[512,512]{1,0:T(8,128)S(1)}, f32[512,512]{1,0:T(8,128)S(1)}) custom-call(s32[1]{0:T(128)} %bitcast._me.me, f32[512,256]{1,0:T(8,128)S(1)} %get-tuple-element.165.mixed_t, bf16[512,256]{1,0:T(8,128)(2,1)S(1)} %get-tuple-element.166.ht_h, ...), custom_call_target="tpu_custom_call" | custom-call | flops 1000000 | tf_op jit(solution)/shard_map/pallas_call | solution.py:490
  41.2 2.0 %shard_map.152 = (f32[512,512]{1,0:T(8,128)S(1)}, f32[512,512]{1,0:T(8,128)S(1)}, bf16[256,512]{1,0:T(8,128)(2,1)S(1)}, bf16[256,512]{1,0:T(8,128)(2,1)S(1)}) custom-call(bf16[512,256]{1,0:T(8,128)(2,1)S(1)} %get-tuple-element.166.ht_h, bf16[512,256]{1,0:T(8,128)(2,1)S(1)} %get-tuple-element.167.ht_l, bf16[512,256]{1,0:T(8,128)(2,1)S(1)} %get-tuple-element.168.ht2_h, ...), custom_call_target="tpu_custom_call" | custom-call | flops 1000000 | tf_op jit(solution)/shard_map/pallas_call | solution.py:490
  48.0 3.1 %collective-permute-start.7 = (f32[160,512]{1,0:T(8,128)S(1)}, f32[160,512]{1,0:T(8,128)S(1)}, u32[]{:S(2)}, u32[]{:S(2)}) collective-permute-start(f32[160,512]{1,0:T(8,128)S(1)} %get-tuple-element.205), channel_id=1, source_target_pairs={{0,4},{1,5},{2,6},{3,7},{4,0},{5,1},{6,2},{7,3},{8,12},{9,13},{10,... | collective-permute-start | bytes 983048 | tf_op jit(solution)/shard_map/ppermute | solution.py:526
  51.1 1.5 %collective-permute-start.13 = (f32[160,512]{1,0:T(8,128)S(1)}, f32[160,512]{1,0:T(8,128)S(1)}, u32[]{:S(2)}, u32[]{:S(2)}) collective-permute-start(f32[160,512]{1,0:T(8,128)S(1)} %get-tuple-element.217), channel_id=1, source_target_pairs={{0,2},{1,3},{2,0},{3,1},{4,6},{5,7},{6,4},{7,5},{8,10},{9,11},{10,... | collective-permute-start | bytes 983048 | tf_op jit(solution)/shard_map/ppermute | solution.py:526
  54.0 2.2 %shard_map.157 = (f32[256,512]{1,0:T(8,128)S(1)}, f32[256,512]{1,0:T(8,128)S(1)}, f32[8,128]{1,0:T(8,128)S(1)}) custom-call(f32[160,512]{1,0:T(8,128)S(1)} %get-tuple-element.203._.keep, f32[256,512]{1,0:T(8,128)S(1)} %get-tuple-element.206.d_back, bf16[256,512]{1,0:T(8,128)(2,1)S(1)} %get-tuple-element.207.dq_h, ...), custom_call_target="tpu_custom_call" | custom-call | flops 1000000000 | tf_op jit(solution)/shard_map/pallas_call | solution.py:490
  56.2 2.9 %collective-permute-done.24.other = f32[192,512]{1,0:T(8,128)S(1)} collective-permute-done((f32[192,512]{1,0:T(8,128)S(1)}, f32[192,512]{1,0:T(8,128)S(1)}, u32[]{:S(2)}, u32[]{:S(2)}) %collective-permute-start.24) | collective-permute-done | bytes 393248 | tf_op jit(solution)/shard_map/ppermute | solution.py:526
  60.3 1.6 %collective-permute-start.8 = (f32[80,512]{1,0:T(8,128)S(1)}, f32[80,512]{1,0:T(8,128)S(1)}, u32[]{:S(2)}, u32[]{:S(2)}) collective-permute-start(f32[80,512]{1,0:T(8,128)S(1)} %get-tuple-element.212), channel_id=1, source_target_pairs={{0,2},{1,3},{2,0},{3,1},{4,6},{5,7},{6,4},{7,5},{8,10},{9,11},{10,... | collective-permute-start | bytes 491528 | tf_op jit(solution)/shard_map/ppermute | solution.py:526
  62.2 3.1 %collective-permute-done.25.other = f32[96,512]{1,0:T(8,128)S(1)} collective-permute-done((f32[96,512]{1,0:T(8,128)S(1)}, f32[96,512]{1,0:T(8,128)S(1)}, u32[]{:S(2)}, u32[]{:S(2)}) %collective-permute-start.25) | collective-permute-done | bytes 196640 | tf_op jit(solution)/shard_map/ppermute | solution.py:526
  65.4 1.6 %collective-permute-start.26 = (f32[48,512]{1,0:T(8,128)S(1)}, f32[48,512]{1,0:T(8,128)S(1)}, u32[]{:S(2)}, u32[]{:S(2)}) collective-permute-start(f32[48,512]{1,0:T(8,128)S(1)} %get-tuple-element.231), channel_id=1, source_target_pairs={{0,2},{1,3},{2,0},{3,1},{4,6},{5,7},{6,4},{7,5},{8,10},{9,11},{10,... | collective-permute-start | bytes 294920 | tf_op jit(solution)/shard_map/ppermute | solution.py:526
  67.5 1.7 %collective-permute-start.15 = (f32[40,512]{1,0:T(8,128)S(1)}, f32[40,512]{1,0:T(8,128)S(1)}, u32[]{:S(2)}, u32[]{:S(2)}) collective-permute-start(f32[40,512]{1,0:T(8,128)S(1)} %get-tuple-element.221), channel_id=1, source_target_pairs={{0,4},{1,5},{2,6},{3,7},{4,0},{5,1},{6,2},{7,3},{8,12},{9,13},{10,... | collective-permute-start | bytes 245768 | tf_op jit(solution)/shard_map/ppermute | solution.py:526
  70.1 2.5 %collective-permute-start.27 = (f32[48,512]{1,0:T(8,128)S(1)}, f32[48,512]{1,0:T(8,128)S(1)}, u32[]{:S(2)}, u32[]{:S(2)}) collective-permute-start(f32[48,512]{1,0:T(8,128)S(1)} %shard_map.175.a), channel_id=1, source_target_pairs={{0,16},{1,17},{2,18},{3,19},{4,20},{5,21},{6,22},{7,23},{8,24},{9,... | collective-permute-start | bytes 294920 | tf_op jit(solution)/shard_map/ppermute | solution.py:526
  74.2 3.4 %collective-permute-start.10 = (f32[40,512]{1,0:T(8,128)S(1)}, f32[40,512]{1,0:T(8,128)S(1)}, u32[]{:S(2)}, u32[]{:S(2)}) collective-permute-start(f32[40,512]{1,0:T(8,128)S(1)} %shard_map.160.a), channel_id=1, source_target_pairs={{0,16},{1,17},{2,18},{3,19},{4,20},{5,21},{6,22},{7,23},{8,24},{9,... | collective-permute-start | bytes 245768 | tf_op jit(solution)/shard_map/ppermute | solution.py:526
  77.5 1.9 %collective-permute-done.27.b = f32[48,512]{1,0:T(8,128)S(1)} collective-permute-done((f32[48,512]{1,0:T(8,128)S(1)}, f32[48,512]{1,0:T(8,128)S(1)}, u32[]{:S(2)}, u32[]{:S(2)}) %collective-permute-start.27) | collective-permute-done | bytes 98336 | tf_op jit(solution)/shard_map/ppermute | solution.py:526
  79.5 1.7 %collective-permute-start.28 = (f32[48,512]{1,0:T(8,128)S(1)}, f32[48,512]{1,0:T(8,128)S(1)}, u32[]{:S(2)}, u32[]{:S(2)}) collective-permute-start(f32[48,512]{1,0:T(8,128)S(1)} %shard_map.176.mine), channel_id=1, source_target_pairs={{0,2},{1,3},{2,0},{3,1},{4,6},{5,7},{6,4},{7,5},{8,10},{9,11},{10,... | collective-permute-start | bytes 294920 | tf_op jit(solution)/shard_map/ppermute | solution.py:526
  82.1 2.0 %collective-permute-start.11 = (f32[40,512]{1,0:T(8,128)S(1)}, f32[40,512]{1,0:T(8,128)S(1)}, u32[]{:S(2)}, u32[]{:S(2)}) collective-permute-start(f32[40,512]{1,0:T(8,128)S(1)} %shard_map.161.mine), channel_id=1, source_target_pairs={{0,8},{1,9},{2,10},{3,11},{4,12},{5,13},{6,14},{7,15},{8,0},{9,1},... | collective-permute-start | bytes 245768 | tf_op jit(solution)/shard_map/ppermute | solution.py:526
  84.2 2.4 %collective-permute-start.29 = (f32[96,512]{1,0:T(8,128)S(1)}, f32[96,512]{1,0:T(8,128)S(1)}, u32[]{:S(2)}, u32[]{:S(2)}) collective-permute-start(f32[96,512]{1,0:T(8,128)S(1)} %shard_map.177.mine), channel_id=1, source_target_pairs={{0,4},{1,5},{2,6},{3,7},{4,0},{5,1},{6,2},{7,3},{8,12},{9,13},{10,... | collective-permute-start | bytes 589832 | tf_op jit(solution)/shard_map/ppermute | solution.py:526
  86.9 2.5 %collective-permute-start.20 = (f32[40,512]{1,0:T(8,128)S(1)}, f32[40,512]{1,0:T(8,128)S(1)}, u32[]{:S(2)}, u32[]{:S(2)}) collective-permute-start(f32[40,512]{1,0:T(8,128)S(1)} %shard_map.169.mine), channel_id=1, source_target_pairs={{0,4},{1,5},{2,6},{3,7},{4,0},{5,1},{6,2},{7,3},{8,12},{9,13},{10,... | collective-permute-start | bytes 245768 | tf_op jit(solution)/shard_map/ppermute | solution.py:526
  89.5 2.8 %collective-permute-done.20.other = f32[40,512]{1,0:T(8,128)S(1)} collective-permute-done((f32[40,512]{1,0:T(8,128)S(1)}, f32[40,512]{1,0:T(8,128)S(1)}, u32[]{:S(2)}, u32[]{:S(2)}) %collective-permute-start.20) | collective-permute-done | bytes 81952 | tf_op jit(solution)/shard_map/ppermute | solution.py:526
  92.5 2.1 %collective-permute-start.30 = (f32[192,512]{1,0:T(8,128)S(1)}, f32[192,512]{1,0:T(8,128)S(1)}, u32[]{:S(2)}, u32[]{:S(2)}) collective-permute-start(f32[192,512]{1,0:T(8,128)S(1)} %shard_map.178.mine), channel_id=1, source_target_pairs={{0,8},{1,9},{2,10},{3,11},{4,12},{5,13},{6,14},{7,15},{8,0},{9,1},... | collective-permute-start | bytes 1179656 | tf_op jit(solution)/shard_map/ppermute | solution.py:526
  95.4 1.6 %collective-permute-start.17 = (f32[160,512]{1,0:T(8,128)S(1)}, f32[160,512]{1,0:T(8,128)S(1)}, u32[]{:S(2)}, u32[]{:S(2)}) collective-permute-start(f32[160,512]{1,0:T(8,128)S(1)} %shard_map.163._.mine), channel_id=1, source_target_pairs={{0,4},{1,5},{2,6},{3,7},{4,0},{5,1},{6,2},{7,3},{8,12},{9,13},{10,... | collective-permute-start | bytes 983048 | tf_op jit(solution)/shard_map/ppermute | solution.py:526
  99.8 2.1 %collective-permute-done.30.other = f32[192,512]{1,0:T(8,128)S(1)} collective-permute-done((f32[192,512]{1,0:T(8,128)S(1)}, f32[192,512]{1,0:T(8,128)S(1)}, u32[]{:S(2)}, u32[]{:S(2)}) %collective-permute-start.30) | collective-permute-done | bytes 393248 | tf_op jit(solution)/shard_map/ppermute | solution.py:526
  102.7 2.2 %collective-permute-done.22.other = f32[160,512]{1,0:T(8,128)S(1)} collective-permute-done((f32[160,512]{1,0:T(8,128)S(1)}, f32[160,512]{1,0:T(8,128)S(1)}, u32[]{:S(2)}, u32[]{:S(2)}) %collective-permute-start.22) | collective-permute-done | bytes 327712 | tf_op jit(solution)/shard_map/ppermute | solution.py:526
  (89 shorter events, 28.8 us)
Async XLA Ops:
  1.7 10.1 %collective-permute-start = (f32[128,512]{1,0:T(8,128)S(1)}, f32[128,512]{1,0:T(8,128)S(1)}, u32[]{:S(2)}, u32[]{:S(2)}) collective-permute-start(f32[128,512]{1,0:T(8,128)S(1)} %get-tuple-element.244), channel_id=1, source_target_pairs={{0,4},{4,0},{8,12},{12,8},{16,20},{20,16},{24,28},{28,24},{1,5},{5... | collective-permute-start | bytes 786440 | tf_op jit(solution)/shard_map/ppermute | solution.py:506
  4.7 11.9 %collective-permute-start.2 = (f32[128,512]{1,0:T(8,128)S(1)}, f32[128,512]{1,0:T(8,128)S(1)}, u32[]{:S(2)}, u32[]{:S(2)}) collective-permute-start(f32[128,512]{1,0:T(8,128)S(1)} %get-tuple-element.243), channel_id=1, source_target_pairs={{0,4},{4,0},{8,12},{12,8},{16,20},{20,16},{24,28},{28,24},{1,5},{5... | collective-permute-start | bytes 786440 | tf_op jit(solution)/shard_map/ppermute | solution.py:506
  11.8 8.5 %collective-permute-start.1 = (f32[128,512]{1,0:T(8,128)S(1)}, f32[128,512]{1,0:T(8,128)S(1)}, u32[]{:S(2)}, u32[]{:S(2)}) collective-permute-start(f32[128,512]{1,0:T(8,128)S(1)} %collective-permute-done._.patch_0), channel_id=1, source_target_pairs={{0,8},{4,28},{8,16},{12,4},{16,24},{20,12},{24,0},{28,20},{1,9},{5... | collective-permute-start | bytes 786440 | tf_op jit(solution)/shard_map/ppermute | solution.py:506
  16.6 9.4 %collective-permute-start.3 = (f32[128,512]{1,0:T(8,128)S(1)}, f32[128,512]{1,0:T(8,128)S(1)}, u32[]{:S(2)}, u32[]{:S(2)}) collective-permute-start(f32[128,512]{1,0:T(8,128)S(1)} %collective-permute-done.2.patch_1), channel_id=1, source_target_pairs={{0,8},{4,28},{8,16},{12,4},{16,24},{20,12},{24,0},{28,20},{1,9},{5... | collective-permute-start | bytes 786440 | tf_op jit(solution)/shard_map/ppermute | solution.py:506
  32.6 12.5 %collective-permute-start.4 = (f32[256,512]{1,0:T(8,128)S(1)}, f32[256,512]{1,0:T(8,128)S(1)}, u32[]{:S(2)}, u32[]{:S(2)}) collective-permute-start(f32[256,512]{1,0:T(8,128)S(1)} %get-tuple-element.199), channel_id=1, source_target_pairs={{0,24},{4,12},{8,0},{12,20},{16,8},{20,28},{24,16},{28,4},{1,25},{... | collective-permute-start | bytes 1572872 | tf_op jit(solution)/shard_map/ppermute | solution.py:506
  43.3 2.7 %collective-permute-start.6 = (f32[512,512]{1,0:T(8,128)S(1)}, f32[512,512]{1,0:T(8,128)S(1)}, u32[]{:S(2)}, u32[]{:S(2)}) collective-permute-start(f32[512,512]{1,0:T(8,128)S(1)} %get-tuple-element.202), channel_id=1, source_target_pairs={{0,1},{1,0},{2,3},{3,2},{4,5},{5,4},{6,7},{7,6},{8,9},{9,8},{10,11... | collective-permute-start | bytes 3145736 | tf_op jit(solution)/shard_map/ppermute | solution.py:526
  43.4 4.1 %collective-permute-start.5 = (f32[512,512]{1,0:T(8,128)S(1)}, f32[512,512]{1,0:T(8,128)S(1)}, u32[]{:S(2)}, u32[]{:S(2)}) collective-permute-start(f32[512,512]{1,0:T(8,128)S(1)} %get-tuple-element.201), channel_id=1, source_target_pairs={{0,1},{1,0},{2,3},{3,2},{4,5},{5,4},{6,7},{7,6},{8,9},{9,8},{10,11... | collective-permute-start | bytes 3145736 | tf_op jit(solution)/shard_map/ppermute | solution.py:526
  47.9 11.2 %collective-permute-start.24 = (f32[192,512]{1,0:T(8,128)S(1)}, f32[192,512]{1,0:T(8,128)S(1)}, u32[]{:S(2)}, u32[]{:S(2)}) collective-permute-start(f32[192,512]{1,0:T(8,128)S(1)} %get-tuple-element.227), channel_id=1, source_target_pairs={{0,8},{1,9},{2,10},{3,11},{4,12},{5,13},{6,14},{7,15},{8,0},{9,1},... | collective-permute-start | bytes 1179656 | tf_op jit(solution)/shard_map/ppermute | solution.py:526
  48.0 12.2 %collective-permute-start.7 = (f32[160,512]{1,0:T(8,128)S(1)}, f32[160,512]{1,0:T(8,128)S(1)}, u32[]{:S(2)}, u32[]{:S(2)}) collective-permute-start(f32[160,512]{1,0:T(8,128)S(1)} %get-tuple-element.205), channel_id=1, source_target_pairs={{0,4},{1,5},{2,6},{3,7},{4,0},{5,1},{6,2},{7,3},{8,12},{9,13},{10,... | collective-permute-start | bytes 983048 | tf_op jit(solution)/shard_map/ppermute | solution.py:526
  51.1 10.8 %collective-permute-start.13 = (f32[160,512]{1,0:T(8,128)S(1)}, f32[160,512]{1,0:T(8,128)S(1)}, u32[]{:S(2)}, u32[]{:S(2)}) collective-permute-start(f32[160,512]{1,0:T(8,128)S(1)} %get-tuple-element.217), channel_id=1, source_target_pairs={{0,2},{1,3},{2,0},{3,1},{4,6},{5,7},{6,4},{7,5},{8,10},{9,11},{10,... | collective-permute-start | bytes 983048 | tf_op jit(solution)/shard_map/ppermute | solution.py:526
  59.2 6.2 %collective-permute-start.25 = (f32[96,512]{1,0:T(8,128)S(1)}, f32[96,512]{1,0:T(8,128)S(1)}, u32[]{:S(2)}, u32[]{:S(2)}) collective-permute-start(f32[96,512]{1,0:T(8,128)S(1)} %get-tuple-element.229), channel_id=1, source_target_pairs={{0,4},{1,5},{2,6},{3,7},{4,0},{5,1},{6,2},{7,3},{8,12},{9,13},{10,... | collective-permute-start | bytes 589832 | tf_op jit(solution)/shard_map/ppermute | solution.py:526
  60.3 6.7 %collective-permute-start.8 = (f32[80,512]{1,0:T(8,128)S(1)}, f32[80,512]{1,0:T(8,128)S(1)}, u32[]{:S(2)}, u32[]{:S(2)}) collective-permute-start(f32[80,512]{1,0:T(8,128)S(1)} %get-tuple-element.212), channel_id=1, source_target_pairs={{0,2},{1,3},{2,0},{3,1},{4,6},{5,7},{6,4},{7,5},{8,10},{9,11},{10,... | collective-permute-start | bytes 491528 | tf_op jit(solution)/shard_map/ppermute | solution.py:526
  61.9 5.6 %collective-permute-start.14 = (f32[80,512]{1,0:T(8,128)S(1)}, f32[80,512]{1,0:T(8,128)S(1)}, u32[]{:S(2)}, u32[]{:S(2)}) collective-permute-start(f32[80,512]{1,0:T(8,128)S(1)} %get-tuple-element.219), channel_id=1, source_target_pairs={{0,8},{1,9},{2,10},{3,11},{4,12},{5,13},{6,14},{7,15},{8,0},{9,1},... | collective-permute-start | bytes 491528 | tf_op jit(solution)/shard_map/ppermute | solution.py:526
  65.4 4.7 %collective-permute-start.26 = (f32[48,512]{1,0:T(8,128)S(1)}, f32[48,512]{1,0:T(8,128)S(1)}, u32[]{:S(2)}, u32[]{:S(2)}) collective-permute-start(f32[48,512]{1,0:T(8,128)S(1)} %get-tuple-element.231), channel_id=1, source_target_pairs={{0,2},{1,3},{2,0},{3,1},{4,6},{5,7},{6,4},{7,5},{8,10},{9,11},{10,... | collective-permute-start | bytes 294920 | tf_op jit(solution)/shard_map/ppermute | solution.py:526
  67.0 7.1 %collective-permute-start.9 = (f32[40,512]{1,0:T(8,128)S(1)}, f32[40,512]{1,0:T(8,128)S(1)}, u32[]{:S(2)}, u32[]{:S(2)}) collective-permute-start(f32[40,512]{1,0:T(8,128)S(1)} %get-tuple-element.214), channel_id=1, source_target_pairs={{0,8},{1,9},{2,10},{3,11},{4,12},{5,13},{6,14},{7,15},{8,0},{9,1},... | collective-permute-start | bytes 245768 | tf_op jit(solution)/shard_map/ppermute | solution.py:526
  67.5 5.1 %collective-permute-start.15 = (f32[40,512]{1,0:T(8,128)S(1)}, f32[40,512]{1,0:T(8,128)S(1)}, u32[]{:S(2)}, u32[]{:S(2)}) collective-permute-start(f32[40,512]{1,0:T(8,128)S(1)} %get-tuple-element.221), channel_id=1, source_target_pairs={{0,4},{1,5},{2,6},{3,7},{4,0},{5,1},{6,2},{7,3},{8,12},{9,13},{10,... | collective-permute-start | bytes 245768 | tf_op jit(solution)/shard_map/ppermute | solution.py:526
  70.1 9.4 %collective-permute-start.27 = (f32[48,512]{1,0:T(8,128)S(1)}, f32[48,512]{1,0:T(8,128)S(1)}, u32[]{:S(2)}, u32[]{:S(2)}) collective-permute-start(f32[48,512]{1,0:T(8,128)S(1)} %shard_map.175.a), channel_id=1, source_target_pairs={{0,16},{1,17},{2,18},{3,19},{4,20},{5,21},{6,22},{7,23},{8,24},{9,... | collective-permute-start | bytes 294920 | tf_op jit(solution)/shard_map/ppermute | solution.py:526
  72.6 19.7 %collective-permute-start.16 = (f32[256,512]{1,0:T(8,128)S(1)}, f32[256,512]{1,0:T(8,128)S(1)}, u32[]{:S(2)}, u32[]{:S(2)}) collective-permute-start(f32[256,512]{1,0:T(8,128)S(1)} %get-tuple-element.223), channel_id=1, source_target_pairs={{0,4},{4,0},{8,12},{12,8},{16,20},{20,16},{24,28},{28,24},{1,5},{5... | collective-permute-start | bytes 1572872 | tf_op jit(solution)/shard_map/ppermute | solution.py:506
  74.2 7.9 %collective-permute-start.10 = (f32[40,512]{1,0:T(8,128)S(1)}, f32[40,512]{1,0:T(8,128)S(1)}, u32[]{:S(2)}, u32[]{:S(2)}) collective-permute-start(f32[40,512]{1,0:T(8,128)S(1)} %shard_map.160.a), channel_id=1, source_target_pairs={{0,16},{1,17},{2,18},{3,19},{4,20},{5,21},{6,22},{7,23},{8,24},{9,... | collective-permute-start | bytes 245768 | tf_op jit(solution)/shard_map/ppermute | solution.py:526
  79.5 4.7 %collective-permute-start.28 = (f32[48,512]{1,0:T(8,128)S(1)}, f32[48,512]{1,0:T(8,128)S(1)}, u32[]{:S(2)}, u32[]{:S(2)}) collective-permute-start(f32[48,512]{1,0:T(8,128)S(1)} %shard_map.176.mine), channel_id=1, source_target_pairs={{0,2},{1,3},{2,0},{3,1},{4,6},{5,7},{6,4},{7,5},{8,10},{9,11},{10,... | collective-permute-start | bytes 294920 | tf_op jit(solution)/shard_map/ppermute | solution.py:526
  81.1 5.7 %collective-permute-start.19 = (f32[40,512]{1,0:T(8,128)S(1)}, f32[40,512]{1,0:T(8,128)S(1)}, u32[]{:S(2)}, u32[]{:S(2)}) collective-permute-start(f32[40,512]{1,0:T(8,128)S(1)} %get-tuple-element.225.a), channel_id=1, source_target_pairs={{0,16},{1,17},{2,18},{3,19},{4,20},{5,21},{6,22},{7,23},{8,24},{9,... | collective-permute-start | bytes 245768 | tf_op jit(solution)/shard_map/ppermute | solution.py:526
  82.1 7.2 %collective-permute-start.11 = (f32[40,512]{1,0:T(8,128)S(1)}, f32[40,512]{1,0:T(8,128)S(1)}, u32[]{:S(2)}, u32[]{:S(2)}) collective-permute-start(f32[40,512]{1,0:T(8,128)S(1)} %shard_map.161.mine), channel_id=1, source_target_pairs={{0,8},{1,9},{2,10},{3,11},{4,12},{5,13},{6,14},{7,15},{8,0},{9,1},... | collective-permute-start | bytes 245768 | tf_op jit(solution)/shard_map/ppermute | solution.py:526
  84.2 8.2 %collective-permute-start.29 = (f32[96,512]{1,0:T(8,128)S(1)}, f32[96,512]{1,0:T(8,128)S(1)}, u32[]{:S(2)}, u32[]{:S(2)}) collective-permute-start(f32[96,512]{1,0:T(8,128)S(1)} %shard_map.177.mine), channel_id=1, source_target_pairs={{0,4},{1,5},{2,6},{3,7},{4,0},{5,1},{6,2},{7,3},{8,12},{9,13},{10,... | collective-permute-start | bytes 589832 | tf_op jit(solution)/shard_map/ppermute | solution.py:526
  86.9 5.4 %collective-permute-start.20 = (f32[40,512]{1,0:T(8,128)S(1)}, f32[40,512]{1,0:T(8,128)S(1)}, u32[]{:S(2)}, u32[]{:S(2)}) collective-permute-start(f32[40,512]{1,0:T(8,128)S(1)} %shard_map.169.mine), channel_id=1, source_target_pairs={{0,4},{1,5},{2,6},{3,7},{4,0},{5,1},{6,2},{7,3},{8,12},{9,13},{10,... | collective-permute-start | bytes 245768 | tf_op jit(solution)/shard_map/ppermute | solution.py:526
  89.4 5.9 %collective-permute-start.12 = (f32[80,512]{1,0:T(8,128)S(1)}, f32[80,512]{1,0:T(8,128)S(1)}, u32[]{:S(2)}, u32[]{:S(2)}) collective-permute-start(f32[80,512]{1,0:T(8,128)S(1)} %shard_map.162.mine), channel_id=1, source_target_pairs={{0,2},{1,3},{2,0},{3,1},{4,6},{5,7},{6,4},{7,5},{8,10},{9,11},{10,... | collective-permute-start | bytes 491528 | tf_op jit(solution)/shard_map/ppermute | solution.py:526
  92.3 5.4 %collective-permute-start.21 = (f32[80,512]{1,0:T(8,128)S(1)}, f32[80,512]{1,0:T(8,128)S(1)}, u32[]{:S(2)}, u32[]{:S(2)}) collective-permute-start(f32[80,512]{1,0:T(8,128)S(1)} %shard_map.170.mine), channel_id=1, source_target_pairs={{0,8},{1,9},{2,10},{3,11},{4,12},{5,13},{6,14},{7,15},{8,0},{9,1},... | collective-permute-start | bytes 491528 | tf_op jit(solution)/shard_map/ppermute | solution.py:526
  92.5 9.5 %collective-permute-start.30 = (f32[192,512]{1,0:T(8,128)S(1)}, f32[192,512]{1,0:T(8,128)S(1)}, u32[]{:S(2)}, u32[]{:S(2)}) collective-permute-start(f32[192,512]{1,0:T(8,128)S(1)} %shard_map.178.mine), channel_id=1, source_target_pairs={{0,8},{1,9},{2,10},{3,11},{4,12},{5,13},{6,14},{7,15},{8,0},{9,1},... | collective-permute-start | bytes 1179656 | tf_op jit(solution)/shard_map/ppermute | solution.py:526
  95.4 7.1 %collective-permute-start.17 = (f32[160,512]{1,0:T(8,128)S(1)}, f32[160,512]{1,0:T(8,128)S(1)}, u32[]{:S(2)}, u32[]{:S(2)}) collective-permute-start(f32[160,512]{1,0:T(8,128)S(1)} %shard_map.163._.mine), channel_id=1, source_target_pairs={{0,4},{1,5},{2,6},{3,7},{4,0},{5,1},{6,2},{7,3},{8,12},{9,13},{10,... | collective-permute-start | bytes 983048 | tf_op jit(solution)/shard_map/ppermute | solution.py:526
  97.8 7.1 %collective-permute-start.22 = (f32[160,512]{1,0:T(8,128)S(1)}, f32[160,512]{1,0:T(8,128)S(1)}, u32[]{:S(2)}, u32[]{:S(2)}) collective-permute-start(f32[160,512]{1,0:T(8,128)S(1)} %shard_map.171.mine), channel_id=1, source_target_pairs={{0,2},{1,3},{2,0},{3,1},{4,6},{5,7},{6,4},{7,5},{8,10},{9,11},{10,... | collective-permute-start | bytes 983048 | tf_op jit(solution)/shard_map/ppermute | solution.py:526
  102.0 5.1 %collective-permute-start.31 = (f32[384,512]{1,0:T(8,128)S(1)}, f32[384,512]{1,0:T(8,128)S(1)}, u32[]{:S(2)}, u32[]{:S(2)}) collective-permute-start(f32[384,512]{1,0:T(8,128)S(1)} %shard_map.179.refs_2_), channel_id=1, source_target_pairs={{0,1},{1,0},{2,3},{3,2},{4,5},{5,4},{6,7},{7,6},{8,9},{9,8},{10,11... | collective-permute-start | bytes 2359304 | tf_op jit(solution)/shard_map/ppermute | solution.py:526
  102.6 3.9 %collective-permute-start.18 = (f32[320,512]{1,0:T(8,128)S(1)}, f32[320,512]{1,0:T(8,128)S(1)}, u32[]{:S(2)}, u32[]{:S(2)}) collective-permute-start(f32[320,512]{1,0:T(8,128)S(1)} %shard_map.168.refs_0_), channel_id=1, source_target_pairs={{0,1},{1,0},{2,3},{3,2},{4,5},{5,4},{6,7},{7,6},{8,9},{9,8},{10,11... | collective-permute-start | bytes 1966088 | tf_op jit(solution)/shard_map/ppermute | solution.py:526
  105.0 2.2 %collective-permute-start.23 = (f32[320,512]{1,0:T(8,128)S(1)}, f32[320,512]{1,0:T(8,128)S(1)}, u32[]{:S(2)}, u32[]{:S(2)}) collective-permute-start(f32[320,512]{1,0:T(8,128)S(1)} %shard_map.172.refs_1_), channel_id=1, source_target_pairs={{0,1},{1,0},{2,3},{3,2},{4,5},{5,4},{6,7},{7,6},{8,9},{9,8},{10,11... | collective-permute-start | bytes 1966088 | tf_op jit(solution)/shard_map/ppermute | solution.py:526
  (9 other events, 26.2 us)

commit v8 on v7

--- a/solution.py
+++ b/solution.py
@@ -574,7 +574,7 @@
                 functools.partial(double_kernel, mask), (me, parts[i], swapped(parts[i], mask), *place),
                 [shape(2 * parts[i].shape[0], width)], scalars=1,
             )
-        if step == 1:
+        if step == 2:
             d_tokens, mark = tokens_of(parts[0], d_own, d_other)
     others = [swapped(part, 1) for part in parts]
     ranges, at = [], 0

time: 109 us -> 109 us (level)
  no operation moved by 1% of the time
where the time goes in v8:
time: 109 us
  starting transfers between devices  42.5 us (39%)
  Pallas kernels  33.3 us (31%)
  waiting for transfers between devices  25.8 us (24%)
  local copies, waits for them, and re-layouts  5.99 us (5%)
  between operations  1.1 us (1%)
    ppermute x26, starting transfers between devices, swapped(): lax.ppermute(value, ('space', 'slab'), [(i, i ^ mask) for i in range(devi...  31.4 us
    pallas_call x36, Pallas kernels, call(): pl.pallas_call(kernel, out_shape=outputs, in_specs=[SMEM] * scalars + [VM...  30.6 us
    ppermute x26, waiting for transfers between devices, swapped(): lax.ppermute(value, ('space', 'slab'), [(i, i ^ mask) for i in range(devi...  22.2 us
    ppermute x6, starting transfers between devices, along_space(): lax.ppermute(value, 'space', [(i, target(i) % count) for i in range(count)])  11.1 us
    unnamed x18, local copies, waits for them, and re-layouts  4.92 us
    ppermute x6, waiting for transfers between devices, along_space(): lax.ppermute(value, 'space', [(i, target(i) % count) for i in range(count)])  3.59 us
    pallas_call x2, Pallas kernels, written(): pl.pallas_call(functools.partial(write_kernel, ranges, core), out_shape=[...  2.73 us
  transfers between devices with their start and end apart: 32, of which 20 were waited for; matrix products, arithmetic and copies ran while one was open for 0% of the time, Pallas kernels for 23%

profile of v8, /device:TPU:0, one launch (start us, length us, event | category | flops | bytes accessed | tf_op | source)
XLA Modules:
  0.0 108.7 jit_solution(16656327465854621762)
XLA Ops:
  1.7 3.0 %collective-permute-start = (f32[128,512]{1,0:T(8,128)S(1)}, f32[128,512]{1,0:T(8,128)S(1)}, u32[]{:S(2)}, u32[]{:S(2)}) collective-permute-start(f32[128,512]{1,0:T(8,128)S(1)} %get-tuple-element.244), channel_id=1, source_target_pairs={{0,4},{4,0},{8,12},{12,8},{16,20},{20,16},{24,28},{28,24},{1,5},{5... | collective-permute-start | bytes 786440 | tf_op jit(solution)/shard_map/ppermute | solution.py:506
  10.3 1.5 %collective-permute-done._.patch_0 = f32[128,512]{1,0:T(8,128)S(1)} collective-permute-done((f32[128,512]{1,0:T(8,128)S(1)}, f32[128,512]{1,0:T(8,128)S(1)}, u32[]{:S(2)}, u32[]{:S(2)}) %collective-permute-start) | collective-permute-done | bytes 262176 | tf_op jit(solution)/shard_map/ppermute | solution.py:506
  11.8 2.1 %collective-permute-start.1 = (f32[128,512]{1,0:T(8,128)S(1)}, f32[128,512]{1,0:T(8,128)S(1)}, u32[]{:S(2)}, u32[]{:S(2)}) collective-permute-start(f32[128,512]{1,0:T(8,128)S(1)} %collective-permute-done._.patch_0), channel_id=1, source_target_pairs={{0,8},{4,28},{8,16},{12,4},{16,24},{20,12},{24,0},{28,20},{1,9},{5... | collective-permute-start | bytes 786440 | tf_op jit(solution)/shard_map/ppermute | solution.py:506
  14.0 2.1 %shard_map.145 = (bf16[512,256]{1,0:T(8,128)(2,1)S(1)}, bf16[512,256]{1,0:T(8,128)(2,1)S(1)}, f32[512,256]{1,0:T(8,128)S(1)}, bf16[2048,256]{1,0:T(8,128)(2,1)S(...) custom-call(f32[128,512]{1,0:T(8,128)S(1)} %collective-permute-done., ...), custom_call_target="tpu_custom_call" | custom-call | flops 1000000000 | tf_op jit(solution)/shard_map/pallas_call | solution.py:490
  16.6 1.8 %collective-permute-start.3 = (f32[128,512]{1,0:T(8,128)S(1)}, f32[128,512]{1,0:T(8,128)S(1)}, u32[]{:S(2)}, u32[]{:S(2)}) collective-permute-start(f32[128,512]{1,0:T(8,128)S(1)} %collective-permute-done.2.patch_1), channel_id=1, source_target_pairs={{0,8},{4,28},{8,16},{12,4},{16,24},{20,12},{24,0},{28,20},{1,9},{5... | collective-permute-start | bytes 786440 | tf_op jit(solution)/shard_map/ppermute | solution.py:506
  18.5 1.6 %shard_map.146 = (bf16[512,256]{1,0:T(8,128)(2,1)S(1)}, bf16[512,256]{1,0:T(8,128)(2,1)S(1)}, bf16[512,256]{1,0:T(8,128)(2,1)S(1)}, bf16[512,256]{1,0:T(8,128)(2...) custom-call(f32[128,512]{1,0:T(8,128)S(1)} %collective-permute-done., ...), custom_call_target="tpu_custom_call" | custom-call | flops 1000000000 | tf_op jit(solution)/shard_map/pallas_call | solution.py:490
  20.4 4.7 %shard_map.147 = (bf16[8,512,256]{2,1,0:T(8,128)(2,1)S(1)}, bf16[8,512,256]{2,1,0:T(8,128)(2,1)S(1)}, f32[8,512,256]{2,1,0:T(8,128)S(1)}, f32[512,256]{1,0:T(8,1...) custom-call(s32[1]{0:T(128)} %bitcast.1._parity.parity, s32[2,3]{1,0:T(2,128)S(1)} %copy-done.7, ...), custom_call_target="tpu_custom_call" | custom-call | flops 1000000000 | tf_op jit(solution)/shard_map/pallas_call | solution.py:490
  26.0 6.6 %shard_map.149 = (f32[256,512]{1,0:T(8,128)S(1)}, f32[256,512]{1,0:T(8,128)S(1)}, bf16[8,256,256]{2,1,0:T(8,128)(2,1)S(1)}, bf16[8,256,256]{2,1,0:T(8,128)(2,1)S...) custom-call(s32[1]{0:T(128)} %bitcast.1._parity.parity, ...), custom_call_target="tpu_custom_call" | custom-call | flops 1000000000 | tf_op jit(solution)/shard_map/pallas_call | solution.py:490
  32.6 2.6 %collective-permute-start.4 = (f32[256,512]{1,0:T(8,128)S(1)}, f32[256,512]{1,0:T(8,128)S(1)}, u32[]{:S(2)}, u32[]{:S(2)}) collective-permute-start(f32[256,512]{1,0:T(8,128)S(1)} %get-tuple-element.199), channel_id=1, source_target_pairs={{0,24},{4,12},{8,0},{12,20},{16,8},{20,28},{24,16},{28,4},{1,25},{... | collective-permute-start | bytes 1572872 | tf_op jit(solution)/shard_map/ppermute | solution.py:506
  35.2 4.0 %shard_map.150 = (f32[512,256]{1,0:T(8,128)S(1)}, bf16[512,512]{1,0:T(8,128)(2,1)S(1)}, bf16[512,512]{1,0:T(8,128)(2,1)S(1)}, bf16[512,512]{1,0:T(8,128)(2,1)S(1)}, bf16[512,512]{1,0:T(8,128)(2,1)S(1)}) custom-call(f32[512,256]{1,0:T(8,128)S(1)} %get-tuple-element.161.q_t, f32[512,256]{1,0:T(8,128)S(1)} %get-tuple-element.162.d_mixed_t, ...), custom_call_target="tpu_custom_call" | custom-call | flops 1000000 | tf_op jit(solution)/shard_map/pallas_call | solution.py:490
  39.2 1.9 %shard_map.151 = (bf16[512,256]{1,0:T(8,128)(2,1)S(1)}, bf16[512,256]{1,0:T(8,128)(2,1)S(1)}, f32[512,512]{1,0:T(8,128)S(1)}, f32[512,512]{1,0:T(8,128)S(1)}) custom-call(s32[1]{0:T(128)} %bitcast._me.me, f32[512,256]{1,0:T(8,128)S(1)} %get-tuple-element.165.mixed_t, bf16[512,256]{1,0:T(8,128)(2,1)S(1)} %get-tuple-element.166.ht_h, ...), custom_call_target="tpu_custom_call" | custom-call | flops 1000000 | tf_op jit(solution)/shard_map/pallas_call | solution.py:490
  41.2 2.0 %shard_map.152 = (f32[512,512]{1,0:T(8,128)S(1)}, f32[512,512]{1,0:T(8,128)S(1)}, bf16[256,512]{1,0:T(8,128)(2,1)S(1)}, bf16[256,512]{1,0:T(8,128)(2,1)S(1)}) custom-call(bf16[512,256]{1,0:T(8,128)(2,1)S(1)} %get-tuple-element.166.ht_h, bf16[512,256]{1,0:T(8,128)(2,1)S(1)} %get-tuple-element.167.ht_l, bf16[512,256]{1,0:T(8,128)(2,1)S(1)} %get-tuple-element.168.ht2_h, ...), custom_call_target="tpu_custom_call" | custom-call | flops 1000000 | tf_op jit(solution)/shard_map/pallas_call | solution.py:490
  48.0 3.1 %collective-permute-start.7 = (f32[160,512]{1,0:T(8,128)S(1)}, f32[160,512]{1,0:T(8,128)S(1)}, u32[]{:S(2)}, u32[]{:S(2)}) collective-permute-start(f32[160,512]{1,0:T(8,128)S(1)} %get-tuple-element.205), channel_id=1, source_target_pairs={{0,4},{1,5},{2,6},{3,7},{4,0},{5,1},{6,2},{7,3},{8,12},{9,13},{10,... | collective-permute-start | bytes 983048 | tf_op jit(solution)/shard_map/ppermute | solution.py:526
  51.1 1.5 %collective-permute-start.12 = (f32[160,512]{1,0:T(8,128)S(1)}, f32[160,512]{1,0:T(8,128)S(1)}, u32[]{:S(2)}, u32[]{:S(2)}) collective-permute-start(f32[160,512]{1,0:T(8,128)S(1)} %get-tuple-element.217), channel_id=1, source_target_pairs={{0,2},{1,3},{2,0},{3,1},{4,6},{5,7},{6,4},{7,5},{8,10},{9,11},{10,... | collective-permute-start | bytes 983048 | tf_op jit(solution)/shard_map/ppermute | solution.py:526
  54.0 2.2 %shard_map.157 = (f32[256,512]{1,0:T(8,128)S(1)}, f32[256,512]{1,0:T(8,128)S(1)}, f32[8,128]{1,0:T(8,128)S(1)}) custom-call(f32[160,512]{1,0:T(8,128)S(1)} %get-tuple-element.203._.keep, f32[256,512]{1,0:T(8,128)S(1)} %get-tuple-element.206.d_back, bf16[256,512]{1,0:T(8,128)(2,1)S(1)} %get-tuple-element.207.dq_h, ...), custom_call_target="tpu_custom_call" | custom-call | flops 1000000000 | tf_op jit(solution)/shard_map/pallas_call | solution.py:490
  56.2 2.9 %collective-permute-done.24.other = f32[192,512]{1,0:T(8,128)S(1)} collective-permute-done((f32[192,512]{1,0:T(8,128)S(1)}, f32[192,512]{1,0:T(8,128)S(1)}, u32[]{:S(2)}, u32[]{:S(2)}) %collective-permute-start.24) | collective-permute-done | bytes 393248 | tf_op jit(solution)/shard_map/ppermute | solution.py:526
  60.3 1.6 %collective-permute-start.8 = (f32[80,512]{1,0:T(8,128)S(1)}, f32[80,512]{1,0:T(8,128)S(1)}, u32[]{:S(2)}, u32[]{:S(2)}) collective-permute-start(f32[80,512]{1,0:T(8,128)S(1)} %get-tuple-element.212), channel_id=1, source_target_pairs={{0,2},{1,3},{2,0},{3,1},{4,6},{5,7},{6,4},{7,5},{8,10},{9,11},{10,... | collective-permute-start | bytes 491528 | tf_op jit(solution)/shard_map/ppermute | solution.py:526
  62.2 3.1 %collective-permute-done.25.other = f32[96,512]{1,0:T(8,128)S(1)} collective-permute-done((f32[96,512]{1,0:T(8,128)S(1)}, f32[96,512]{1,0:T(8,128)S(1)}, u32[]{:S(2)}, u32[]{:S(2)}) %collective-permute-start.25) | collective-permute-done | bytes 196640 | tf_op jit(solution)/shard_map/ppermute | solution.py:526
  65.4 1.6 %collective-permute-start.26 = (f32[48,512]{1,0:T(8,128)S(1)}, f32[48,512]{1,0:T(8,128)S(1)}, u32[]{:S(2)}, u32[]{:S(2)}) collective-permute-start(f32[48,512]{1,0:T(8,128)S(1)} %get-tuple-element.231), channel_id=1, source_target_pairs={{0,2},{1,3},{2,0},{3,1},{4,6},{5,7},{6,4},{7,5},{8,10},{9,11},{10,... | collective-permute-start | bytes 294920 | tf_op jit(solution)/shard_map/ppermute | solution.py:526
  67.5 1.7 %collective-permute-start.14 = (f32[40,512]{1,0:T(8,128)S(1)}, f32[40,512]{1,0:T(8,128)S(1)}, u32[]{:S(2)}, u32[]{:S(2)}) collective-permute-start(f32[40,512]{1,0:T(8,128)S(1)} %get-tuple-element.221), channel_id=1, source_target_pairs={{0,4},{1,5},{2,6},{3,7},{4,0},{5,1},{6,2},{7,3},{8,12},{9,13},{10,... | collective-permute-start | bytes 245768 | tf_op jit(solution)/shard_map/ppermute | solution.py:526
  70.1 2.5 %collective-permute-start.27 = (f32[48,512]{1,0:T(8,128)S(1)}, f32[48,512]{1,0:T(8,128)S(1)}, u32[]{:S(2)}, u32[]{:S(2)}) collective-permute-start(f32[48,512]{1,0:T(8,128)S(1)} %shard_map.175.a), channel_id=1, source_target_pairs={{0,16},{1,17},{2,18},{3,19},{4,20},{5,21},{6,22},{7,23},{8,24},{9,... | collective-permute-start | bytes 294920 | tf_op jit(solution)/shard_map/ppermute | solution.py:526
  74.2 3.4 %collective-permute-start.10 = (f32[40,512]{1,0:T(8,128)S(1)}, f32[40,512]{1,0:T(8,128)S(1)}, u32[]{:S(2)}, u32[]{:S(2)}) collective-permute-start(f32[40,512]{1,0:T(8,128)S(1)} %shard_map.160.a), channel_id=1, source_target_pairs={{0,16},{1,17},{2,18},{3,19},{4,20},{5,21},{6,22},{7,23},{8,24},{9,... | collective-permute-start | bytes 245768 | tf_op jit(solution)/shard_map/ppermute | solution.py:526
  77.5 1.9 %collective-permute-done.27.b = f32[48,512]{1,0:T(8,128)S(1)} collective-permute-done((f32[48,512]{1,0:T(8,128)S(1)}, f32[48,512]{1,0:T(8,128)S(1)}, u32[]{:S(2)}, u32[]{:S(2)}) %collective-permute-start.27) | collective-permute-done | bytes 98336 | tf_op jit(solution)/shard_map/ppermute | solution.py:526
  79.5 1.7 %collective-permute-start.28 = (f32[48,512]{1,0:T(8,128)S(1)}, f32[48,512]{1,0:T(8,128)S(1)}, u32[]{:S(2)}, u32[]{:S(2)}) collective-permute-start(f32[48,512]{1,0:T(8,128)S(1)} %shard_map.176.mine), channel_id=1, source_target_pairs={{0,2},{1,3},{2,0},{3,1},{4,6},{5,7},{6,4},{7,5},{8,10},{9,11},{10,... | collective-permute-start | bytes 294920 | tf_op jit(solution)/shard_map/ppermute | solution.py:526
  82.1 2.0 %collective-permute-start.11 = (f32[40,512]{1,0:T(8,128)S(1)}, f32[40,512]{1,0:T(8,128)S(1)}, u32[]{:S(2)}, u32[]{:S(2)}) collective-permute-start(f32[40,512]{1,0:T(8,128)S(1)} %shard_map.161.mine), channel_id=1, source_target_pairs={{0,8},{1,9},{2,10},{3,11},{4,12},{5,13},{6,14},{7,15},{8,0},{9,1},... | collective-permute-start | bytes 245768 | tf_op jit(solution)/shard_map/ppermute | solution.py:526
  84.2 2.4 %collective-permute-start.29 = (f32[96,512]{1,0:T(8,128)S(1)}, f32[96,512]{1,0:T(8,128)S(1)}, u32[]{:S(2)}, u32[]{:S(2)}) collective-permute-start(f32[96,512]{1,0:T(8,128)S(1)} %shard_map.177.mine), channel_id=1, source_target_pairs={{0,4},{1,5},{2,6},{3,7},{4,0},{5,1},{6,2},{7,3},{8,12},{9,13},{10,... | collective-permute-start | bytes 589832 | tf_op jit(solution)/shard_map/ppermute | solution.py:526
  86.9 2.5 %collective-permute-start.20 = (f32[40,512]{1,0:T(8,128)S(1)}, f32[40,512]{1,0:T(8,128)S(1)}, u32[]{:S(2)}, u32[]{:S(2)}) collective-permute-start(f32[40,512]{1,0:T(8,128)S(1)} %shard_map.169.mine), channel_id=1, source_target_pairs={{0,4},{1,5},{2,6},{3,7},{4,0},{5,1},{6,2},{7,3},{8,12},{9,13},{10,... | collective-permute-start | bytes 245768 | tf_op jit(solution)/shard_map/ppermute | solution.py:526
  89.5 2.8 %collective-permute-done.20.other = f32[40,512]{1,0:T(8,128)S(1)} collective-permute-done((f32[40,512]{1,0:T(8,128)S(1)}, f32[40,512]{1,0:T(8,128)S(1)}, u32[]{:S(2)}, u32[]{:S(2)}) %collective-permute-start.20) | collective-permute-done | bytes 81952 | tf_op jit(solution)/shard_map/ppermute | solution.py:526
  92.5 2.1 %collective-permute-start.30 = (f32[192,512]{1,0:T(8,128)S(1)}, f32[192,512]{1,0:T(8,128)S(1)}, u32[]{:S(2)}, u32[]{:S(2)}) collective-permute-start(f32[192,512]{1,0:T(8,128)S(1)} %shard_map.178.mine), channel_id=1, source_target_pairs={{0,8},{1,9},{2,10},{3,11},{4,12},{5,13},{6,14},{7,15},{8,0},{9,1},... | collective-permute-start | bytes 1179656 | tf_op jit(solution)/shard_map/ppermute | solution.py:526
  95.4 1.6 %collective-permute-start.17 = (f32[160,512]{1,0:T(8,128)S(1)}, f32[160,512]{1,0:T(8,128)S(1)}, u32[]{:S(2)}, u32[]{:S(2)}) collective-permute-start(f32[160,512]{1,0:T(8,128)S(1)} %shard_map.167.mine), channel_id=1, source_target_pairs={{0,4},{1,5},{2,6},{3,7},{4,0},{5,1},{6,2},{7,3},{8,12},{9,13},{10,... | collective-permute-start | bytes 983048 | tf_op jit(solution)/shard_map/ppermute | solution.py:526
  99.8 2.1 %collective-permute-done.30.other = f32[192,512]{1,0:T(8,128)S(1)} collective-permute-done((f32[192,512]{1,0:T(8,128)S(1)}, f32[192,512]{1,0:T(8,128)S(1)}, u32[]{:S(2)}, u32[]{:S(2)}) %collective-permute-start.30) | collective-permute-done | bytes 393248 | tf_op jit(solution)/shard_map/ppermute | solution.py:526
  102.7 2.2 %collective-permute-done.22.other = f32[160,512]{1,0:T(8,128)S(1)} collective-permute-done((f32[160,512]{1,0:T(8,128)S(1)}, f32[160,512]{1,0:T(8,128)S(1)}, u32[]{:S(2)}, u32[]{:S(2)}) %collective-permute-start.22) | collective-permute-done | bytes 327712 | tf_op jit(solution)/shard_map/ppermute | solution.py:526
  (89 shorter events, 28.8 us)
Async XLA Ops:
  1.7 10.1 %collective-permute-start = (f32[128,512]{1,0:T(8,128)S(1)}, f32[128,512]{1,0:T(8,128)S(1)}, u32[]{:S(2)}, u32[]{:S(2)}) collective-permute-start(f32[128,512]{1,0:T(8,128)S(1)} %get-tuple-element.244), channel_id=1, source_target_pairs={{0,4},{4,0},{8,12},{12,8},{16,20},{20,16},{24,28},{28,24},{1,5},{5... | collective-permute-start | bytes 786440 | tf_op jit(solution)/shard_map/ppermute | solution.py:506
  4.7 11.9 %collective-permute-start.2 = (f32[128,512]{1,0:T(8,128)S(1)}, f32[128,512]{1,0:T(8,128)S(1)}, u32[]{:S(2)}, u32[]{:S(2)}) collective-permute-start(f32[128,512]{1,0:T(8,128)S(1)} %get-tuple-element.243), channel_id=1, source_target_pairs={{0,4},{4,0},{8,12},{12,8},{16,20},{20,16},{24,28},{28,24},{1,5},{5... | collective-permute-start | bytes 786440 | tf_op jit(solution)/shard_map/ppermute | solution.py:506
  11.8 8.5 %collective-permute-start.1 = (f32[128,512]{1,0:T(8,128)S(1)}, f32[128,512]{1,0:T(8,128)S(1)}, u32[]{:S(2)}, u32[]{:S(2)}) collective-permute-start(f32[128,512]{1,0:T(8,128)S(1)} %collective-permute-done._.patch_0), channel_id=1, source_target_pairs={{0,8},{4,28},{8,16},{12,4},{16,24},{20,12},{24,0},{28,20},{1,9},{5... | collective-permute-start | bytes 786440 | tf_op jit(solution)/shard_map/ppermute | solution.py:506
  16.6 9.4 %collective-permute-start.3 = (f32[128,512]{1,0:T(8,128)S(1)}, f32[128,512]{1,0:T(8,128)S(1)}, u32[]{:S(2)}, u32[]{:S(2)}) collective-permute-start(f32[128,512]{1,0:T(8,128)S(1)} %collective-permute-done.2.patch_1), channel_id=1, source_target_pairs={{0,8},{4,28},{8,16},{12,4},{16,24},{20,12},{24,0},{28,20},{1,9},{5... | collective-permute-start | bytes 786440 | tf_op jit(solution)/shard_map/ppermute | solution.py:506
  32.6 12.5 %collective-permute-start.4 = (f32[256,512]{1,0:T(8,128)S(1)}, f32[256,512]{1,0:T(8,128)S(1)}, u32[]{:S(2)}, u32[]{:S(2)}) collective-permute-start(f32[256,512]{1,0:T(8,128)S(1)} %get-tuple-element.199), channel_id=1, source_target_pairs={{0,24},{4,12},{8,0},{12,20},{16,8},{20,28},{24,16},{28,4},{1,25},{... | collective-permute-start | bytes 1572872 | tf_op jit(solution)/shard_map/ppermute | solution.py:506
  43.3 2.7 %collective-permute-start.6 = (f32[512,512]{1,0:T(8,128)S(1)}, f32[512,512]{1,0:T(8,128)S(1)}, u32[]{:S(2)}, u32[]{:S(2)}) collective-permute-start(f32[512,512]{1,0:T(8,128)S(1)} %get-tuple-element.202), channel_id=1, source_target_pairs={{0,1},{1,0},{2,3},{3,2},{4,5},{5,4},{6,7},{7,6},{8,9},{9,8},{10,11... | collective-permute-start | bytes 3145736 | tf_op jit(solution)/shard_map/ppermute | solution.py:526
  43.4 4.1 %collective-permute-start.5 = (f32[512,512]{1,0:T(8,128)S(1)}, f32[512,512]{1,0:T(8,128)S(1)}, u32[]{:S(2)}, u32[]{:S(2)}) collective-permute-start(f32[512,512]{1,0:T(8,128)S(1)} %get-tuple-element.201), channel_id=1, source_target_pairs={{0,1},{1,0},{2,3},{3,2},{4,5},{5,4},{6,7},{7,6},{8,9},{9,8},{10,11... | collective-permute-start | bytes 3145736 | tf_op jit(solution)/shard_map/ppermute | solution.py:526
  47.9 11.2 %collective-permute-start.24 = (f32[192,512]{1,0:T(8,128)S(1)}, f32[192,512]{1,0:T(8,128)S(1)}, u32[]{:S(2)}, u32[]{:S(2)}) collective-permute-start(f32[192,512]{1,0:T(8,128)S(1)} %get-tuple-element.227), channel_id=1, source_target_pairs={{0,8},{1,9},{2,10},{3,11},{4,12},{5,13},{6,14},{7,15},{8,0},{9,1},... | collective-permute-start | bytes 1179656 | tf_op jit(solution)/shard_map/ppermute | solution.py:526
  48.0 12.2 %collective-permute-start.7 = (f32[160,512]{1,0:T(8,128)S(1)}, f32[160,512]{1,0:T(8,128)S(1)}, u32[]{:S(2)}, u32[]{:S(2)}) collective-permute-start(f32[160,512]{1,0:T(8,128)S(1)} %get-tuple-element.205), channel_id=1, source_target_pairs={{0,4},{1,5},{2,6},{3,7},{4,0},{5,1},{6,2},{7,3},{8,12},{9,13},{10,... | collective-permute-start | bytes 983048 | tf_op jit(solution)/shard_map/ppermute | solution.py:526
  51.1 10.8 %collective-permute-start.12 = (f32[160,512]{1,0:T(8,128)S(1)}, f32[160,512]{1,0:T(8,128)S(1)}, u32[]{:S(2)}, u32[]{:S(2)}) collective-permute-start(f32[160,512]{1,0:T(8,128)S(1)} %get-tuple-element.217), channel_id=1, source_target_pairs={{0,2},{1,3},{2,0},{3,1},{4,6},{5,7},{6,4},{7,5},{8,10},{9,11},{10,... | collective-permute-start | bytes 983048 | tf_op jit(solution)/shard_map/ppermute | solution.py:526
  59.2 6.2 %collective-permute-start.25 = (f32[96,512]{1,0:T(8,128)S(1)}, f32[96,512]{1,0:T(8,128)S(1)}, u32[]{:S(2)}, u32[]{:S(2)}) collective-permute-start(f32[96,512]{1,0:T(8,128)S(1)} %get-tuple-element.229), channel_id=1, source_target_pairs={{0,4},{1,5},{2,6},{3,7},{4,0},{5,1},{6,2},{7,3},{8,12},{9,13},{10,... | collective-permute-start | bytes 589832 | tf_op jit(solution)/shard_map/ppermute | solution.py:526
  60.3 6.7 %collective-permute-start.8 = (f32[80,512]{1,0:T(8,128)S(1)}, f32[80,512]{1,0:T(8,128)S(1)}, u32[]{:S(2)}, u32[]{:S(2)}) collective-permute-start(f32[80,512]{1,0:T(8,128)S(1)} %get-tuple-element.212), channel_id=1, source_target_pairs={{0,2},{1,3},{2,0},{3,1},{4,6},{5,7},{6,4},{7,5},{8,10},{9,11},{10,... | collective-permute-start | bytes 491528 | tf_op jit(solution)/shard_map/ppermute | solution.py:526
  61.9 5.6 %collective-permute-start.13 = (f32[80,512]{1,0:T(8,128)S(1)}, f32[80,512]{1,0:T(8,128)S(1)}, u32[]{:S(2)}, u32[]{:S(2)}) collective-permute-start(f32[80,512]{1,0:T(8,128)S(1)} %get-tuple-element.219), channel_id=1, source_target_pairs={{0,8},{1,9},{2,10},{3,11},{4,12},{5,13},{6,14},{7,15},{8,0},{9,1},... | collective-permute-start | bytes 491528 | tf_op jit(solution)/shard_map/ppermute | solution.py:526
  65.4 4.7 %collective-permute-start.26 = (f32[48,512]{1,0:T(8,128)S(1)}, f32[48,512]{1,0:T(8,128)S(1)}, u32[]{:S(2)}, u32[]{:S(2)}) collective-permute-start(f32[48,512]{1,0:T(8,128)S(1)} %get-tuple-element.231), channel_id=1, source_target_pairs={{0,2},{1,3},{2,0},{3,1},{4,6},{5,7},{6,4},{7,5},{8,10},{9,11},{10,... | collective-permute-start | bytes 294920 | tf_op jit(solution)/shard_map/ppermute | solution.py:526
  67.0 7.1 %collective-permute-start.9 = (f32[40,512]{1,0:T(8,128)S(1)}, f32[40,512]{1,0:T(8,128)S(1)}, u32[]{:S(2)}, u32[]{:S(2)}) collective-permute-start(f32[40,512]{1,0:T(8,128)S(1)} %get-tuple-element.214), channel_id=1, source_target_pairs={{0,8},{1,9},{2,10},{3,11},{4,12},{5,13},{6,14},{7,15},{8,0},{9,1},... | collective-permute-start | bytes 245768 | tf_op jit(solution)/shard_map/ppermute | solution.py:526
  67.5 5.1 %collective-permute-start.14 = (f32[40,512]{1,0:T(8,128)S(1)}, f32[40,512]{1,0:T(8,128)S(1)}, u32[]{:S(2)}, u32[]{:S(2)}) collective-permute-start(f32[40,512]{1,0:T(8,128)S(1)} %get-tuple-element.221), channel_id=1, source_target_pairs={{0,4},{1,5},{2,6},{3,7},{4,0},{5,1},{6,2},{7,3},{8,12},{9,13},{10,... | collective-permute-start | bytes 245768 | tf_op jit(solution)/shard_map/ppermute | solution.py:526
  70.1 9.4 %collective-permute-start.27 = (f32[48,512]{1,0:T(8,128)S(1)}, f32[48,512]{1,0:T(8,128)S(1)}, u32[]{:S(2)}, u32[]{:S(2)}) collective-permute-start(f32[48,512]{1,0:T(8,128)S(1)} %shard_map.175.a), channel_id=1, source_target_pairs={{0,16},{1,17},{2,18},{3,19},{4,20},{5,21},{6,22},{7,23},{8,24},{9,... | collective-permute-start | bytes 294920 | tf_op jit(solution)/shard_map/ppermute | solution.py:526
  72.6 19.7 %collective-permute-start.15 = (f32[256,512]{1,0:T(8,128)S(1)}, f32[256,512]{1,0:T(8,128)S(1)}, u32[]{:S(2)}, u32[]{:S(2)}) collective-permute-start(f32[256,512]{1,0:T(8,128)S(1)} %get-tuple-element.223), channel_id=1, source_target_pairs={{0,4},{4,0},{8,12},{12,8},{16,20},{20,16},{24,28},{28,24},{1,5},{5... | collective-permute-start | bytes 1572872 | tf_op jit(solution)/shard_map/ppermute | solution.py:506
  74.2 7.9 %collective-permute-start.10 = (f32[40,512]{1,0:T(8,128)S(1)}, f32[40,512]{1,0:T(8,128)S(1)}, u32[]{:S(2)}, u32[]{:S(2)}) collective-permute-start(f32[40,512]{1,0:T(8,128)S(1)} %shard_map.160.a), channel_id=1, source_target_pairs={{0,16},{1,17},{2,18},{3,19},{4,20},{5,21},{6,22},{7,23},{8,24},{9,... | collective-permute-start | bytes 245768 | tf_op jit(solution)/shard_map/ppermute | solution.py:526
  79.5 4.7 %collective-permute-start.28 = (f32[48,512]{1,0:T(8,128)S(1)}, f32[48,512]{1,0:T(8,128)S(1)}, u32[]{:S(2)}, u32[]{:S(2)}) collective-permute-start(f32[48,512]{1,0:T(8,128)S(1)} %shard_map.176.mine), channel_id=1, source_target_pairs={{0,2},{1,3},{2,0},{3,1},{4,6},{5,7},{6,4},{7,5},{8,10},{9,11},{10,... | collective-permute-start | bytes 294920 | tf_op jit(solution)/shard_map/ppermute | solution.py:526
  81.1 5.7 %collective-permute-start.19 = (f32[40,512]{1,0:T(8,128)S(1)}, f32[40,512]{1,0:T(8,128)S(1)}, u32[]{:S(2)}, u32[]{:S(2)}) collective-permute-start(f32[40,512]{1,0:T(8,128)S(1)} %get-tuple-element.225.a), channel_id=1, source_target_pairs={{0,16},{1,17},{2,18},{3,19},{4,20},{5,21},{6,22},{7,23},{8,24},{9,... | collective-permute-start | bytes 245768 | tf_op jit(solution)/shard_map/ppermute | solution.py:526
  82.1 7.2 %collective-permute-start.11 = (f32[40,512]{1,0:T(8,128)S(1)}, f32[40,512]{1,0:T(8,128)S(1)}, u32[]{:S(2)}, u32[]{:S(2)}) collective-permute-start(f32[40,512]{1,0:T(8,128)S(1)} %shard_map.161.mine), channel_id=1, source_target_pairs={{0,8},{1,9},{2,10},{3,11},{4,12},{5,13},{6,14},{7,15},{8,0},{9,1},... | collective-permute-start | bytes 245768 | tf_op jit(solution)/shard_map/ppermute | solution.py:526
  84.2 8.2 %collective-permute-start.29 = (f32[96,512]{1,0:T(8,128)S(1)}, f32[96,512]{1,0:T(8,128)S(1)}, u32[]{:S(2)}, u32[]{:S(2)}) collective-permute-start(f32[96,512]{1,0:T(8,128)S(1)} %shard_map.177.mine), channel_id=1, source_target_pairs={{0,4},{1,5},{2,6},{3,7},{4,0},{5,1},{6,2},{7,3},{8,12},{9,13},{10,... | collective-permute-start | bytes 589832 | tf_op jit(solution)/shard_map/ppermute | solution.py:526
  86.9 5.4 %collective-permute-start.20 = (f32[40,512]{1,0:T(8,128)S(1)}, f32[40,512]{1,0:T(8,128)S(1)}, u32[]{:S(2)}, u32[]{:S(2)}) collective-permute-start(f32[40,512]{1,0:T(8,128)S(1)} %shard_map.169.mine), channel_id=1, source_target_pairs={{0,4},{1,5},{2,6},{3,7},{4,0},{5,1},{6,2},{7,3},{8,12},{9,13},{10,... | collective-permute-start | bytes 245768 | tf_op jit(solution)/shard_map/ppermute | solution.py:526
  89.4 5.9 %collective-permute-start.16 = (f32[80,512]{1,0:T(8,128)S(1)}, f32[80,512]{1,0:T(8,128)S(1)}, u32[]{:S(2)}, u32[]{:S(2)}) collective-permute-start(f32[80,512]{1,0:T(8,128)S(1)} %shard_map.162._.mine), channel_id=1, source_target_pairs={{0,2},{1,3},{2,0},{3,1},{4,6},{5,7},{6,4},{7,5},{8,10},{9,11},{10,... | collective-permute-start | bytes 491528 | tf_op jit(solution)/shard_map/ppermute | solution.py:526
  92.3 5.4 %collective-permute-start.21 = (f32[80,512]{1,0:T(8,128)S(1)}, f32[80,512]{1,0:T(8,128)S(1)}, u32[]{:S(2)}, u32[]{:S(2)}) collective-permute-start(f32[80,512]{1,0:T(8,128)S(1)} %shard_map.170.mine), channel_id=1, source_target_pairs={{0,8},{1,9},{2,10},{3,11},{4,12},{5,13},{6,14},{7,15},{8,0},{9,1},... | collective-permute-start | bytes 491528 | tf_op jit(solution)/shard_map/ppermute | solution.py:526
  92.5 9.5 %collective-permute-start.30 = (f32[192,512]{1,0:T(8,128)S(1)}, f32[192,512]{1,0:T(8,128)S(1)}, u32[]{:S(2)}, u32[]{:S(2)}) collective-permute-start(f32[192,512]{1,0:T(8,128)S(1)} %shard_map.178.mine), channel_id=1, source_target_pairs={{0,8},{1,9},{2,10},{3,11},{4,12},{5,13},{6,14},{7,15},{8,0},{9,1},... | collective-permute-start | bytes 1179656 | tf_op jit(solution)/shard_map/ppermute | solution.py:526
  95.4 7.1 %collective-permute-start.17 = (f32[160,512]{1,0:T(8,128)S(1)}, f32[160,512]{1,0:T(8,128)S(1)}, u32[]{:S(2)}, u32[]{:S(2)}) collective-permute-start(f32[160,512]{1,0:T(8,128)S(1)} %shard_map.167.mine), channel_id=1, source_target_pairs={{0,4},{1,5},{2,6},{3,7},{4,0},{5,1},{6,2},{7,3},{8,12},{9,13},{10,... | collective-permute-start | bytes 983048 | tf_op jit(solution)/shard_map/ppermute | solution.py:526
  97.8 7.1 %collective-permute-start.22 = (f32[160,512]{1,0:T(8,128)S(1)}, f32[160,512]{1,0:T(8,128)S(1)}, u32[]{:S(2)}, u32[]{:S(2)}) collective-permute-start(f32[160,512]{1,0:T(8,128)S(1)} %shard_map.171.mine), channel_id=1, source_target_pairs={{0,2},{1,3},{2,0},{3,1},{4,6},{5,7},{6,4},{7,5},{8,10},{9,11},{10,... | collective-permute-start | bytes 983048 | tf_op jit(solution)/shard_map/ppermute | solution.py:526
  102.0 5.1 %collective-permute-start.31 = (f32[384,512]{1,0:T(8,128)S(1)}, f32[384,512]{1,0:T(8,128)S(1)}, u32[]{:S(2)}, u32[]{:S(2)}) collective-permute-start(f32[384,512]{1,0:T(8,128)S(1)} %shard_map.179.refs_2_), channel_id=1, source_target_pairs={{0,1},{1,0},{2,3},{3,2},{4,5},{5,4},{6,7},{7,6},{8,9},{9,8},{10,11... | collective-permute-start | bytes 2359304 | tf_op jit(solution)/shard_map/ppermute | solution.py:526
  102.6 3.9 %collective-permute-start.18 = (f32[320,512]{1,0:T(8,128)S(1)}, f32[320,512]{1,0:T(8,128)S(1)}, u32[]{:S(2)}, u32[]{:S(2)}) collective-permute-start(f32[320,512]{1,0:T(8,128)S(1)} %shard_map.168.refs_0_), channel_id=1, source_target_pairs={{0,1},{1,0},{2,3},{3,2},{4,5},{5,4},{6,7},{7,6},{8,9},{9,8},{10,11... | collective-permute-start | bytes 1966088 | tf_op jit(solution)/shard_map/ppermute | solution.py:526
  105.0 2.2 %collective-permute-start.23 = (f32[320,512]{1,0:T(8,128)S(1)}, f32[320,512]{1,0:T(8,128)S(1)}, u32[]{:S(2)}, u32[]{:S(2)}) collective-permute-start(f32[320,512]{1,0:T(8,128)S(1)} %shard_map.172.refs_1_), channel_id=1, source_target_pairs={{0,1},{1,0},{2,3},{3,2},{4,5},{5,4},{6,7},{7,6},{8,9},{9,8},{10,11... | collective-permute-start | bytes 1966088 | tf_op jit(solution)/shard_map/ppermute | solution.py:526
  (9 other events, 26.2 us)
